TPU v7x, 32 devices: a whole 2x2x4 slice. The times are simulated.
32 devices in a mesh: seq: 8 (over z, y), fsdp: 4 (over x, core).
Axes of the slice: x: 2, y: 2, z: 4, core: 2. Of those that a mesh axis runs over, the one named last changes fastest.
Arguments:
- tokens: bfloat16 [1024, 4096], P('seq', 'fsdp'), may hold values from -6 to 6
- in_weight: bfloat16 [3, 4096, 4096], P(None, 'seq', 'fsdp'), may hold values from -0.09375 to 0.09375
- out_weight: bfloat16 [4096, 4096], P('fsdp', 'seq'), may hold values from -0.09375 to 0.09375
- filters: float32 [4096, 128], P('fsdp'), may hold values from -0.5 to 0.5
- cotangent: bfloat16 [1024, 4096], P('seq', 'fsdp'), may hold values from -6 to 6
Outputs:
- mixed_out: bfloat16 [1024, 4096], P('seq', 'fsdp')
- grad_tokens: bfloat16 [1024, 4096], P('seq', 'fsdp')
- grad_in_weight: float32 [3, 4096, 4096], P(None, 'seq', 'fsdp')
- grad_out_weight: float32 [4096, 4096], P('fsdp', 'seq')
- grad_filters: float32 [4096, 128], P('fsdp')
All inputs are finite; a program needn't handle non-finite values.
Results may differ from a plain program's by a relative error of at most 0.018.
Values may be sent and summed in bfloat16 or wider, within the bound.
No kernel may reach another device: no remote copies, remote signals or barrier semaphores. Data moves between devices by JAX's collectives and lax.ppermute only.
A program may use at most 128 MiB of HBM per device.

v0:
```python
import jax
import jax.numpy as jnp
from jax import lax
from jax.sharding import PartitionSpec as P

highest = lax.Precision.HIGHEST


def from_behind(value, axis, by):
    length = lax.axis_size(axis)
    pairs = [(i, i + by) for i in range(length) if 0 <= i + by < length]
    return lax.ppermute(value, axis, pairs)


def causal_filter(extended, filters):
    kernel = jnp.flip(jnp.transpose(filters), 0)[:, None, :]
    result = lax.conv_general_dilated(
        extended[None],
        kernel,
        (1,),
        "VALID",
        dimension_numbers=("NWC", "WIO", "NWC"),
        feature_group_count=filters.shape[0],
        precision=highest,
    )
    return result[0]


def reverse_filter(extended, filters):
    kernel = jnp.transpose(filters)[:, None, :]
    result = lax.conv_general_dilated(
        extended[None],
        kernel,
        (1,),
        "VALID",
        dimension_numbers=("NWC", "WIO", "NWC"),
        feature_group_count=filters.shape[0],
        precision=highest,
    )
    return result[0]


def filter_grad(extended, gradient):
    result = lax.conv_general_dilated(
        extended[None],
        gradient[:, None, :],
        (1,),
        "VALID",
        dimension_numbers=("NWC", "WIO", "NWC"),
        feature_group_count=gradient.shape[1],
        precision=highest,
    )
    return jnp.transpose(jnp.flip(result[0], 0))


def on_device(tokens, in_weight, out_weight, filters, cotangent):
    margin = filters.shape[1] - 1
    gathered = lax.all_gather(tokens, "fsdp", axis=1, tiled=True)
    out_full = lax.all_gather(out_weight, "seq", axis=1, tiled=True)
    in_full = lax.all_gather(in_weight, "seq", axis=1, tiled=True)
    projected = jnp.einsum("td,idc->itc", gathered, in_full, preferred_element_type=jnp.float32)
    projected = projected.astype(jnp.bfloat16)
    queries = projected[0].astype(jnp.float32)
    key_part = projected[1].astype(jnp.float32)
    value_part = projected[2].astype(jnp.float32)
    signal = (key_part * value_part).astype(jnp.bfloat16)
    earlier = from_behind(signal[-margin:], "seq", 1)
    extended = jnp.concatenate([earlier, signal], 0).astype(jnp.float32)
    filtered = causal_filter(extended, filters)
    gated_rows = (queries * filtered).astype(jnp.bfloat16)
    partial_value = jnp.dot(gated_rows, out_full, preferred_element_type=jnp.float32)
    mixed_out = lax.psum_scatter(
        partial_value.astype(jnp.bfloat16), "fsdp", scatter_dimension=1, tiled=True
    )
    grad_full = lax.all_gather(cotangent, "fsdp", axis=1, tiled=True)
    grad_gated = lax.dot_general(
        grad_full, out_full, (((1,), (1,)), ((), ())), preferred_element_type=jnp.float32
    )
    grad_queries = grad_gated * filtered
    grad_filtered = (grad_gated * queries).astype(jnp.bfloat16)
    later_rows = from_behind(grad_filtered[:margin], "seq", -1)
    grad_signal = reverse_filter(
        jnp.concatenate([grad_filtered, later_rows], 0).astype(jnp.float32), filters
    )
    grad_filters = lax.psum(
        filter_grad(extended, grad_filtered.astype(jnp.float32)).astype(jnp.bfloat16), "seq"
    ).astype(jnp.float32)
    grad_projected = jnp.stack(
        [grad_queries, grad_signal * value_part, grad_signal * key_part]
    ).astype(jnp.bfloat16)
    grad_partial = jnp.einsum(
        "itc,idc->td", grad_projected, in_full, preferred_element_type=jnp.float32
    )
    grad_tokens = lax.psum_scatter(
        grad_partial.astype(jnp.bfloat16), "fsdp", scatter_dimension=1, tiled=True
    )
    weight_in_part = jnp.einsum(
        "td,itc->idc", gathered, grad_projected, preferred_element_type=jnp.float32
    )
    weight_out_part = lax.dot_general(
        gated_rows, grad_full, (((0,), (0,)), ((), ())), preferred_element_type=jnp.float32
    )
    grad_in_weight, grad_out_weight = (
        lax.psum_scatter(
            weight_in_part.astype(jnp.bfloat16), "seq", scatter_dimension=1, tiled=True
        ).astype(jnp.float32),
        lax.psum_scatter(
            weight_out_part.astype(jnp.bfloat16), "seq", scatter_dimension=1, tiled=True
        ).astype(jnp.float32),
    )
    return (mixed_out, grad_tokens, grad_in_weight, grad_out_weight, grad_filters)


def solution(mesh):
    placed = (
        P("seq", "fsdp"),
        P(None, "seq", "fsdp"),
        P("fsdp", "seq"),
        P("fsdp", None),
        P("seq", "fsdp"),
    )
    return jax.shard_map(
        on_device,
        mesh=mesh,
        in_specs=placed,
        out_specs=(
            P("seq", "fsdp"),
            P("seq", "fsdp"),
            P(None, "seq", "fsdp"),
            P("fsdp", "seq"),
            P("fsdp", None),
        ),
        check_vma=False,
    )
```

profile of v0, /device:TPU:0, one launch (start us, length us, event | category | flops | bytes accessed | tf_op | source)
XLA Modules:
  0.0 1397.6 jit_solution(14165653867180584064)
XLA Ops:
  7.2 0.7 all-gather.7.cloned.1.call-update
  7.9 0.7 all-gather.5.cloned.1.call-update
  8.7 0.7 all-gather.11.cloned.1.call-update
  10.0 19.0 %all-gather.7.cloned.1.call-done = bf16[128,4096]{1,0:T(8,128)(2,1)} async-done(((bf16[128,1024]{1,0:T(8,128)(2,1)}), bf16[128,4096]{1,0:T(8,128)(2,1)}) %all-gather.7.cloned.1.call-update) | async-done | bytes 1048592 | tf_op jit(solution)/shard_map/all_gather | solution.py:58
  29.0 482.0 %all-gather.5.cloned.1.call-done = bf16[3,4096,1024]{2,1,0:T(8,128)(2,1)} async-done(((bf16[3,512,1024]{2,1,0:T(8,128)(2,1)}), bf16[3,4096,1024]{2,1,0:T(8,128)(2,1)}) %all-gather.5.cloned.1.call-update) | async-done | bytes 25165840 | tf_op jit(solution)/shard_map/all_gather | solution.py:60
  511.0 12.0 fusion.1
  523.1 6.2 all-gather.11.cloned.1.call-done
  529.3 127.3 %all-gather.9.cloned.1.call-done = bf16[1024,4096]{1,0:T(8,128)(2,1)} async-done(((bf16[1024,512]{1,0:T(8,128)(2,1)}), bf16[1024,4096]{1,0:T(8,128)(2,1)}) %all-gather.9.cloned.1.call-update) | async-done | bytes 8388624 | tf_op jit(solution)/shard_map/all_gather | solution.py:59
  656.7 7.4 fusion.14
  664.1 1.3 collective-permute-start.1
  665.8 8.1 collective-permute-done.1
  674.0 5.6 fusion.4
  679.6 1.0 fusion.12
  680.7 4.6 collective-permute-start
  685.3 0.7 rev.7
  686.4 3.8 collective-permute-done
  690.3 5.6 fusion.8
  695.9 7.4 fusion.6
  703.4 2.6 rev.8
  706.1 5.6 convolution_convert_fusion
  712.0 1.2 fusion.17
  713.1 11.7 convert_bitcast_fusion
  724.9 14.1 %fusion = bf16[128,4096]{1,0:T(8,128)(2,1)} fusion(bf16[3,4096,1024]{2,1,0:T(8,128)(2,1)} %all-gather.5.cloned.1.call-done, bf16[1,128,1024]{2,1,0:T(8,128)(2,1)S(1)} %copy-done.3, bf16[1,128,1024]{2,1,0:T(8,128)(2,1)S(1)} %copy-done.2, bf16[1,128,1024]{2,1,0:T(8,128)(2,1)S(1)} %fusion.17), kind=kOutput, calls=%fused_computation.3 | convolution fusion | flops 3222536192 | bytes 27000832 | tf_op jit(solution)/shard_map/itc,idc->td/dot_general | solution.py:91
  739.1 5.7 convolution_convert_fusion.1
  744.8 31.1 %all-reduce.2.cloned.1.call-done = bf16[1024,128]{0,1:T(8,128)(2,1)} async-done(((bf16[1024,128]{0,1:T(8,128)(2,1)}), bf16[1024,128]{0,1:T(8,128)(2,1)}) %all-reduce.2.cloned.1.call-update) | async-done | bytes 262160 | tf_op jit(solution)/shard_map/psum | solution.py:85
  775.9 1.9 copy.20
  777.8 150.8 %reduce-scatter.11.cloned.1.call-done = bf16[1024,512]{1,0:T(8,128)(2,1)} async-done(((bf16[1024,4096]{1,0:T(8,128)(2,1)}), bf16[1024,512]{1,0:T(8,128)(2,1)}) %reduce-scatter.11.cloned.1.call-update) | async-done | bytes 1048592 | tf_op jit(solution)/shard_map/reduce_scatter | solution.py:107
  928.6 2.8 convert_element_type.84
  931.4 404.3 %reduce-scatter.9.cloned.1.call-done = bf16[3,512,1024]{1,2,0:T(8,128)(2,1)} async-done(((bf16[3,4096,1024]{1,2,0:T(8,128)(2,1)}), bf16[3,512,1024]{1,2,0:T(8,128)(2,1)}) %reduce-scatter.9.cloned.1.call-update) | async-done | bytes 3145744 | tf_op jit(solution)/shard_map/reduce_scatter | solution.py:104
  1335.7 5.4 copy.19
  1341.1 21.8 %reduce-scatter.7.cloned.1.call-done = bf16[128,1024]{1,0:T(8,128)(2,1)} async-done(((bf16[128,4096]{1,0:T(8,128)(2,1)}), bf16[128,1024]{1,0:T(8,128)(2,1)}) %reduce-scatter.7.cloned.1.call-update) | async-done | bytes 262160 | tf_op jit(solution)/shard_map/reduce_scatter | solution.py:94
  1362.9 28.2 %reduce-scatter.5.cloned.1.call-done = bf16[128,1024]{1,0:T(8,128)(2,1)} async-done(((bf16[128,4096]{1,0:T(8,128)(2,1)}), bf16[128,1024]{1,0:T(8,128)(2,1)}) %reduce-scatter.5.cloned.1.call-update) | async-done | bytes 262160 | tf_op jit(solution)/shard_map/reduce_scatter | solution.py:72
  (31 shorter events, 2.3 us)
Async XLA Ops:
  7.2 21.9 %all-gather.7.cloned.1.call-start = ((), (), s32[]{:S(2)}) async-start(), calls=%async_computation.5 | async-start | bytes 1310720 | tf_op jit(solution)/shard_map/all_gather | solution.py:58
  7.9 503.1 %all-gather.5.cloned.1.call-start = ((), (), s32[]{:S(2)}) async-start(), calls=%async_computation.4 | async-start | bytes 28311552 | tf_op jit(solution)/shard_map/all_gather | solution.py:60
  8.7 520.7 %all-gather.11.cloned.1.call-start = ((), (), s32[]{:S(2)}) async-start(), calls=%async_computation.8 | async-start | bytes 1310720 | tf_op jit(solution)/shard_map/all_gather | solution.py:75
  9.4 647.3 %all-gather.9.cloned.1.call-start = ((), (), s32[]{:S(2)}) async-start(), calls=%async_computation.6 | async-start | bytes 9437184 | tf_op jit(solution)/shard_map/all_gather | solution.py:59
  10.0 765.9 %all-reduce.2.cloned.1.call-start = ((), (), s32[]{:S(2)}) async-start(), calls=%async_computation.12 | async-start | bytes 524288 | tf_op jit(solution)/shard_map/psum | solution.py:85
  523.1 142.3 %copy-start.4 = (f32[1024,128]{1,0:T(8,128)S(1)}, f32[1024,128]{1,0:T(8,128)}, u32[]{:S(2)}) copy-start(f32[1024,128]{1,0:T(8,128)} %param.8) | copy-start | bytes 1572868
  664.1 9.9 collective-permute-start.1
  680.7 9.5 collective-permute-start
  695.9 10.2 copy-start.1
  706.0 7.1 copy-start
  706.0 222.5 %reduce-scatter.11.cloned.1.call-start = ((), (), s32[]{:S(2)}) async-start(), calls=%async_computation.11 | async-start | bytes 9437184 | tf_op jit(solution)/shard_map/reduce_scatter | solution.py:107
  711.7 1.4 copy-start.2
  711.7 1.4 copy-start.3
  711.7 624.0 %reduce-scatter.9.cloned.1.call-start = ((), (), s32[]{:S(2)}) async-start(), calls=%async_computation.10 | async-start | bytes 28311552 | tf_op jit(solution)/shard_map/reduce_scatter | solution.py:104
  724.9 638.0 %reduce-scatter.7.cloned.1.call-start = ((), (), s32[]{:S(2)}) async-start(), calls=%async_computation.9 | async-start | bytes 1310720 | tf_op jit(solution)/shard_map/reduce_scatter | solution.py:94
  739.0 652.1 %reduce-scatter.5.cloned.1.call-start = ((), (), s32[]{:S(2)}) async-start(), calls=%async_computation.7 | async-start | bytes 1310720 | tf_op jit(solution)/shard_map/reduce_scatter | solution.py:72
Sparse Core Ops, SparseCore 0:
  9.6 19.4 all-gather.6
  30.6 480.4 all-gather.4
  512.6 16.6 all-gather.10
  531.2 125.3 all-gather.8
  706.1 69.7 all-reduce.1
  779.8 148.7 reduce-scatter.10
  932.5 403.2 reduce-scatter.8
  1338.8 24.0 reduce-scatter.6
  1366.2 24.8 reduce-scatter.4
where the time goes:
time: 1400 us
  waiting for transfers between devices  1290 us (92%)
  matrix products  75.1 us (5%)
  between operations  14 us (1%)
    all_gather x1, waiting for transfers between devices, on_device(): in_full = lax.all_gather(in_weight, 'seq', axis=1, tiled=True)  482 us
    reduce_scatter x1, waiting for transfers between devices, on_device(): lax.psum_scatter(weight_in_part.astype(jnp.bfloat16), 'seq', scatter_dime...  404 us
    reduce_scatter x1, waiting for transfers between devices, on_device(): lax.psum_scatter(weight_out_part.astype(jnp.bfloat16), 'seq', scatter_dim...  151 us
    all_gather x1, waiting for transfers between devices, on_device(): out_full = lax.all_gather(out_weight, 'seq', axis=1, tiled=True)  127 us
    psum x1, waiting for transfers between devices, on_device(): lax.psum(filter_grad(extended, grad_filtered.astype(jnp.float32)).astype(...  31.1 us
    reduce_scatter x1, waiting for transfers between devices, on_device(): lax.psum_scatter(partial_value.astype(jnp.bfloat16), 'fsdp', scatter_dime...  28.2 us
  transfers between devices with their start and end apart: 11, of which 11 were waited for; matrix products, arithmetic and copies ran while one was open for 4% of the time, Pallas kernels for 0%

commit v1 on v0

v1 whole, which is shorter than its diff:
```python
import jax
import jax.numpy as jnp
from jax import lax
from jax.sharding import PartitionSpec as P

highest = lax.Precision.HIGHEST


def from_behind(value, axis, by):
    length = lax.axis_size(axis)
    pairs = [(i, i + by) for i in range(length) if 0 <= i + by < length]
    return lax.ppermute(value, axis, pairs)


def causal_filter(extended, filters):
    kernel = jnp.flip(jnp.transpose(filters), 0)[:, None, :]
    result = lax.conv_general_dilated(
        extended[None],
        kernel,
        (1,),
        "VALID",
        dimension_numbers=("NWC", "WIO", "NWC"),
        feature_group_count=filters.shape[0],
        precision=highest,
    )
    return result[0]


def reverse_filter(extended, filters):
    kernel = jnp.transpose(filters)[:, None, :]
    result = lax.conv_general_dilated(
        extended[None],
        kernel,
        (1,),
        "VALID",
        dimension_numbers=("NWC", "WIO", "NWC"),
        feature_group_count=filters.shape[0],
        precision=highest,
    )
    return result[0]


def filter_grad(extended, gradient):
    result = lax.conv_general_dilated(
        extended[None],
        gradient[:, None, :],
        (1,),
        "VALID",
        dimension_numbers=("NWC", "WIO", "NWC"),
        feature_group_count=gradient.shape[1],
        precision=highest,
    )
    return jnp.transpose(jnp.flip(result[0], 0))


def to_feature_rows(value):
    wide = lax.all_gather(value, "fsdp", axis=value.ndim - 1, tiled=True)
    return lax.all_to_all(wide, "seq", split_axis=wide.ndim - 1, concat_axis=wide.ndim - 2, tiled=True)


def to_token_rows(partial):
    swapped = lax.all_to_all(
        partial, "seq", split_axis=partial.ndim - 2, concat_axis=partial.ndim - 1, tiled=True
    )
    return lax.psum_scatter(swapped, "fsdp", scatter_dimension=partial.ndim - 1, tiled=True)


def on_device(tokens, in_weight, out_weight, filters, cotangent):
    taps = filters.shape[1]
    margin = taps - 1
    activations = to_feature_rows(jnp.stack([tokens, cotangent]))
    features, cot_rows = activations[0], activations[1]
    projected_part = jnp.einsum(
        "td,idc->itc", features, in_weight, preferred_element_type=jnp.float32
    ).astype(jnp.bfloat16)
    gated_part = lax.dot_general(
        cot_rows, out_weight, (((1,), (1,)), ((), ())), preferred_element_type=jnp.float32
    ).astype(jnp.bfloat16)
    summed = lax.psum_scatter(
        jnp.concatenate([projected_part, gated_part[None]], 0),
        "seq",
        scatter_dimension=2,
        tiled=True,
    ).astype(jnp.float32)
    queries, key_part, value_part, grad_gated = summed[0], summed[1], summed[2], summed[3]
    channels = queries.shape[1]
    own_filters = lax.dynamic_slice_in_dim(
        filters, lax.axis_index("seq") * channels, channels, 0
    )
    signal = (key_part * value_part).astype(jnp.bfloat16)
    extended = jnp.pad(signal, ((margin, 0), (0, 0))).astype(jnp.float32)
    filtered = causal_filter(extended, own_filters)
    gated = (queries * filtered).astype(jnp.bfloat16)
    grad_queries = grad_gated * filtered
    grad_filtered = (grad_gated * queries).astype(jnp.bfloat16)
    grad_signal = reverse_filter(
        jnp.pad(grad_filtered, ((0, margin), (0, 0))).astype(jnp.float32), own_filters
    )
    own_grad_filters = filter_grad(extended, grad_filtered.astype(jnp.float32))
    grad_projected = jnp.stack(
        [grad_queries, grad_signal * value_part, grad_signal * key_part]
    ).astype(jnp.bfloat16)
    rows = lax.all_gather(
        jnp.concatenate([grad_projected, gated[None]], 0), "seq", axis=2, tiled=True
    )
    grad_filters = lax.all_gather(own_grad_filters, "seq", axis=0, tiled=True)
    mixed_part = jnp.dot(rows[3], out_weight, preferred_element_type=jnp.float32)
    grad_part = jnp.einsum(
        "itc,idc->td", rows[:3], in_weight, preferred_element_type=jnp.float32
    )
    outward = to_token_rows(jnp.stack([mixed_part, grad_part]).astype(jnp.bfloat16))
    grad_in_weight = jnp.einsum(
        "td,itc->idc", features, rows[:3], preferred_element_type=jnp.float32
    )
    grad_out_weight = lax.dot_general(
        rows[3], cot_rows, (((0,), (0,)), ((), ())), preferred_element_type=jnp.float32
    )
    return (outward[0], outward[1], grad_in_weight, grad_out_weight, grad_filters)


def solution(mesh):
    placed = (
        P("seq", "fsdp"),
        P(None, "seq", "fsdp"),
        P("fsdp", "seq"),
        P("fsdp", None),
        P("seq", "fsdp"),
    )
    return jax.shard_map(
        on_device,
        mesh=mesh,
        in_specs=placed,
        out_specs=(
            P("seq", "fsdp"),
            P("seq", "fsdp"),
            P(None, "seq", "fsdp"),
            P("fsdp", "seq"),
            P("fsdp", None),
        ),
        check_vma=False,
    )
```

time: 1400 us -> 589 us (0.42)
  waiting for transfers between devices: 1290 us -> 296 us
  blocking collectives: 0 us -> 139 us
  local copies, waits for them, and re-layouts: 11.6 us -> 68.6 us
  matrix products: 75.1 us -> 49.8 us
    reduce_scatter x4 -> x1, waiting for transfers between devices: 605 us -> 0.01 us  [to_token_rows(): lax.psum_scatter(swapped, 'fsdp', scatter_dimension=partial.ndim - 1, til...]
    all_gather x4 -> x2, waiting for transfers between devices: 635 us -> 151 us  [the longest x1 124 us: on_device(): lax.all_gather(jnp.concatenate([grad_projected, gated[None]], 0), 'seq',...]
    unnamed x9 -> x5, waiting for transfers between devices: 2.66 us -> 146 us
    all_to_all x0 -> x2, blocking collectives: none -> 105 us  [the longest x1 54.2 us: to_feature_rows(): lax.all_to_all(wide, 'seq', split_axis=wide.ndim - 1, concat_axis=wide.nd...]
    unnamed x13 -> x23, local copies, waits for them, and re-layouts: 7.37 us -> 41.6 us
    all_gather x0 -> x1, blocking collectives: none -> 33.3 us  [on_device(): grad_filters = lax.all_gather(own_grad_filters, 'seq', axis=0, tiled=True)]
    psum x1 -> x0, waiting for transfers between devices: 31.1 us -> none  [on_device(): lax.psum(filter_grad(extended, grad_filtered.astype(jnp.float32)).astype(...]
    dot_general x6, matrix products: 56.5 us -> 29.4 us  [the longest x1 9.22 us: on_device(): jnp.einsum('td,itc->idc', features, rows[:3], preferred_element_type=jnp....]
  transfers between devices with their start and end apart: 11 -> 4, of which waited for: 11 -> 3; matrix products, arithmetic and copies ran while one was open for 4% -> 5% of each run, Pallas kernels for 0% -> 0%
where the time goes in v1:
time: 589 us; the launch traced here: 580 us
  waiting for transfers between devices  296 us (50%)
  blocking collectives  139 us (24%)
  local copies, waits for them, and re-layouts  68.6 us (12%)
  matrix products  49.8 us (8%)
  between operations  14.5 us (2%)
  other arithmetic  11.7 us (2%)
    unnamed x5, waiting for transfers between devices  146 us
    all_gather x1, waiting for transfers between devices, on_device(): lax.all_gather(jnp.concatenate([grad_projected, gated[None]], 0), 'seq',...  124 us
    all_to_all x1, blocking collectives, to_feature_rows(): lax.all_to_all(wide, 'seq', split_axis=wide.ndim - 1, concat_axis=wide.nd...  54.2 us
    all_to_all x1, blocking collectives, to_token_rows(): lax.all_to_all(partial, 'seq', split_axis=partial.ndim - 2, concat_axis=p...  51.2 us
    unnamed x23, local copies, waits for them, and re-layouts  41.6 us
    all_gather x1, blocking collectives, on_device(): grad_filters = lax.all_gather(own_grad_filters, 'seq', axis=0, tiled=True)  33.3 us
    all_gather x1, waiting for transfers between devices, to_feature_rows(): wide = lax.all_gather(value, 'fsdp', axis=value.ndim - 1, tiled=True)  26.1 us
  transfers between devices with their start and end apart: 4, of which 3 were waited for; matrix products, arithmetic and copies ran while one was open for 5% of the time, Pallas kernels for 0%

profile of v1, /device:TPU:0, one launch (start us, length us, event | category | flops | bytes accessed | tf_op | source)
XLA Modules:
  0.0 579.8 jit_solution(6055241084623649195)
XLA Ops:
  7.2 2.0 pad_maximum_fusion.3
  9.3 26.1 %all-gather.3.cloned.1.call-done = bf16[2,128,4096]{2,1,0:T(8,128)(2,1)} async-done(((bf16[2,128,1024]{2,1,0:T(8,128)(2,1)}), bf16[2,128,4096]{2,1,0:T(8,128)(2,1)}) %all-gather.3.cloned.1.call-update) | async-done | bytes 2097168 | tf_op jit(solution)/shard_map/all_gather | solution.py:57
  35.5 6.2 %copy.37 = bf16[2,128,4096]{1,0,2:T(2,128)(2,1)} copy(bf16[2,128,4096]{2,1,0:T(8,128)(2,1)} %all-gather.3.cloned.1.call-done) | data formatting | bytes 4194304 | tf_op jit(solution)/shard_map/all_gather | solution.py:57
  41.6 54.2 %all_to_all.33 = bf16[2,128,4096]{1,0,2:T(2,128)(2,1)} all-to-all(bf16[2,128,4096]{1,0,2:T(2,128)(2,1)} %copy.37), channel_id=1, replica_groups=mesh['seq'=8,'fsdp'=4] {'seq'}, dimensions={2} | all-to-all | bytes 4194304 | tf_op jit(solution)/shard_map/all_to_all | solution.py:58
  95.8 6.1 %copy.38 = bf16[2,128,8,512]{3,1,2,0:T(8,128)(2,1)} copy(bf16[2,128,8,512]{1,0,3,2:T(2,128)(2,1)} %bitcast.84) | data formatting | bytes 4194304 | tf_op jit(solution)/shard_map/all_to_all | solution.py:58
  102.0 1.8 fusion.31
  103.9 1.3 convert_bitcast_fusion.1
  105.2 5.3 convert_bitcast_fusion
  110.5 6.7 %pad_maximum_fusion = bf16[4,1024,1024]{2,1,0:T(8,128)(2,1)} fusion(bf16[1,1024,1024]{2,1,0:T(8,128)(2,1)S(1)} %convert_bitcast_fusion.1, bf16[3,1024,1024]{2,1,0:T(8,128)(2,1)} %convert_bitcast_fusion), kind=kLoop, calls=%fused_computation | loop fusion | flops 4194304 | bytes 16777216 | tf_op jit(solution)/shard_map/concatenate | solution.py:80
  117.2 14.9 %copy.55 = bf16[4,1024,1024]{1,0,2:T(4,128)(2,1)} copy(bf16[4,1024,1024]{2,1,0:T(8,128)(2,1)} %pad_maximum_fusion) | data formatting | bytes 16777216
  132.1 12.1 %copy.58 = bf16[128,8,4,1024]{3,1,2,0:T(8,128)(2,1)} copy(bf16[128,8,4,1024]{3,2,1,0:T(4,128)(2,1)} %bitcast.82) | data formatting | bytes 16777216
  145.9 145.7 %reduce-scatter.7.cloned.1.call-done = bf16[128,4096]{1,0:T(8,128)(2,1)} async-done(((bf16[1024,4096]{1,0:T(8,128)(2,1)}), bf16[128,4096]{1,0:T(8,128)(2,1)}) %reduce-scatter.7.cloned.1.call-update) | async-done | bytes 1048592
  291.6 2.6 reshape.63
  294.2 2.8 copy.56
  297.0 1.4 convert_element_type.50
  299.2 6.2 %convolution_select_fusion.1 = f32[8,144,128]{2,0,1:T(8,128)S(1)} fusion(f32[128,1,128]{2,1,0:T(1,128)S(1)} %bitcast.102, bf16[1,7,127,128]{3,1,2,0:T(8,128)(2,1)S(1)} %slice.53, bf16[1,8,144,128]{3,1,2,0:T(8,128)(2,1)S(1)} %copy.40, pred[8,144]{0,1:T(8,128)(4,1)S(1)} %copy-done.7), kind=kOutput, calls=%fused_computation.13 | convolution fusion | flops 228304896 | bytes 1179008 | tf_op jit(solution)/shard_map/conv_general_dilated | solution.py:17
  305.8 6.4 %convolution_select_fusion = f32[8,144,128]{2,0,1:T(8,128)S(1)} fusion(f32[128,1,128]{2,1,0:T(1,128)S(1)} %bitcast.99, bf16[1,7,127,128]{3,1,2,0:T(8,128)(2,1)S(1)} %slice.56, bf16[1,8,144,128]{3,1,2,0:T(8,128)(2,1)S(1)} %copy.45, pred[8,144]{0,1:T(8,128)(4,1)S(1)} %copy-done.7), kind=kOutput, calls=%fused_computation.12 | convolution fusion | flops 228304896 | bytes 1179008 | tf_op jit(solution)/shard_map/conv_general_dilated | solution.py:31
  312.5 1.1 pad_maximum_fusion.2
  313.7 124.5 %all-gather.5.cloned.1.call-done = bf16[4,1024,1024]{2,1,0:T(8,128)(2,1)} async-done(((bf16[4,1024,128]{2,1,0:T(8,128)(2,1)}), bf16[4,1024,1024]{2,1,0:T(8,128)(2,1)}) %all-gather.5.cloned.1.call-update) | async-done | bytes 8388624 | tf_op jit(solution)/shard_map/all_gather | solution.py:103
  438.2 6.3 %fusion.4 = bf16[1,1024,512]{2,1,0:T(8,128)(2,1)S(1)} fusion(bf16[4,1024,1024]{2,1,0:T(8,128)(2,1)} %all-gather.5.cloned.1.call-done, bf16[3,512,1024]{2,1,0:T(8,128)(2,1)S(1)} %copy-done), kind=kOutput, calls=%fused_computation.11 | convolution fusion | flops 3221749760 | bytes 12582912 | tf_op jit(solution)/shard_map/itc,idc->td/dot_general | solution.py:108
  444.5 2.8 fusion.3
  447.6 2.2 copy.47
  449.8 51.2 %all_to_all.34 = bf16[2,1024,512]{2,0,1:T(2,128)(2,1)S(1)} all-to-all(bf16[2,1024,512]{2,0,1:T(2,128)(2,1)S(1)} %copy.47), channel_id=1, replica_groups=mesh['seq'=8,'fsdp'=4] {'seq'}, dimensions={1} | all-to-all | bytes 4194304 | tf_op jit(solution)/shard_map/all_to_all | solution.py:62
  500.9 2.5 copy.48
  503.4 4.2 all_to_all.30
  507.7 7.7 %fusion.7 = f32[1,128,128]{2,0,1:T(1,128)S(1)} fusion(bf16[1,1151,128]{2,1,0:T(8,128)(2,1)S(1)} %pad_bitcast_fusion.1, bf16[1024,1,128]{2,0,1:T(8,128)(2,1)} %bitcast.92), kind=kOutput, calls=%fused_computation.18 | convolution fusion | flops 33554432 | bytes 622336 | tf_op jit(solution)/shard_map/conv_general_dilated | solution.py:44
  515.4 33.3 %all_gather.11 = f32[1024,128]{0,1:T(8,128)} all-gather(f32[128,128]{0,1:T(8,128)S(1)} %bitcast.97), channel_id=1, replica_groups=mesh['seq'=8,'fsdp'=4] {'seq'}, dimensions={0}, use_global_device_ids=true | all-gather | bytes 589824 | tf_op jit(solution)/shard_map/all_gather | solution.py:106
  548.7 2.0 copy.53
  550.7 9.2 %convolution_bitcast_fusion = f32[3,512,1024]{1,2,0:T(8,128)} fusion(bf16[4,1024,1024]{2,1,0:T(8,128)(2,1)} %all-gather.5.cloned.1.call-done, bf16[1024,512,1]{1,0,2:T(8,128)(2,1)} %bitcast.96), kind=kOutput, calls=%fused_computation.2 | convolution fusion | flops 3221225472 | bytes 15728640 | tf_op jit(solution)/shard_map/td,itc->idc/dot_general | solution.py:112
  560.0 6.6 %copy.52 = f32[3,512,1024]{2,1,0:T(8,128)} copy(f32[3,512,1024]{1,2,0:T(8,128)} %convolution_bitcast_fusion) | data formatting | bytes 12582912
  566.5 4.5 fusion
  571.0 1.9 slice_bitcast_fusion.7
  (42 shorter events, 3.4 us)
Async XLA Ops:
  7.2 98.0 %copy-start = (bf16[3,512,1024]{2,1,0:T(8,128)(2,1)S(1)}, bf16[3,512,1024]{2,1,0:T(8,128)(2,1)}, u32[]{:S(2)}) copy-start(bf16[3,512,1024]{2,1,0:T(8,128)(2,1)} %param.6) | copy-start | bytes 9437188
  7.2 28.3 %all-gather.3.cloned.1.call-start = ((), (), s32[]{:S(2)}) async-start(), calls=%async_computation.4 | async-start | bytes 2621440 | tf_op jit(solution)/shard_map/all_gather | solution.py:57
  9.3 282.3 %reduce-scatter.7.cloned.1.call-start = ((), (), s32[]{:S(2)}) async-start(), calls=%async_computation.7 | async-start | bytes 9437184
  102.0 1.9 copy-start.5
  103.8 1.3 copy-start.2
  103.8 1.3 copy-start.3
  144.3 293.9 %all-gather.5.cloned.1.call-start = ((), (), s32[]{:S(2)}) async-start(), calls=%async_computation.5 | async-start | bytes 9437184 | tf_op jit(solution)/shard_map/all_gather | solution.py:103
  298.4 0.8 copy-start.4
  298.4 0.8 copy-start.7
  298.5 7.0 %copy-start.1 = (bf16[1,1024,128]{2,1,0:T(8,128)(2,1)}, bf16[1,1024,128]{2,1,0:T(8,128)(2,1)S(1)}, u32[]{:S(2)}) copy-start(bf16[1,1024,128]{2,1,0:T(8,128)(2,1)S(1)} %get-tuple-element.26) | copy-start | bytes 786436
  313.7 257.3 %reduce-scatter.5.cloned.1.call-start = ((), (), s32[]{:S(2)}) async-start(), calls=%async_computation.6 | async-start | bytes 2621440 | tf_op jit(solution)/shard_map/reduce_scatter | solution.py:65
  438.2 6.3 %copy-start.6 = (bf16[1024,512]{1,0:T(8,128)(2,1)S(1)}, bf16[1024,512]{1,0:T(8,128)(2,1)}, u32[]{:S(2)}) copy-start(bf16[1024,512]{1,0:T(8,128)(2,1)} %param.7) | copy-start | bytes 3145732
Sparse Core Ops, SparseCore 0:
  10.2 25.2 all-gather.2
  144.4 147.1 reduce-scatter.6
  313.8 124.3 all-gather.4
  507.8 30.4 reduce-scatter.4

commit v2 on v1

--- a/solution.py
+++ b/solution.py
@@ -1,15 +1,16 @@
 import jax
 import jax.numpy as jnp
 from jax import lax
+from jax.experimental import pallas as pl
+from jax.experimental.pallas import tpu as pltpu
 from jax.sharding import PartitionSpec as P
 
 highest = lax.Precision.HIGHEST
-
-
-def from_behind(value, axis, by):
-    length = lax.axis_size(axis)
-    pairs = [(i, i + by) for i in range(length) if 0 <= i + by < length]
-    return lax.ppermute(value, axis, pairs)
+bf16 = jnp.bfloat16
+f32 = jnp.float32
+lanes = 128
+sublanes = 8
+vmem_bytes = 48 * 1024 * 1024
 
 
 def causal_filter(extended, filters):
@@ -65,7 +66,7 @@
     return lax.psum_scatter(swapped, "fsdp", scatter_dimension=partial.ndim - 1, tiled=True)
 
 
-def on_device(tokens, in_weight, out_weight, filters, cotangent):
+def on_any_mesh(tokens, in_weight, out_weight, filters, cotangent):
     taps = filters.shape[1]
     margin = taps - 1
     activations = to_feature_rows(jnp.stack([tokens, cotangent]))
@@ -118,6 +119,709 @@
     return (outward[0], outward[1], grad_in_weight, grad_out_weight, grad_filters)
 
 
+def params(**more):
+    return pltpu.CompilerParams(vmem_limit_bytes=vmem_bytes, **more)
+
+
+def cost(flops, moved):
+    return pl.CostEstimate(flops=flops, bytes_accessed=moved, transcendentals=0)
+
+
+def flip(value, axis, bit):
+    return lax.ppermute(value, axis, [(i, i ^ bit) for i in range(lax.axis_size(axis))])
+
+
+def trade_places(value):
+    size = lax.axis_size("fsdp")
+    pairs = [
+        ((2 * line + pair) * size + own, (2 * own + pair) * size + line)
+        for line in range(size)
+        for pair in range(2)
+        for own in range(size)
+    ]
+    return lax.ppermute(value, ("seq", "fsdp"), pairs)
+
+
+def along_line(value, by, holds):
+    length = lax.axis_size("seq") // 2
+    pairs = [
+        (2 * i + pair, 2 * (i + by) + pair)
+        for i in range(length)
+        for pair in range(2)
+        if 0 <= i + by < length and holds(i)
+    ]
+    return lax.ppermute(value, "seq", pairs)
+
+
+def added(one, other):
+    return (one.astype(f32) + other.astype(f32)).astype(bf16)
+
+
+def line_scatter(blocks):
+    length = blocks.shape[0]
+    up, down = blocks[length - 1], blocks[1]
+    for step in range(1, length):
+        up_in = along_line(up, 1, lambda i: i <= step - 1)
+        down_in = along_line(down, -1, lambda i: i >= length - step)
+        if step < length - 1:
+            up = added(blocks[length - 1 - step], up_in)
+            down = added(blocks[1 + step], down_in)
+    return up_in, down_in
+
+
+def line_gather(block):
+    length = lax.axis_size("seq") // 2
+    before, after = [], []
+    up = down = block
+    for step in range(1, length):
+        up = along_line(up, 1, lambda i: i >= step - 1)
+        down = along_line(down, -1, lambda i: i <= length - step)
+        before.append(up)
+        after.append(down)
+    return before, after
+
+
+def project_pair(place, first, second):
+    tokens, width = first[0].shape
+    half = width // 2
+    rows = 256
+    count = half // lanes
+
+    def body(place_ref, *refs):
+        out = refs[-1]
+        line = place_ref[0]
+        for which in range(2):
+            own, other, kept, given = refs[4 * which : 4 * which + 4]
+            turned = (first, second)[which][3]
+            dims = (((1,), (1,)), ((), ())) if turned else (((1,), (0,)), ((), ()))
+            kept_value = kept[...].reshape(half, half)
+            given_value = given[...].reshape(half, half)
+            result = lax.dot_general(own[...], kept_value, dims, preferred_element_type=f32)
+            result += lax.dot_general(other[...], given_value, dims, preferred_element_type=f32)
+            result = result.astype(bf16)
+            for j in range(count):
+                out[lax.rem(j - line + count, count), which] = result[:, j * lanes : (j + 1) * lanes]
+
+    operands, specs = [], []
+    for value, kept, given, turned, index in (first, second):
+        operands += [value, value, kept, given]
+        specs += [
+            pl.BlockSpec((rows, half), lambda g, place: (g, place[1])),
+            pl.BlockSpec((rows, half), lambda g, place: (g, 1 - place[1])),
+        ]
+        if turned:
+            specs += [
+                pl.BlockSpec((half, half), lambda g, place: (place[1], 0)),
+                pl.BlockSpec((half, half), lambda g, place: (0, 0)),
+            ]
+        else:
+            specs += [
+                pl.BlockSpec((1, half, half), lambda g, place, index=index: (index, 0, place[1])),
+                pl.BlockSpec((half, half), lambda g, place: (0, 0)),
+            ]
+    return pl.pallas_call(
+        body,
+        out_shape=jax.ShapeDtypeStruct((count, 2, tokens, lanes), bf16),
+        grid_spec=pltpu.PrefetchScalarGridSpec(
+            num_scalar_prefetch=1,
+            grid=(tokens // rows,),
+            in_specs=specs,
+            out_specs=pl.BlockSpec((count, 2, rows, lanes), lambda g, place: (0, 0, g, 0)),
+        ),
+        compiler_params=params(),
+        cost_estimate=cost(4 * tokens * width * half, 8 * tokens * width),
+        name="project_pair",
+    )(place, *operands)
+
+
+def block_rows(order, r, size):
+    return pl.ds(pl.multiple_of(order[r] * size, size), size)
+
+
+def window_filter(load, tap, tiles, reach):
+    steps = range(reach // sublanes)
+    sums = [jnp.zeros((sublanes, lanes), f32) for _ in range(tiles)]
+    for shift in range(sublanes):
+        held = {}
+        for q in steps:
+            weight = tap(shift, q)
+            for i in range(tiles):
+                if i - q not in held:
+                    held[i - q] = load(shift, i - q)
+                sums[i] = sums[i] + weight * held[i - q]
+    return sums
+
+
+def own_sum(blocks, up, down, which, rows):
+    return (
+        blocks[0, which, rows, :].astype(f32)
+        + up[which, rows, :].astype(f32)
+        + down[which, rows, :].astype(f32)
+    ).astype(bf16)
+
+
+def forward_filter(order, blocks, up, down, spread_taps):
+    tokens = up.shape[1]
+    taps = spread_taps.shape[0] // sublanes
+    n_blocks = order.shape[0]
+    size = tokens // n_blocks
+    tiles = 8
+
+    def body(order_ref, blocks_ref, up_ref, down_ref, taps_ref, kv_ref, signal_ref, filtered_ref, moved):
+        for shift in range(sublanes):
+            moved[shift, : taps + sublanes, :] = jnp.zeros((taps + sublanes, lanes), f32)
+
+        def one_block(r, carry):
+            rows = pl.ds(pl.multiple_of(r * size, size), size)
+            place = block_rows(order_ref, r, size)
+            key_part = own_sum(blocks_ref, up_ref, down_ref, 0, rows)
+            value_part = own_sum(blocks_ref, up_ref, down_ref, 1, rows)
+            kv_ref[0, place, :] = key_part
+            kv_ref[1, place, :] = value_part
+            product = (key_part.astype(f32) * value_part.astype(f32)).astype(bf16)
+            signal_ref[place, :] = product
+            moved[0, pl.ds(pl.multiple_of(taps + order_ref[r] * size, size), size), :] = product.astype(f32)
+            return carry
+
+        lax.fori_loop(0, n_blocks, one_block, 0)
+        for shift in range(1, sublanes):
+            moved[shift, taps : taps + tokens, :] = moved[0, taps - shift : taps - shift + tokens, :]
+
+        def run(g, carry):
+            start = pl.multiple_of(g * tiles * sublanes, tiles * sublanes)
+
+            def load(shift, at):
+                return moved[shift, pl.ds(start + taps + at * sublanes, sublanes), :]
+
+            def tap(shift, q):
+                index = q * sublanes + shift
+                return taps_ref[index * sublanes : (index + 1) * sublanes, :]
+
+            sums = window_filter(load, tap, tiles, taps)
+            for i in range(tiles):
+                filtered_ref[pl.ds(start + i * sublanes, sublanes), :] = sums[i]
+            return carry
+
+        lax.fori_loop(0, tokens // (tiles * sublanes), run, 0)
+
+    whole = lambda shape: pl.BlockSpec(shape, lambda g, order: (0,) * len(shape))
+    return pl.pallas_call(
+        body,
+        out_shape=(
+            jax.ShapeDtypeStruct((2, tokens, lanes), bf16),
+            jax.ShapeDtypeStruct((tokens, lanes), bf16),
+            jax.ShapeDtypeStruct((tokens, lanes), f32),
+        ),
+        grid_spec=pltpu.PrefetchScalarGridSpec(
+            num_scalar_prefetch=1,
+            grid=(1,),
+            in_specs=[
+                whole((1, 2, tokens, lanes)),
+                whole((2, tokens, lanes)),
+                whole((2, tokens, lanes)),
+                whole(spread_taps.shape),
+            ],
+            out_specs=(
+                whole((2, tokens, lanes)),
+                whole((tokens, lanes)),
+                whole((tokens, lanes)),
+            ),
+            scratch_shapes=[pltpu.VMEM((sublanes, taps + tokens, lanes), f32)],
+        ),
+        compiler_params=params(),
+        cost_estimate=cost(400 * tokens * lanes * taps, 12 * tokens * lanes),
+        name="forward_filter",
+    )(order, blocks, up, down, spread_taps)
+
+
+def gate_rows(order, blocks, up, down, filtered):
+    tokens = up.shape[1]
+    n_blocks = order.shape[0]
+    size = tokens // n_blocks
+
+    def body(order_ref, blocks_ref, up_ref, down_ref, filtered_ref, out_ref, grad_ref):
+        def one_block(r, carry):
+            rows = pl.ds(pl.multiple_of(r * size, size), size)
+            place = block_rows(order_ref, r, size)
+            queries = own_sum(blocks_ref, up_ref, down_ref, 0, rows).astype(f32)
+            grad_gated = (
+                blocks_ref[0, 1, rows, :].astype(f32)
+                + up_ref[1, rows, :].astype(f32)
+                + down_ref[1, rows, :].astype(f32)
+            )
+            kept = filtered_ref[place, :]
+            out_ref[0, rows, :] = (queries * kept).astype(bf16)
+            out_ref[1, rows, :] = (grad_gated * kept).astype(bf16)
+            grad_ref[place, :] = (grad_gated * queries).astype(bf16)
+            return carry
+
+        lax.fori_loop(0, n_blocks, one_block, 0)
+
+    whole = lambda shape: pl.BlockSpec(shape, lambda g, order: (0,) * len(shape))
+    return pl.pallas_call(
+        body,
+        out_shape=(
+            jax.ShapeDtypeStruct((2, tokens, lanes), bf16),
+            jax.ShapeDtypeStruct((tokens, lanes), bf16),
+        ),
+        grid_spec=pltpu.PrefetchScalarGridSpec(
+            num_scalar_prefetch=1,
+            grid=(1,),
+            in_specs=[
+                whole((1, 2, tokens, lanes)),
+                whole((2, tokens, lanes)),
+                whole((2, tokens, lanes)),
+                whole((tokens, lanes)),
+            ],
+            out_specs=(whole((2, tokens, lanes)), whole((tokens, lanes))),
+        ),
+        compiler_params=params(),
+        cost_estimate=cost(20 * tokens * lanes, 20 * tokens * lanes),
+        name="gate_rows",
+    )(order, blocks, up, down, filtered)
+
+
+def backward_filter(order, grad_filtered, key_values, spread_taps):
+    tokens = grad_filtered.shape[0]
+    taps = spread_taps.shape[0] // sublanes
+    n_blocks = order.shape[0]
+    size = tokens // n_blocks
+    tiles = 8
+
+    def body(order_ref, grad_ref, kv_ref, taps_ref, out_ref, moved, signal_grad):
+        for shift in range(sublanes):
+            moved[shift, tokens - sublanes :, :] = jnp.zeros((taps + sublanes, lanes), f32)
+        moved[0, :tokens, :] = grad_ref[...].astype(f32)
+        for shift in range(1, sublanes):
+            moved[shift, :tokens, :] = moved[0, shift : shift + tokens, :]
+
+        def run(g, carry):
+            start = pl.multiple_of(g * tiles * sublanes, tiles * sublanes)
+
+            def load(shift, at):
+                return moved[shift, pl.ds(start + (tiles - 1 - at) * sublanes, sublanes), :]
+
+            def tap(shift, q):
+                index = q * sublanes + shift
+                return taps_ref[index * sublanes : (index + 1) * sublanes, :]
+
+            sums = window_filter(load, tap, tiles, taps)
+            for i in range(tiles):
+                signal_grad[pl.ds(start + (tiles - 1 - i) * sublanes, sublanes), :] = sums[i]
+            return carry
+
+        lax.fori_loop(0, tokens // (tiles * sublanes), run, 0)
+
+        def one_block(r, carry):
+            rows = pl.ds(pl.multiple_of(r * size, size), size)
+            place = block_rows(order_ref, r, size)
+            gradient = signal_grad[place, :]
+            out_ref[0, rows, :] = (gradient * kv_ref[1, place, :].astype(f32)).astype(bf16)
+            out_ref[1, rows, :] = (gradient * kv_ref[0, place, :].astype(f32)).astype(bf16)
+            return carry
+
+        lax.fori_loop(0, n_blocks, one_block, 0)
+
+    whole = lambda shape: pl.BlockSpec(shape, lambda g, order: (0,) * len(shape))
+    return pl.pallas_call(
+        body,
+        out_shape=jax.ShapeDtypeStruct((2, tokens, lanes), bf16),
+        grid_spec=pltpu.PrefetchScalarGridSpec(
+            num_scalar_prefetch=1,
+            grid=(1,),
+            in_specs=[
+                whole((tokens, lanes)),
+                whole((2, tokens, lanes)),
+                whole(spread_taps.shape),
+            ],
+            out_specs=whole((2, tokens, lanes)),
+            scratch_shapes=[
+                pltpu.VMEM((sublanes, tokens + taps, lanes), f32),
+                pltpu.VMEM((tokens, lanes), f32),
+            ],
+        ),
+        compiler_params=params(),
+        cost_estimate=cost(400 * tokens * lanes * taps, 12 * tokens * lanes),
+        name="backward_filter",
+    )(order, grad_filtered, key_values, spread_taps)
+
+
+def taps_gradient(signal, grad_filtered, taps):
+    tokens = signal.shape[0]
+    tiles = 8
+    steps = taps // sublanes
+
+    def body(signal_ref, grad_ref, out_ref, moved, gradient):
+        for shift in range(sublanes):
+            moved[shift, : taps + sublanes, :] = jnp.zeros((taps + sublanes, lanes), f32)
+        moved[0, taps:, :] = signal_ref[...].astype(f32)
+        gradient[...] = grad_ref[...].astype(f32)
+        for shift in range(1, sublanes):
+            moved[shift, taps : taps + tokens, :] = moved[0, taps - shift : taps - shift + tokens, :]
+        for shift in range(sublanes):
+
+            def run(g, sums):
+                start = pl.multiple_of(g * tiles * sublanes, tiles * sublanes)
+                sums = list(sums)
+                held = {}
+                for i in range(tiles):
+                    here = gradient[pl.ds(start + i * sublanes, sublanes), :]
+                    for q in range(steps):
+                        if i - q not in held:
+                            held[i - q] = moved[shift, pl.ds(start + taps + (i - q) * sublanes, sublanes), :]
+                        sums[q] = sums[q] + here * held[i - q]
+                return tuple(sums)
+
+            zero = tuple(jnp.zeros((sublanes, lanes), f32) for _ in range(steps))
+            sums = lax.fori_loop(0, tokens // (tiles * sublanes), run, zero)
+            for q in range(steps):
+                index = q * sublanes + shift
+                out_ref[index : index + 1, :] = jnp.sum(sums[q], axis=0, keepdims=True)
+
+    return pl.pallas_call(
+        body,
+        out_shape=jax.ShapeDtypeStruct((taps, lanes), f32),
+        in_specs=[pl.BlockSpec(memory_space=pltpu.VMEM)] * 2,
+        out_specs=pl.BlockSpec(memory_space=pltpu.VMEM),
+        scratch_shapes=[
+            pltpu.VMEM((sublanes, tokens + taps, lanes), f32),
+            pltpu.VMEM((tokens, lanes), f32),
+        ],
+        compiler_params=params(),
+        cost_estimate=cost(400 * tokens * lanes * taps, 8 * tokens * lanes),
+        name="taps_gradient",
+    )(signal, grad_filtered)
+
+
+def merge_blocks(place, block, before, after):
+    tokens = block.shape[1]
+    length = len(before) + 1
+    rows = 256
+
+    def body(place_ref, *refs):
+        out = refs[-1]
+        own, ups, downs = refs[0], refs[1:length], refs[length : 2 * length - 1]
+        line = place_ref[0]
+        for offset in range(length):
+            if offset == 0:
+                value = own[...]
+            else:
+                value = downs[offset - 1][...] + ups[length - offset - 1][...]
+            at = pl.multiple_of(lax.rem(line + offset, length) * lanes, lanes)
+            out[:, :, pl.ds(at, lanes)] = value
+
+    spec = pl.BlockSpec((2, rows, lanes), lambda g, place: (0, g, 0))
+    return pl.pallas_call(
+        body,
+        out_shape=jax.ShapeDtypeStruct((2, tokens, length * lanes), bf16),
+        grid_spec=pltpu.PrefetchScalarGridSpec(
+            num_scalar_prefetch=1,
+            grid=(tokens // rows,),
+            in_specs=[spec] * (2 * length - 1),
+            out_specs=pl.BlockSpec((2, rows, length * lanes), lambda g, place: (0, g, 0)),
+        ),
+        compiler_params=params(),
+        cost_estimate=cost(tokens * lanes * 8, 2 * 2 * tokens * lanes * 11),
+        name="merge_blocks",
+    )(place, block, *before, *after)
+
+
+def project_back(place, merged, in_weight, given, indices):
+    tokens, half = merged[0][0].shape[1:]
+    rows = 256
+    n = len(merged)
+
+    def body(place_ref, *refs):
+        out = refs[-1]
+        dims = (((1,), (1,)), ((), ()))
+        own = jnp.zeros((rows, half), f32)
+        other = jnp.zeros((rows, half), f32)
+        for k in range(n):
+            value, kept, sent = refs[3 * k], refs[3 * k + 1], refs[3 * k + 2]
+            value = value[...].reshape(rows, half)
+            own += lax.dot_general(value, kept[...].reshape(half, half), dims, preferred_element_type=f32)
+            other += lax.dot_general(value, sent[...], dims, preferred_element_type=f32)
+        at = place_ref[1]
+        out[:, pl.ds(pl.multiple_of(at * half, half), half)] = own.astype(bf16)
+        out[:, pl.ds(pl.multiple_of((1 - at) * half, half), half)] = other.astype(bf16)
+
+    operands, specs = [], []
+    for (value, which), sent, index in zip(merged, given, indices):
+        operands += [value, in_weight, sent]
+        specs += [
+            pl.BlockSpec((1, rows, half), lambda g, place, which=which: (which, g, 0)),
+            pl.BlockSpec((1, half, half), lambda g, place, index=index: (index, 0, place[1])),
+            pl.BlockSpec((half, half), lambda g, place: (0, 0)),
+        ]
+    return pl.pallas_call(
+        body,
+        out_shape=jax.ShapeDtypeStruct((tokens, 2 * half), bf16),
+        grid_spec=pltpu.PrefetchScalarGridSpec(
+            num_scalar_prefetch=1,
+            grid=(tokens // rows,),
+            in_specs=specs,
+            out_specs=pl.BlockSpec((rows, 2 * half), lambda g, place: (g, 0)),
+        ),
+        compiler_params=params(),
+        cost_estimate=cost(4 * n * tokens * half * half, 8 * tokens * half),
+        name="project_back",
+    )(place, *operands)
+
+
+def project_out(place, merged, out_weight, given):
+    tokens, half = merged.shape[1:]
+    rows = 256
+
+    def body(place_ref, value_ref, kept, sent, out):
+        value = value_ref[...].reshape(rows, half)
+        at = place_ref[1]
+        own = jnp.dot(value, kept[...], preferred_element_type=f32)
+        other = jnp.dot(value, sent[...], preferred_element_type=f32)
+        out[:, pl.ds(pl.multiple_of(at * half, half), half)] = own.astype(bf16)
+        out[:, pl.ds(pl.multiple_of((1 - at) * half, half), half)] = other.astype(bf16)
+
+    return pl.pallas_call(
+        body,
+        out_shape=jax.ShapeDtypeStruct((tokens, 2 * half), bf16),
+        grid_spec=pltpu.PrefetchScalarGridSpec(
+            num_scalar_prefetch=1,
+            grid=(tokens // rows,),
+            in_specs=[
+                pl.BlockSpec((1, rows, half), lambda g, place: (0, g, 0)),
+                pl.BlockSpec((half, half), lambda g, place: (place[1], 0)),
+                pl.BlockSpec((half, half), lambda g, place: (0, 0)),
+            ],
+            out_specs=pl.BlockSpec((rows, 2 * half), lambda g, place: (g, 0)),
+        ),
+        compiler_params=params(),
+        cost_estimate=cost(4 * tokens * half * half, 8 * tokens * half),
+        name="project_out",
+    )(place, merged, out_weight, given)
+
+
+def in_gradient(place, turned, merged, which, index, total, running):
+    tokens, half = merged.shape[1:]
+    rows = 256
+
+    def body(place_ref, own, other, value_ref, *refs):
+        kept, sent = refs[-2:]
+        value = value_ref[...].reshape(tokens, half)
+        kept[...] = jnp.dot(own[...], value, preferred_element_type=f32)[None]
+        sent[...] = jnp.dot(other[...], value, preferred_element_type=f32).astype(bf16)
+
+    steps = half // rows
+    more = [] if running is None else [running]
+    return pl.pallas_call(
+        body,
+        out_shape=(
+            jax.ShapeDtypeStruct((total, half, 2 * half), f32),
+            jax.ShapeDtypeStruct((half, half), bf16),
+        ),
+        grid_spec=pltpu.PrefetchScalarGridSpec(
+            num_scalar_prefetch=1,
+            grid=(steps,),
+            in_specs=[
+                pl.BlockSpec((rows, tokens), lambda g, place: (place[1] * steps + g, 0)),
+                pl.BlockSpec((rows, tokens), lambda g, place: ((1 - place[1]) * steps + g, 0)),
+                pl.BlockSpec((1, tokens, half), lambda g, place: (which, 0, 0)),
+            ]
+            + [pl.BlockSpec(memory_space=pl.ANY)] * len(more),
+            out_specs=(
+                pl.BlockSpec((1, rows, half), lambda g, place: (index, g, place[1])),
+                pl.BlockSpec((rows, half), lambda g, place: (g, 0)),
+            ),
+        ),
+        input_output_aliases={4: 0} if more else {},
+        compiler_params=params(),
+        cost_estimate=cost(4 * tokens * half * half, 8 * tokens * half),
+        name="in_gradient",
+    )(place, turned, turned, merged, *more)
+
+
+def out_gradient(place, merged, rows_of):
+    tokens, half = merged.shape[1:]
+    rows = 256
+    steps = half // rows
+
+    def body(place_ref, value_ref, own, other, kept, sent):
+        value = value_ref[...].reshape(tokens, rows)
+        dims = (((0,), (0,)), ((), ()))
+        kept[...] = lax.dot_general(value, own[...], dims, preferred_element_type=f32)
+        sent[...] = lax.dot_general(value, other[...], dims, preferred_element_type=f32).astype(bf16)
+
+    return pl.pallas_call(
+        body,
+        out_shape=(
+            jax.ShapeDtypeStruct((2 * half, half), f32),
+            jax.ShapeDtypeStruct((half, half), bf16),
+        ),
+        grid_spec=pltpu.PrefetchScalarGridSpec(
+            num_scalar_prefetch=1,
+            grid=(steps,),
+            in_specs=[
+                pl.BlockSpec((1, tokens, rows), lambda g, place: (0, 0, g)),
+                pl.BlockSpec((tokens, half), lambda g, place: (0, place[1])),
+                pl.BlockSpec((tokens, half), lambda g, place: (0, 1 - place[1])),
+            ],
+            out_specs=(
+                pl.BlockSpec((rows, half), lambda g, place: (place[1] * steps + g, 0)),
+                pl.BlockSpec((rows, half), lambda g, place: (g, 0)),
+            ),
+        ),
+        compiler_params=params(),
+        cost_estimate=cost(4 * tokens * half * half, 8 * tokens * half),
+        name="out_gradient",
+    )(place, merged, rows_of, rows_of)
+
+
+def take_in_half(place, running, pieces):
+    n = len(pieces)
+    half = pieces[0].shape[0]
+
+    def body(place_ref, *refs):
+        out = refs[-1]
+        for k in range(n):
+
+            @pl.when(pl.program_id(0) == k)
+            def _():
+                out[...] = refs[k][...].astype(f32)[None]
+
+    return pl.pallas_call(
+        body,
+        out_shape=jax.ShapeDtypeStruct(running.shape, f32),
+        grid_spec=pltpu.PrefetchScalarGridSpec(
+            num_scalar_prefetch=1,
+            grid=(n,),
+            in_specs=[pl.BlockSpec((half, half), lambda g, place: (0, 0))] * n
+            + [pl.BlockSpec(memory_space=pl.ANY)],
+            out_specs=pl.BlockSpec((1, half, half), lambda g, place: (g, 0, 1 - place[1])),
+        ),
+        input_output_aliases={n + 1: 0},
+        compiler_params=params(),
+        cost_estimate=cost(n * half * half, 6 * n * half * half),
+        name="take_in_half",
+    )(place, *pieces, running)
+
+
+def take_out_half(place, running, piece):
+    half = piece.shape[0]
+
+    def body(place_ref, piece_ref, running_ref, out):
+        out[...] = piece_ref[...].astype(f32)
+
+    return pl.pallas_call(
+        body,
+        out_shape=jax.ShapeDtypeStruct(running.shape, f32),
+        grid_spec=pltpu.PrefetchScalarGridSpec(
+            num_scalar_prefetch=1,
+            grid=(1,),
+            in_specs=[
+                pl.BlockSpec((half, half), lambda g, place: (0, 0)),
+                pl.BlockSpec(memory_space=pl.ANY),
+            ],
+            out_specs=pl.BlockSpec((half, half), lambda g, place: (1 - place[1], 0)),
+        ),
+        input_output_aliases={2: 0},
+        compiler_params=params(),
+        cost_estimate=cost(half * half, 6 * half * half),
+        name="take_out_half",
+    )(place, piece, running)
+
+
+def on_paired_mesh(tokens, in_weight, out_weight, filters, cotangent):
+    taps = filters.shape[1]
+    seq_at, fsdp_at = lax.axis_index("seq"), lax.axis_index("fsdp")
+    line, pair = seq_at // 2, seq_at % 2
+    place = jnp.stack([line, pair]).astype(jnp.int32)
+    half_in, half_out = in_weight.shape[2] // 2, out_weight.shape[0] // 2
+    relative = jnp.arange(8, dtype=jnp.int32)
+    order = (
+        2 * (fsdp_at ^ (2 * (relative % 2) + relative // 4)) + (pair ^ (relative // 2 % 2))
+    ).astype(jnp.int32)
+
+    tokens_here = trade_places(tokens)
+    cot_here = trade_places(cotangent)
+    given_in = {}
+    for i in (1, 2, 0):
+        sent = lax.dynamic_slice_in_dim(in_weight[i], (1 - pair) * half_in, half_in, 1)
+        given_in[i] = flip(sent, "seq", 1)
+    given_out = flip(
+        lax.dynamic_slice_in_dim(out_weight, (1 - pair) * half_out, half_out, 0), "seq", 1
+    )
+    x_rows = jnp.stack([tokens_here, flip(tokens_here, "fsdp", 2)])
+    x_rows = jnp.stack([x_rows, flip(x_rows, "seq", 1)])
+    x_rows = jnp.stack([x_rows, flip(x_rows, "fsdp", 1)])
+    g_rows = jnp.stack([cot_here, flip(cot_here, "seq", 1)])
+    g_rows = jnp.stack([g_rows, flip(g_rows, "fsdp", 2)], axis=1)
+    g_rows = jnp.stack([g_rows, flip(g_rows, "fsdp", 1)])
+    width = tokens.shape[1]
+    x_rows = x_rows.reshape(-1, width)
+    g_rows = g_rows.reshape(-1, width)
+    turned = jnp.transpose(x_rows)
+    own_filters = lax.dynamic_slice_in_dim(
+        filters, pair * half_in + line * lanes, lanes, 0
+    )
+    spread_taps = jnp.repeat(jnp.transpose(own_filters), sublanes, axis=0)
+
+    kv_blocks = project_pair(
+        place,
+        (x_rows, in_weight, given_in[1], False, 1),
+        (x_rows, in_weight, given_in[2], False, 2),
+    )
+    qg_blocks = project_pair(
+        place,
+        (x_rows, in_weight, given_in[0], False, 0),
+        (g_rows, out_weight, given_out, True, 0),
+    )
+    kv_up, kv_down = line_scatter(kv_blocks)
+    qg_up, qg_down = line_scatter(qg_blocks)
+    key_values, signal, filtered = forward_filter(order, kv_blocks, kv_up, kv_down, spread_taps)
+    gated_pair, grad_filtered = gate_rows(order, qg_blocks, qg_up, qg_down, filtered)
+    gated_before, gated_after = line_gather(gated_pair)
+    kv_grads = backward_filter(order, grad_filtered, key_values, spread_taps)
+    kv_before, kv_after = line_gather(kv_grads)
+    own_taps = taps_gradient(signal, grad_filtered, taps)
+    all_taps = lax.all_gather(jnp.transpose(own_taps), "seq", axis=0)
+    length = lax.axis_size("seq") // 2
+    grad_filters = jnp.swapaxes(all_taps.reshape(length, 2, lanes, taps), 0, 1).reshape(filters.shape)
+
+    first = merge_blocks(place, gated_pair, gated_before, gated_after)
+    mixed_part = project_out(place, first, out_weight, given_out)
+    out_kept, out_sent = out_gradient(place, first, g_rows)
+    in_kept, q_sent = in_gradient(place, turned, first, 1, 0, in_weight.shape[0], None)
+    out_given = flip(out_sent, "seq", 1)
+    q_given = flip(q_sent, "seq", 1)
+
+    second = merge_blocks(place, kv_grads, kv_before, kv_after)
+    grad_part = project_back(
+        place,
+        [(first, 1), (second, 0), (second, 1)],
+        in_weight,
+        [given_in[0], given_in[1], given_in[2]],
+        [0, 1, 2],
+    )
+    in_kept, k_sent = in_gradient(place, turned, second, 0, 1, in_weight.shape[0], in_kept)
+    in_kept, v_sent = in_gradient(place, turned, second, 1, 2, in_weight.shape[0], in_kept)
+    k_given, v_given = flip(k_sent, "seq", 1), flip(v_sent, "seq", 1)
+
+    def outward(part, x_first):
+        parts = part.reshape(2, 2, 2, part.shape[0] // 8, width)
+        parts = added(parts[0], flip(parts[1], "fsdp", 1))
+        if x_first:
+            parts = added(parts[:, 0], flip(parts[:, 1], "fsdp", 2))
+            parts = added(parts[0], flip(parts[1], "seq", 1))
+        else:
+            parts = added(parts[0], flip(parts[1], "seq", 1))
+            parts = added(parts[0], flip(parts[1], "fsdp", 2))
+        return trade_places(parts)
+
+    mixed_out = outward(mixed_part, True)
+    grad_tokens = outward(grad_part, False)
+    grad_out_weight = take_out_half(place, out_kept, out_given)
+    grad_in_weight = take_in_half(place, in_kept, [q_given, k_given, v_given])
+    return (mixed_out, grad_tokens, grad_in_weight, grad_out_weight, grad_filters)
+
+
 def solution(mesh):
     placed = (
         P("seq", "fsdp"),
@@ -126,8 +830,9 @@
         P("fsdp", None),
         P("seq", "fsdp"),
     )
+    paired = (mesh.shape["seq"], mesh.shape["fsdp"]) == (8, 4)
     return jax.shard_map(
-        on_device,
+        on_paired_mesh if paired else on_any_mesh,
         mesh=mesh,
         in_specs=placed,
         out_specs=(

time: 589 us -> 392 us (0.67); the launches traced: 580 us -> 390 us
  waiting for transfers between devices: 296 us -> 139 us
  starting transfers between devices: 0.16 us -> 103 us
  blocking collectives: 139 us -> 41.7 us
  Pallas kernels: 0 us -> 65.5 us
  matrix products: 49.8 us -> 0 us
  local copies, waits for them, and re-layouts: 68.6 us -> 24.7 us
  between operations: 14.5 us -> 1.32 us
    all_gather x2 -> x0, waiting for transfers between devices: 151 us -> none  [the longest x1 124 us: on_device(): lax.all_gather(jnp.concatenate([grad_projected, gated[None]], 0), 'seq',...]
    unnamed x5 -> x0, waiting for transfers between devices: 146 us -> none
    ppermute x0 -> x48, waiting for transfers between devices: none -> 139 us  [the longest x20 75.3 us: flip(): lax.ppermute(value, axis, [(i, i ^ bit) for i in range(lax.axis_size(axis...]
    all_to_all x2 -> x0, blocking collectives: 105 us -> none  [the longest x1 54.2 us: to_feature_rows(): lax.all_to_all(wide, 'seq', split_axis=wide.ndim - 1, concat_axis=wide.nd...]
    ppermute x0 -> x48, starting transfers between devices: none -> 103 us  [the longest x24 60.4 us: along_line(): return lax.ppermute(value, 'seq', pairs)]
    pallas_call x0 -> x16, Pallas kernels: none -> 65.5 us  [the longest x2 11.4 us: project_pair(): pl.pallas_call(body, out_shape=jax.ShapeDtypeStruct((count, 2, tokens, la...]
    unnamed x23 -> x48, local copies, waits for them, and re-layouts: 41.6 us -> 9.26 us
    dot_general x6 -> x0, matrix products: 29.4 us -> none  [the longest x1 9.22 us: on_device(): jnp.einsum('td,itc->idc', features, rows[:3], preferred_element_type=jnp....]
  transfers between devices with their start and end apart: 4 -> 48, of which waited for: 3 -> 20; matrix products, arithmetic and copies ran while one was open for 5% -> 7% of each run, Pallas kernels for 0% -> 12%
where the time goes in v2:
time: 392 us; the launch traced here: 390 us
  waiting for transfers between devices  139 us (35%)
  starting transfers between devices  103 us (26%)
  Pallas kernels  65.5 us (17%)
  blocking collectives  41.7 us (11%)
  local copies, waits for them, and re-layouts  24.7 us (6%)
  other arithmetic  15 us (4%)
    ppermute x20, waiting for transfers between devices, flip(): lax.ppermute(value, axis, [(i, i ^ bit) for i in range(lax.axis_size(axis...  75.3 us
    ppermute x24, waiting for transfers between devices, along_line(): return lax.ppermute(value, 'seq', pairs)  63.3 us
    ppermute x24, starting transfers between devices, along_line(): return lax.ppermute(value, 'seq', pairs)  60.4 us
    all_gather x1, blocking collectives, on_paired_mesh(): all_taps = lax.all_gather(jnp.transpose(own_taps), 'seq', axis=0)  41.7 us
    ppermute x20, starting transfers between devices, flip(): lax.ppermute(value, axis, [(i, i ^ bit) for i in range(lax.axis_size(axis...  34.8 us
    pallas_call x2, Pallas kernels, project_pair(): pl.pallas_call(body, out_shape=jax.ShapeDtypeStruct((count, 2, tokens, la...  11.4 us
    pallas_call x1, Pallas kernels, forward_filter(): pl.pallas_call(body, out_shape=(jax.ShapeDtypeStruct((2, tokens, lanes),...  9.86 us
    pallas_call x1, Pallas kernels, backward_filter(): pl.pallas_call(body, out_shape=jax.ShapeDtypeStruct((2, tokens, lanes), b...  9.8 us
  transfers between devices with their start and end apart: 48, of which 20 were waited for; matrix products, arithmetic and copies ran while one was open for 7% of the time, Pallas kernels for 12%

profile of v2, /device:TPU:0, one launch (start us, length us, event | category | flops | bytes accessed | tf_op | source)
XLA Modules:
  0.0 390.3 jit_solution(13223361438595736566)
XLA Ops:
  2.4 19.7 %collective-permute-start.1 = (bf16[128,1024]{1,0:T(8,128)(2,1)S(1)}, bf16[128,1024]{1,0:T(8,128)(2,1)S(1)}, u32[]{:S(2)}, u32[]{:S(2)}) collective-permute-start(bf16[128,1024]{1,0:T(8,128)(2,1)S(1)} %collective-permute-done), channel_id=1, source_target_pairs={{0,2},{1,3},{2,0},{3,1},{4,6},{5,7},{6,4},{7,5},{8,10},{9,11},{10,... | collective-permute-start | bytes 786440 | tf_op jit(solution)/shard_map/ppermute | solution.py:131
  23.7 4.0 %collective-permute-done.1 = bf16[128,1024]{1,0:T(8,128)(2,1)S(1)} collective-permute-done((bf16[128,1024]{1,0:T(8,128)(2,1)S(1)}, bf16[128,1024]{1,0:T(8,128)(2,1)S(1)}, u32[]{:S(2)}, u32[]{:S(2)}) %collective-permute-start.1) | collective-permute-done | bytes 262176 | tf_op jit(solution)/shard_map/ppermute | solution.py:131
  29.9 13.9 %collective-permute-done.6 = bf16[128,1024]{1,0:T(8,128)(2,1)S(1)} collective-permute-done((bf16[128,1024]{1,0:T(8,128)(2,1)S(1)}, bf16[128,1024]{1,0:T(8,128)(2,1)S(1)}, u32[]{:S(2)}, u32[]{:S(2)}) %collective-permute-start.6) | collective-permute-done | bytes 262176 | tf_op jit(solution)/shard_map/ppermute | solution.py:131
  48.7 4.6 %collective-permute-done.7 = bf16[2,128,1024]{2,1,0:T(8,128)(2,1)S(1)} collective-permute-done((bf16[2,128,1024]{2,1,0:T(8,128)(2,1)S(1)}, bf16[2,128,1024]{2,1,0:T(8,128)(2,1)S(1)}, u32[]{:S(2)}, u32[]{:S(2)}) %collective-permute-start.7) | collective-permute-done | bytes 524320 | tf_op jit(solution)/shard_map/ppermute | solution.py:131
  62.3 11.3 %collective-permute-done.17.refs_7_.refs_8_ = bf16[512,512]{1,0:T(8,128)(2,1)} collective-permute-done((bf16[512,512]{1,0:T(8,128)(2,1)}, bf16[512,512]{1,0:T(8,128)(2,1)}, u32[]{:S(2)}, u32[]{:S(2)}) %collective-permute-start.17) | collective-permute-done | bytes 524320 | tf_op jit(solution)/shard_map/ppermute | solution.py:131
  73.6 5.5 %project_pair.3.blocks_ref = bf16[4,2,1024,128]{3,2,1,0:T(8,128)(2,1)S(1)} custom-call(s32[2]{0:T(128)S(1)} %pad_add_fusion.place_ref, bf16[1024,1024]{1,0:T(8,128)(2,1)S(1)} %bitcast.100, bf16[1024,1024]{1,0:T(8,128)(2,1)S(1)} %bitcast.101, bf16[3,512,1024]{2,1,0:T(8,128)(2,1)} %refs_7_.1, bf16[512,512]{1,0:T(8,128)(2,1)S(1)} %collective-permute-done.16.refs_3_.refs_5_, ...), custom_call_target="tpu_custom_call" | custom-call | flops 2147483648 | bytes 8388608 | tf_op jit(solution)/shard_map/project_pair/pallas_call | solution.py:222
  80.0 5.3 %collective-permute-start.18 = (bf16[2,1024,128]{2,1,0:T(8,128)(2,1)S(1)}, bf16[2,1024,128]{2,1,0:T(8,128)(2,1)S(1)}, u32[]{:S(2)}, u32[]{:S(2)}) collective-permute-start(bf16[2,1024,128]{2,1,0:T(8,128)(2,1)S(1)} %get-tuple-element.43), channel_id=1, source_target_pairs={{0,8},{4,12},{1,9},{5,13},{2,10},{6,14},{3,11},{7,15}} | collective-permute-start | bytes 1572872 | tf_op jit(solution)/shard_map/ppermute | solution.py:153
  88.3 6.2 %collective-permute-done.4.refs_3_.refs_2_ = bf16[512,512]{1,0:T(8,128)(2,1)S(1)} collective-permute-done((bf16[512,512]{1,0:T(8,128)(2,1)S(1)}, bf16[512,512]{1,0:T(8,128)(2,1)S(1)}, u32[]{:S(2)}, u32[]{:S(2)}) %collective-permute-start.4) | collective-permute-done | bytes 524320 | tf_op jit(solution)/shard_map/ppermute | solution.py:131
  94.5 5.9 %project_pair.2.blocks_ref = bf16[4,2,1024,128]{3,2,1,0:T(8,128)(2,1)S(1)} custom-call(s32[2]{0:T(128)S(1)} %pad_add_fusion.place_ref, bf16[1024,1024]{1,0:T(8,128)(2,1)} %bitcast.104, bf16[1024,1024]{1,0:T(8,128)(2,1)} %bitcast.105, bf16[3,512,1024]{2,1,0:T(8,128)(2,1)} %refs_7_.1, bf16[512,512]{1,0:T(8,128)(2,1)S(1)} %collective-permute-done.4.refs_3_.refs_2_, ...), custom_call_target="tpu_custom_call" | custom-call | flops 2147483648 | bytes 8388608 | tf_op jit(solution)/shard_map/project_pair/pallas_call | solution.py:222
  102.9 7.0 %collective-permute-start.10 = (bf16[2,1024,128]{2,1,0:T(8,128)(2,1)}, bf16[2,1024,128]{2,1,0:T(8,128)(2,1)}, u32[]{:S(2)}, u32[]{:S(2)}) collective-permute-start(bf16[2,1024,128]{2,1,0:T(8,128)(2,1)} %get-tuple-element.49), channel_id=1, source_target_pairs={{0,8},{4,12},{1,9},{5,13},{2,10},{6,14},{3,11},{7,15}} | collective-permute-start | bytes 1572872 | tf_op jit(solution)/shard_map/ppermute | solution.py:153
  114.9 6.9 %collective-permute-done.10 = bf16[2,1024,128]{2,1,0:T(8,128)(2,1)} collective-permute-done((bf16[2,1024,128]{2,1,0:T(8,128)(2,1)}, bf16[2,1024,128]{2,1,0:T(8,128)(2,1)}, u32[]{:S(2)}, u32[]{:S(2)}) %collective-permute-start.10) | collective-permute-done | bytes 524320 | tf_op jit(solution)/shard_map/ppermute | solution.py:153
  123.9 5.0 %collective-permute-start.11 = (bf16[2,1024,128]{2,1,0:T(8,128)(2,1)S(1)}, bf16[2,1024,128]{2,1,0:T(8,128)(2,1)S(1)}, u32[]{:S(2)}, u32[]{:S(2)}) collective-permute-start(bf16[2,1024,128]{2,1,0:T(8,128)(2,1)S(1)} %get-tuple-element.47), channel_id=1, source_target_pairs={{0,8},{4,12},{8,16},{12,20},{1,9},{5,13},{9,17},{13,21},{2,10},{6,... | collective-permute-start | bytes 1572872 | tf_op jit(solution)/shard_map/ppermute | solution.py:153
  128.9 4.1 %collective-permute-done.19 = bf16[2,1024,128]{2,1,0:T(8,128)(2,1)} collective-permute-done((bf16[2,1024,128]{2,1,0:T(8,128)(2,1)}, bf16[2,1024,128]{2,1,0:T(8,128)(2,1)}, u32[]{:S(2)}, u32[]{:S(2)}) %collective-permute-start.19) | collective-permute-done | bytes 524320 | tf_op jit(solution)/shard_map/ppermute | solution.py:153
  135.9 5.0 %collective-permute-start.20 = (bf16[2,1024,128]{2,1,0:T(8,128)(2,1)S(1)}, bf16[2,1024,128]{2,1,0:T(8,128)(2,1)S(1)}, u32[]{:S(2)}, u32[]{:S(2)}) collective-permute-start(bf16[2,1024,128]{2,1,0:T(8,128)(2,1)S(1)} %get-tuple-element.39), channel_id=1, source_target_pairs={{0,8},{4,12},{8,16},{12,20},{16,24},{20,28},{1,9},{5,13},{9,17},{1... | collective-permute-start | bytes 1572872 | tf_op jit(solution)/shard_map/ppermute | solution.py:153
  145.7 5.0 %collective-permute-start.12 = (bf16[2,1024,128]{2,1,0:T(8,128)(2,1)S(1)}, bf16[2,1024,128]{2,1,0:T(8,128)(2,1)S(1)}, u32[]{:S(2)}, u32[]{:S(2)}) collective-permute-start(bf16[2,1024,128]{2,1,0:T(8,128)(2,1)S(1)} %get-tuple-element.45), channel_id=1, source_target_pairs={{0,8},{4,12},{8,16},{12,20},{16,24},{20,28},{1,9},{5,13},{9,17},{1... | collective-permute-start | bytes 1572872 | tf_op jit(solution)/shard_map/ppermute | solution.py:153
  150.8 4.6 %collective-permute-done.20.up_ref = bf16[2,1024,128]{2,1,0:T(8,128)(2,1)S(1)} collective-permute-done((bf16[2,1024,128]{2,1,0:T(8,128)(2,1)S(1)}, bf16[2,1024,128]{2,1,0:T(8,128)(2,1)S(1)}, u32[]{:S(2)}, u32[]{:S(2)}) %collective-permute-start.20) | collective-permute-done | bytes 524320 | tf_op jit(solution)/shard_map/ppermute | solution.py:153
  155.4 9.9 %forward_filter.1 = (bf16[2,1024,128]{2,1,0:T(8,128)(2,1)S(1)}, bf16[1024,128]{1,0:T(8,128)(2,1)S(1)}, f32[1024,128]{1,0:T(8,128)S(1)}) custom-call(s32[8]{0:T(128)S(1)} %fusion.14.order_ref, bf16[4,2,1024,128]{3,2,1,0:T(8,128)(2,1)S(1)} %copy-done.11, bf16[2,1024,128]{2,1,0:T(8,128)(2,1)S(1)} %collective-permute-done.20.up_ref, ...), custom_call_target="tpu_custom_call" | custom-call | flops 6710886400 | bytes 1572864 | tf_op jit(solution)/shard_map/forward_filter/pallas_call | solution.py:308
  166.2 9.8 %backward_filter.1.refs_0_ = bf16[2,1024,128]{2,1,0:T(8,128)(2,1)S(1)} custom-call(s32[8]{0:T(128)S(1)} %fusion.14.order_ref, bf16[1024,128]{1,0:T(8,128)(2,1)S(1)} %get-tuple-element.20.grad_ref, bf16[2,1024,128]{2,1,0:T(8,128)(2,1)S(1)} %get-tuple-element.21.kv_ref, f32[1024,128]{1,0:T(8,128)S(1)} %broadcast_bitcast_fusion.taps_ref), custom_call_target="tpu_custom_call" | custom-call | flops 6710886400 | bytes 1572864 | tf_op jit(solution)/shard_map/backward_filter/pallas_call | solution.py:426
  177.3 5.0 %collective-permute-start.34 = (bf16[2,1024,128]{2,1,0:T(8,128)(2,1)S(1)}, bf16[2,1024,128]{2,1,0:T(8,128)(2,1)S(1)}, u32[]{:S(2)}, u32[]{:S(2)}) collective-permute-start(bf16[2,1024,128]{2,1,0:T(8,128)(2,1)S(1)} %backward_filter.1.refs_0_), channel_id=1, source_target_pairs={{0,8},{4,12},{8,16},{12,20},{16,24},{20,28},{1,9},{5,13},{9,17},{1... | collective-permute-start | bytes 1572872 | tf_op jit(solution)/shard_map/ppermute | solution.py:153
  183.7 8.1 %collective-permute-start.24 = (bf16[2,1024,128]{2,1,0:T(8,128)(2,1)S(1)}, bf16[2,1024,128]{2,1,0:T(8,128)(2,1)S(1)}, u32[]{:S(2)}, u32[]{:S(2)}) collective-permute-start(bf16[2,1024,128]{2,1,0:T(8,128)(2,1)S(1)} %get-tuple-element.19.refs_0_), channel_id=1, source_target_pairs={{0,8},{4,12},{8,16},{12,20},{16,24},{20,28},{1,9},{5,13},{9,17},{1... | collective-permute-start | bytes 1572872 | tf_op jit(solution)/shard_map/ppermute | solution.py:153
  195.2 9.2 %collective-permute-done.27.refs_4_ = bf16[2,1024,128]{2,1,0:T(8,128)(2,1)S(1)} collective-permute-done((bf16[2,1024,128]{2,1,0:T(8,128)(2,1)S(1)}, bf16[2,1024,128]{2,1,0:T(8,128)(2,1)S(1)}, u32[]{:S(2)}, u32[]{:S(2)}) %collective-permute-start.27) | collective-permute-done | bytes 524320 | tf_op jit(solution)/shard_map/ppermute | solution.py:153
  206.5 9.2 %collective-permute-done.38.refs_5_ = bf16[2,1024,128]{2,1,0:T(8,128)(2,1)S(1)} collective-permute-done((bf16[2,1024,128]{2,1,0:T(8,128)(2,1)S(1)}, bf16[2,1024,128]{2,1,0:T(8,128)(2,1)S(1)}, u32[]{:S(2)}, u32[]{:S(2)}) %collective-permute-start.38) | collective-permute-done | bytes 524320 | tf_op jit(solution)/shard_map/ppermute | solution.py:153
  217.7 9.2 %collective-permute-done.28.refs_5_ = bf16[2,1024,128]{2,1,0:T(8,128)(2,1)S(1)} collective-permute-done((bf16[2,1024,128]{2,1,0:T(8,128)(2,1)S(1)}, bf16[2,1024,128]{2,1,0:T(8,128)(2,1)S(1)}, u32[]{:S(2)}, u32[]{:S(2)}) %collective-permute-start.28) | collective-permute-done | bytes 524320 | tf_op jit(solution)/shard_map/ppermute | solution.py:153
  229.1 9.1 %collective-permute-done.39.refs_6_ = bf16[2,1024,128]{2,1,0:T(8,128)(2,1)S(1)} collective-permute-done((bf16[2,1024,128]{2,1,0:T(8,128)(2,1)S(1)}, bf16[2,1024,128]{2,1,0:T(8,128)(2,1)S(1)}, u32[]{:S(2)}, u32[]{:S(2)}) %collective-permute-start.39) | collective-permute-done | bytes 524320 | tf_op jit(solution)/shard_map/ppermute | solution.py:153
  241.1 6.4 %collective-permute-done.29.refs_6_ = bf16[2,1024,128]{2,1,0:T(8,128)(2,1)S(1)} collective-permute-done((bf16[2,1024,128]{2,1,0:T(8,128)(2,1)S(1)}, bf16[2,1024,128]{2,1,0:T(8,128)(2,1)S(1)}, u32[]{:S(2)}, u32[]{:S(2)}) %collective-permute-start.29) | collective-permute-done | bytes 524320 | tf_op jit(solution)/shard_map/ppermute | solution.py:153
  249.1 6.6 %project_back.1 = bf16[1024,1024]{1,0:T(8,128)(2,1)S(1)} custom-call(s32[2]{0:T(128)S(1)} %pad_add_fusion.place_ref, bf16[2,1024,512]{2,1,0:T(8,128)(2,1)S(1)} %merge_blocks.2.value_ref.refs_0_, bf16[3,512,1024]{2,1,0:T(8,128)(2,1)} %refs_7_.1, bf16[512,512]{1,0:T(8,128)(2,1)S(1)} %copy-done.16, bf16[2,1024,512]{2,1,0:T(8,128)(2,1)} %copy-done.8, ...), custom_call_target="tpu_custom_call" | custom-call | flops 3221225472 | bytes 4194304 | tf_op jit(solution)/shard_map/project_back/pallas_call | solution.py:556
  257.3 3.4 project_out.1
  285.6 24.1 %collective-permute-done.41 = bf16[2,128,1024]{2,1,0:T(8,128)(2,1)S(1)} collective-permute-done((bf16[2,128,1024]{2,1,0:T(8,128)(2,1)S(1)}, bf16[2,128,1024]{2,1,0:T(8,128)(2,1)S(1)}, u32[]{:S(2)}, u32[]{:S(2)}) %collective-permute-start.41) | collective-permute-done | bytes 524320 | tf_op jit(solution)/shard_map/ppermute | solution.py:131
  319.0 7.4 %collective-permute-done.32 = bf16[128,1024]{1,0:T(8,128)(2,1)S(1)} collective-permute-done((bf16[128,1024]{1,0:T(8,128)(2,1)S(1)}, bf16[128,1024]{1,0:T(8,128)(2,1)S(1)}, u32[]{:S(2)}, u32[]{:S(2)}) %collective-permute-start.32) | collective-permute-done | bytes 262176 | tf_op jit(solution)/shard_map/ppermute | solution.py:131
  328.6 3.6 collective-permute-start.33
  332.2 5.5 %taps_gradient.1 = f32[128,128]{1,0:T(8,128)S(1)} custom-call(bf16[1024,128]{1,0:T(8,128)(2,1)S(1)} %copy-done.18, bf16[1024,128]{1,0:T(8,128)(2,1)S(1)} %get-tuple-element.20.grad_ref), custom_call_target="tpu_custom_call" | custom-call | flops 6710886400 | bytes 1048576 | tf_op jit(solution)/shard_map/taps_gradient/pallas_call | solution.py:481
  337.6 41.7 %all-gather = f32[1024,128]{0,1:T(8,128)S(1)} all-gather(f32[128,128]{0,1:T(8,128)S(1)} %bitcast.117), channel_id=2, replica_groups=mesh['seq'=8,'fsdp'=4] {'seq'}, dimensions={0}, use_global_device_ids=true | all-gather | bytes 589824 | tf_op jit(solution)/shard_map/all_gather | solution.py:784
  (168 shorter events, 106.7 us)
Async XLA Ops:
  2.4 25.3 %collective-permute-start.1 = (bf16[128,1024]{1,0:T(8,128)(2,1)S(1)}, bf16[128,1024]{1,0:T(8,128)(2,1)S(1)}, u32[]{:S(2)}, u32[]{:S(2)}) collective-permute-start(bf16[128,1024]{1,0:T(8,128)(2,1)S(1)} %collective-permute-done), channel_id=1, source_target_pairs={{0,2},{1,3},{2,0},{3,1},{4,6},{5,7},{6,4},{7,5},{8,10},{9,11},{10,... | collective-permute-start | bytes 786440 | tf_op jit(solution)/shard_map/ppermute | solution.py:131
  54.8 30.5 %collective-permute-start.8 = (bf16[2,2,128,1024]{3,2,0,1:T(8,128)(2,1)}, bf16[2,2,128,1024]{3,2,0,1:T(8,128)(2,1)}, u32[]{:S(2)}, u32[]{:S(2)}) collective-permute-start(bf16[2,2,128,1024]{3,2,0,1:T(8,128)(2,1)} %get-tuple-element.51), channel_id=1, source_target_pairs={{0,1},{1,0},{2,3},{3,2},{4,5},{5,4},{6,7},{7,6},{8,9},{9,8},{10,11... | collective-permute-start | bytes 3145736 | tf_op jit(solution)/shard_map/ppermute | solution.py:131
  55.6 18.0 %collective-permute-start.17 = (bf16[512,512]{1,0:T(8,128)(2,1)}, bf16[512,512]{1,0:T(8,128)(2,1)}, u32[]{:S(2)}, u32[]{:S(2)}) collective-permute-start(bf16[512,512]{1,0:T(8,128)(2,1)} %dynamic-slice_bitcast_fusion), channel_id=1, source_target_pairs={{0,4},{4,0},{8,12},{12,8},{16,20},{20,16},{24,28},{28,24},{1,5},{5... | collective-permute-start | bytes 1572872 | tf_op jit(solution)/shard_map/ppermute | solution.py:131
  58.0 30.3 %collective-permute-start.9 = (bf16[512,512]{1,0:T(8,128)(2,1)}, bf16[512,512]{1,0:T(8,128)(2,1)}, u32[]{:S(2)}, u32[]{:S(2)}) collective-permute-start(bf16[512,512]{1,0:T(8,128)(2,1)} %constant_dynamic-slice_fusion), channel_id=1, source_target_pairs={{0,4},{4,0},{8,12},{12,8},{16,20},{20,16},{24,28},{28,24},{1,5},{5... | collective-permute-start | bytes 1572872 | tf_op jit(solution)/shard_map/ppermute | solution.py:131
  58.6 35.9 %collective-permute-start.4 = (bf16[512,512]{1,0:T(8,128)(2,1)S(1)}, bf16[512,512]{1,0:T(8,128)(2,1)S(1)}, u32[]{:S(2)}, u32[]{:S(2)}) collective-permute-start(bf16[512,512]{1,0:T(8,128)(2,1)S(1)} %dynamic-slice_bitcast_fusion.2), channel_id=1, source_target_pairs={{0,4},{4,0},{8,12},{12,8},{16,20},{20,16},{24,28},{28,24},{1,5},{5... | collective-permute-start | bytes 1572872 | tf_op jit(solution)/shard_map/ppermute | solution.py:131
  79.2 30.7 %collective-permute-start.21 = (bf16[2,1024,128]{2,1,0:T(8,128)(2,1)S(1)}, bf16[2,1024,128]{2,1,0:T(8,128)(2,1)S(1)}, u32[]{:S(2)}, u32[]{:S(2)}) collective-permute-start(bf16[2,1024,128]{2,1,0:T(8,128)(2,1)S(1)} %get-tuple-element.42), channel_id=1, source_target_pairs={{24,16},{28,20},{25,17},{29,21},{26,18},{30,22},{27,19},{31,23}} | collective-permute-start | bytes 1572872 | tf_op jit(solution)/shard_map/ppermute | solution.py:153
  80.0 29.9 %collective-permute-start.18 = (bf16[2,1024,128]{2,1,0:T(8,128)(2,1)S(1)}, bf16[2,1024,128]{2,1,0:T(8,128)(2,1)S(1)}, u32[]{:S(2)}, u32[]{:S(2)}) collective-permute-start(bf16[2,1024,128]{2,1,0:T(8,128)(2,1)S(1)} %get-tuple-element.43), channel_id=1, source_target_pairs={{0,8},{4,12},{1,9},{5,13},{2,10},{6,14},{3,11},{7,15}} | collective-permute-start | bytes 1572872 | tf_op jit(solution)/shard_map/ppermute | solution.py:153
  102.9 18.9 %collective-permute-start.10 = (bf16[2,1024,128]{2,1,0:T(8,128)(2,1)}, bf16[2,1024,128]{2,1,0:T(8,128)(2,1)}, u32[]{:S(2)}, u32[]{:S(2)}) collective-permute-start(bf16[2,1024,128]{2,1,0:T(8,128)(2,1)} %get-tuple-element.49), channel_id=1, source_target_pairs={{0,8},{4,12},{1,9},{5,13},{2,10},{6,14},{3,11},{7,15}} | collective-permute-start | bytes 1572872 | tf_op jit(solution)/shard_map/ppermute | solution.py:153
  112.7 20.3 %collective-permute-start.19 = (bf16[2,1024,128]{2,1,0:T(8,128)(2,1)}, bf16[2,1024,128]{2,1,0:T(8,128)(2,1)}, u32[]{:S(2)}, u32[]{:S(2)}) collective-permute-start(bf16[2,1024,128]{2,1,0:T(8,128)(2,1)} %get-tuple-element.41), channel_id=1, source_target_pairs={{0,8},{4,12},{8,16},{12,20},{1,9},{5,13},{9,17},{13,21},{2,10},{6,... | collective-permute-start | bytes 1572872 | tf_op jit(solution)/shard_map/ppermute | solution.py:153
  123.9 20.2 %collective-permute-start.11 = (bf16[2,1024,128]{2,1,0:T(8,128)(2,1)S(1)}, bf16[2,1024,128]{2,1,0:T(8,128)(2,1)S(1)}, u32[]{:S(2)}, u32[]{:S(2)}) collective-permute-start(bf16[2,1024,128]{2,1,0:T(8,128)(2,1)S(1)} %get-tuple-element.47), channel_id=1, source_target_pairs={{0,8},{4,12},{8,16},{12,20},{1,9},{5,13},{9,17},{13,21},{2,10},{6,... | collective-permute-start | bytes 1572872 | tf_op jit(solution)/shard_map/ppermute | solution.py:153
  135.9 19.5 %collective-permute-start.20 = (bf16[2,1024,128]{2,1,0:T(8,128)(2,1)S(1)}, bf16[2,1024,128]{2,1,0:T(8,128)(2,1)S(1)}, u32[]{:S(2)}, u32[]{:S(2)}) collective-permute-start(bf16[2,1024,128]{2,1,0:T(8,128)(2,1)S(1)} %get-tuple-element.39), channel_id=1, source_target_pairs={{0,8},{4,12},{8,16},{12,20},{16,24},{20,28},{1,9},{5,13},{9,17},{1... | collective-permute-start | bytes 1572872 | tf_op jit(solution)/shard_map/ppermute | solution.py:153
  144.4 20.8 %collective-permute-start.15 = (bf16[2,1024,128]{2,1,0:T(8,128)(2,1)S(1)}, bf16[2,1024,128]{2,1,0:T(8,128)(2,1)S(1)}, u32[]{:S(2)}, u32[]{:S(2)}) collective-permute-start(bf16[2,1024,128]{2,1,0:T(8,128)(2,1)S(1)} %get-tuple-element.44), channel_id=1, source_target_pairs={{8,0},{12,4},{16,8},{20,12},{24,16},{28,20},{9,1},{13,5},{17,9},{2... | collective-permute-start | bytes 1572872 | tf_op jit(solution)/shard_map/ppermute | solution.py:153
  145.7 19.6 %collective-permute-start.12 = (bf16[2,1024,128]{2,1,0:T(8,128)(2,1)S(1)}, bf16[2,1024,128]{2,1,0:T(8,128)(2,1)S(1)}, u32[]{:S(2)}, u32[]{:S(2)}) collective-permute-start(bf16[2,1024,128]{2,1,0:T(8,128)(2,1)S(1)} %get-tuple-element.45), channel_id=1, source_target_pairs={{0,8},{4,12},{8,16},{12,20},{16,24},{20,28},{1,9},{5,13},{9,17},{1... | collective-permute-start | bytes 1572872 | tf_op jit(solution)/shard_map/ppermute | solution.py:153
  182.4 22.1 %collective-permute-start.27 = (bf16[2,1024,128]{2,1,0:T(8,128)(2,1)S(1)}, bf16[2,1024,128]{2,1,0:T(8,128)(2,1)S(1)}, u32[]{:S(2)}, u32[]{:S(2)}) collective-permute-start(bf16[2,1024,128]{2,1,0:T(8,128)(2,1)S(1)} %get-tuple-element.19.refs_0_), channel_id=1, source_target_pairs={{8,0},{12,4},{16,8},{20,12},{24,16},{28,20},{9,1},{13,5},{17,9},{2... | collective-permute-start | bytes 1572872 | tf_op jit(solution)/shard_map/ppermute | solution.py:153
  183.7 22.1 %collective-permute-start.24 = (bf16[2,1024,128]{2,1,0:T(8,128)(2,1)S(1)}, bf16[2,1024,128]{2,1,0:T(8,128)(2,1)S(1)}, u32[]{:S(2)}, u32[]{:S(2)}) collective-permute-start(bf16[2,1024,128]{2,1,0:T(8,128)(2,1)S(1)} %get-tuple-element.19.refs_0_), channel_id=1, source_target_pairs={{0,8},{4,12},{8,16},{12,20},{16,24},{20,28},{1,9},{5,13},{9,17},{1... | collective-permute-start | bytes 1572872 | tf_op jit(solution)/shard_map/ppermute | solution.py:153
  193.2 22.5 %collective-permute-start.38 = (bf16[2,1024,128]{2,1,0:T(8,128)(2,1)S(1)}, bf16[2,1024,128]{2,1,0:T(8,128)(2,1)S(1)}, u32[]{:S(2)}, u32[]{:S(2)}) collective-permute-start(bf16[2,1024,128]{2,1,0:T(8,128)(2,1)S(1)} %collective-permute-done.37.refs_4_), channel_id=1, source_target_pairs={{8,0},{12,4},{16,8},{20,12},{9,1},{13,5},{17,9},{21,13},{10,2},{14... | collective-permute-start | bytes 1572872 | tf_op jit(solution)/shard_map/ppermute | solution.py:153
  194.5 22.5 %collective-permute-start.35 = (bf16[2,1024,128]{2,1,0:T(8,128)(2,1)S(1)}, bf16[2,1024,128]{2,1,0:T(8,128)(2,1)S(1)}, u32[]{:S(2)}, u32[]{:S(2)}) collective-permute-start(bf16[2,1024,128]{2,1,0:T(8,128)(2,1)S(1)} %collective-permute-done.34.refs_1_), channel_id=1, source_target_pairs={{8,16},{12,20},{16,24},{20,28},{9,17},{13,21},{17,25},{21,29},{10,... | collective-permute-start | bytes 1572872 | tf_op jit(solution)/shard_map/ppermute | solution.py:153
  204.5 22.5 %collective-permute-start.28 = (bf16[2,1024,128]{2,1,0:T(8,128)(2,1)S(1)}, bf16[2,1024,128]{2,1,0:T(8,128)(2,1)S(1)}, u32[]{:S(2)}, u32[]{:S(2)}) collective-permute-start(bf16[2,1024,128]{2,1,0:T(8,128)(2,1)S(1)} %collective-permute-done.27.refs_4_), channel_id=1, source_target_pairs={{8,0},{12,4},{16,8},{20,12},{9,1},{13,5},{17,9},{21,13},{10,2},{14... | collective-permute-start | bytes 1572872 | tf_op jit(solution)/shard_map/ppermute | solution.py:153
  205.8 22.5 %collective-permute-start.25 = (bf16[2,1024,128]{2,1,0:T(8,128)(2,1)S(1)}, bf16[2,1024,128]{2,1,0:T(8,128)(2,1)S(1)}, u32[]{:S(2)}, u32[]{:S(2)}) collective-permute-start(bf16[2,1024,128]{2,1,0:T(8,128)(2,1)S(1)} %collective-permute-done.24.refs_1_), channel_id=1, source_target_pairs={{8,16},{12,20},{16,24},{20,28},{9,17},{13,21},{17,25},{21,29},{10,... | collective-permute-start | bytes 1572872 | tf_op jit(solution)/shard_map/ppermute | solution.py:153
  215.7 22.5 %collective-permute-start.39 = (bf16[2,1024,128]{2,1,0:T(8,128)(2,1)S(1)}, bf16[2,1024,128]{2,1,0:T(8,128)(2,1)S(1)}, u32[]{:S(2)}, u32[]{:S(2)}) collective-permute-start(bf16[2,1024,128]{2,1,0:T(8,128)(2,1)S(1)} %collective-permute-done.38.refs_5_), channel_id=1, source_target_pairs={{8,0},{12,4},{9,1},{13,5},{10,2},{14,6},{11,3},{15,7}} | collective-permute-start | bytes 1572872 | tf_op jit(solution)/shard_map/ppermute | solution.py:153
  217.0 21.2 %collective-permute-start.36 = (bf16[2,1024,128]{2,1,0:T(8,128)(2,1)S(1)}, bf16[2,1024,128]{2,1,0:T(8,128)(2,1)S(1)}, u32[]{:S(2)}, u32[]{:S(2)}) collective-permute-start(bf16[2,1024,128]{2,1,0:T(8,128)(2,1)S(1)} %collective-permute-done.35.refs_2_), channel_id=1, source_target_pairs={{16,24},{20,28},{17,25},{21,29},{18,26},{22,30},{19,27},{23,31}} | collective-permute-start | bytes 1572872 | tf_op jit(solution)/shard_map/ppermute | solution.py:153
  226.9 20.6 %collective-permute-start.29 = (bf16[2,1024,128]{2,1,0:T(8,128)(2,1)S(1)}, bf16[2,1024,128]{2,1,0:T(8,128)(2,1)S(1)}, u32[]{:S(2)}, u32[]{:S(2)}) collective-permute-start(bf16[2,1024,128]{2,1,0:T(8,128)(2,1)S(1)} %collective-permute-done.28.refs_5_), channel_id=1, source_target_pairs={{8,0},{12,4},{9,1},{13,5},{10,2},{14,6},{11,3},{15,7}} | collective-permute-start | bytes 1572872 | tf_op jit(solution)/shard_map/ppermute | solution.py:153
  228.2 19.3 %collective-permute-start.26 = (bf16[2,1024,128]{2,1,0:T(8,128)(2,1)S(1)}, bf16[2,1024,128]{2,1,0:T(8,128)(2,1)S(1)}, u32[]{:S(2)}, u32[]{:S(2)}) collective-permute-start(bf16[2,1024,128]{2,1,0:T(8,128)(2,1)S(1)} %collective-permute-done.25.refs_2_), channel_id=1, source_target_pairs={{16,24},{20,28},{17,25},{21,29},{18,26},{22,30},{19,27},{23,31}} | collective-permute-start | bytes 1572872 | tf_op jit(solution)/shard_map/ppermute | solution.py:153
  257.2 19.8 %collective-permute-start.40 = (bf16[2,2,128,1024]{3,2,1,0:T(8,128)(2,1)}, bf16[2,2,128,1024]{3,2,1,0:T(8,128)(2,1)}, u32[]{:S(2)}, u32[]{:S(2)}) collective-permute-start(bf16[2,2,128,1024]{3,2,1,0:T(8,128)(2,1)} %bitcast.36), channel_id=1, source_target_pairs={{0,1},{1,0},{2,3},{3,2},{4,5},{5,4},{6,7},{7,6},{8,9},{9,8},{10,11... | collective-permute-start | bytes 3145736 | tf_op jit(solution)/shard_map/ppermute | solution.py:131
  272.4 56.2 %collective-permute-start.47 = (bf16[512,512]{1,0:T(8,128)(2,1)S(1)}, bf16[512,512]{1,0:T(8,128)(2,1)S(1)}, u32[]{:S(2)}, u32[]{:S(2)}) collective-permute-start(bf16[512,512]{1,0:T(8,128)(2,1)S(1)} %get-tuple-element.28), channel_id=1, source_target_pairs={{0,4},{4,0},{8,12},{12,8},{16,20},{20,16},{24,28},{28,24},{1,5},{5... | collective-permute-start | bytes 1572872 | tf_op jit(solution)/shard_map/ppermute | solution.py:131
  276.5 107.7 %collective-permute-start.44 = (bf16[512,512]{1,0:T(8,128)(2,1)S(1)}, bf16[512,512]{1,0:T(8,128)(2,1)S(1)}, u32[]{:S(2)}, u32[]{:S(2)}) collective-permute-start(bf16[512,512]{1,0:T(8,128)(2,1)S(1)} %get-tuple-element.22), channel_id=1, source_target_pairs={{0,4},{4,0},{8,12},{12,8},{16,20},{20,16},{24,28},{28,24},{1,5},{5... | collective-permute-start | bytes 1572872 | tf_op jit(solution)/shard_map/ppermute | solution.py:131
  278.8 30.8 %collective-permute-start.41 = (bf16[2,128,1024]{2,1,0:T(8,128)(2,1)S(1)}, bf16[2,128,1024]{2,1,0:T(8,128)(2,1)S(1)}, u32[]{:S(2)}, u32[]{:S(2)}) collective-permute-start(bf16[2,128,1024]{2,1,0:T(8,128)(2,1)S(1)} %slice_bitcast_fusion), channel_id=1, source_target_pairs={{0,4},{4,0},{8,12},{12,8},{16,20},{20,16},{24,28},{28,24},{1,5},{5... | collective-permute-start | bytes 1572872 | tf_op jit(solution)/shard_map/ppermute | solution.py:131
  282.3 27.7 %collective-permute-start.31 = (bf16[2,128,1024]{2,1,0:T(8,128)(2,1)S(1)}, bf16[2,128,1024]{2,1,0:T(8,128)(2,1)S(1)}, u32[]{:S(2)}, u32[]{:S(2)}) collective-permute-start(bf16[2,128,1024]{2,1,0:T(8,128)(2,1)S(1)} %slice_bitcast_fusion.2), channel_id=1, source_target_pairs={{0,2},{1,3},{2,0},{3,1},{4,6},{5,7},{6,4},{7,5},{8,10},{9,11},{10,... | collective-permute-start | bytes 1572872 | tf_op jit(solution)/shard_map/ppermute | solution.py:131
  285.0 99.2 %collective-permute-start.45 = (bf16[512,512]{1,0:T(8,128)(2,1)}, bf16[512,512]{1,0:T(8,128)(2,1)S(1)}, u32[]{:S(2)}, u32[]{:S(2)}) collective-permute-start(bf16[512,512]{1,0:T(8,128)(2,1)} %get-tuple-element.24), channel_id=1, source_target_pairs={{0,4},{4,0},{8,12},{12,8},{16,20},{20,16},{24,28},{28,24},{1,5},{5... | collective-permute-start | bytes 1572872 | tf_op jit(solution)/shard_map/ppermute | solution.py:131
  317.5 66.8 %collective-permute-start.46 = (bf16[512,512]{1,0:T(8,128)(2,1)}, bf16[512,512]{1,0:T(8,128)(2,1)S(1)}, u32[]{:S(2)}, u32[]{:S(2)}) collective-permute-start(bf16[512,512]{1,0:T(8,128)(2,1)} %get-tuple-element.26), channel_id=1, source_target_pairs={{0,4},{4,0},{8,12},{12,8},{16,20},{20,16},{24,28},{28,24},{1,5},{5... | collective-permute-start | bytes 1572872 | tf_op jit(solution)/shard_map/ppermute | solution.py:131
  326.5 60.4 %collective-permute-start.43 = (bf16[128,1024]{1,0:T(8,128)(2,1)S(1)}, bf16[128,1024]{1,0:T(8,128)(2,1)}, u32[]{:S(2)}, u32[]{:S(2)}) collective-permute-start(bf16[128,1024]{1,0:T(8,128)(2,1)S(1)} %fusion.8), channel_id=1, source_target_pairs={{0,0},{1,8},{2,16},{3,24},{4,4},{5,12},{6,20},{7,28},{8,1},{9,9},{... | collective-permute-start | bytes 786440 | tf_op jit(solution)/shard_map/ppermute | solution.py:142
  328.6 58.3 %collective-permute-start.33 = (bf16[128,1024]{1,0:T(8,128)(2,1)}, bf16[128,1024]{1,0:T(8,128)(2,1)}, u32[]{:S(2)}, u32[]{:S(2)}) collective-permute-start(bf16[128,1024]{1,0:T(8,128)(2,1)} %fusion.9), channel_id=1, source_target_pairs={{0,0},{1,8},{2,16},{3,24},{4,4},{5,12},{6,20},{7,28},{8,1},{9,9},{... | collective-permute-start | bytes 786440 | tf_op jit(solution)/shard_map/ppermute | solution.py:142
  (39 other events, 499.3 us)

commit v3 on v2

--- a/solution.py
+++ b/solution.py
@@ -131,15 +131,33 @@
     return lax.ppermute(value, axis, [(i, i ^ bit) for i in range(lax.axis_size(axis))])
 
 
-def trade_places(value):
+def crossed(index):
+    return 2 * (index % 2) + index // 2
+
+
+def trade_places(value, back):
     size = lax.axis_size("fsdp")
     pairs = [
-        ((2 * line + pair) * size + own, (2 * own + pair) * size + line)
+        ((2 * line + pair) * size + own, (2 * own + pair) * size + crossed(line))
         for line in range(size)
         for pair in range(2)
         for own in range(size)
     ]
+    return lax.ppermute(value, ("seq", "fsdp"), [p[::-1] for p in pairs] if back else pairs)
+
+
+def flip_both(value):
+    size = lax.axis_size("fsdp")
+    pairs = [
+        (seq * size + own, (seq ^ 1) * size + (own ^ 2))
+        for seq in range(lax.axis_size("seq"))
+        for own in range(size)
+    ]
     return lax.ppermute(value, ("seq", "fsdp"), pairs)
+
+
+def after(values, *others):
+    return lax.optimization_barrier((values, others))[0]
 
 
 def along_line(value, by, holds):
@@ -169,16 +187,11 @@
     return up_in, down_in
 
 
-def line_gather(block):
+def next_block(block, by, step):
     length = lax.axis_size("seq") // 2
-    before, after = [], []
-    up = down = block
-    for step in range(1, length):
-        up = along_line(up, 1, lambda i: i >= step - 1)
-        down = along_line(down, -1, lambda i: i <= length - step)
-        before.append(up)
-        after.append(down)
-    return before, after
+    if by > 0:
+        return along_line(block, 1, lambda i: i >= step - 1)
+    return along_line(block, -1, lambda i: i <= length - step)
 
 
 def project_pair(place, first, second):
@@ -350,8 +363,9 @@
                 + down_ref[1, rows, :].astype(f32)
             )
             kept = filtered_ref[place, :]
-            out_ref[0, rows, :] = (queries * kept).astype(bf16)
-            out_ref[1, rows, :] = (grad_gated * kept).astype(bf16)
+            out_ref[rows, :] = (queries * kept).astype(bf16)
+            later = pl.ds(pl.multiple_of(tokens + r * size, size), size)
+            out_ref[later, :] = (grad_gated * kept).astype(bf16)
             grad_ref[place, :] = (grad_gated * queries).astype(bf16)
             return carry
 
@@ -361,7 +375,7 @@
     return pl.pallas_call(
         body,
         out_shape=(
-            jax.ShapeDtypeStruct((2, tokens, lanes), bf16),
+            jax.ShapeDtypeStruct((2 * tokens, lanes), bf16),
             jax.ShapeDtypeStruct((tokens, lanes), bf16),
         ),
         grid_spec=pltpu.PrefetchScalarGridSpec(
@@ -373,7 +387,7 @@
                 whole((2, tokens, lanes)),
                 whole((tokens, lanes)),
             ],
-            out_specs=(whole((2, tokens, lanes)), whole((tokens, lanes))),
+            out_specs=(whole((2 * tokens, lanes)), whole((tokens, lanes))),
         ),
         compiler_params=params(),
         cost_estimate=cost(20 * tokens * lanes, 20 * tokens * lanes),
@@ -381,19 +395,24 @@
     )(order, blocks, up, down, filtered)
 
 
-def backward_filter(order, grad_filtered, key_values, spread_taps):
+def backward_filter(order, grad_filtered, key_values, signal, spread_taps):
     tokens = grad_filtered.shape[0]
     taps = spread_taps.shape[0] // sublanes
     n_blocks = order.shape[0]
     size = tokens // n_blocks
     tiles = 8
-
-    def body(order_ref, grad_ref, kv_ref, taps_ref, out_ref, moved, signal_grad):
+    steps = taps // sublanes
+
+    def body(order_ref, grad_ref, kv_ref, signal_ref, taps_ref, out_ref, moved, signal_grad, behind, gradient):
         for shift in range(sublanes):
             moved[shift, tokens - sublanes :, :] = jnp.zeros((taps + sublanes, lanes), f32)
+            behind[shift, : taps + sublanes, :] = jnp.zeros((taps + sublanes, lanes), f32)
         moved[0, :tokens, :] = grad_ref[...].astype(f32)
+        behind[0, taps:, :] = signal_ref[...].astype(f32)
+        gradient[...] = grad_ref[...].astype(f32)
         for shift in range(1, sublanes):
             moved[shift, :tokens, :] = moved[0, shift : shift + tokens, :]
+            behind[shift, taps:, :] = behind[0, taps - shift : taps - shift + tokens, :]
 
         def run(g, carry):
             start = pl.multiple_of(g * tiles * sublanes, tiles * sublanes)
@@ -413,54 +432,18 @@
         lax.fori_loop(0, tokens // (tiles * sublanes), run, 0)
 
         def one_block(r, carry):
-            rows = pl.ds(pl.multiple_of(r * size, size), size)
+            start = pl.multiple_of(r * size, size)
             place = block_rows(order_ref, r, size)
-            gradient = signal_grad[place, :]
-            out_ref[0, rows, :] = (gradient * kv_ref[1, place, :].astype(f32)).astype(bf16)
-            out_ref[1, rows, :] = (gradient * kv_ref[0, place, :].astype(f32)).astype(bf16)
+            value = signal_grad[place, :]
+            out_ref[pl.ds(start, size), :] = (value * kv_ref[1, place, :].astype(f32)).astype(bf16)
+            out_ref[pl.ds(tokens + start, size), :] = (value * kv_ref[0, place, :].astype(f32)).astype(bf16)
             return carry
 
         lax.fori_loop(0, n_blocks, one_block, 0)
 
-    whole = lambda shape: pl.BlockSpec(shape, lambda g, order: (0,) * len(shape))
-    return pl.pallas_call(
-        body,
-        out_shape=jax.ShapeDtypeStruct((2, tokens, lanes), bf16),
-        grid_spec=pltpu.PrefetchScalarGridSpec(
-            num_scalar_prefetch=1,
-            grid=(1,),
-            in_specs=[
-                whole((tokens, lanes)),
-                whole((2, tokens, lanes)),
-                whole(spread_taps.shape),
-            ],
-            out_specs=whole((2, tokens, lanes)),
-            scratch_shapes=[
-                pltpu.VMEM((sublanes, tokens + taps, lanes), f32),
-                pltpu.VMEM((tokens, lanes), f32),
-            ],
-        ),
-        compiler_params=params(),
-        cost_estimate=cost(400 * tokens * lanes * taps, 12 * tokens * lanes),
-        name="backward_filter",
-    )(order, grad_filtered, key_values, spread_taps)
-
-
-def taps_gradient(signal, grad_filtered, taps):
-    tokens = signal.shape[0]
-    tiles = 8
-    steps = taps // sublanes
-
-    def body(signal_ref, grad_ref, out_ref, moved, gradient):
         for shift in range(sublanes):
-            moved[shift, : taps + sublanes, :] = jnp.zeros((taps + sublanes, lanes), f32)
-        moved[0, taps:, :] = signal_ref[...].astype(f32)
-        gradient[...] = grad_ref[...].astype(f32)
-        for shift in range(1, sublanes):
-            moved[shift, taps : taps + tokens, :] = moved[0, taps - shift : taps - shift + tokens, :]
-        for shift in range(sublanes):
-
-            def run(g, sums):
+
+            def sum_run(g, sums):
                 start = pl.multiple_of(g * tiles * sublanes, tiles * sublanes)
                 sums = list(sums)
                 held = {}
@@ -468,35 +451,48 @@
                     here = gradient[pl.ds(start + i * sublanes, sublanes), :]
                     for q in range(steps):
                         if i - q not in held:
-                            held[i - q] = moved[shift, pl.ds(start + taps + (i - q) * sublanes, sublanes), :]
+                            held[i - q] = behind[shift, pl.ds(start + taps + (i - q) * sublanes, sublanes), :]
                         sums[q] = sums[q] + here * held[i - q]
                 return tuple(sums)
 
             zero = tuple(jnp.zeros((sublanes, lanes), f32) for _ in range(steps))
-            sums = lax.fori_loop(0, tokens // (tiles * sublanes), run, zero)
+            sums = lax.fori_loop(0, tokens // (tiles * sublanes), sum_run, zero)
             for q in range(steps):
                 index = q * sublanes + shift
-                out_ref[index : index + 1, :] = jnp.sum(sums[q], axis=0, keepdims=True)
-
-    return pl.pallas_call(
-        body,
-        out_shape=jax.ShapeDtypeStruct((taps, lanes), f32),
-        in_specs=[pl.BlockSpec(memory_space=pltpu.VMEM)] * 2,
-        out_specs=pl.BlockSpec(memory_space=pltpu.VMEM),
-        scratch_shapes=[
-            pltpu.VMEM((sublanes, tokens + taps, lanes), f32),
-            pltpu.VMEM((tokens, lanes), f32),
-        ],
-        compiler_params=params(),
-        cost_estimate=cost(400 * tokens * lanes * taps, 8 * tokens * lanes),
-        name="taps_gradient",
-    )(signal, grad_filtered)
-
-
-def merge_blocks(place, block, before, after):
-    tokens = block.shape[1]
+                signal_grad[index : index + 1, :] = jnp.sum(sums[q], axis=0, keepdims=True)
+        out_ref[2 * tokens :, :] = signal_grad[:taps, :].astype(bf16)
+
+    whole = lambda shape: pl.BlockSpec(shape, lambda g, order: (0,) * len(shape))
+    return pl.pallas_call(
+        body,
+        out_shape=jax.ShapeDtypeStruct((2 * tokens + taps, lanes), bf16),
+        grid_spec=pltpu.PrefetchScalarGridSpec(
+            num_scalar_prefetch=1,
+            grid=(1,),
+            in_specs=[
+                whole((tokens, lanes)),
+                whole((2, tokens, lanes)),
+                whole((tokens, lanes)),
+                whole(spread_taps.shape),
+            ],
+            out_specs=whole((2 * tokens + taps, lanes)),
+            scratch_shapes=[
+                pltpu.VMEM((sublanes, tokens + taps, lanes), f32),
+                pltpu.VMEM((tokens, lanes), f32),
+                pltpu.VMEM((sublanes, tokens + taps, lanes), f32),
+                pltpu.VMEM((tokens, lanes), f32),
+            ],
+        ),
+        compiler_params=params(),
+        cost_estimate=cost(800 * tokens * lanes * taps, 12 * tokens * lanes),
+        name="backward_filter",
+    )(order, grad_filtered, key_values, signal, spread_taps)
+
+
+def merge_blocks(place, block, before, behind, tokens):
     length = len(before) + 1
     rows = 256
+    steps = tokens // rows
 
     def body(place_ref, *refs):
         out = refs[-1]
@@ -508,22 +504,53 @@
             else:
                 value = downs[offset - 1][...] + ups[length - offset - 1][...]
             at = pl.multiple_of(lax.rem(line + offset, length) * lanes, lanes)
-            out[:, :, pl.ds(at, lanes)] = value
-
-    spec = pl.BlockSpec((2, rows, lanes), lambda g, place: (0, g, 0))
+            out[0, :, pl.ds(at, lanes)] = value
+
+    spec = pl.BlockSpec((rows, lanes), lambda which, g, place: (which * steps + g, 0))
     return pl.pallas_call(
         body,
         out_shape=jax.ShapeDtypeStruct((2, tokens, length * lanes), bf16),
         grid_spec=pltpu.PrefetchScalarGridSpec(
             num_scalar_prefetch=1,
-            grid=(tokens // rows,),
+            grid=(2, steps),
             in_specs=[spec] * (2 * length - 1),
-            out_specs=pl.BlockSpec((2, rows, length * lanes), lambda g, place: (0, g, 0)),
+            out_specs=pl.BlockSpec((1, rows, length * lanes), lambda which, g, place: (which, g, 0)),
         ),
         compiler_params=params(),
         cost_estimate=cost(tokens * lanes * 8, 2 * 2 * tokens * lanes * 11),
         name="merge_blocks",
-    )(place, block, *before, *after)
+    )(place, block, *before, *behind)
+
+
+def merge_taps(place, block, before, behind, taps):
+    length = len(before) + 1
+    last = block.shape[0] // taps - 1
+
+    def body(place_ref, *refs):
+        out = refs[-1]
+        own, ups, downs = refs[0], refs[1:length], refs[length : 2 * length - 1]
+        line = place_ref[0]
+        for offset in range(length):
+            if offset == 0:
+                value = own[...]
+            else:
+                value = downs[offset - 1][...] + ups[length - offset - 1][...]
+            at = pl.multiple_of(lax.rem(line + offset, length) * lanes, lanes)
+            out[pl.ds(at, lanes), :] = jnp.transpose(value.astype(f32)).astype(bf16)
+
+    return pl.pallas_call(
+        body,
+        out_shape=jax.ShapeDtypeStruct((length * lanes, taps), bf16),
+        grid_spec=pltpu.PrefetchScalarGridSpec(
+            num_scalar_prefetch=1,
+            grid=(1,),
+            in_specs=[pl.BlockSpec((taps, lanes), lambda g, place: (last, 0))] * (2 * length - 1),
+            out_specs=pl.BlockSpec((length * lanes, taps), lambda g, place: (0, 0)),
+        ),
+        compiler_params=params(),
+        cost_estimate=cost(taps * lanes * 8, 2 * taps * lanes * 11),
+        name="merge_taps",
+    )(place, block, *before, *behind)
 
 
 def project_back(place, merged, in_weight, given, indices):
@@ -734,89 +761,105 @@
     line, pair = seq_at // 2, seq_at % 2
     place = jnp.stack([line, pair]).astype(jnp.int32)
     half_in, half_out = in_weight.shape[2] // 2, out_weight.shape[0] // 2
+    width = tokens.shape[1]
+    count = tokens.shape[0] * lax.axis_size("seq")
     relative = jnp.arange(8, dtype=jnp.int32)
     order = (
-        2 * (fsdp_at ^ (2 * (relative % 2) + relative // 4)) + (pair ^ (relative // 2 % 2))
+        2 * crossed(fsdp_at ^ (2 * (relative % 2) + relative // 4)) + (pair ^ (relative // 2 % 2))
     ).astype(jnp.int32)
 
-    tokens_here = trade_places(tokens)
-    cot_here = trade_places(cotangent)
-    given_in = {}
-    for i in (1, 2, 0):
-        sent = lax.dynamic_slice_in_dim(in_weight[i], (1 - pair) * half_in, half_in, 1)
-        given_in[i] = flip(sent, "seq", 1)
-    given_out = flip(
-        lax.dynamic_slice_in_dim(out_weight, (1 - pair) * half_out, half_out, 0), "seq", 1
-    )
-    x_rows = jnp.stack([tokens_here, flip(tokens_here, "fsdp", 2)])
-    x_rows = jnp.stack([x_rows, flip(x_rows, "seq", 1)])
-    x_rows = jnp.stack([x_rows, flip(x_rows, "fsdp", 1)])
-    g_rows = jnp.stack([cot_here, flip(cot_here, "seq", 1)])
-    g_rows = jnp.stack([g_rows, flip(g_rows, "fsdp", 2)], axis=1)
-    g_rows = jnp.stack([g_rows, flip(g_rows, "fsdp", 1)])
-    width = tokens.shape[1]
-    x_rows = x_rows.reshape(-1, width)
-    g_rows = g_rows.reshape(-1, width)
-    turned = jnp.transpose(x_rows)
-    own_filters = lax.dynamic_slice_in_dim(
-        filters, pair * half_in + line * lanes, lanes, 0
-    )
+    def sent_in(i):
+        return lax.dynamic_slice_in_dim(in_weight[i], (1 - pair) * half_in, half_in, 1)
+
+    given_k, given_v = flip(sent_in(1), "seq", 1), flip(sent_in(2), "seq", 1)
+    x_own, g_own = trade_places(tokens, False), trade_places(cotangent, False)
+    x_own, given_k = lax.optimization_barrier((x_own, given_k))
+    x_rows = jnp.stack([x_own, flip(x_own, "fsdp", 2), flip(x_own, "seq", 1), flip_both(x_own)])
+    x_rows, given_v, g_own = lax.optimization_barrier((x_rows, given_v, g_own))
+    x_rows = jnp.stack([x_rows, flip(x_rows, "fsdp", 1)]).reshape(-1, width)
+    g_pair = jnp.stack([g_own, flip(g_own, "seq", 1)])
+    sent_out = lax.dynamic_slice_in_dim(out_weight, (1 - pair) * half_out, half_out, 0)
+    sent_q, sent_out = after((sent_in(0), sent_out), x_rows)
+    given_q, given_out = flip(sent_q, "seq", 1), flip(sent_out, "seq", 1)
+    g_rows = jnp.stack([g_pair, flip(g_pair, "fsdp", 2)], axis=1)
+    g_rows = jnp.stack([g_rows, flip(g_rows, "fsdp", 1)]).reshape(-1, width)
+    own_filters = lax.dynamic_slice_in_dim(filters, pair * half_in + line * lanes, lanes, 0)
     spread_taps = jnp.repeat(jnp.transpose(own_filters), sublanes, axis=0)
 
     kv_blocks = project_pair(
         place,
-        (x_rows, in_weight, given_in[1], False, 1),
-        (x_rows, in_weight, given_in[2], False, 2),
-    )
+        (x_rows, in_weight, given_k, False, 1),
+        (x_rows, in_weight, given_v, False, 2),
+    )
+    kv_up, kv_down = line_scatter(kv_blocks)
     qg_blocks = project_pair(
         place,
-        (x_rows, in_weight, given_in[0], False, 0),
+        (x_rows, in_weight, given_q, False, 0),
         (g_rows, out_weight, given_out, True, 0),
     )
-    kv_up, kv_down = line_scatter(kv_blocks)
+    turned = jnp.transpose(after(x_rows, qg_blocks))
     qg_up, qg_down = line_scatter(qg_blocks)
     key_values, signal, filtered = forward_filter(order, kv_blocks, kv_up, kv_down, spread_taps)
-    gated_pair, grad_filtered = gate_rows(order, qg_blocks, qg_up, qg_down, filtered)
-    gated_before, gated_after = line_gather(gated_pair)
-    kv_grads = backward_filter(order, grad_filtered, key_values, spread_taps)
-    kv_before, kv_after = line_gather(kv_grads)
-    own_taps = taps_gradient(signal, grad_filtered, taps)
-    all_taps = lax.all_gather(jnp.transpose(own_taps), "seq", axis=0)
-    length = lax.axis_size("seq") // 2
-    grad_filters = jnp.swapaxes(all_taps.reshape(length, 2, lanes, taps), 0, 1).reshape(filters.shape)
-
-    first = merge_blocks(place, gated_pair, gated_before, gated_after)
-    mixed_part = project_out(place, first, out_weight, given_out)
+    gated_rows, grad_filtered = gate_rows(order, qg_blocks, qg_up, qg_down, filtered)
+
+    gated_before = [next_block(gated_rows, 1, 1)]
+    gated_behind = [next_block(gated_rows, -1, 1)]
+    grad_filtered = after(grad_filtered, gated_before[0], gated_behind[0])
+    kv_grads = backward_filter(order, grad_filtered, key_values, signal, spread_taps)
+    for step in (2, 3):
+        gated_before.append(next_block(gated_before[-1], 1, step))
+        gated_behind.append(next_block(gated_behind[-1], -1, step))
+        if step == 2:
+            kv_grads = after(kv_grads, gated_before[-1], gated_behind[-1])
+    kv_before = [next_block(kv_grads, 1, 1)]
+    kv_behind = [next_block(kv_grads, -1, 1)]
+    kv_before.append(next_block(kv_before[0], 1, 2))
+    kv_behind.append(next_block(kv_behind[0], -1, 2))
+
+    first = merge_blocks(place, gated_rows, gated_before, gated_behind, count)
     out_kept, out_sent = out_gradient(place, first, g_rows)
     in_kept, q_sent = in_gradient(place, turned, first, 1, 0, in_weight.shape[0], None)
-    out_given = flip(out_sent, "seq", 1)
-    q_given = flip(q_sent, "seq", 1)
-
-    second = merge_blocks(place, kv_grads, kv_before, kv_after)
+    mixed_part = project_out(place, first, out_weight, given_out)
+    out_given, q_given = flip(out_sent, "seq", 1), flip(q_sent, "seq", 1)
+    last_up, last_down = after((kv_before[1], kv_behind[1]), out_sent, q_sent, mixed_part)
+    kv_before.append(next_block(last_up, 1, 3))
+    kv_behind.append(next_block(last_down, -1, 3))
+
+    def across_cores(part):
+        parts = part.reshape(2, 4, count // 8, width)
+        return added(parts[0], flip(parts[1], "fsdp", 1))
+
+    mixed_part = across_cores(mixed_part)
+    kv_behind[2], kv_before[2], mixed_part, out_given, q_given = lax.optimization_barrier(
+        (kv_behind[2], kv_before[2], mixed_part, out_given, q_given)
+    )
+    second = merge_blocks(place, kv_grads, kv_before, kv_behind, count)
     grad_part = project_back(
         place,
         [(first, 1), (second, 0), (second, 1)],
         in_weight,
-        [given_in[0], given_in[1], given_in[2]],
+        [given_q, given_k, given_v],
         [0, 1, 2],
     )
+
+    def outward(parts):
+        total = parts[0].astype(f32) + flip(parts[1], "fsdp", 2).astype(f32)
+        total += flip(parts[2], "seq", 1).astype(f32) + flip_both(parts[3]).astype(f32)
+        return trade_places(total.astype(bf16), True)
+
+    mixed_out = outward(mixed_part)
+    grad_part = across_cores(grad_part)
+    grad_tokens = outward(grad_part)
     in_kept, k_sent = in_gradient(place, turned, second, 0, 1, in_weight.shape[0], in_kept)
     in_kept, v_sent = in_gradient(place, turned, second, 1, 2, in_weight.shape[0], in_kept)
+    half_taps = merge_taps(place, kv_grads, kv_before, kv_behind, taps)
     k_given, v_given = flip(k_sent, "seq", 1), flip(v_sent, "seq", 1)
-
-    def outward(part, x_first):
-        parts = part.reshape(2, 2, 2, part.shape[0] // 8, width)
-        parts = added(parts[0], flip(parts[1], "fsdp", 1))
-        if x_first:
-            parts = added(parts[:, 0], flip(parts[:, 1], "fsdp", 2))
-            parts = added(parts[0], flip(parts[1], "seq", 1))
-        else:
-            parts = added(parts[0], flip(parts[1], "seq", 1))
-            parts = added(parts[0], flip(parts[1], "fsdp", 2))
-        return trade_places(parts)
-
-    mixed_out = outward(mixed_part, True)
-    grad_tokens = outward(grad_part, False)
+    given_taps = flip(half_taps, "seq", 1)
+    grad_filters = jnp.where(
+        pair == 0,
+        jnp.concatenate([half_taps, given_taps], 0),
+        jnp.concatenate([given_taps, half_taps], 0),
+    ).astype(f32)
     grad_out_weight = take_out_half(place, out_kept, out_given)
     grad_in_weight = take_in_half(place, in_kept, [q_given, k_given, v_given])
     return (mixed_out, grad_tokens, grad_in_weight, grad_out_weight, grad_filters)

time: 392 us -> 337 us (0.86)
  blocking collectives: 41.7 us -> 0 us
  starting transfers between devices: 103 us -> 81.5 us
  waiting for transfers between devices: 139 us -> 156 us
  local copies, waits for them, and re-layouts: 24.7 us -> 19.2 us
    all_gather x1 -> x0, blocking collectives: 41.7 us -> none  [on_paired_mesh(): all_taps = lax.all_gather(jnp.transpose(own_taps), 'seq', axis=0)]
    ppermute x20 -> x21, waiting for transfers between devices: 75.3 us -> 93.6 us  [flip(): lax.ppermute(value, axis, [(i, i ^ bit) for i in range(lax.axis_size(axis...]
    ppermute x20 -> x21, starting transfers between devices: 34.8 us -> 20.9 us  [flip(): lax.ppermute(value, axis, [(i, i ^ bit) for i in range(lax.axis_size(axis...]
    ppermute x24, waiting for transfers between devices: 63.3 us -> 50.1 us  [along_line(): return lax.ppermute(value, 'seq', pairs)]
    ppermute x4 -> x7, waiting for transfers between devices: 0.01 us -> 12.4 us  [the longest x3 12.3 us: flip_both(): return lax.ppermute(value, ('seq', 'fsdp'), pairs)]
    ppermute x24, starting transfers between devices: 60.4 us -> 54 us  [along_line(): return lax.ppermute(value, 'seq', pairs)]
    convert_element_type x10 -> x6, other arithmetic: 9.34 us -> 5.22 us  [added(): return (one.astype(f32) + other.astype(f32)).astype(bf16)]
    unnamed x48 -> x60, local copies, waits for them, and re-layouts: 9.26 us -> 7.37 us
  transfers between devices with their start and end apart: 48 -> 52, of which waited for: 20 -> 24; matrix products, arithmetic and copies ran while one was open for 7% -> 6% of each run, Pallas kernels for 12% -> 17%
where the time goes in v3:
time: 337 us; the launch traced here: 334 us
  waiting for transfers between devices  156 us (46%)
  starting transfers between devices  81.5 us (24%)
  Pallas kernels  64.9 us (19%)
  local copies, waits for them, and re-layouts  19.2 us (6%)
  other arithmetic  11.3 us (3%)
    ppermute x21, waiting for transfers between devices, flip(): lax.ppermute(value, axis, [(i, i ^ bit) for i in range(lax.axis_size(axis...  93.6 us
    ppermute x24, starting transfers between devices, along_line(): return lax.ppermute(value, 'seq', pairs)  54 us
    ppermute x24, waiting for transfers between devices, along_line(): return lax.ppermute(value, 'seq', pairs)  50.1 us
    ppermute x21, starting transfers between devices, flip(): lax.ppermute(value, axis, [(i, i ^ bit) for i in range(lax.axis_size(axis...  20.9 us
    pallas_call x1, Pallas kernels, backward_filter(): pl.pallas_call(body, out_shape=jax.ShapeDtypeStruct((2 * tokens + taps, l...  15.2 us
    ppermute x3, waiting for transfers between devices, flip_both(): return lax.ppermute(value, ('seq', 'fsdp'), pairs)  12.3 us
    pallas_call x2, Pallas kernels, project_pair(): pl.pallas_call(body, out_shape=jax.ShapeDtypeStruct((count, 2, tokens, la...  11 us
    pallas_call x1, Pallas kernels, forward_filter(): pl.pallas_call(body, out_shape=(jax.ShapeDtypeStruct((2, tokens, lanes),...  9.86 us
  transfers between devices with their start and end apart: 52, of which 24 were waited for; matrix products, arithmetic and copies ran while one was open for 6% of the time, Pallas kernels for 17%

profile of v3, /device:TPU:0, one launch (start us, length us, event | category | flops | bytes accessed | tf_op | source)
XLA Modules:
  0.0 334.4 jit_solution(18162823225806306027)
XLA Ops:
  0.7 3.2 fusion.21
  7.8 11.9 %collective-permute-done.1.refs_3_.refs_5_ = bf16[512,512]{1,0:T(8,128)(2,1)S(1)} collective-permute-done((bf16[512,512]{1,0:T(8,128)(2,1)S(1)}, bf16[512,512]{1,0:T(8,128)(2,1)S(1)}, u32[]{:S(2)}, u32[]{:S(2)}) %collective-permute-start.1) | collective-permute-done | bytes 524320 | tf_op jit(solution)/shard_map/ppermute | solution.py:131
  23.9 5.6 %collective-permute-done.4 = bf16[128,1024]{1,0:T(8,128)(2,1)S(1)} collective-permute-done((bf16[128,1024]{1,0:T(8,128)(2,1)S(1)}, bf16[128,1024]{1,0:T(8,128)(2,1)S(1)}, u32[]{:S(2)}, u32[]{:S(2)}) %collective-permute-start.4) | collective-permute-done | bytes 262176 | tf_op jit(solution)/shard_map/ppermute | solution.py:156
  29.5 11.8 %collective-permute-done.3 = bf16[128,1024]{1,0:T(8,128)(2,1)S(1)} collective-permute-done((bf16[128,1024]{1,0:T(8,128)(2,1)S(1)}, bf16[128,1024]{1,0:T(8,128)(2,1)S(1)}, u32[]{:S(2)}, u32[]{:S(2)}) %collective-permute-start.3) | collective-permute-done | bytes 262176 | tf_op jit(solution)/shard_map/ppermute | solution.py:131
  44.2 6.7 %collective-permute-done.9 = bf16[128,1024]{1,0:T(8,128)(2,1)S(1)} collective-permute-done((bf16[128,1024]{1,0:T(8,128)(2,1)S(1)}, bf16[128,1024]{1,0:T(8,128)(2,1)S(1)}, u32[]{:S(2)}, u32[]{:S(2)}) %collective-permute-start.9) | collective-permute-done | bytes 262176 | tf_op jit(solution)/shard_map/ppermute | solution.py:131
  52.1 12.2 %collective-permute-done.10 = bf16[2,128,1024]{2,1,0:T(8,128)(2,1)S(1)} collective-permute-done((bf16[2,128,1024]{2,1,0:T(8,128)(2,1)S(1)}, bf16[2,128,1024]{2,1,0:T(8,128)(2,1)S(1)}, u32[]{:S(2)}, u32[]{:S(2)}) %collective-permute-start.10) | collective-permute-done | bytes 524320 | tf_op jit(solution)/shard_map/ppermute | solution.py:131
  75.9 5.3 %project_pair.3.blocks_ref = bf16[4,2,1024,128]{3,2,1,0:T(8,128)(2,1)S(1)} custom-call(s32[2]{0:T(128)S(1)} %pad_add_fusion.place_ref, bf16[1024,1024]{1,0:T(8,128)(2,1)S(1)} %bitcast.86, bf16[1024,1024]{1,0:T(8,128)(2,1)S(1)} %bitcast.87, bf16[3,512,1024]{2,1,0:T(8,128)(2,1)} %refs_7_.1, bf16[512,512]{1,0:T(8,128)(2,1)S(1)} %collective-permute-done.1.refs_3_.refs_5_, ...), custom_call_target="tpu_custom_call" | custom-call | flops 2147483648 | bytes 8388608 | tf_op jit(solution)/shard_map/project_pair/pallas_call | solution.py:235
  82.2 4.4 %collective-permute-start.19 = (bf16[2,1024,128]{2,1,0:T(8,128)(2,1)S(1)}, bf16[2,1024,128]{2,1,0:T(8,128)(2,1)S(1)}, u32[]{:S(2)}, u32[]{:S(2)}) collective-permute-start(bf16[2,1024,128]{2,1,0:T(8,128)(2,1)S(1)} %get-tuple-element.77), channel_id=1, source_target_pairs={{0,8},{4,12},{1,9},{5,13},{2,10},{6,14},{3,11},{7,15}} | collective-permute-start | bytes 1572872 | tf_op jit(solution)/shard_map/ppermute | solution.py:171
  89.6 9.1 %collective-permute-done.12.refs_7_.sent = bf16[512,512]{1,0:T(8,128)(2,1)S(1)} collective-permute-done((bf16[512,512]{1,0:T(8,128)(2,1)}, bf16[512,512]{1,0:T(8,128)(2,1)S(1)}, u32[]{:S(2)}, u32[]{:S(2)}) %collective-permute-start.12) | collective-permute-done | bytes 524320 | tf_op jit(solution)/shard_map/ppermute | solution.py:131
  98.7 5.7 %project_pair.2.blocks_ref = bf16[4,2,1024,128]{3,2,1,0:T(8,128)(2,1)S(1)} custom-call(s32[2]{0:T(128)S(1)} %pad_add_fusion.place_ref, bf16[1024,1024]{1,0:T(8,128)(2,1)} %bitcast.90, bf16[1024,1024]{1,0:T(8,128)(2,1)} %bitcast.91, bf16[3,512,1024]{2,1,0:T(8,128)(2,1)} %refs_7_.1, bf16[512,512]{1,0:T(8,128)(2,1)S(1)} %collective-permute-done.8.refs_3_.refs_2_, ...), custom_call_target="tpu_custom_call" | custom-call | flops 2147483648 | bytes 8388608 | tf_op jit(solution)/shard_map/project_pair/pallas_call | solution.py:235
  106.2 5.1 %collective-permute-start.13 = (bf16[2,1024,128]{2,1,0:T(8,128)(2,1)}, bf16[2,1024,128]{2,1,0:T(8,128)(2,1)}, u32[]{:S(2)}, u32[]{:S(2)}) collective-permute-start(bf16[2,1024,128]{2,1,0:T(8,128)(2,1)} %get-tuple-element.83), channel_id=1, source_target_pairs={{0,8},{4,12},{1,9},{5,13},{2,10},{6,14},{3,11},{7,15}} | collective-permute-start | bytes 1572872 | tf_op jit(solution)/shard_map/ppermute | solution.py:171
  116.2 6.9 %collective-permute-done.13 = bf16[2,1024,128]{2,1,0:T(8,128)(2,1)} collective-permute-done((bf16[2,1024,128]{2,1,0:T(8,128)(2,1)}, bf16[2,1024,128]{2,1,0:T(8,128)(2,1)}, u32[]{:S(2)}, u32[]{:S(2)}) %collective-permute-start.13) | collective-permute-done | bytes 524320 | tf_op jit(solution)/shard_map/ppermute | solution.py:171
  125.1 5.0 %collective-permute-start.14 = (bf16[2,1024,128]{2,1,0:T(8,128)(2,1)S(1)}, bf16[2,1024,128]{2,1,0:T(8,128)(2,1)S(1)}, u32[]{:S(2)}, u32[]{:S(2)}) collective-permute-start(bf16[2,1024,128]{2,1,0:T(8,128)(2,1)S(1)} %get-tuple-element.81), channel_id=1, source_target_pairs={{0,8},{4,12},{8,16},{12,20},{1,9},{5,13},{9,17},{13,21},{2,10},{6,... | collective-permute-start | bytes 1572872 | tf_op jit(solution)/shard_map/ppermute | solution.py:171
  130.1 4.2 %collective-permute-done.20 = bf16[2,1024,128]{2,1,0:T(8,128)(2,1)} collective-permute-done((bf16[2,1024,128]{2,1,0:T(8,128)(2,1)}, bf16[2,1024,128]{2,1,0:T(8,128)(2,1)}, u32[]{:S(2)}, u32[]{:S(2)}) %collective-permute-start.20) | collective-permute-done | bytes 524320 | tf_op jit(solution)/shard_map/ppermute | solution.py:171
  137.2 5.0 %collective-permute-start.21 = (bf16[2,1024,128]{2,1,0:T(8,128)(2,1)S(1)}, bf16[2,1024,128]{2,1,0:T(8,128)(2,1)S(1)}, u32[]{:S(2)}, u32[]{:S(2)}) collective-permute-start(bf16[2,1024,128]{2,1,0:T(8,128)(2,1)S(1)} %get-tuple-element.73), channel_id=1, source_target_pairs={{0,8},{4,12},{8,16},{12,20},{16,24},{20,28},{1,9},{5,13},{9,17},{1... | collective-permute-start | bytes 1572872 | tf_op jit(solution)/shard_map/ppermute | solution.py:171
  142.3 3.2 collective-permute-done.14
  147.0 5.0 %collective-permute-start.15 = (bf16[2,1024,128]{2,1,0:T(8,128)(2,1)S(1)}, bf16[2,1024,128]{2,1,0:T(8,128)(2,1)S(1)}, u32[]{:S(2)}, u32[]{:S(2)}) collective-permute-start(bf16[2,1024,128]{2,1,0:T(8,128)(2,1)S(1)} %get-tuple-element.79), channel_id=1, source_target_pairs={{0,8},{4,12},{8,16},{12,20},{16,24},{20,28},{1,9},{5,13},{9,17},{1... | collective-permute-start | bytes 1572872 | tf_op jit(solution)/shard_map/ppermute | solution.py:171
  152.1 4.6 %collective-permute-done.21.up_ref = bf16[2,1024,128]{2,1,0:T(8,128)(2,1)S(1)} collective-permute-done((bf16[2,1024,128]{2,1,0:T(8,128)(2,1)S(1)}, bf16[2,1024,128]{2,1,0:T(8,128)(2,1)S(1)}, u32[]{:S(2)}, u32[]{:S(2)}) %collective-permute-start.21) | collective-permute-done | bytes 524320 | tf_op jit(solution)/shard_map/ppermute | solution.py:171
  156.7 9.9 %forward_filter.1 = (bf16[2,1024,128]{2,1,0:T(8,128)(2,1)S(1)}, bf16[1024,128]{1,0:T(8,128)(2,1)S(1)}, f32[1024,128]{1,0:T(8,128)S(1)}) custom-call(s32[8]{0:T(128)S(1)} %fusion.17.order_ref, bf16[4,2,1024,128]{3,2,1,0:T(8,128)(2,1)S(1)} %copy-done.8, bf16[2,1024,128]{2,1,0:T(8,128)(2,1)S(1)} %collective-permute-done.21.up_ref, ...), custom_call_target="tpu_custom_call" | custom-call | flops 6710886400 | bytes 1572864 | tf_op jit(solution)/shard_map/forward_filter/pallas_call | solution.py:321
  168.8 5.0 %collective-permute-start.25 = (bf16[2048,128]{1,0:T(8,128)(2,1)S(1)}, bf16[2048,128]{1,0:T(8,128)(2,1)S(1)}, u32[]{:S(2)}, u32[]{:S(2)}) collective-permute-start(bf16[2048,128]{1,0:T(8,128)(2,1)S(1)} %get-tuple-element.44.refs_0_), channel_id=1, source_target_pairs={{0,8},{4,12},{8,16},{12,20},{16,24},{20,28},{1,9},{5,13},{9,17},{1... | collective-permute-start | bytes 1572872 | tf_op jit(solution)/shard_map/ppermute | solution.py:171
  173.8 9.0 %collective-permute-done.26.refs_4_ = bf16[2048,128]{1,0:T(8,128)(2,1)S(1)} collective-permute-done((bf16[2048,128]{1,0:T(8,128)(2,1)S(1)}, bf16[2048,128]{1,0:T(8,128)(2,1)S(1)}, u32[]{:S(2)}, u32[]{:S(2)}) %collective-permute-start.26) | collective-permute-done | bytes 524320 | tf_op jit(solution)/shard_map/ppermute | solution.py:171
  184.8 11.9 %collective-permute-done.28.refs_5_ = bf16[2048,128]{1,0:T(8,128)(2,1)S(1)} collective-permute-done((bf16[2048,128]{1,0:T(8,128)(2,1)S(1)}, bf16[2048,128]{1,0:T(8,128)(2,1)S(1)}, u32[]{:S(2)}, u32[]{:S(2)}) %collective-permute-start.28) | collective-permute-done | bytes 524320 | tf_op jit(solution)/shard_map/ppermute | solution.py:171
  198.7 15.2 %backward_filter.1.refs_0_ = bf16[2176,128]{1,0:T(8,128)(2,1)S(1)} custom-call(s32[8]{0:T(128)S(1)} %fusion.17.order_ref, bf16[1024,128]{1,0:T(8,128)(2,1)S(1)} %get-tuple-element.45.grad_ref, bf16[2,1024,128]{2,1,0:T(8,128)(2,1)S(1)} %get-tuple-element.46.kv_ref, bf16[1024,128]{1,0:T(8,128)(2,1)S(1)} %get-tuple-element.47.signal_ref, ...), custom_call_target="tpu_custom_call" | custom-call | flops 13421772800 | bytes 1572864 | tf_op jit(solution)/shard_map/backward_filter/pallas_call | solution.py:466
  215.4 5.2 %collective-permute-start.29 = (bf16[2176,128]{1,0:T(8,128)(2,1)S(1)}, bf16[2176,128]{1,0:T(8,128)(2,1)S(1)}, u32[]{:S(2)}, u32[]{:S(2)}) collective-permute-start(bf16[2176,128]{1,0:T(8,128)(2,1)S(1)} %backward_filter.1.refs_0_), channel_id=1, source_target_pairs={{0,8},{4,12},{8,16},{12,20},{16,24},{20,28},{1,9},{5,13},{9,17},{1... | collective-permute-start | bytes 1671176 | tf_op jit(solution)/shard_map/ppermute | solution.py:171
  224.6 3.9 %collective-permute-done.31.refs_4_ = bf16[2176,128]{1,0:T(8,128)(2,1)S(1)} collective-permute-done((bf16[2176,128]{1,0:T(8,128)(2,1)S(1)}, bf16[2176,128]{1,0:T(8,128)(2,1)S(1)}, u32[]{:S(2)}, u32[]{:S(2)}) %collective-permute-start.31) | collective-permute-done | bytes 557088 | tf_op jit(solution)/shard_map/ppermute | solution.py:171
  236.0 6.4 %collective-permute-done.32.refs_5_ = bf16[2176,128]{1,0:T(8,128)(2,1)S(1)} collective-permute-done((bf16[2176,128]{1,0:T(8,128)(2,1)S(1)}, bf16[2176,128]{1,0:T(8,128)(2,1)S(1)}, u32[]{:S(2)}, u32[]{:S(2)}) %collective-permute-start.32) | collective-permute-done | bytes 557088 | tf_op jit(solution)/shard_map/ppermute | solution.py:171
  247.0 12.4 %collective-permute-done.38.piece_ref = bf16[512,512]{1,0:T(8,128)(2,1)S(1)} collective-permute-done((bf16[512,512]{1,0:T(8,128)(2,1)S(1)}, bf16[512,512]{1,0:T(8,128)(2,1)S(1)}, u32[]{:S(2)}, u32[]{:S(2)}) %collective-permute-start.38) | collective-permute-done | bytes 524320 | tf_op jit(solution)/shard_map/ppermute | solution.py:131
  260.1 5.6 %collective-permute-done.39.refs_0_ = bf16[512,512]{1,0:T(8,128)(2,1)S(1)} collective-permute-done((bf16[512,512]{1,0:T(8,128)(2,1)S(1)}, bf16[512,512]{1,0:T(8,128)(2,1)S(1)}, u32[]{:S(2)}, u32[]{:S(2)}) %collective-permute-start.39) | collective-permute-done | bytes 524320 | tf_op jit(solution)/shard_map/ppermute | solution.py:131
  269.0 6.2 %project_back.1 = bf16[1024,1024]{1,0:T(8,128)(2,1)S(1)} custom-call(s32[2]{0:T(128)S(1)} %pad_add_fusion.place_ref, bf16[2,1024,512]{2,1,0:T(8,128)(2,1)S(1)} %merge_blocks.2.value_ref.refs_0_, bf16[3,512,1024]{2,1,0:T(8,128)(2,1)} %refs_7_.1, bf16[512,512]{1,0:T(8,128)(2,1)S(1)} %copy-done.18, bf16[2,1024,512]{2,1,0:T(8,128)(2,1)} %copy-done.5, ...), custom_call_target="tpu_custom_call" | custom-call | flops 3221225472 | bytes 4194304 | tf_op jit(solution)/shard_map/project_back/pallas_call | solution.py:583
  296.8 4.8 %collective-permute-done.47 = bf16[128,1024]{1,0:T(8,128)(2,1)S(1)} collective-permute-done((bf16[128,1024]{1,0:T(8,128)(2,1)S(1)}, bf16[128,1024]{1,0:T(8,128)(2,1)S(1)}, u32[]{:S(2)}, u32[]{:S(2)}) %collective-permute-start.47) | collective-permute-done | bytes 262176 | tf_op jit(solution)/shard_map/ppermute | solution.py:156
  309.4 18.8 %collective-permute-done.51 = bf16[512,128]{1,0:T(8,128)(2,1)S(1)} collective-permute-done((bf16[512,128]{1,0:T(8,128)(2,1)S(1)}, bf16[512,128]{1,0:T(8,128)(2,1)S(1)}, u32[]{:S(2)}, u32[]{:S(2)}) %collective-permute-start.51) | collective-permute-done | bytes 131104 | tf_op jit(solution)/shard_map/ppermute | solution.py:131
  329.1 3.9 %take_in_half.1 = f32[3,512,1024]{2,1,0:T(8,128)} custom-call(s32[2]{0:T(128)S(1)} %pad_add_fusion.place_ref, bf16[512,512]{1,0:T(8,128)(2,1)S(1)} %copy-done.22, bf16[512,512]{1,0:T(8,128)(2,1)} %collective-permute-done.49.refs_1_, bf16[512,512]{1,0:T(8,128)(2,1)} %collective-permute-done.50.refs_2_, ...), custom_call_target="tpu_custom_call", output_to_operand_aliasing={{}: (4, {})} | custom-call | flops 786432 | bytes 4718592 | tf_op jit(solution)/shard_map/take_in_half/pallas_call | solution.py:716
  (180 shorter events, 99.8 us)
Async XLA Ops:
  7.7 33.8 %collective-permute-start.5 = (bf16[512,512]{1,0:T(8,128)(2,1)S(1)}, bf16[512,512]{1,0:T(8,128)(2,1)S(1)}, u32[]{:S(2)}, u32[]{:S(2)}) collective-permute-start(bf16[512,512]{1,0:T(8,128)(2,1)S(1)} %dynamic-slice_bitcast_fusion.1), channel_id=1, source_target_pairs={{0,4},{4,0},{8,12},{12,8},{16,20},{20,16},{24,28},{28,24},{1,5},{5... | collective-permute-start | bytes 1572872 | tf_op jit(solution)/shard_map/ppermute | solution.py:131
  22.7 18.7 %collective-permute-start.3 = (bf16[128,1024]{1,0:T(8,128)(2,1)S(1)}, bf16[128,1024]{1,0:T(8,128)(2,1)S(1)}, u32[]{:S(2)}, u32[]{:S(2)}) collective-permute-start(bf16[128,1024]{1,0:T(8,128)(2,1)S(1)} %collective-permute-done), channel_id=1, source_target_pairs={{0,4},{4,0},{8,12},{12,8},{16,20},{20,16},{24,28},{28,24},{1,5},{5... | collective-permute-start | bytes 786440 | tf_op jit(solution)/shard_map/ppermute | solution.py:131
  23.2 18.1 %collective-permute-start.2 = (bf16[128,1024]{1,0:T(8,128)(2,1)S(1)}, bf16[128,1024]{1,0:T(8,128)(2,1)S(1)}, u32[]{:S(2)}, u32[]{:S(2)}) collective-permute-start(bf16[128,1024]{1,0:T(8,128)(2,1)S(1)} %collective-permute-done), channel_id=1, source_target_pairs={{0,2},{1,3},{2,0},{3,1},{4,6},{5,7},{6,4},{7,5},{8,10},{9,11},{10,... | collective-permute-start | bytes 786440 | tf_op jit(solution)/shard_map/ppermute | solution.py:131
  23.3 18.2 %collective-permute-start.6 = (bf16[128,1024]{1,0:T(8,128)(2,1)S(1)}, bf16[128,1024]{1,0:T(8,128)(2,1)S(1)}, u32[]{:S(2)}, u32[]{:S(2)}) collective-permute-start(bf16[128,1024]{1,0:T(8,128)(2,1)S(1)} %copy-done.28), channel_id=1, source_target_pairs={{0,0},{1,8},{2,16},{3,24},{4,4},{5,12},{6,20},{7,28},{8,2},{9,10},... | collective-permute-start | bytes 786440 | tf_op jit(solution)/shard_map/ppermute | solution.py:146
  52.1 16.4 %collective-permute-start.7 = (bf16[4,128,1024]{2,1,0:T(8,128)(2,1)S(1)}, bf16[4,128,1024]{2,1,0:T(8,128)(2,1)}, u32[]{:S(2)}, u32[]{:S(2)}) collective-permute-start(bf16[4,128,1024]{2,1,0:T(8,128)(2,1)S(1)} %pad_maximum_fusion.2), channel_id=1, source_target_pairs={{0,1},{1,0},{2,3},{3,2},{4,5},{5,4},{6,7},{7,6},{8,9},{9,8},{10,11... | collective-permute-start | bytes 3145736 | tf_op jit(solution)/shard_map/ppermute | solution.py:131
  65.7 20.9 %collective-permute-start.11 = (bf16[2,2,128,1024]{3,2,0,1:T(8,128)(2,1)}, bf16[2,2,128,1024]{3,2,0,1:T(8,128)(2,1)}, u32[]{:S(2)}, u32[]{:S(2)}) collective-permute-start(bf16[2,2,128,1024]{3,2,0,1:T(8,128)(2,1)} %get-tuple-element.91), channel_id=1, source_target_pairs={{0,1},{1,0},{2,3},{3,2},{4,5},{5,4},{6,7},{7,6},{8,9},{9,8},{10,11... | collective-permute-start | bytes 3145736 | tf_op jit(solution)/shard_map/ppermute | solution.py:131
  72.9 16.7 %collective-permute-start.8 = (bf16[512,512]{1,0:T(8,128)(2,1)}, bf16[512,512]{1,0:T(8,128)(2,1)S(1)}, u32[]{:S(2)}, u32[]{:S(2)}) collective-permute-start(bf16[512,512]{1,0:T(8,128)(2,1)} %dynamic-slice_bitcast_fusion), channel_id=1, source_target_pairs={{0,4},{4,0},{8,12},{12,8},{16,20},{20,16},{24,28},{28,24},{1,5},{5... | collective-permute-start | bytes 1572872 | tf_op jit(solution)/shard_map/ppermute | solution.py:131
  72.9 25.8 %collective-permute-start.12 = (bf16[512,512]{1,0:T(8,128)(2,1)}, bf16[512,512]{1,0:T(8,128)(2,1)S(1)}, u32[]{:S(2)}, u32[]{:S(2)}) collective-permute-start(bf16[512,512]{1,0:T(8,128)(2,1)} %constant_dynamic-slice_fusion), channel_id=1, source_target_pairs={{0,4},{4,0},{8,12},{12,8},{16,20},{20,16},{24,28},{28,24},{1,5},{5... | collective-permute-start | bytes 1572872 | tf_op jit(solution)/shard_map/ppermute | solution.py:131
  81.4 29.9 %collective-permute-start.22 = (bf16[2,1024,128]{2,1,0:T(8,128)(2,1)S(1)}, bf16[2,1024,128]{2,1,0:T(8,128)(2,1)S(1)}, u32[]{:S(2)}, u32[]{:S(2)}) collective-permute-start(bf16[2,1024,128]{2,1,0:T(8,128)(2,1)S(1)} %get-tuple-element.76), channel_id=1, source_target_pairs={{24,16},{28,20},{25,17},{29,21},{26,18},{30,22},{27,19},{31,23}} | collective-permute-start | bytes 1572872 | tf_op jit(solution)/shard_map/ppermute | solution.py:171
  82.2 29.1 %collective-permute-start.19 = (bf16[2,1024,128]{2,1,0:T(8,128)(2,1)S(1)}, bf16[2,1024,128]{2,1,0:T(8,128)(2,1)S(1)}, u32[]{:S(2)}, u32[]{:S(2)}) collective-permute-start(bf16[2,1024,128]{2,1,0:T(8,128)(2,1)S(1)} %get-tuple-element.77), channel_id=1, source_target_pairs={{0,8},{4,12},{1,9},{5,13},{2,10},{6,14},{3,11},{7,15}} | collective-permute-start | bytes 1572872 | tf_op jit(solution)/shard_map/ppermute | solution.py:171
  106.2 16.9 %collective-permute-start.13 = (bf16[2,1024,128]{2,1,0:T(8,128)(2,1)}, bf16[2,1024,128]{2,1,0:T(8,128)(2,1)}, u32[]{:S(2)}, u32[]{:S(2)}) collective-permute-start(bf16[2,1024,128]{2,1,0:T(8,128)(2,1)} %get-tuple-element.83), channel_id=1, source_target_pairs={{0,8},{4,12},{1,9},{5,13},{2,10},{6,14},{3,11},{7,15}} | collective-permute-start | bytes 1572872 | tf_op jit(solution)/shard_map/ppermute | solution.py:171
  112.5 17.6 %collective-permute-start.23 = (bf16[2,1024,128]{2,1,0:T(8,128)(2,1)}, bf16[2,1024,128]{2,1,0:T(8,128)(2,1)}, u32[]{:S(2)}, u32[]{:S(2)}) collective-permute-start(bf16[2,1024,128]{2,1,0:T(8,128)(2,1)} %get-tuple-element.74), channel_id=1, source_target_pairs={{16,8},{20,12},{24,16},{28,20},{17,9},{21,13},{25,17},{29,21},{18,... | collective-permute-start | bytes 1572872 | tf_op jit(solution)/shard_map/ppermute | solution.py:171
  114.0 20.3 %collective-permute-start.20 = (bf16[2,1024,128]{2,1,0:T(8,128)(2,1)}, bf16[2,1024,128]{2,1,0:T(8,128)(2,1)}, u32[]{:S(2)}, u32[]{:S(2)}) collective-permute-start(bf16[2,1024,128]{2,1,0:T(8,128)(2,1)} %get-tuple-element.75), channel_id=1, source_target_pairs={{0,8},{4,12},{8,16},{12,20},{1,9},{5,13},{9,17},{13,21},{2,10},{6,... | collective-permute-start | bytes 1572872 | tf_op jit(solution)/shard_map/ppermute | solution.py:171
  124.4 17.9 %collective-permute-start.17 = (bf16[2,1024,128]{2,1,0:T(8,128)(2,1)S(1)}, bf16[2,1024,128]{2,1,0:T(8,128)(2,1)S(1)}, u32[]{:S(2)}, u32[]{:S(2)}) collective-permute-start(bf16[2,1024,128]{2,1,0:T(8,128)(2,1)S(1)} %get-tuple-element.80), channel_id=1, source_target_pairs={{16,8},{20,12},{24,16},{28,20},{17,9},{21,13},{25,17},{29,21},{18,... | collective-permute-start | bytes 1572872 | tf_op jit(solution)/shard_map/ppermute | solution.py:171
  125.1 20.3 %collective-permute-start.14 = (bf16[2,1024,128]{2,1,0:T(8,128)(2,1)S(1)}, bf16[2,1024,128]{2,1,0:T(8,128)(2,1)S(1)}, u32[]{:S(2)}, u32[]{:S(2)}) collective-permute-start(bf16[2,1024,128]{2,1,0:T(8,128)(2,1)S(1)} %get-tuple-element.81), channel_id=1, source_target_pairs={{0,8},{4,12},{8,16},{12,20},{1,9},{5,13},{9,17},{13,21},{2,10},{6,... | collective-permute-start | bytes 1572872 | tf_op jit(solution)/shard_map/ppermute | solution.py:171
  135.9 16.2 %collective-permute-start.24 = (bf16[2,1024,128]{2,1,0:T(8,128)(2,1)S(1)}, bf16[2,1024,128]{2,1,0:T(8,128)(2,1)S(1)}, u32[]{:S(2)}, u32[]{:S(2)}) collective-permute-start(bf16[2,1024,128]{2,1,0:T(8,128)(2,1)S(1)} %get-tuple-element.72), channel_id=1, source_target_pairs={{8,0},{12,4},{16,8},{20,12},{24,16},{28,20},{9,1},{13,5},{17,9},{2... | collective-permute-start | bytes 1572872 | tf_op jit(solution)/shard_map/ppermute | solution.py:171
  137.2 19.5 %collective-permute-start.21 = (bf16[2,1024,128]{2,1,0:T(8,128)(2,1)S(1)}, bf16[2,1024,128]{2,1,0:T(8,128)(2,1)S(1)}, u32[]{:S(2)}, u32[]{:S(2)}) collective-permute-start(bf16[2,1024,128]{2,1,0:T(8,128)(2,1)S(1)} %get-tuple-element.73), channel_id=1, source_target_pairs={{0,8},{4,12},{8,16},{12,20},{16,24},{20,28},{1,9},{5,13},{9,17},{1... | collective-permute-start | bytes 1572872 | tf_op jit(solution)/shard_map/ppermute | solution.py:171
  145.7 20.8 %collective-permute-start.18 = (bf16[2,1024,128]{2,1,0:T(8,128)(2,1)S(1)}, bf16[2,1024,128]{2,1,0:T(8,128)(2,1)S(1)}, u32[]{:S(2)}, u32[]{:S(2)}) collective-permute-start(bf16[2,1024,128]{2,1,0:T(8,128)(2,1)S(1)} %get-tuple-element.78), channel_id=1, source_target_pairs={{8,0},{12,4},{16,8},{20,12},{24,16},{28,20},{9,1},{13,5},{17,9},{2... | collective-permute-start | bytes 1572872 | tf_op jit(solution)/shard_map/ppermute | solution.py:171
  147.0 19.6 %collective-permute-start.15 = (bf16[2,1024,128]{2,1,0:T(8,128)(2,1)S(1)}, bf16[2,1024,128]{2,1,0:T(8,128)(2,1)S(1)}, u32[]{:S(2)}, u32[]{:S(2)}) collective-permute-start(bf16[2,1024,128]{2,1,0:T(8,128)(2,1)S(1)} %get-tuple-element.79), channel_id=1, source_target_pairs={{0,8},{4,12},{8,16},{12,20},{16,24},{20,28},{1,9},{5,13},{9,17},{1... | collective-permute-start | bytes 1572872 | tf_op jit(solution)/shard_map/ppermute | solution.py:171
  196.7 24.0 %collective-permute-start.34 = (bf16[2048,128]{1,0:T(8,128)(2,1)S(1)}, bf16[2048,128]{1,0:T(8,128)(2,1)S(1)}, u32[]{:S(2)}, u32[]{:S(2)}) collective-permute-start(bf16[2048,128]{1,0:T(8,128)(2,1)S(1)} %collective-permute-done.28.refs_5_), channel_id=1, source_target_pairs={{8,0},{12,4},{9,1},{13,5},{10,2},{14,6},{11,3},{15,7}} | collective-permute-start | bytes 1572872 | tf_op jit(solution)/shard_map/ppermute | solution.py:171
  198.0 22.7 %collective-permute-start.33 = (bf16[2048,128]{1,0:T(8,128)(2,1)S(1)}, bf16[2048,128]{1,0:T(8,128)(2,1)S(1)}, u32[]{:S(2)}, u32[]{:S(2)}) collective-permute-start(bf16[2048,128]{1,0:T(8,128)(2,1)S(1)} %collective-permute-done.27.refs_2_), channel_id=1, source_target_pairs={{16,24},{20,28},{17,25},{21,29},{18,26},{22,30},{19,27},{23,31}} | collective-permute-start | bytes 1572872 | tf_op jit(solution)/shard_map/ppermute | solution.py:171
  224.5 22.0 %collective-permute-start.37 = (bf16[4,128,1024]{2,1,0:T(8,128)(2,1)S(1)}, bf16[4,128,1024]{2,1,0:T(8,128)(2,1)S(1)}, u32[]{:S(2)}, u32[]{:S(2)}) collective-permute-start(bf16[4,128,1024]{2,1,0:T(8,128)(2,1)S(1)} %bitcast.105), channel_id=1, source_target_pairs={{0,1},{1,0},{2,3},{3,2},{4,5},{5,4},{6,7},{7,6},{8,9},{9,8},{10,11... | collective-permute-start | bytes 3145736 | tf_op jit(solution)/shard_map/ppermute | solution.py:131
  242.4 24.1 %collective-permute-start.35 = (bf16[2176,128]{1,0:T(8,128)(2,1)S(1)}, bf16[2176,128]{1,0:T(8,128)(2,1)S(1)}, u32[]{:S(2)}, u32[]{:S(2)}) collective-permute-start(bf16[2176,128]{1,0:T(8,128)(2,1)S(1)} %collective-permute-done.32.refs_5_), channel_id=1, source_target_pairs={{8,0},{12,4},{9,1},{13,5},{10,2},{14,6},{11,3},{15,7}} | collective-permute-start | bytes 1671176 | tf_op jit(solution)/shard_map/ppermute | solution.py:171
  243.7 22.8 %collective-permute-start.36 = (bf16[2176,128]{1,0:T(8,128)(2,1)S(1)}, bf16[2176,128]{1,0:T(8,128)(2,1)S(1)}, u32[]{:S(2)}, u32[]{:S(2)}) collective-permute-start(bf16[2176,128]{1,0:T(8,128)(2,1)S(1)} %collective-permute-done.30.refs_2_), channel_id=1, source_target_pairs={{16,24},{20,28},{17,25},{21,29},{18,26},{22,30},{19,27},{23,31}} | collective-permute-start | bytes 1671176 | tf_op jit(solution)/shard_map/ppermute | solution.py:171
  245.4 20.3 %collective-permute-start.39 = (bf16[512,512]{1,0:T(8,128)(2,1)S(1)}, bf16[512,512]{1,0:T(8,128)(2,1)S(1)}, u32[]{:S(2)}, u32[]{:S(2)}) collective-permute-start(bf16[512,512]{1,0:T(8,128)(2,1)S(1)} %get-tuple-element.51), channel_id=1, source_target_pairs={{0,4},{4,0},{8,12},{12,8},{16,20},{20,16},{24,28},{28,24},{1,5},{5... | collective-permute-start | bytes 1572872 | tf_op jit(solution)/shard_map/ppermute | solution.py:131
  284.2 17.3 %collective-permute-start.47 = (bf16[128,1024]{1,0:T(8,128)(2,1)S(1)}, bf16[128,1024]{1,0:T(8,128)(2,1)S(1)}, u32[]{:S(2)}, u32[]{:S(2)}) collective-permute-start(bf16[128,1024]{1,0:T(8,128)(2,1)S(1)} %get-tuple-element.85), channel_id=1, source_target_pairs={{0,6},{1,7},{2,4},{3,5},{4,2},{5,3},{6,0},{7,1},{8,14},{9,15},{10,... | collective-permute-start | bytes 786440 | tf_op jit(solution)/shard_map/ppermute | solution.py:156
  284.8 19.1 %collective-permute-start.46 = (bf16[128,1024]{1,0:T(8,128)(2,1)S(1)}, bf16[128,1024]{1,0:T(8,128)(2,1)S(1)}, u32[]{:S(2)}, u32[]{:S(2)}) collective-permute-start(bf16[128,1024]{1,0:T(8,128)(2,1)S(1)} %get-tuple-element.86), channel_id=1, source_target_pairs={{0,4},{4,0},{8,12},{12,8},{16,20},{20,16},{24,28},{28,24},{1,5},{5... | collective-permute-start | bytes 786440 | tf_op jit(solution)/shard_map/ppermute | solution.py:131
  290.6 38.5 %collective-permute-start.49 = (bf16[512,512]{1,0:T(8,128)(2,1)}, bf16[512,512]{1,0:T(8,128)(2,1)}, u32[]{:S(2)}, u32[]{:S(2)}) collective-permute-start(bf16[512,512]{1,0:T(8,128)(2,1)} %get-tuple-element.59), channel_id=1, source_target_pairs={{0,4},{4,0},{8,12},{12,8},{16,20},{20,16},{24,28},{28,24},{1,5},{5... | collective-permute-start | bytes 1572872 | tf_op jit(solution)/shard_map/ppermute | solution.py:131
  292.7 36.4 %collective-permute-start.50 = (bf16[512,512]{1,0:T(8,128)(2,1)}, bf16[512,512]{1,0:T(8,128)(2,1)}, u32[]{:S(2)}, u32[]{:S(2)}) collective-permute-start(bf16[512,512]{1,0:T(8,128)(2,1)} %get-tuple-element.61), channel_id=1, source_target_pairs={{0,4},{4,0},{8,12},{12,8},{16,20},{20,16},{24,28},{28,24},{1,5},{5... | collective-permute-start | bytes 1572872 | tf_op jit(solution)/shard_map/ppermute | solution.py:131
  296.1 33.0 %collective-permute-start.43 = (bf16[128,1024]{1,0:T(8,128)(2,1)S(1)}, bf16[128,1024]{1,0:T(8,128)(2,1)S(1)}, u32[]{:S(2)}, u32[]{:S(2)}) collective-permute-start(bf16[128,1024]{1,0:T(8,128)(2,1)S(1)} %fusion.9), channel_id=1, source_target_pairs={{0,0},{8,1},{16,2},{24,3},{4,4},{12,5},{20,6},{28,7},{2,8},{10,9},... | collective-permute-start | bytes 786440 | tf_op jit(solution)/shard_map/ppermute | solution.py:146
  304.1 28.9 %collective-permute-start.48 = (bf16[128,1024]{1,0:T(8,128)(2,1)S(1)}, bf16[128,1024]{1,0:T(8,128)(2,1)S(1)}, u32[]{:S(2)}, u32[]{:S(2)}) collective-permute-start(bf16[128,1024]{1,0:T(8,128)(2,1)S(1)} %fusion.7), channel_id=1, source_target_pairs={{0,0},{8,1},{16,2},{24,3},{4,4},{12,5},{20,6},{28,7},{2,8},{10,9},... | collective-permute-start | bytes 786440 | tf_op jit(solution)/shard_map/ppermute | solution.py:146
  305.4 22.8 %collective-permute-start.51 = (bf16[512,128]{1,0:T(8,128)(2,1)S(1)}, bf16[512,128]{1,0:T(8,128)(2,1)S(1)}, u32[]{:S(2)}, u32[]{:S(2)}) collective-permute-start(bf16[512,128]{1,0:T(8,128)(2,1)S(1)} %merge_taps.1), channel_id=1, source_target_pairs={{0,4},{4,0},{8,12},{12,8},{16,20},{20,16},{24,28},{28,24},{1,5},{5... | collective-permute-start | bytes 393224 | tf_op jit(solution)/shard_map/ppermute | solution.py:131
  (49 other events, 706.4 us)

commit v4 on v3

--- a/solution.py
+++ b/solution.py
@@ -175,16 +175,21 @@
     return (one.astype(f32) + other.astype(f32)).astype(bf16)
 
 
-def line_scatter(blocks):
+def scatter_step(blocks, up, down, step):
     length = blocks.shape[0]
-    up, down = blocks[length - 1], blocks[1]
-    for step in range(1, length):
-        up_in = along_line(up, 1, lambda i: i <= step - 1)
-        down_in = along_line(down, -1, lambda i: i >= length - step)
-        if step < length - 1:
-            up = added(blocks[length - 1 - step], up_in)
-            down = added(blocks[1 + step], down_in)
+    up_in = along_line(up, 1, lambda i: i <= step - 1)
+    down_in = along_line(down, -1, lambda i: i >= length - step)
     return up_in, down_in
+
+
+def scatter_start(blocks):
+    return scatter_step(blocks, blocks[blocks.shape[0] - 1], blocks[1], 1)
+
+
+def scatter_next(blocks, up_in, down_in, step):
+    up = added(blocks[blocks.shape[0] - step], up_in)
+    down = added(blocks[step], down_in)
+    return scatter_step(blocks, up, down, step)
 
 
 def next_block(block, by, step):
@@ -195,43 +200,47 @@
 
 
 def project_pair(place, first, second):
-    tokens, width = first[0].shape
+    near = first[0][0]
+    tokens = 2 * near.shape[0] * near.shape[1] * near.shape[2]
+    width = near.shape[3]
     half = width // 2
-    rows = 256
+    rows = 2 * near.shape[2]
     count = half // lanes
 
     def body(place_ref, *refs):
         out = refs[-1]
         line = place_ref[0]
+        is_near = pl.program_id(0) < 2
         for which in range(2):
-            own, other, kept, given = refs[4 * which : 4 * which + 4]
+            own, own_far, other, other_far, kept, given = refs[6 * which : 6 * which + 6]
             turned = (first, second)[which][3]
             dims = (((1,), (1,)), ((), ())) if turned else (((1,), (0,)), ((), ()))
             kept_value = kept[...].reshape(half, half)
             given_value = given[...].reshape(half, half)
-            result = lax.dot_general(own[...], kept_value, dims, preferred_element_type=f32)
-            result += lax.dot_general(other[...], given_value, dims, preferred_element_type=f32)
+            own_value = jnp.where(is_near, own[...], own_far[...]).reshape(rows, half)
+            other_value = jnp.where(is_near, other[...], other_far[...]).reshape(rows, half)
+            result = lax.dot_general(own_value, kept_value, dims, preferred_element_type=f32)
+            result += lax.dot_general(other_value, given_value, dims, preferred_element_type=f32)
             result = result.astype(bf16)
             for j in range(count):
                 out[lax.rem(j - line + count, count), which] = result[:, j * lanes : (j + 1) * lanes]
 
     operands, specs = [], []
-    for value, kept, given, turned, index in (first, second):
-        operands += [value, value, kept, given]
-        specs += [
-            pl.BlockSpec((rows, half), lambda g, place: (g, place[1])),
-            pl.BlockSpec((rows, half), lambda g, place: (g, 1 - place[1])),
-        ]
+    for (near, far), kept, (given, given_at), turned, index in (first, second):
+        operands += [near, far, near, far, kept, given]
+        for mine in (True, False):
+            for is_far in (False, True):
+
+                def index_of(g, place, mine=mine, is_far=is_far):
+                    at = jnp.maximum(g - 2, 0) if is_far else jnp.minimum(g, 1)
+                    return (at, 0, 0, place[1] if mine else 1 - place[1])
+
+                specs.append(pl.BlockSpec((1, 2, rows // 2, half), index_of))
         if turned:
-            specs += [
-                pl.BlockSpec((half, half), lambda g, place: (place[1], 0)),
-                pl.BlockSpec((half, half), lambda g, place: (0, 0)),
-            ]
+            specs.append(pl.BlockSpec((half, half), lambda g, place: (place[1], 0)))
         else:
-            specs += [
-                pl.BlockSpec((1, half, half), lambda g, place, index=index: (index, 0, place[1])),
-                pl.BlockSpec((half, half), lambda g, place: (0, 0)),
-            ]
+            specs.append(pl.BlockSpec((1, half, half), lambda g, place, index=index: (index, 0, place[1])))
+        specs.append(pl.BlockSpec((1, half, half), lambda g, place, at=given_at: (at, 0, 0)))
     return pl.pallas_call(
         body,
         out_shape=jax.ShapeDtypeStruct((count, 2, tokens, lanes), bf16),
@@ -490,6 +499,7 @@
 
 
 def merge_blocks(place, block, before, behind, tokens):
+    matrices = block.shape[0] // tokens
     length = len(before) + 1
     rows = 256
     steps = tokens // rows
@@ -509,10 +519,10 @@
     spec = pl.BlockSpec((rows, lanes), lambda which, g, place: (which * steps + g, 0))
     return pl.pallas_call(
         body,
-        out_shape=jax.ShapeDtypeStruct((2, tokens, length * lanes), bf16),
-        grid_spec=pltpu.PrefetchScalarGridSpec(
-            num_scalar_prefetch=1,
-            grid=(2, steps),
+        out_shape=jax.ShapeDtypeStruct((matrices, tokens, length * lanes), bf16),
+        grid_spec=pltpu.PrefetchScalarGridSpec(
+            num_scalar_prefetch=1,
+            grid=(matrices, steps),
             in_specs=[spec] * (2 * length - 1),
             out_specs=pl.BlockSpec((1, rows, length * lanes), lambda which, g, place: (which, g, 0)),
         ),
@@ -553,10 +563,11 @@
     )(place, block, *before, *behind)
 
 
-def project_back(place, merged, in_weight, given, indices):
+def project_back(place, merged, in_weight, given, indices, part):
     tokens, half = merged[0][0].shape[1:]
     rows = 256
     n = len(merged)
+    steps = tokens // rows // 2
 
     def body(place_ref, *refs):
         out = refs[-1]
@@ -567,45 +578,45 @@
             value, kept, sent = refs[3 * k], refs[3 * k + 1], refs[3 * k + 2]
             value = value[...].reshape(rows, half)
             own += lax.dot_general(value, kept[...].reshape(half, half), dims, preferred_element_type=f32)
-            other += lax.dot_general(value, sent[...], dims, preferred_element_type=f32)
+            other += lax.dot_general(value, sent[...].reshape(half, half), dims, preferred_element_type=f32)
         at = place_ref[1]
         out[:, pl.ds(pl.multiple_of(at * half, half), half)] = own.astype(bf16)
         out[:, pl.ds(pl.multiple_of((1 - at) * half, half), half)] = other.astype(bf16)
 
     operands, specs = [], []
-    for (value, which), sent, index in zip(merged, given, indices):
+    for (value, which), (sent, at), index in zip(merged, given, indices):
         operands += [value, in_weight, sent]
         specs += [
-            pl.BlockSpec((1, rows, half), lambda g, place, which=which: (which, g, 0)),
+            pl.BlockSpec((1, rows, half), lambda g, place, which=which: (which, part * steps + g, 0)),
             pl.BlockSpec((1, half, half), lambda g, place, index=index: (index, 0, place[1])),
-            pl.BlockSpec((half, half), lambda g, place: (0, 0)),
+            pl.BlockSpec((1, half, half), lambda g, place, at=at: (at, 0, 0)),
         ]
     return pl.pallas_call(
         body,
-        out_shape=jax.ShapeDtypeStruct((tokens, 2 * half), bf16),
-        grid_spec=pltpu.PrefetchScalarGridSpec(
-            num_scalar_prefetch=1,
-            grid=(tokens // rows,),
+        out_shape=jax.ShapeDtypeStruct((tokens // 2, 2 * half), bf16),
+        grid_spec=pltpu.PrefetchScalarGridSpec(
+            num_scalar_prefetch=1,
+            grid=(steps,),
             in_specs=specs,
             out_specs=pl.BlockSpec((rows, 2 * half), lambda g, place: (g, 0)),
         ),
         compiler_params=params(),
-        cost_estimate=cost(4 * n * tokens * half * half, 8 * tokens * half),
+        cost_estimate=cost(2 * n * tokens * half * half, 4 * tokens * half),
         name="project_back",
     )(place, *operands)
 
 
-def project_out(place, merged, out_weight, given):
+def project_out(place, merged, out_weight, given, at):
     tokens, half = merged.shape[1:]
     rows = 256
 
     def body(place_ref, value_ref, kept, sent, out):
         value = value_ref[...].reshape(rows, half)
-        at = place_ref[1]
+        pair = place_ref[1]
         own = jnp.dot(value, kept[...], preferred_element_type=f32)
-        other = jnp.dot(value, sent[...], preferred_element_type=f32)
-        out[:, pl.ds(pl.multiple_of(at * half, half), half)] = own.astype(bf16)
-        out[:, pl.ds(pl.multiple_of((1 - at) * half, half), half)] = other.astype(bf16)
+        other = jnp.dot(value, sent[...].reshape(half, half), preferred_element_type=f32)
+        out[:, pl.ds(pl.multiple_of(pair * half, half), half)] = own.astype(bf16)
+        out[:, pl.ds(pl.multiple_of((1 - pair) * half, half), half)] = other.astype(bf16)
 
     return pl.pallas_call(
         body,
@@ -616,7 +627,7 @@
             in_specs=[
                 pl.BlockSpec((1, rows, half), lambda g, place: (0, g, 0)),
                 pl.BlockSpec((half, half), lambda g, place: (place[1], 0)),
-                pl.BlockSpec((half, half), lambda g, place: (0, 0)),
+                pl.BlockSpec((1, half, half), lambda g, place: (at, 0, 0)),
             ],
             out_specs=pl.BlockSpec((rows, 2 * half), lambda g, place: (g, 0)),
         ),
@@ -626,18 +637,27 @@
     )(place, merged, out_weight, given)
 
 
-def in_gradient(place, turned, merged, which, index, total, running):
+def in_gradient(place, near, far, merged, which, index, total, running):
     tokens, half = merged.shape[1:]
     rows = 256
-
-    def body(place_ref, own, other, value_ref, *refs):
+    steps = half // rows
+    block = near.shape[:3] + (rows,)
+
+    def body(place_ref, own, own_far, other, other_far, value_ref, *refs):
         kept, sent = refs[-2:]
         value = value_ref[...].reshape(tokens, half)
-        kept[...] = jnp.dot(own[...], value, preferred_element_type=f32)[None]
-        sent[...] = jnp.dot(other[...], value, preferred_element_type=f32).astype(bf16)
-
-    steps = half // rows
+        dims = (((0,), (0,)), ((), ()))
+
+        def product(one, two):
+            rows_of = jnp.concatenate([one[...].reshape(tokens // 2, rows), two[...].reshape(tokens // 2, rows)], 0)
+            return lax.dot_general(rows_of, value, dims, preferred_element_type=f32)
+
+        kept[...] = product(own, own_far)[None]
+        sent[...] = product(other, other_far).astype(bf16)
+
     more = [] if running is None else [running]
+    own_spec = pl.BlockSpec(block, lambda g, place: (0, 0, 0, place[1] * steps + g))
+    other_spec = pl.BlockSpec(block, lambda g, place: (0, 0, 0, (1 - place[1]) * steps + g))
     return pl.pallas_call(
         body,
         out_shape=(
@@ -647,35 +667,41 @@
         grid_spec=pltpu.PrefetchScalarGridSpec(
             num_scalar_prefetch=1,
             grid=(steps,),
-            in_specs=[
-                pl.BlockSpec((rows, tokens), lambda g, place: (place[1] * steps + g, 0)),
-                pl.BlockSpec((rows, tokens), lambda g, place: ((1 - place[1]) * steps + g, 0)),
-                pl.BlockSpec((1, tokens, half), lambda g, place: (which, 0, 0)),
-            ]
+            in_specs=[own_spec, own_spec, other_spec, other_spec]
+            + [pl.BlockSpec((1, tokens, half), lambda g, place: (which, 0, 0))]
             + [pl.BlockSpec(memory_space=pl.ANY)] * len(more),
             out_specs=(
                 pl.BlockSpec((1, rows, half), lambda g, place: (index, g, place[1])),
                 pl.BlockSpec((rows, half), lambda g, place: (g, 0)),
             ),
         ),
-        input_output_aliases={4: 0} if more else {},
+        input_output_aliases={6: 0} if more else {},
         compiler_params=params(),
         cost_estimate=cost(4 * tokens * half * half, 8 * tokens * half),
         name="in_gradient",
-    )(place, turned, turned, merged, *more)
-
-
-def out_gradient(place, merged, rows_of):
+    )(place, near, far, near, far, merged, *more)
+
+
+def out_gradient(place, merged, near, far):
     tokens, half = merged.shape[1:]
     rows = 256
     steps = half // rows
-
-    def body(place_ref, value_ref, own, other, kept, sent):
+    block = near.shape[:3] + (half,)
+
+    def body(place_ref, value_ref, own, own_far, other, other_far, kept, sent):
         value = value_ref[...].reshape(tokens, rows)
         dims = (((0,), (0,)), ((), ()))
-        kept[...] = lax.dot_general(value, own[...], dims, preferred_element_type=f32)
-        sent[...] = lax.dot_general(value, other[...], dims, preferred_element_type=f32).astype(bf16)
-
+
+        def in_order(one, two):
+            return jnp.concatenate([ref[...].reshape(tokens // 2, half) for ref in (one, two)], 0)
+
+        kept[...] = lax.dot_general(value, in_order(own, own_far), dims, preferred_element_type=f32)
+        sent[...] = lax.dot_general(
+            value, in_order(other, other_far), dims, preferred_element_type=f32
+        ).astype(bf16)
+
+    own_spec = pl.BlockSpec(block, lambda g, place: (0, 0, 0, place[1]))
+    other_spec = pl.BlockSpec(block, lambda g, place: (0, 0, 0, 1 - place[1]))
     return pl.pallas_call(
         body,
         out_shape=(
@@ -687,8 +713,10 @@
             grid=(steps,),
             in_specs=[
                 pl.BlockSpec((1, tokens, rows), lambda g, place: (0, 0, g)),
-                pl.BlockSpec((tokens, half), lambda g, place: (0, place[1])),
-                pl.BlockSpec((tokens, half), lambda g, place: (0, 1 - place[1])),
+                own_spec,
+                own_spec,
+                other_spec,
+                other_spec,
             ],
             out_specs=(
                 pl.BlockSpec((rows, half), lambda g, place: (place[1] * steps + g, 0)),
@@ -698,36 +726,32 @@
         compiler_params=params(),
         cost_estimate=cost(4 * tokens * half * half, 8 * tokens * half),
         name="out_gradient",
-    )(place, merged, rows_of, rows_of)
-
-
-def take_in_half(place, running, pieces):
-    n = len(pieces)
-    half = pieces[0].shape[0]
-
-    def body(place_ref, *refs):
-        out = refs[-1]
-        for k in range(n):
-
-            @pl.when(pl.program_id(0) == k)
-            def _():
-                out[...] = refs[k][...].astype(f32)[None]
+    )(place, merged, near, far, near, far)
+
+
+def take_in_half(place, running, piece, index):
+    half = piece.shape[0]
+
+    def body(place_ref, piece_ref, running_ref, out):
+        out[...] = piece_ref[...].astype(f32)[None]
 
     return pl.pallas_call(
         body,
         out_shape=jax.ShapeDtypeStruct(running.shape, f32),
         grid_spec=pltpu.PrefetchScalarGridSpec(
             num_scalar_prefetch=1,
-            grid=(n,),
-            in_specs=[pl.BlockSpec((half, half), lambda g, place: (0, 0))] * n
-            + [pl.BlockSpec(memory_space=pl.ANY)],
-            out_specs=pl.BlockSpec((1, half, half), lambda g, place: (g, 0, 1 - place[1])),
-        ),
-        input_output_aliases={n + 1: 0},
-        compiler_params=params(),
-        cost_estimate=cost(n * half * half, 6 * n * half * half),
+            grid=(1,),
+            in_specs=[
+                pl.BlockSpec((half, half), lambda g, place: (0, 0)),
+                pl.BlockSpec(memory_space=pl.ANY),
+            ],
+            out_specs=pl.BlockSpec((1, half, half), lambda g, place: (index, 0, 1 - place[1])),
+        ),
+        input_output_aliases={2: 0},
+        compiler_params=params(),
+        cost_estimate=cost(half * half, 6 * half * half),
         name="take_in_half",
-    )(place, *pieces, running)
+    )(place, piece, running)
 
 
 def take_out_half(place, running, piece):
@@ -768,37 +792,47 @@
         2 * crossed(fsdp_at ^ (2 * (relative % 2) + relative // 4)) + (pair ^ (relative // 2 % 2))
     ).astype(jnp.int32)
 
-    def sent_in(i):
-        return lax.dynamic_slice_in_dim(in_weight[i], (1 - pair) * half_in, half_in, 1)
-
-    given_k, given_v = flip(sent_in(1), "seq", 1), flip(sent_in(2), "seq", 1)
-    x_own, g_own = trade_places(tokens, False), trade_places(cotangent, False)
-    x_own, given_k = lax.optimization_barrier((x_own, given_k))
-    x_rows = jnp.stack([x_own, flip(x_own, "fsdp", 2), flip(x_own, "seq", 1), flip_both(x_own)])
-    x_rows, given_v, g_own = lax.optimization_barrier((x_rows, given_v, g_own))
-    x_rows = jnp.stack([x_rows, flip(x_rows, "fsdp", 1)]).reshape(-1, width)
-    g_pair = jnp.stack([g_own, flip(g_own, "seq", 1)])
-    sent_out = lax.dynamic_slice_in_dim(out_weight, (1 - pair) * half_out, half_out, 0)
-    sent_q, sent_out = after((sent_in(0), sent_out), x_rows)
-    given_q, given_out = flip(sent_q, "seq", 1), flip(sent_out, "seq", 1)
-    g_rows = jnp.stack([g_pair, flip(g_pair, "fsdp", 2)], axis=1)
-    g_rows = jnp.stack([g_rows, flip(g_rows, "fsdp", 1)]).reshape(-1, width)
+    def sent_in(weight, i):
+        return lax.dynamic_slice_in_dim(weight[i], (1 - pair) * half_in, half_in, 1)
+
+    def gathered(own):
+        return [own, flip(own, "fsdp", 2), flip(own, "seq", 1), flip_both(own)]
+
+    given_kv = flip(jnp.stack([sent_in(in_weight, 1), sent_in(in_weight, 2)]), "seq", 1)
+    x_own = trade_places(tokens, False)
+    late_in, late_out, late_cot = after((in_weight, out_weight, cotangent), x_own)
+    g_own = trade_places(late_cot, False)
+    x_near = jnp.stack(gathered(x_own))
+    sent_qo = jnp.stack(
+        [sent_in(late_in, 0), lax.dynamic_slice_in_dim(late_out, (1 - pair) * half_out, half_out, 0)]
+    )
+    x_near, given_kv, sent_qo, g_own = lax.optimization_barrier((x_near, given_kv, sent_qo, g_own))
+    x_near = x_near.reshape(2, 2, -1, width)
+    x_far = flip(x_near, "fsdp", 1)
+    given_qo = flip(sent_qo, "seq", 1)
     own_filters = lax.dynamic_slice_in_dim(filters, pair * half_in + line * lanes, lanes, 0)
     spread_taps = jnp.repeat(jnp.transpose(own_filters), sublanes, axis=0)
 
     kv_blocks = project_pair(
         place,
-        (x_rows, in_weight, given_k, False, 1),
-        (x_rows, in_weight, given_v, False, 2),
-    )
-    kv_up, kv_down = line_scatter(kv_blocks)
+        ((x_near, x_far), in_weight, (given_kv, 0), False, 1),
+        ((x_near, x_far), in_weight, (given_kv, 1), False, 2),
+    )
+    kv_up, kv_down = scatter_start(kv_blocks)
+    kv_up, kv_down, given_qo = lax.optimization_barrier((kv_up, kv_down, given_qo))
+    g_near = jnp.stack(gathered(after(g_own, kv_blocks))).reshape(2, 2, -1, width)
+    kv_up, kv_down = scatter_next(kv_blocks, kv_up, kv_down, 2)
+    g_near, kv_up, kv_down = lax.optimization_barrier((g_near, kv_up, kv_down))
+    g_far = flip(g_near, "fsdp", 1)
     qg_blocks = project_pair(
         place,
-        (x_rows, in_weight, given_q, False, 0),
-        (g_rows, out_weight, given_out, True, 0),
-    )
-    turned = jnp.transpose(after(x_rows, qg_blocks))
-    qg_up, qg_down = line_scatter(qg_blocks)
+        ((x_near, x_far), in_weight, (given_qo, 0), False, 0),
+        ((g_near, g_far), out_weight, (given_qo, 1), True, 0),
+    )
+    kv_up, kv_down = scatter_next(kv_blocks, kv_up, kv_down, 3)
+    qg_up, qg_down = scatter_start(qg_blocks)
+    for step in (2, 3):
+        qg_up, qg_down = scatter_next(qg_blocks, qg_up, qg_down, step)
     key_values, signal, filtered = forward_filter(order, kv_blocks, kv_up, kv_down, spread_taps)
     gated_rows, grad_filtered = gate_rows(order, qg_blocks, qg_up, qg_down, filtered)
 
@@ -806,63 +840,73 @@
     gated_behind = [next_block(gated_rows, -1, 1)]
     grad_filtered = after(grad_filtered, gated_before[0], gated_behind[0])
     kv_grads = backward_filter(order, grad_filtered, key_values, signal, spread_taps)
-    for step in (2, 3):
-        gated_before.append(next_block(gated_before[-1], 1, step))
-        gated_behind.append(next_block(gated_behind[-1], -1, step))
-        if step == 2:
-            kv_grads = after(kv_grads, gated_before[-1], gated_behind[-1])
+    gated_before.append(next_block(gated_before[0], 1, 2))
+    gated_behind.append(next_block(gated_behind[0], -1, 2))
+    kv_grads, gated_before[1], gated_behind[1] = lax.optimization_barrier(
+        (kv_grads, gated_before[1], gated_behind[1])
+    )
+    gated_before.append(next_block(gated_before[1], 1, 3))
+    gated_behind.append(next_block(gated_behind[1], -1, 3))
     kv_before = [next_block(kv_grads, 1, 1)]
     kv_behind = [next_block(kv_grads, -1, 1)]
     kv_before.append(next_block(kv_before[0], 1, 2))
     kv_behind.append(next_block(kv_behind[0], -1, 2))
 
+    total_in = in_weight.shape[0]
     first = merge_blocks(place, gated_rows, gated_before, gated_behind, count)
-    out_kept, out_sent = out_gradient(place, first, g_rows)
-    in_kept, q_sent = in_gradient(place, turned, first, 1, 0, in_weight.shape[0], None)
-    mixed_part = project_out(place, first, out_weight, given_out)
-    out_given, q_given = flip(out_sent, "seq", 1), flip(q_sent, "seq", 1)
-    last_up, last_down = after((kv_before[1], kv_behind[1]), out_sent, q_sent, mixed_part)
+    out_kept, out_sent = out_gradient(place, first, g_near, g_far)
+    out_given = flip(out_sent, "seq", 1)
+    in_kept, q_sent = in_gradient(place, x_near, x_far, first, 1, 0, total_in, None)
+    q_given = flip(q_sent, "seq", 1)
+    mixed_part = project_out(place, after(first, out_sent), out_weight, given_qo, 1)
+    last_up, last_down, out_given = lax.optimization_barrier(
+        after((kv_before[1], kv_behind[1], out_given), q_sent, mixed_part)
+    )
     kv_before.append(next_block(last_up, 1, 3))
     kv_behind.append(next_block(last_down, -1, 3))
 
-    def across_cores(part):
-        parts = part.reshape(2, 4, count // 8, width)
-        return added(parts[0], flip(parts[1], "fsdp", 1))
-
-    mixed_part = across_cores(mixed_part)
-    kv_behind[2], kv_before[2], mixed_part, out_given, q_given = lax.optimization_barrier(
-        (kv_behind[2], kv_before[2], mixed_part, out_given, q_given)
+    mixed_part = mixed_part.reshape(2, 2, 2, count // 8, width)
+    mixed_part = added(mixed_part[0], flip(mixed_part[1], "fsdp", 1))
+    kv_behind[2], kv_before[2], mixed_part, q_given = lax.optimization_barrier(
+        (kv_behind[2], kv_before[2], mixed_part, q_given)
     )
     second = merge_blocks(place, kv_grads, kv_before, kv_behind, count)
-    grad_part = project_back(
-        place,
-        [(first, 1), (second, 0), (second, 1)],
-        in_weight,
-        [given_q, given_k, given_v],
-        [0, 1, 2],
-    )
-
-    def outward(parts):
-        total = parts[0].astype(f32) + flip(parts[1], "fsdp", 2).astype(f32)
-        total += flip(parts[2], "seq", 1).astype(f32) + flip_both(parts[3]).astype(f32)
-        return trade_places(total.astype(bf16), True)
-
-    mixed_out = outward(mixed_part)
-    grad_part = across_cores(grad_part)
-    grad_tokens = outward(grad_part)
-    in_kept, k_sent = in_gradient(place, turned, second, 0, 1, in_weight.shape[0], in_kept)
-    in_kept, v_sent = in_gradient(place, turned, second, 1, 2, in_weight.shape[0], in_kept)
+    in_kept, k_sent = in_gradient(place, x_near, x_far, second, 0, 1, total_in, in_kept)
+    k_given = flip(k_sent, "seq", 1)
+
+    def back(part, value):
+        return project_back(
+            place,
+            [(first, 1), (value, 0), (value, 1)],
+            in_weight,
+            [(given_qo, 0), (given_kv, 0), (given_kv, 1)],
+            [0, 1, 2],
+            part,
+        )
+
+    far_part = back(1, after(second, k_sent))
+    near_part = back(0, after(second, far_part))
+    parts = added(near_part, flip(far_part, "fsdp", 1)).reshape(4, count // 8, width)
+    mixed_part = added(mixed_part[:, 0], flip(mixed_part[:, 1], "fsdp", 2))
+    mixed_part = added(mixed_part[0], flip(mixed_part[1], "seq", 1))
+    mixed_out = trade_places(mixed_part, True)
+    total = parts[0].astype(f32) + flip(parts[1], "fsdp", 2).astype(f32)
+    total += flip(parts[2], "seq", 1).astype(f32) + flip_both(parts[3]).astype(f32)
+    in_kept, v_sent = in_gradient(place, x_near, x_far, after(second, parts), 1, 2, total_in, in_kept)
     half_taps = merge_taps(place, kv_grads, kv_before, kv_behind, taps)
-    k_given, v_given = flip(k_sent, "seq", 1), flip(v_sent, "seq", 1)
-    given_taps = flip(half_taps, "seq", 1)
+    total, k_given, mixed_out = lax.optimization_barrier((total, k_given, mixed_out))
+    v_given = flip(v_sent, "seq", 1)
+    given_taps = flip(after(half_taps, v_sent), "seq", 1)
+    grad_tokens = trade_places(total.astype(bf16), True)
     grad_filters = jnp.where(
         pair == 0,
         jnp.concatenate([half_taps, given_taps], 0),
         jnp.concatenate([given_taps, half_taps], 0),
     ).astype(f32)
     grad_out_weight = take_out_half(place, out_kept, out_given)
-    grad_in_weight = take_in_half(place, in_kept, [q_given, k_given, v_given])
-    return (mixed_out, grad_tokens, grad_in_weight, grad_out_weight, grad_filters)
+    for index, given in enumerate((q_given, k_given, v_given)):
+        in_kept = take_in_half(place, in_kept, given, index)
+    return (mixed_out, grad_tokens, in_kept, grad_out_weight, grad_filters)
 
 
 def solution(mesh):

time: 337 us -> 319 us (0.947)
  waiting for transfers between devices: 156 us -> 124 us
  starting transfers between devices: 81.5 us -> 103 us
  local copies, waits for them, and re-layouts: 19.2 us -> 10.3 us
  Pallas kernels: 64.9 us -> 71.3 us
  other arithmetic: 11.3 us -> 6.99 us
    ppermute x21 -> x19, waiting for transfers between devices: 93.6 us -> 68.3 us  [flip(): lax.ppermute(value, axis, [(i, i ^ bit) for i in range(lax.axis_size(axis...]
    ppermute x3, starting transfers between devices: 3.86 us -> 21.4 us  [flip_both(): return lax.ppermute(value, ('seq', 'fsdp'), pairs)]
    ppermute x24, waiting for transfers between devices: 50.1 us -> 39.8 us  [along_line(): return lax.ppermute(value, 'seq', pairs)]
    ppermute x24, starting transfers between devices: 54 us -> 61.3 us  [along_line(): return lax.ppermute(value, 'seq', pairs)]
    ppermute x3, waiting for transfers between devices: 12.3 us -> 16.4 us  [flip_both(): return lax.ppermute(value, ('seq', 'fsdp'), pairs)]
    ppermute x21 -> x19, starting transfers between devices: 20.9 us -> 17.3 us  [flip(): lax.ppermute(value, axis, [(i, i ^ bit) for i in range(lax.axis_size(axis...]
    another operation x5 -> x4, other arithmetic: 4.82 us -> 1.43 us  [the longest x1 1.06 us: on_paired_mesh(): jnp.stack([sent_in(late_in, 0), lax.dynamic_slice_in_dim(late_out, (1 - p...]
    pallas_call x3 -> x4, Pallas kernels: 8.66 us -> 10.7 us  [the longest x2 8.34 us: project_back(): pl.pallas_call(body, out_shape=jax.ShapeDtypeStruct((tokens // 2, 2 * hal...]
  transfers between devices with their start and end apart: 52 -> 50, of which waited for: 24 -> 23; matrix products, arithmetic and copies ran while one was open for 6% -> 2% of each run, Pallas kernels for 17% -> 18%
where the time goes in v4:
time: 319 us; the launch traced here: 317 us
  waiting for transfers between devices  124 us (39%)
  starting transfers between devices  103 us (32%)
  Pallas kernels  71.3 us (22%)
  local copies, waits for them, and re-layouts  10.3 us (3%)
  other arithmetic  6.99 us (2%)
    ppermute x19, waiting for transfers between devices, flip(): lax.ppermute(value, axis, [(i, i ^ bit) for i in range(lax.axis_size(axis...  68.3 us
    ppermute x24, starting transfers between devices, along_line(): return lax.ppermute(value, 'seq', pairs)  61.3 us
    ppermute x24, waiting for transfers between devices, along_line(): return lax.ppermute(value, 'seq', pairs)  39.8 us
    ppermute x3, starting transfers between devices, flip_both(): return lax.ppermute(value, ('seq', 'fsdp'), pairs)  21.4 us
    ppermute x19, starting transfers between devices, flip(): lax.ppermute(value, axis, [(i, i ^ bit) for i in range(lax.axis_size(axis...  17.3 us
    ppermute x3, waiting for transfers between devices, flip_both(): return lax.ppermute(value, ('seq', 'fsdp'), pairs)  16.4 us
    pallas_call x1, Pallas kernels, backward_filter(): pl.pallas_call(body, out_shape=jax.ShapeDtypeStruct((2 * tokens + taps, l...  15.2 us
    pallas_call x2, Pallas kernels, project_pair(): pl.pallas_call(body, out_shape=jax.ShapeDtypeStruct((count, 2, tokens, la...  11.8 us
  transfers between devices with their start and end apart: 50, of which 23 were waited for; matrix products, arithmetic and copies ran while one was open for 2% of the time, Pallas kernels for 18%

profile of v4, /device:TPU:0, one launch (start us, length us, event | category | flops | bytes accessed | tf_op | source)
XLA Modules:
  0.0 317.3 jit_solution(6587695681757813719)
XLA Ops:
  7.1 18.2 %collective-permute-start.3 = (bf16[128,1024]{1,0:T(8,128)(2,1)S(1)}, bf16[128,1024]{1,0:T(8,128)(2,1)S(1)}, u32[]{:S(2)}, u32[]{:S(2)}) collective-permute-start(bf16[128,1024]{1,0:T(8,128)(2,1)S(1)} %collective-permute-done), channel_id=1, source_target_pairs={{0,6},{1,7},{2,4},{3,5},{4,2},{5,3},{6,0},{7,1},{8,14},{9,15},{10,... | collective-permute-start | bytes 786440 | tf_op jit(solution)/shard_map/ppermute | solution.py:156
  27.6 6.4 %collective-permute-done.3 = bf16[128,1024]{1,0:T(8,128)(2,1)S(1)} collective-permute-done((bf16[128,1024]{1,0:T(8,128)(2,1)S(1)}, bf16[128,1024]{1,0:T(8,128)(2,1)S(1)}, u32[]{:S(2)}, u32[]{:S(2)}) %collective-permute-start.3) | collective-permute-done | bytes 262176 | tf_op jit(solution)/shard_map/ppermute | solution.py:156
  34.0 6.1 %collective-permute-done.2 = bf16[128,1024]{1,0:T(8,128)(2,1)S(1)} collective-permute-done((bf16[128,1024]{1,0:T(8,128)(2,1)S(1)}, bf16[128,1024]{1,0:T(8,128)(2,1)S(1)}, u32[]{:S(2)}, u32[]{:S(2)}) %collective-permute-start.2) | collective-permute-done | bytes 262176 | tf_op jit(solution)/shard_map/ppermute | solution.py:131
  45.2 5.6 %project_pair.2.blocks_ref = bf16[4,2,1024,128]{3,2,1,0:T(8,128)(2,1)S(1)} custom-call(s32[2]{0:T(128)S(1)} %pad_add_fusion.place_ref, bf16[2,2,128,1024]{3,2,1,0:T(8,128)(2,1)S(1)} %bitcast.64, bf16[2,2,128,1024]{3,2,1,0:T(8,128)(2,1)S(1)} %collective-permute-done.6.refs_1_.refs_3_.refs_7_.refs_9_.own_far.other_far, bf16[2,2,128,1024]{3,2,1,0:T(8,128)(2,1)S(1)} %bitcast.65, ...), custom_call_target="tpu_custom_call" | custom-call | flops 2147483648 | bytes 8388608 | tf_op jit(solution)/shard_map/project_pair/pallas_call | solution.py:244
  51.6 5.1 %collective-permute-start.7 = (bf16[2,1024,128]{2,1,0:T(8,128)(2,1)S(1)}, bf16[2,1024,128]{2,1,0:T(8,128)(2,1)S(1)}, u32[]{:S(2)}, u32[]{:S(2)}) collective-permute-start(bf16[2,1024,128]{2,1,0:T(8,128)(2,1)S(1)} %get-tuple-element.116), channel_id=1, source_target_pairs={{0,8},{4,12},{1,9},{5,13},{2,10},{6,14},{3,11},{7,15}} | collective-permute-start | bytes 1572872 | tf_op jit(solution)/shard_map/ppermute | solution.py:171
  56.7 10.4 %collective-permute-done.9.refs_5_.refs_11_.sent.refs_2_ = bf16[2,512,512]{2,1,0:T(8,128)(2,1)S(1)} collective-permute-done((bf16[2,512,512]{2,1,0:T(8,128)(2,1)}, bf16[2,512,512]{2,1,0:T(8,128)(2,1)S(1)}, u32[]{:S(2)}, u32[]{:S(2)}) %collective-permute-start.9) | collective-permute-done | bytes 1048608 | tf_op jit(solution)/shard_map/ppermute | solution.py:131
  69.3 5.0 %collective-permute-start.13 = (bf16[2,1024,128]{2,1,0:T(8,128)(2,1)S(1)}, bf16[2,1024,128]{2,1,0:T(8,128)(2,1)S(1)}, u32[]{:S(2)}, u32[]{:S(2)}) collective-permute-start(bf16[2,1024,128]{2,1,0:T(8,128)(2,1)S(1)} %get-tuple-element.114), channel_id=1, source_target_pairs={{0,8},{4,12},{8,16},{12,20},{1,9},{5,13},{9,17},{13,21},{2,10},{6,... | collective-permute-start | bytes 1572872 | tf_op jit(solution)/shard_map/ppermute | solution.py:171
  78.0 6.5 %collective-permute-done.12 = bf16[128,1024]{1,0:T(8,128)(2,1)S(1)} collective-permute-done((bf16[128,1024]{1,0:T(8,128)(2,1)S(1)}, bf16[128,1024]{1,0:T(8,128)(2,1)S(1)}, u32[]{:S(2)}, u32[]{:S(2)}) %collective-permute-start.12) | collective-permute-done | bytes 262176 | tf_op jit(solution)/shard_map/ppermute | solution.py:156
  84.5 3.8 %collective-permute-done.11 = bf16[128,1024]{1,0:T(8,128)(2,1)S(1)} collective-permute-done((bf16[128,1024]{1,0:T(8,128)(2,1)S(1)}, bf16[128,1024]{1,0:T(8,128)(2,1)S(1)}, u32[]{:S(2)}, u32[]{:S(2)}) %collective-permute-start.11) | collective-permute-done | bytes 262176 | tf_op jit(solution)/shard_map/ppermute | solution.py:131
  92.0 6.2 %project_pair.3.blocks_ref = bf16[4,2,1024,128]{3,2,1,0:T(8,128)(2,1)} custom-call(s32[2]{0:T(128)S(1)} %pad_add_fusion.place_ref, bf16[2,2,128,1024]{3,2,1,0:T(8,128)(2,1)S(1)} %bitcast.68, bf16[2,2,128,1024]{3,2,1,0:T(8,128)(2,1)S(1)} %collective-permute-done.6.refs_1_.refs_3_.refs_7_.refs_9_.own_far.other_far, bf16[2,2,128,1024]{3,2,1,0:T(8,128)(2,1)S(1)} %bitcast.69, ...), custom_call_target="tpu_custom_call" | custom-call | flops 2147483648 | bytes 8388608 | tf_op jit(solution)/shard_map/project_pair/pallas_call | solution.py:244
  101.2 5.2 %collective-permute-start.16 = (bf16[2,1024,128]{2,1,0:T(8,128)(2,1)}, bf16[2,1024,128]{2,1,0:T(8,128)(2,1)}, u32[]{:S(2)}, u32[]{:S(2)}) collective-permute-start(bf16[2,1024,128]{2,1,0:T(8,128)(2,1)} %get-tuple-element.112), channel_id=1, source_target_pairs={{0,8},{4,12},{1,9},{5,13},{2,10},{6,14},{3,11},{7,15}} | collective-permute-start | bytes 1572872 | tf_op jit(solution)/shard_map/ppermute | solution.py:171
  106.5 10.8 %collective-permute-done.16 = bf16[2,1024,128]{2,1,0:T(8,128)(2,1)} collective-permute-done((bf16[2,1024,128]{2,1,0:T(8,128)(2,1)}, bf16[2,1024,128]{2,1,0:T(8,128)(2,1)}, u32[]{:S(2)}, u32[]{:S(2)}) %collective-permute-start.16) | collective-permute-done | bytes 524320 | tf_op jit(solution)/shard_map/ppermute | solution.py:171
  119.7 5.0 %collective-permute-start.17 = (bf16[2,1024,128]{2,1,0:T(8,128)(2,1)S(1)}, bf16[2,1024,128]{2,1,0:T(8,128)(2,1)S(1)}, u32[]{:S(2)}, u32[]{:S(2)}) collective-permute-start(bf16[2,1024,128]{2,1,0:T(8,128)(2,1)S(1)} %get-tuple-element.110), channel_id=1, source_target_pairs={{0,8},{4,12},{8,16},{12,20},{1,9},{5,13},{9,17},{13,21},{2,10},{6,... | collective-permute-start | bytes 1572872 | tf_op jit(solution)/shard_map/ppermute | solution.py:171
  127.4 5.2 %collective-permute-start.22 = (bf16[2,1024,128]{2,1,0:T(8,128)(2,1)S(1)}, bf16[2,1024,128]{2,1,0:T(8,128)(2,1)S(1)}, u32[]{:S(2)}, u32[]{:S(2)}) collective-permute-start(bf16[2,1024,128]{2,1,0:T(8,128)(2,1)S(1)} %get-tuple-element.106), channel_id=1, source_target_pairs={{0,8},{4,12},{8,16},{12,20},{16,24},{20,28},{1,9},{5,13},{9,17},{1... | collective-permute-start | bytes 1572872 | tf_op jit(solution)/shard_map/ppermute | solution.py:171
  132.7 4.4 %collective-permute-done.17 = bf16[2,1024,128]{2,1,0:T(8,128)(2,1)S(1)} collective-permute-done((bf16[2,1024,128]{2,1,0:T(8,128)(2,1)S(1)}, bf16[2,1024,128]{2,1,0:T(8,128)(2,1)S(1)}, u32[]{:S(2)}, u32[]{:S(2)}) %collective-permute-start.17) | collective-permute-done | bytes 524320 | tf_op jit(solution)/shard_map/ppermute | solution.py:171
  138.6 5.2 %collective-permute-start.18 = (bf16[2,1024,128]{2,1,0:T(8,128)(2,1)S(1)}, bf16[2,1024,128]{2,1,0:T(8,128)(2,1)S(1)}, u32[]{:S(2)}, u32[]{:S(2)}) collective-permute-start(bf16[2,1024,128]{2,1,0:T(8,128)(2,1)S(1)} %get-tuple-element.108), channel_id=1, source_target_pairs={{0,8},{4,12},{8,16},{12,20},{16,24},{20,28},{1,9},{5,13},{9,17},{1... | collective-permute-start | bytes 1572872 | tf_op jit(solution)/shard_map/ppermute | solution.py:171
  143.9 4.4 %collective-permute-done.22.up_ref = bf16[2,1024,128]{2,1,0:T(8,128)(2,1)S(1)} collective-permute-done((bf16[2,1024,128]{2,1,0:T(8,128)(2,1)S(1)}, bf16[2,1024,128]{2,1,0:T(8,128)(2,1)S(1)}, u32[]{:S(2)}, u32[]{:S(2)}) %collective-permute-start.22) | collective-permute-done | bytes 524320 | tf_op jit(solution)/shard_map/ppermute | solution.py:171
  148.3 9.9 %forward_filter.1 = (bf16[2,1024,128]{2,1,0:T(8,128)(2,1)S(1)}, bf16[1024,128]{1,0:T(8,128)(2,1)S(1)}, f32[1024,128]{1,0:T(8,128)S(1)}) custom-call(s32[8]{0:T(128)S(1)} %fusion.14.order_ref, bf16[4,2,1024,128]{3,2,1,0:T(8,128)(2,1)S(1)} %copy-done.17, bf16[2,1024,128]{2,1,0:T(8,128)(2,1)S(1)} %collective-permute-done.22.up_ref, ...), custom_call_target="tpu_custom_call" | custom-call | flops 6710886400 | bytes 1572864 | tf_op jit(solution)/shard_map/forward_filter/pallas_call | solution.py:330
  160.3 5.2 %collective-permute-start.24 = (bf16[2048,128]{1,0:T(8,128)(2,1)S(1)}, bf16[2048,128]{1,0:T(8,128)(2,1)S(1)}, u32[]{:S(2)}, u32[]{:S(2)}) collective-permute-start(bf16[2048,128]{1,0:T(8,128)(2,1)S(1)} %get-tuple-element.68.refs_0_), channel_id=1, source_target_pairs={{0,8},{4,12},{8,16},{12,20},{16,24},{20,28},{1,9},{5,13},{9,17},{1... | collective-permute-start | bytes 1572872 | tf_op jit(solution)/shard_map/ppermute | solution.py:171
  165.6 8.0 %collective-permute-done.25.refs_4_ = bf16[2048,128]{1,0:T(8,128)(2,1)S(1)} collective-permute-done((bf16[2048,128]{1,0:T(8,128)(2,1)S(1)}, bf16[2048,128]{1,0:T(8,128)(2,1)S(1)}, u32[]{:S(2)}, u32[]{:S(2)}) %collective-permute-start.25) | collective-permute-done | bytes 524320 | tf_op jit(solution)/shard_map/ppermute | solution.py:171
  176.7 15.2 %backward_filter.1.refs_0_ = bf16[2176,128]{1,0:T(8,128)(2,1)S(1)} custom-call(s32[8]{0:T(128)S(1)} %fusion.14.order_ref, bf16[1024,128]{1,0:T(8,128)(2,1)S(1)} %get-tuple-element.70.grad_ref, bf16[2,1024,128]{2,1,0:T(8,128)(2,1)S(1)} %get-tuple-element.71.kv_ref, bf16[1024,128]{1,0:T(8,128)(2,1)S(1)} %get-tuple-element.72.signal_ref, ...), custom_call_target="tpu_custom_call" | custom-call | flops 13421772800 | bytes 1572864 | tf_op jit(solution)/shard_map/backward_filter/pallas_call | solution.py:475
  195.4 9.0 %collective-permute-start.30 = (bf16[2176,128]{1,0:T(8,128)(2,1)S(1)}, bf16[2176,128]{1,0:T(8,128)(2,1)S(1)}, u32[]{:S(2)}, u32[]{:S(2)}) collective-permute-start(bf16[2176,128]{1,0:T(8,128)(2,1)S(1)} %backward_filter.1.refs_0_), channel_id=1, source_target_pairs={{0,8},{4,12},{8,16},{12,20},{16,24},{20,28},{1,9},{5,13},{9,17},{1... | collective-permute-start | bytes 1671176 | tf_op jit(solution)/shard_map/ppermute | solution.py:171
  204.4 8.9 %collective-permute-done.29.refs_6_ = bf16[2048,128]{1,0:T(8,128)(2,1)S(1)} collective-permute-done((bf16[2048,128]{1,0:T(8,128)(2,1)S(1)}, bf16[2048,128]{1,0:T(8,128)(2,1)S(1)}, u32[]{:S(2)}, u32[]{:S(2)}) %collective-permute-start.29) | collective-permute-done | bytes 524320 | tf_op jit(solution)/shard_map/ppermute | solution.py:171
  217.5 3.8 %project_out.1 = bf16[1024,1024]{1,0:T(8,128)(2,1)S(1)} custom-call(s32[2]{0:T(128)S(1)} %pad_add_fusion.place_ref, bf16[2,1024,512]{2,1,0:T(8,128)(2,1)} %copy-done.4, bf16[1024,512]{1,0:T(8,128)(2,1)S(1)} %copy-done.19, bf16[2,512,512]{2,1,0:T(8,128)(2,1)S(1)} %copy-done.10), custom_call_target="tpu_custom_call" | custom-call | flops 1073741824 | bytes 4194304 | tf_op jit(solution)/shard_map/project_out/pallas_call | solution.py:621
  227.9 10.4 %collective-permute-done.34.piece_ref = bf16[512,512]{1,0:T(8,128)(2,1)S(1)} collective-permute-done((bf16[512,512]{1,0:T(8,128)(2,1)S(1)}, bf16[512,512]{1,0:T(8,128)(2,1)S(1)}, u32[]{:S(2)}, u32[]{:S(2)}) %collective-permute-start.34) | collective-permute-done | bytes 524320 | tf_op jit(solution)/shard_map/ppermute | solution.py:131
  241.9 12.1 %collective-permute-done.38.piece_ref = bf16[512,512]{1,0:T(8,128)(2,1)S(1)} collective-permute-done((bf16[512,512]{1,0:T(8,128)(2,1)S(1)}, bf16[512,512]{1,0:T(8,128)(2,1)S(1)}, u32[]{:S(2)}, u32[]{:S(2)}) %collective-permute-start.38) | collective-permute-done | bytes 524320 | tf_op jit(solution)/shard_map/ppermute | solution.py:131
  258.7 4.2 %project_back.2 = bf16[512,1024]{1,0:T(8,128)(2,1)S(1)} custom-call(s32[2]{0:T(128)S(1)} %pad_add_fusion.place_ref, bf16[2,1024,512]{2,1,0:T(8,128)(2,1)S(1)} %copy-done.5, bf16[3,512,1024]{2,1,0:T(8,128)(2,1)} %refs_7_.3, bf16[2,512,512]{2,1,0:T(8,128)(2,1)S(1)} %copy-done.10, bf16[2,1024,512]{2,1,0:T(8,128)(2,1)} %copy-done.2, ...), custom_call_target="tpu_custom_call" | custom-call | flops 1610612736 | bytes 2097152 | tf_op jit(solution)/shard_map/project_back/pallas_call | solution.py:594
  266.5 4.2 %project_back.3 = bf16[512,1024]{1,0:T(8,128)(2,1)S(1)} custom-call(s32[2]{0:T(128)S(1)} %pad_add_fusion.place_ref, bf16[2,1024,512]{2,1,0:T(8,128)(2,1)S(1)} %copy-done.5, bf16[3,512,1024]{2,1,0:T(8,128)(2,1)} %refs_7_.3, bf16[2,512,512]{2,1,0:T(8,128)(2,1)S(1)} %copy-done.10, bf16[2,1024,512]{2,1,0:T(8,128)(2,1)} %copy-done.2, ...), custom_call_target="tpu_custom_call" | custom-call | flops 1610612736 | bytes 2097152 | tf_op jit(solution)/shard_map/project_back/pallas_call | solution.py:594
  270.6 7.7 %collective-permute-done.44 = bf16[2,128,1024]{2,1,0:T(8,128)(2,1)S(1)} collective-permute-done((bf16[2,128,1024]{2,1,0:T(8,128)(2,1)}, bf16[2,128,1024]{2,1,0:T(8,128)(2,1)S(1)}, u32[]{:S(2)}, u32[]{:S(2)}) %collective-permute-start.44) | collective-permute-done | bytes 524320 | tf_op jit(solution)/shard_map/ppermute | solution.py:131
  290.6 3.5 %collective-permute-done.42 = bf16[128,1024]{1,0:T(8,128)(2,1)S(1)} collective-permute-done((bf16[128,1024]{1,0:T(8,128)(2,1)S(1)}, bf16[128,1024]{1,0:T(8,128)(2,1)S(1)}, u32[]{:S(2)}, u32[]{:S(2)}) %collective-permute-start.42) | collective-permute-done | bytes 262176 | tf_op jit(solution)/shard_map/ppermute | solution.py:156
  294.0 5.1 %collective-permute-done.41 = bf16[128,1024]{1,0:T(8,128)(2,1)S(1)} collective-permute-done((bf16[128,1024]{1,0:T(8,128)(2,1)S(1)}, bf16[128,1024]{1,0:T(8,128)(2,1)S(1)}, u32[]{:S(2)}, u32[]{:S(2)}) %collective-permute-start.41) | collective-permute-done | bytes 262176 | tf_op jit(solution)/shard_map/ppermute | solution.py:131
  304.8 7.1 %collective-permute-done.49 = bf16[512,128]{1,0:T(8,128)(2,1)S(1)} collective-permute-done((bf16[512,128]{1,0:T(8,128)(2,1)S(1)}, bf16[512,128]{1,0:T(8,128)(2,1)S(1)}, u32[]{:S(2)}, u32[]{:S(2)}) %collective-permute-start.49) | collective-permute-done | bytes 131104 | tf_op jit(solution)/shard_map/ppermute | solution.py:131
  (179 shorter events, 88.0 us)
Async XLA Ops:
  2.7 37.6 %collective-permute-start.4 = (bf16[2,512,512]{2,1,0:T(8,128)(2,1)S(1)}, bf16[2,512,512]{2,1,0:T(8,128)(2,1)S(1)}, u32[]{:S(2)}, u32[]{:S(2)}) collective-permute-start(bf16[2,512,512]{2,1,0:T(8,128)(2,1)S(1)} %pad_maximum_fusion.1), channel_id=1, source_target_pairs={{0,4},{4,0},{8,12},{12,8},{16,20},{20,16},{24,28},{28,24},{1,5},{5... | collective-permute-start | bytes 3145736 | tf_op jit(solution)/shard_map/ppermute | solution.py:131
  6.4 33.8 %collective-permute-start.5 = (bf16[128,1024]{1,0:T(8,128)(2,1)S(1)}, bf16[128,1024]{1,0:T(8,128)(2,1)S(1)}, u32[]{:S(2)}, u32[]{:S(2)}) collective-permute-start(bf16[128,1024]{1,0:T(8,128)(2,1)S(1)} %copy-done.28), channel_id=1, source_target_pairs={{0,0},{1,8},{2,16},{3,24},{4,4},{5,12},{6,20},{7,28},{8,2},{9,10},... | collective-permute-start | bytes 786440 | tf_op jit(solution)/shard_map/ppermute | solution.py:146
  7.1 26.9 %collective-permute-start.3 = (bf16[128,1024]{1,0:T(8,128)(2,1)S(1)}, bf16[128,1024]{1,0:T(8,128)(2,1)S(1)}, u32[]{:S(2)}, u32[]{:S(2)}) collective-permute-start(bf16[128,1024]{1,0:T(8,128)(2,1)S(1)} %collective-permute-done), channel_id=1, source_target_pairs={{0,6},{1,7},{2,4},{3,5},{4,2},{5,3},{6,0},{7,1},{8,14},{9,15},{10,... | collective-permute-start | bytes 786440 | tf_op jit(solution)/shard_map/ppermute | solution.py:156
  25.3 14.8 %collective-permute-start.2 = (bf16[128,1024]{1,0:T(8,128)(2,1)S(1)}, bf16[128,1024]{1,0:T(8,128)(2,1)S(1)}, u32[]{:S(2)}, u32[]{:S(2)}) collective-permute-start(bf16[128,1024]{1,0:T(8,128)(2,1)S(1)} %collective-permute-done), channel_id=1, source_target_pairs={{0,4},{4,0},{8,12},{12,8},{16,20},{20,16},{24,28},{28,24},{1,5},{5... | collective-permute-start | bytes 786440 | tf_op jit(solution)/shard_map/ppermute | solution.py:131
  41.3 25.8 %collective-permute-start.9 = (bf16[2,512,512]{2,1,0:T(8,128)(2,1)}, bf16[2,512,512]{2,1,0:T(8,128)(2,1)S(1)}, u32[]{:S(2)}, u32[]{:S(2)}) collective-permute-start(bf16[2,512,512]{2,1,0:T(8,128)(2,1)} %pad_maximum_fusion.2), channel_id=1, source_target_pairs={{0,4},{4,0},{8,12},{12,8},{16,20},{20,16},{24,28},{28,24},{1,5},{5... | collective-permute-start | bytes 3145736 | tf_op jit(solution)/shard_map/ppermute | solution.py:131
  50.9 16.2 %collective-permute-start.8 = (bf16[2,1024,128]{2,1,0:T(8,128)(2,1)S(1)}, bf16[2,1024,128]{2,1,0:T(8,128)(2,1)S(1)}, u32[]{:S(2)}, u32[]{:S(2)}) collective-permute-start(bf16[2,1024,128]{2,1,0:T(8,128)(2,1)S(1)} %get-tuple-element.115), channel_id=1, source_target_pairs={{24,16},{28,20},{25,17},{29,21},{26,18},{30,22},{27,19},{31,23}} | collective-permute-start | bytes 1572872 | tf_op jit(solution)/shard_map/ppermute | solution.py:171
  51.6 16.7 %collective-permute-start.7 = (bf16[2,1024,128]{2,1,0:T(8,128)(2,1)S(1)}, bf16[2,1024,128]{2,1,0:T(8,128)(2,1)S(1)}, u32[]{:S(2)}, u32[]{:S(2)}) collective-permute-start(bf16[2,1024,128]{2,1,0:T(8,128)(2,1)S(1)} %get-tuple-element.116), channel_id=1, source_target_pairs={{0,8},{4,12},{1,9},{5,13},{2,10},{6,14},{3,11},{7,15}} | collective-permute-start | bytes 1572872 | tf_op jit(solution)/shard_map/ppermute | solution.py:171
  68.6 19.9 %collective-permute-start.14 = (bf16[2,1024,128]{2,1,0:T(8,128)(2,1)S(1)}, bf16[2,1024,128]{2,1,0:T(8,128)(2,1)S(1)}, u32[]{:S(2)}, u32[]{:S(2)}) collective-permute-start(bf16[2,1024,128]{2,1,0:T(8,128)(2,1)S(1)} %get-tuple-element.113), channel_id=1, source_target_pairs={{16,8},{20,12},{24,16},{28,20},{17,9},{21,13},{25,17},{29,21},{18,... | collective-permute-start | bytes 1572872 | tf_op jit(solution)/shard_map/ppermute | solution.py:171
  69.3 19.3 %collective-permute-start.13 = (bf16[2,1024,128]{2,1,0:T(8,128)(2,1)S(1)}, bf16[2,1024,128]{2,1,0:T(8,128)(2,1)S(1)}, u32[]{:S(2)}, u32[]{:S(2)}) collective-permute-start(bf16[2,1024,128]{2,1,0:T(8,128)(2,1)S(1)} %get-tuple-element.114), channel_id=1, source_target_pairs={{0,8},{4,12},{8,16},{12,20},{1,9},{5,13},{9,17},{13,21},{2,10},{6,... | collective-permute-start | bytes 1572872 | tf_op jit(solution)/shard_map/ppermute | solution.py:171
  101.2 16.2 %collective-permute-start.16 = (bf16[2,1024,128]{2,1,0:T(8,128)(2,1)}, bf16[2,1024,128]{2,1,0:T(8,128)(2,1)}, u32[]{:S(2)}, u32[]{:S(2)}) collective-permute-start(bf16[2,1024,128]{2,1,0:T(8,128)(2,1)} %get-tuple-element.112), channel_id=1, source_target_pairs={{0,8},{4,12},{1,9},{5,13},{2,10},{6,14},{3,11},{7,15}} | collective-permute-start | bytes 1572872 | tf_op jit(solution)/shard_map/ppermute | solution.py:171
  119.7 17.4 %collective-permute-start.17 = (bf16[2,1024,128]{2,1,0:T(8,128)(2,1)S(1)}, bf16[2,1024,128]{2,1,0:T(8,128)(2,1)S(1)}, u32[]{:S(2)}, u32[]{:S(2)}) collective-permute-start(bf16[2,1024,128]{2,1,0:T(8,128)(2,1)S(1)} %get-tuple-element.110), channel_id=1, source_target_pairs={{0,8},{4,12},{8,16},{12,20},{1,9},{5,13},{9,17},{13,21},{2,10},{6,... | collective-permute-start | bytes 1572872 | tf_op jit(solution)/shard_map/ppermute | solution.py:171
  126.1 17.8 %collective-permute-start.23 = (bf16[2,1024,128]{2,1,0:T(8,128)(2,1)S(1)}, bf16[2,1024,128]{2,1,0:T(8,128)(2,1)S(1)}, u32[]{:S(2)}, u32[]{:S(2)}) collective-permute-start(bf16[2,1024,128]{2,1,0:T(8,128)(2,1)S(1)} %get-tuple-element.105), channel_id=1, source_target_pairs={{8,0},{12,4},{16,8},{20,12},{24,16},{28,20},{9,1},{13,5},{17,9},{2... | collective-permute-start | bytes 1572872 | tf_op jit(solution)/shard_map/ppermute | solution.py:171
  127.4 20.9 %collective-permute-start.22 = (bf16[2,1024,128]{2,1,0:T(8,128)(2,1)S(1)}, bf16[2,1024,128]{2,1,0:T(8,128)(2,1)S(1)}, u32[]{:S(2)}, u32[]{:S(2)}) collective-permute-start(bf16[2,1024,128]{2,1,0:T(8,128)(2,1)S(1)} %get-tuple-element.106), channel_id=1, source_target_pairs={{0,8},{4,12},{8,16},{12,20},{16,24},{20,28},{1,9},{5,13},{9,17},{1... | collective-permute-start | bytes 1572872 | tf_op jit(solution)/shard_map/ppermute | solution.py:171
  137.3 20.8 %collective-permute-start.21 = (bf16[2,1024,128]{2,1,0:T(8,128)(2,1)S(1)}, bf16[2,1024,128]{2,1,0:T(8,128)(2,1)S(1)}, u32[]{:S(2)}, u32[]{:S(2)}) collective-permute-start(bf16[2,1024,128]{2,1,0:T(8,128)(2,1)S(1)} %get-tuple-element.107), channel_id=1, source_target_pairs={{8,0},{12,4},{16,8},{20,12},{24,16},{28,20},{9,1},{13,5},{17,9},{2... | collective-permute-start | bytes 1572872 | tf_op jit(solution)/shard_map/ppermute | solution.py:171
  138.6 19.5 %collective-permute-start.18 = (bf16[2,1024,128]{2,1,0:T(8,128)(2,1)S(1)}, bf16[2,1024,128]{2,1,0:T(8,128)(2,1)S(1)}, u32[]{:S(2)}, u32[]{:S(2)}) collective-permute-start(bf16[2,1024,128]{2,1,0:T(8,128)(2,1)S(1)} %get-tuple-element.108), channel_id=1, source_target_pairs={{0,8},{4,12},{8,16},{12,20},{16,24},{20,28},{1,9},{5,13},{9,17},{1... | collective-permute-start | bytes 1572872 | tf_op jit(solution)/shard_map/ppermute | solution.py:171
  159.0 14.5 %collective-permute-start.25 = (bf16[2048,128]{1,0:T(8,128)(2,1)S(1)}, bf16[2048,128]{1,0:T(8,128)(2,1)S(1)}, u32[]{:S(2)}, u32[]{:S(2)}) collective-permute-start(bf16[2048,128]{1,0:T(8,128)(2,1)S(1)} %get-tuple-element.68.refs_0_), channel_id=1, source_target_pairs={{8,0},{12,4},{16,8},{20,12},{24,16},{28,20},{9,1},{13,5},{17,9},{2... | collective-permute-start | bytes 1572872 | tf_op jit(solution)/shard_map/ppermute | solution.py:171
  174.7 17.3 %collective-permute-start.27 = (bf16[2048,128]{1,0:T(8,128)(2,1)S(1)}, bf16[2048,128]{1,0:T(8,128)(2,1)S(1)}, u32[]{:S(2)}, u32[]{:S(2)}) collective-permute-start(bf16[2048,128]{1,0:T(8,128)(2,1)S(1)} %collective-permute-done.25.refs_4_), channel_id=1, source_target_pairs={{8,0},{12,4},{16,8},{20,12},{9,1},{13,5},{17,9},{21,13},{10,2},{14... | collective-permute-start | bytes 1572872 | tf_op jit(solution)/shard_map/ppermute | solution.py:171
  176.0 16.0 %collective-permute-start.26 = (bf16[2048,128]{1,0:T(8,128)(2,1)S(1)}, bf16[2048,128]{1,0:T(8,128)(2,1)S(1)}, u32[]{:S(2)}, u32[]{:S(2)}) collective-permute-start(bf16[2048,128]{1,0:T(8,128)(2,1)S(1)} %collective-permute-done.24.refs_1_), channel_id=1, source_target_pairs={{8,16},{12,20},{16,24},{20,28},{9,17},{13,21},{17,25},{21,29},{10,... | collective-permute-start | bytes 1572872 | tf_op jit(solution)/shard_map/ppermute | solution.py:171
  192.8 20.5 %collective-permute-start.29 = (bf16[2048,128]{1,0:T(8,128)(2,1)S(1)}, bf16[2048,128]{1,0:T(8,128)(2,1)S(1)}, u32[]{:S(2)}, u32[]{:S(2)}) collective-permute-start(bf16[2048,128]{1,0:T(8,128)(2,1)S(1)} %collective-permute-done.27.refs_5_), channel_id=1, source_target_pairs={{8,0},{12,4},{9,1},{13,5},{10,2},{14,6},{11,3},{15,7}} | collective-permute-start | bytes 1572872 | tf_op jit(solution)/shard_map/ppermute | solution.py:171
  194.1 27.5 %collective-permute-start.32 = (bf16[2176,128]{1,0:T(8,128)(2,1)S(1)}, bf16[2176,128]{1,0:T(8,128)(2,1)S(1)}, u32[]{:S(2)}, u32[]{:S(2)}) collective-permute-start(bf16[2176,128]{1,0:T(8,128)(2,1)S(1)} %backward_filter.1.refs_0_), channel_id=1, source_target_pairs={{8,0},{12,4},{16,8},{20,12},{24,16},{28,20},{9,1},{13,5},{17,9},{2... | collective-permute-start | bytes 1671176 | tf_op jit(solution)/shard_map/ppermute | solution.py:171
  195.4 27.7 %collective-permute-start.30 = (bf16[2176,128]{1,0:T(8,128)(2,1)S(1)}, bf16[2176,128]{1,0:T(8,128)(2,1)S(1)}, u32[]{:S(2)}, u32[]{:S(2)}) collective-permute-start(bf16[2176,128]{1,0:T(8,128)(2,1)S(1)} %backward_filter.1.refs_0_), channel_id=1, source_target_pairs={{0,8},{4,12},{8,16},{12,20},{16,24},{20,28},{1,9},{5,13},{9,17},{1... | collective-permute-start | bytes 1671176 | tf_op jit(solution)/shard_map/ppermute | solution.py:171
  221.6 19.9 %collective-permute-start.37 = (bf16[2,2,128,1024]{3,2,0,1:T(8,128)(2,1)S(1)}, bf16[2,2,128,1024]{3,2,0,1:T(8,128)(2,1)S(1)}, u32[]{:S(2)}, u32[]{:S(2)}) collective-permute-start(bf16[2,2,128,1024]{3,2,0,1:T(8,128)(2,1)S(1)} %copy.17), channel_id=1, source_target_pairs={{0,1},{1,0},{2,3},{3,2},{4,5},{5,4},{6,7},{7,6},{8,9},{9,8},{10,11... | collective-permute-start | bytes 3145736 | tf_op jit(solution)/shard_map/ppermute | solution.py:131
  221.6 16.9 %collective-permute-start.33 = (bf16[2176,128]{1,0:T(8,128)(2,1)S(1)}, bf16[2176,128]{1,0:T(8,128)(2,1)S(1)}, u32[]{:S(2)}, u32[]{:S(2)}) collective-permute-start(bf16[2176,128]{1,0:T(8,128)(2,1)S(1)} %collective-permute-done.32.refs_4_), channel_id=1, source_target_pairs={{8,0},{12,4},{16,8},{20,12},{9,1},{13,5},{17,9},{21,13},{10,2},{14... | collective-permute-start | bytes 1671176 | tf_op jit(solution)/shard_map/ppermute | solution.py:171
  223.1 15.5 %collective-permute-start.31 = (bf16[2176,128]{1,0:T(8,128)(2,1)S(1)}, bf16[2176,128]{1,0:T(8,128)(2,1)S(1)}, u32[]{:S(2)}, u32[]{:S(2)}) collective-permute-start(bf16[2176,128]{1,0:T(8,128)(2,1)S(1)} %collective-permute-done.30.refs_1_), channel_id=1, source_target_pairs={{8,16},{12,20},{16,24},{20,28},{9,17},{13,21},{17,25},{21,29},{10,... | collective-permute-start | bytes 1671176 | tf_op jit(solution)/shard_map/ppermute | solution.py:171
  238.6 16.0 %collective-permute-start.35 = (bf16[2176,128]{1,0:T(8,128)(2,1)S(1)}, bf16[2176,128]{1,0:T(8,128)(2,1)S(1)}, u32[]{:S(2)}, u32[]{:S(2)}) collective-permute-start(bf16[2176,128]{1,0:T(8,128)(2,1)S(1)} %collective-permute-done.33.refs_5_), channel_id=1, source_target_pairs={{8,0},{12,4},{9,1},{13,5},{10,2},{14,6},{11,3},{15,7}} | collective-permute-start | bytes 1671176 | tf_op jit(solution)/shard_map/ppermute | solution.py:171
  239.8 14.7 %collective-permute-start.36 = (bf16[2176,128]{1,0:T(8,128)(2,1)S(1)}, bf16[2176,128]{1,0:T(8,128)(2,1)S(1)}, u32[]{:S(2)}, u32[]{:S(2)}) collective-permute-start(bf16[2176,128]{1,0:T(8,128)(2,1)S(1)} %collective-permute-done.31.refs_2_), channel_id=1, source_target_pairs={{16,24},{20,28},{17,25},{21,29},{18,26},{22,30},{19,27},{23,31}} | collective-permute-start | bytes 1671176 | tf_op jit(solution)/shard_map/ppermute | solution.py:171
  262.9 16.6 %collective-permute-start.39 = (bf16[512,1024]{1,0:T(8,128)(2,1)S(1)}, bf16[512,1024]{1,0:T(8,128)(2,1)S(1)}, u32[]{:S(2)}, u32[]{:S(2)}) collective-permute-start(bf16[512,1024]{1,0:T(8,128)(2,1)S(1)} %project_back.2), channel_id=1, source_target_pairs={{0,1},{1,0},{2,3},{3,2},{4,5},{5,4},{6,7},{7,6},{8,9},{9,8},{10,11... | collective-permute-start | bytes 3145736 | tf_op jit(solution)/shard_map/ppermute | solution.py:131
  263.8 14.5 %collective-permute-start.44 = (bf16[2,128,1024]{2,1,0:T(8,128)(2,1)}, bf16[2,128,1024]{2,1,0:T(8,128)(2,1)S(1)}, u32[]{:S(2)}, u32[]{:S(2)}) collective-permute-start(bf16[2,128,1024]{2,1,0:T(8,128)(2,1)} %slice_bitcast_fusion.6), channel_id=1, source_target_pairs={{0,2},{1,3},{2,0},{3,1},{4,6},{5,7},{6,4},{7,5},{8,10},{9,11},{10,... | collective-permute-start | bytes 1572872 | tf_op jit(solution)/shard_map/ppermute | solution.py:131
  265.0 34.2 %collective-permute-start.43 = (bf16[512,512]{1,0:T(8,128)(2,1)S(1)}, bf16[512,512]{1,0:T(8,128)(2,1)S(1)}, u32[]{:S(2)}, u32[]{:S(2)}) collective-permute-start(bf16[512,512]{1,0:T(8,128)(2,1)S(1)} %get-tuple-element.87), channel_id=1, source_target_pairs={{0,4},{4,0},{8,12},{12,8},{16,20},{20,16},{24,28},{28,24},{1,5},{5... | collective-permute-start | bytes 1572872 | tf_op jit(solution)/shard_map/ppermute | solution.py:131
  282.7 16.4 %collective-permute-start.41 = (bf16[128,1024]{1,0:T(8,128)(2,1)S(1)}, bf16[128,1024]{1,0:T(8,128)(2,1)S(1)}, u32[]{:S(2)}, u32[]{:S(2)}) collective-permute-start(bf16[128,1024]{1,0:T(8,128)(2,1)S(1)} %get-tuple-element.119), channel_id=1, source_target_pairs={{0,4},{4,0},{8,12},{12,8},{16,20},{20,16},{24,28},{28,24},{1,5},{5... | collective-permute-start | bytes 786440 | tf_op jit(solution)/shard_map/ppermute | solution.py:131
  289.0 25.3 %collective-permute-start.48 = (bf16[512,512]{1,0:T(8,128)(2,1)}, bf16[512,512]{1,0:T(8,128)(2,1)S(1)}, u32[]{:S(2)}, u32[]{:S(2)}) collective-permute-start(bf16[512,512]{1,0:T(8,128)(2,1)} %get-tuple-element.94), channel_id=1, source_target_pairs={{0,4},{4,0},{8,12},{12,8},{16,20},{20,16},{24,28},{28,24},{1,5},{5... | collective-permute-start | bytes 1572872 | tf_op jit(solution)/shard_map/ppermute | solution.py:131
  299.3 16.6 %collective-permute-start.47 = (bf16[128,1024]{1,0:T(8,128)(2,1)S(1)}, bf16[128,1024]{1,0:T(8,128)(2,1)S(1)}, u32[]{:S(2)}, u32[]{:S(2)}) collective-permute-start(bf16[128,1024]{1,0:T(8,128)(2,1)S(1)} %add_add_fusion), channel_id=1, source_target_pairs={{0,0},{8,1},{16,2},{24,3},{4,4},{12,5},{20,6},{28,7},{2,8},{10,9},... | collective-permute-start | bytes 786440 | tf_op jit(solution)/shard_map/ppermute | solution.py:146
  (48 other events, 543.0 us)

commit v5 on v4

--- a/solution.py
+++ b/solution.py
@@ -819,10 +819,9 @@
         ((x_near, x_far), in_weight, (given_kv, 1), False, 2),
     )
     kv_up, kv_down = scatter_start(kv_blocks)
-    kv_up, kv_down, given_qo = lax.optimization_barrier((kv_up, kv_down, given_qo))
-    g_near = jnp.stack(gathered(after(g_own, kv_blocks))).reshape(2, 2, -1, width)
+    g_near = jnp.stack(gathered(g_own)).reshape(2, 2, -1, width)
+    kv_up, kv_down, given_qo, g_near = lax.optimization_barrier((kv_up, kv_down, given_qo, g_near))
     kv_up, kv_down = scatter_next(kv_blocks, kv_up, kv_down, 2)
-    g_near, kv_up, kv_down = lax.optimization_barrier((g_near, kv_up, kv_down))
     g_far = flip(g_near, "fsdp", 1)
     qg_blocks = project_pair(
         place,

time: 319 us -> 312 us (0.978)
  Pallas kernels: 71.3 us -> 68 us
    ppermute x3, waiting for transfers between devices: 16.4 us -> 10.9 us  [flip_both(): return lax.ppermute(value, ('seq', 'fsdp'), pairs)]
  transfers between devices with their start and end apart: 50 -> 50, of which waited for: 23 -> 23; matrix products, arithmetic and copies ran while one was open for 2% -> 3% of each run, Pallas kernels for 18% -> 17%
where the time goes in v5:
time: 312 us; the launch traced here: 310 us
  waiting for transfers between devices  122 us (39%)
  starting transfers between devices  101 us (32%)
  Pallas kernels  68 us (22%)
  other arithmetic  9.22 us (3%)
  local copies, waits for them, and re-layouts  8.47 us (3%)
    ppermute x19, waiting for transfers between devices, flip(): lax.ppermute(value, axis, [(i, i ^ bit) for i in range(lax.axis_size(axis...  69.5 us
    ppermute x24, starting transfers between devices, along_line(): return lax.ppermute(value, 'seq', pairs)  60.6 us
    ppermute x24, waiting for transfers between devices, along_line(): return lax.ppermute(value, 'seq', pairs)  41.6 us
    ppermute x3, starting transfers between devices, flip_both(): return lax.ppermute(value, ('seq', 'fsdp'), pairs)  21 us
    ppermute x19, starting transfers between devices, flip(): lax.ppermute(value, axis, [(i, i ^ bit) for i in range(lax.axis_size(axis...  16.8 us
    pallas_call x1, Pallas kernels, backward_filter(): pl.pallas_call(body, out_shape=jax.ShapeDtypeStruct((2 * tokens + taps, l...  13.6 us
    pallas_call x2, Pallas kernels, project_pair(): pl.pallas_call(body, out_shape=jax.ShapeDtypeStruct((count, 2, tokens, la...  11.7 us
    ppermute x3, waiting for transfers between devices, flip_both(): return lax.ppermute(value, ('seq', 'fsdp'), pairs)  10.9 us
  transfers between devices with their start and end apart: 50, of which 23 were waited for; matrix products, arithmetic and copies ran while one was open for 3% of the time, Pallas kernels for 17%

profile of v5, /device:TPU:0, one launch (start us, length us, event | category | flops | bytes accessed | tf_op | source)
XLA Modules:
  0.0 310.3 jit_solution(9486427152483931895)
XLA Ops:
  2.7 3.0 collective-permute-start.4
  7.1 18.2 %collective-permute-start.3 = (bf16[128,1024]{1,0:T(8,128)(2,1)S(1)}, bf16[128,1024]{1,0:T(8,128)(2,1)S(1)}, u32[]{:S(2)}, u32[]{:S(2)}) collective-permute-start(bf16[128,1024]{1,0:T(8,128)(2,1)S(1)} %collective-permute-done), channel_id=1, source_target_pairs={{0,6},{1,7},{2,4},{3,5},{4,2},{5,3},{6,0},{7,1},{8,14},{9,15},{10,... | collective-permute-start | bytes 786440 | tf_op jit(solution)/shard_map/ppermute | solution.py:156
  27.6 6.4 %collective-permute-done.3 = bf16[128,1024]{1,0:T(8,128)(2,1)S(1)} collective-permute-done((bf16[128,1024]{1,0:T(8,128)(2,1)S(1)}, bf16[128,1024]{1,0:T(8,128)(2,1)S(1)}, u32[]{:S(2)}, u32[]{:S(2)}) %collective-permute-start.3) | collective-permute-done | bytes 262176 | tf_op jit(solution)/shard_map/ppermute | solution.py:156
  34.0 6.1 %collective-permute-done.2 = bf16[128,1024]{1,0:T(8,128)(2,1)S(1)} collective-permute-done((bf16[128,1024]{1,0:T(8,128)(2,1)S(1)}, bf16[128,1024]{1,0:T(8,128)(2,1)S(1)}, u32[]{:S(2)}, u32[]{:S(2)}) %collective-permute-start.2) | collective-permute-done | bytes 262176 | tf_op jit(solution)/shard_map/ppermute | solution.py:131
  46.0 5.5 %project_pair.2.blocks_ref = bf16[4,2,1024,128]{3,2,1,0:T(8,128)(2,1)S(1)} custom-call(s32[2]{0:T(128)S(1)} %pad_add_fusion.place_ref, bf16[2,2,128,1024]{3,2,1,0:T(8,128)(2,1)S(1)} %bitcast.64, bf16[2,2,128,1024]{3,2,1,0:T(8,128)(2,1)S(1)} %collective-permute-done.6.refs_1_.refs_3_.refs_7_.refs_9_.own_far.other_far, bf16[2,2,128,1024]{3,2,1,0:T(8,128)(2,1)S(1)} %bitcast.65, ...), custom_call_target="tpu_custom_call" | custom-call | flops 2147483648 | bytes 8388608 | tf_op jit(solution)/shard_map/project_pair/pallas_call | solution.py:244
  52.3 5.6 %collective-permute-start.7 = (bf16[2,1024,128]{2,1,0:T(8,128)(2,1)S(1)}, bf16[2,1024,128]{2,1,0:T(8,128)(2,1)S(1)}, u32[]{:S(2)}, u32[]{:S(2)}) collective-permute-start(bf16[2,1024,128]{2,1,0:T(8,128)(2,1)S(1)} %get-tuple-element.110), channel_id=1, source_target_pairs={{0,8},{4,12},{1,9},{5,13},{2,10},{6,14},{3,11},{7,15}} | collective-permute-start | bytes 1572872 | tf_op jit(solution)/shard_map/ppermute | solution.py:171
  59.4 18.9 %collective-permute-done.11 = bf16[128,1024]{1,0:T(8,128)(2,1)S(1)} collective-permute-done((bf16[128,1024]{1,0:T(8,128)(2,1)S(1)}, bf16[128,1024]{1,0:T(8,128)(2,1)S(1)}, u32[]{:S(2)}, u32[]{:S(2)}) %collective-permute-start.11) | collective-permute-done | bytes 262176 | tf_op jit(solution)/shard_map/ppermute | solution.py:131
  81.2 6.2 %project_pair.3.blocks_ref = bf16[4,2,1024,128]{3,2,1,0:T(8,128)(2,1)} custom-call(s32[2]{0:T(128)S(1)} %pad_add_fusion.place_ref, bf16[2,2,128,1024]{3,2,1,0:T(8,128)(2,1)S(1)} %bitcast.68, bf16[2,2,128,1024]{3,2,1,0:T(8,128)(2,1)S(1)} %collective-permute-done.6.refs_1_.refs_3_.refs_7_.refs_9_.own_far.other_far, bf16[2,2,128,1024]{3,2,1,0:T(8,128)(2,1)S(1)} %bitcast.69, ...), custom_call_target="tpu_custom_call" | custom-call | flops 2147483648 | bytes 8388608 | tf_op jit(solution)/shard_map/project_pair/pallas_call | solution.py:244
  91.1 5.7 %collective-permute-start.14 = (bf16[2,1024,128]{2,1,0:T(8,128)(2,1)}, bf16[2,1024,128]{2,1,0:T(8,128)(2,1)}, u32[]{:S(2)}, u32[]{:S(2)}) collective-permute-start(bf16[2,1024,128]{2,1,0:T(8,128)(2,1)} %get-tuple-element.108), channel_id=1, source_target_pairs={{0,8},{4,12},{1,9},{5,13},{2,10},{6,14},{3,11},{7,15}} | collective-permute-start | bytes 1572872 | tf_op jit(solution)/shard_map/ppermute | solution.py:171
  101.6 7.0 %collective-permute-done.14 = bf16[2,1024,128]{2,1,0:T(8,128)(2,1)} collective-permute-done((bf16[2,1024,128]{2,1,0:T(8,128)(2,1)}, bf16[2,1024,128]{2,1,0:T(8,128)(2,1)}, u32[]{:S(2)}, u32[]{:S(2)}) %collective-permute-start.14) | collective-permute-done | bytes 524320 | tf_op jit(solution)/shard_map/ppermute | solution.py:171
  111.0 5.0 %collective-permute-start.15 = (bf16[2,1024,128]{2,1,0:T(8,128)(2,1)S(1)}, bf16[2,1024,128]{2,1,0:T(8,128)(2,1)S(1)}, u32[]{:S(2)}, u32[]{:S(2)}) collective-permute-start(bf16[2,1024,128]{2,1,0:T(8,128)(2,1)S(1)} %get-tuple-element.106), channel_id=1, source_target_pairs={{0,8},{4,12},{8,16},{12,20},{1,9},{5,13},{9,17},{13,21},{2,10},{6,... | collective-permute-start | bytes 1572872 | tf_op jit(solution)/shard_map/ppermute | solution.py:171
  116.1 3.7 %collective-permute-done.20 = bf16[2,1024,128]{2,1,0:T(8,128)(2,1)} collective-permute-done((bf16[2,1024,128]{2,1,0:T(8,128)(2,1)S(1)}, bf16[2,1024,128]{2,1,0:T(8,128)(2,1)}, u32[]{:S(2)}, u32[]{:S(2)}) %collective-permute-start.20) | collective-permute-done | bytes 524320 | tf_op jit(solution)/shard_map/ppermute | solution.py:171
  122.5 5.2 %collective-permute-start.21 = (bf16[2,1024,128]{2,1,0:T(8,128)(2,1)S(1)}, bf16[2,1024,128]{2,1,0:T(8,128)(2,1)S(1)}, u32[]{:S(2)}, u32[]{:S(2)}) collective-permute-start(bf16[2,1024,128]{2,1,0:T(8,128)(2,1)S(1)} %get-tuple-element.100), channel_id=1, source_target_pairs={{0,8},{4,12},{8,16},{12,20},{16,24},{20,28},{1,9},{5,13},{9,17},{1... | collective-permute-start | bytes 1572872 | tf_op jit(solution)/shard_map/ppermute | solution.py:171
  127.7 3.2 %collective-permute-done.15 = bf16[2,1024,128]{2,1,0:T(8,128)(2,1)S(1)} collective-permute-done((bf16[2,1024,128]{2,1,0:T(8,128)(2,1)S(1)}, bf16[2,1024,128]{2,1,0:T(8,128)(2,1)S(1)}, u32[]{:S(2)}, u32[]{:S(2)}) %collective-permute-start.15) | collective-permute-done | bytes 524320 | tf_op jit(solution)/shard_map/ppermute | solution.py:171
  132.5 5.0 %collective-permute-start.16 = (bf16[2,1024,128]{2,1,0:T(8,128)(2,1)S(1)}, bf16[2,1024,128]{2,1,0:T(8,128)(2,1)S(1)}, u32[]{:S(2)}, u32[]{:S(2)}) collective-permute-start(bf16[2,1024,128]{2,1,0:T(8,128)(2,1)S(1)} %get-tuple-element.104), channel_id=1, source_target_pairs={{0,8},{4,12},{8,16},{12,20},{16,24},{20,28},{1,9},{5,13},{9,17},{1... | collective-permute-start | bytes 1572872 | tf_op jit(solution)/shard_map/ppermute | solution.py:171
  137.6 4.6 %collective-permute-done.21.up_ref = bf16[2,1024,128]{2,1,0:T(8,128)(2,1)S(1)} collective-permute-done((bf16[2,1024,128]{2,1,0:T(8,128)(2,1)S(1)}, bf16[2,1024,128]{2,1,0:T(8,128)(2,1)S(1)}, u32[]{:S(2)}, u32[]{:S(2)}) %collective-permute-start.21) | collective-permute-done | bytes 524320 | tf_op jit(solution)/shard_map/ppermute | solution.py:171
  142.2 8.3 %forward_filter.1 = (bf16[2,1024,128]{2,1,0:T(8,128)(2,1)S(1)}, bf16[1024,128]{1,0:T(8,128)(2,1)S(1)}, f32[1024,128]{1,0:T(8,128)S(1)}) custom-call(s32[8]{0:T(128)S(1)} %fusion.14.order_ref, bf16[4,2,1024,128]{3,2,1,0:T(8,128)(2,1)S(1)} %copy-done.17, bf16[2,1024,128]{2,1,0:T(8,128)(2,1)S(1)} %collective-permute-done.21.up_ref, ...), custom_call_target="tpu_custom_call" | custom-call | flops 6710886400 | bytes 1572864 | tf_op jit(solution)/shard_map/forward_filter/pallas_call | solution.py:330
  154.8 5.0 %collective-permute-start.24 = (bf16[2048,128]{1,0:T(8,128)(2,1)S(1)}, bf16[2048,128]{1,0:T(8,128)(2,1)S(1)}, u32[]{:S(2)}, u32[]{:S(2)}) collective-permute-start(bf16[2048,128]{1,0:T(8,128)(2,1)S(1)} %get-tuple-element.62.refs_0_), channel_id=1, source_target_pairs={{0,8},{4,12},{8,16},{12,20},{16,24},{20,28},{1,9},{5,13},{9,17},{1... | collective-permute-start | bytes 1572872 | tf_op jit(solution)/shard_map/ppermute | solution.py:171
  159.8 9.4 %collective-permute-done.25.refs_4_ = bf16[2048,128]{1,0:T(8,128)(2,1)S(1)} collective-permute-done((bf16[2048,128]{1,0:T(8,128)(2,1)S(1)}, bf16[2048,128]{1,0:T(8,128)(2,1)S(1)}, u32[]{:S(2)}, u32[]{:S(2)}) %collective-permute-start.25) | collective-permute-done | bytes 524320 | tf_op jit(solution)/shard_map/ppermute | solution.py:171
  172.4 13.6 %backward_filter.1.refs_0_ = bf16[2176,128]{1,0:T(8,128)(2,1)S(1)} custom-call(s32[8]{0:T(128)S(1)} %fusion.14.order_ref, bf16[1024,128]{1,0:T(8,128)(2,1)S(1)} %get-tuple-element.64.grad_ref, bf16[2,1024,128]{2,1,0:T(8,128)(2,1)S(1)} %get-tuple-element.65.kv_ref, bf16[1024,128]{1,0:T(8,128)(2,1)S(1)} %get-tuple-element.66.signal_ref, ...), custom_call_target="tpu_custom_call" | custom-call | flops 13421772800 | bytes 1572864 | tf_op jit(solution)/shard_map/backward_filter/pallas_call | solution.py:475
  189.5 9.0 %collective-permute-start.30 = (bf16[2176,128]{1,0:T(8,128)(2,1)S(1)}, bf16[2176,128]{1,0:T(8,128)(2,1)S(1)}, u32[]{:S(2)}, u32[]{:S(2)}) collective-permute-start(bf16[2176,128]{1,0:T(8,128)(2,1)S(1)} %backward_filter.1.refs_0_), channel_id=1, source_target_pairs={{0,8},{4,12},{8,16},{12,20},{16,24},{20,28},{1,9},{5,13},{9,17},{1... | collective-permute-start | bytes 1671176 | tf_op jit(solution)/shard_map/ppermute | solution.py:171
  198.5 8.9 %collective-permute-done.29.refs_6_ = bf16[2048,128]{1,0:T(8,128)(2,1)S(1)} collective-permute-done((bf16[2048,128]{1,0:T(8,128)(2,1)S(1)}, bf16[2048,128]{1,0:T(8,128)(2,1)S(1)}, u32[]{:S(2)}, u32[]{:S(2)}) %collective-permute-start.29) | collective-permute-done | bytes 524320 | tf_op jit(solution)/shard_map/ppermute | solution.py:171
  211.6 3.8 %project_out.1 = bf16[1024,1024]{1,0:T(8,128)(2,1)S(1)} custom-call(s32[2]{0:T(128)S(1)} %pad_add_fusion.place_ref, bf16[2,1024,512]{2,1,0:T(8,128)(2,1)} %copy-done.4, bf16[1024,512]{1,0:T(8,128)(2,1)S(1)} %copy-done.19, bf16[2,512,512]{2,1,0:T(8,128)(2,1)S(1)} %copy-done.10), custom_call_target="tpu_custom_call" | custom-call | flops 1073741824 | bytes 4194304 | tf_op jit(solution)/shard_map/project_out/pallas_call | solution.py:621
  222.3 10.1 %collective-permute-done.34.piece_ref = bf16[512,512]{1,0:T(8,128)(2,1)S(1)} collective-permute-done((bf16[512,512]{1,0:T(8,128)(2,1)S(1)}, bf16[512,512]{1,0:T(8,128)(2,1)S(1)}, u32[]{:S(2)}, u32[]{:S(2)}) %collective-permute-start.34) | collective-permute-done | bytes 524320 | tf_op jit(solution)/shard_map/ppermute | solution.py:131
  235.7 11.7 %collective-permute-done.38.piece_ref = bf16[512,512]{1,0:T(8,128)(2,1)S(1)} collective-permute-done((bf16[512,512]{1,0:T(8,128)(2,1)S(1)}, bf16[512,512]{1,0:T(8,128)(2,1)S(1)}, u32[]{:S(2)}, u32[]{:S(2)}) %collective-permute-start.38) | collective-permute-done | bytes 524320 | tf_op jit(solution)/shard_map/ppermute | solution.py:131
  252.2 4.2 %project_back.2 = bf16[512,1024]{1,0:T(8,128)(2,1)S(1)} custom-call(s32[2]{0:T(128)S(1)} %pad_add_fusion.place_ref, bf16[2,1024,512]{2,1,0:T(8,128)(2,1)S(1)} %copy-done.5, bf16[3,512,1024]{2,1,0:T(8,128)(2,1)} %refs_7_.3, bf16[2,512,512]{2,1,0:T(8,128)(2,1)S(1)} %copy-done.10, bf16[2,1024,512]{2,1,0:T(8,128)(2,1)} %copy-done.2, ...), custom_call_target="tpu_custom_call" | custom-call | flops 1610612736 | bytes 2097152 | tf_op jit(solution)/shard_map/project_back/pallas_call | solution.py:594
  259.4 4.2 %project_back.3 = bf16[512,1024]{1,0:T(8,128)(2,1)S(1)} custom-call(s32[2]{0:T(128)S(1)} %pad_add_fusion.place_ref, bf16[2,1024,512]{2,1,0:T(8,128)(2,1)S(1)} %copy-done.5, bf16[3,512,1024]{2,1,0:T(8,128)(2,1)} %refs_7_.3, bf16[2,512,512]{2,1,0:T(8,128)(2,1)S(1)} %copy-done.10, bf16[2,1024,512]{2,1,0:T(8,128)(2,1)} %copy-done.2, ...), custom_call_target="tpu_custom_call" | custom-call | flops 1610612736 | bytes 2097152 | tf_op jit(solution)/shard_map/project_back/pallas_call | solution.py:594
  263.6 7.7 %collective-permute-done.44 = bf16[2,128,1024]{2,1,0:T(8,128)(2,1)S(1)} collective-permute-done((bf16[2,128,1024]{2,1,0:T(8,128)(2,1)S(1)}, bf16[2,128,1024]{2,1,0:T(8,128)(2,1)S(1)}, u32[]{:S(2)}, u32[]{:S(2)}) %collective-permute-start.44) | collective-permute-done | bytes 524320 | tf_op jit(solution)/shard_map/ppermute | solution.py:131
  277.6 3.1 %in_gradient.5 = (f32[3,512,1024]{2,1,0:T(8,128)}, bf16[512,512]{1,0:T(8,128)(2,1)}) custom-call(s32[2]{0:T(128)S(1)} %pad_add_fusion.place_ref, bf16[2,2,128,1024]{3,2,1,0:T(8,128)(2,1)S(1)} %bitcast.74, bf16[2,2,128,1024]{3,2,1,0:T(8,128)(2,1)S(1)} %collective-permute-done.6.refs_1_.refs_3_.refs_7_.refs_9_.own_far.other_far, ...), custom_call_target="tpu_custom_call", output_to_operand_aliasing={{0}: (6, {})} | custom-call | flops 1073741824 | bytes 4194304 | tf_op jit(solution)/shard_map/in_gradient/pallas_call | solution.py:661
  283.9 4.5 %collective-permute-done.42 = bf16[128,1024]{1,0:T(8,128)(2,1)S(1)} collective-permute-done((bf16[128,1024]{1,0:T(8,128)(2,1)S(1)}, bf16[128,1024]{1,0:T(8,128)(2,1)S(1)}, u32[]{:S(2)}, u32[]{:S(2)}) %collective-permute-start.42) | collective-permute-done | bytes 262176 | tf_op jit(solution)/shard_map/ppermute | solution.py:156
  288.4 3.6 %collective-permute-done.41 = bf16[128,1024]{1,0:T(8,128)(2,1)S(1)} collective-permute-done((bf16[128,1024]{1,0:T(8,128)(2,1)S(1)}, bf16[128,1024]{1,0:T(8,128)(2,1)S(1)}, u32[]{:S(2)}, u32[]{:S(2)}) %collective-permute-start.41) | collective-permute-done | bytes 262176 | tf_op jit(solution)/shard_map/ppermute | solution.py:131
  297.4 7.4 %collective-permute-done.49 = bf16[512,128]{1,0:T(8,128)(2,1)S(1)} collective-permute-done((bf16[512,128]{1,0:T(8,128)(2,1)S(1)}, bf16[512,128]{1,0:T(8,128)(2,1)S(1)}, u32[]{:S(2)}, u32[]{:S(2)}) %collective-permute-start.49) | collective-permute-done | bytes 131104 | tf_op jit(solution)/shard_map/ppermute | solution.py:131
  (173 shorter events, 84.8 us)
Async XLA Ops:
  2.7 37.6 %collective-permute-start.4 = (bf16[2,512,512]{2,1,0:T(8,128)(2,1)S(1)}, bf16[2,512,512]{2,1,0:T(8,128)(2,1)S(1)}, u32[]{:S(2)}, u32[]{:S(2)}) collective-permute-start(bf16[2,512,512]{2,1,0:T(8,128)(2,1)S(1)} %pad_maximum_fusion.1), channel_id=1, source_target_pairs={{0,4},{4,0},{8,12},{12,8},{16,20},{20,16},{24,28},{28,24},{1,5},{5... | collective-permute-start | bytes 3145736 | tf_op jit(solution)/shard_map/ppermute | solution.py:131
  6.4 33.8 %collective-permute-start.5 = (bf16[128,1024]{1,0:T(8,128)(2,1)S(1)}, bf16[128,1024]{1,0:T(8,128)(2,1)S(1)}, u32[]{:S(2)}, u32[]{:S(2)}) collective-permute-start(bf16[128,1024]{1,0:T(8,128)(2,1)S(1)} %copy-done.25), channel_id=1, source_target_pairs={{0,0},{1,8},{2,16},{3,24},{4,4},{5,12},{6,20},{7,28},{8,2},{9,10},... | collective-permute-start | bytes 786440 | tf_op jit(solution)/shard_map/ppermute | solution.py:146
  7.1 26.9 %collective-permute-start.3 = (bf16[128,1024]{1,0:T(8,128)(2,1)S(1)}, bf16[128,1024]{1,0:T(8,128)(2,1)S(1)}, u32[]{:S(2)}, u32[]{:S(2)}) collective-permute-start(bf16[128,1024]{1,0:T(8,128)(2,1)S(1)} %collective-permute-done), channel_id=1, source_target_pairs={{0,6},{1,7},{2,4},{3,5},{4,2},{5,3},{6,0},{7,1},{8,14},{9,15},{10,... | collective-permute-start | bytes 786440 | tf_op jit(solution)/shard_map/ppermute | solution.py:156
  41.3 37.2 %collective-permute-start.9 = (bf16[2,512,512]{2,1,0:T(8,128)(2,1)}, bf16[2,512,512]{2,1,0:T(8,128)(2,1)S(1)}, u32[]{:S(2)}, u32[]{:S(2)}) collective-permute-start(bf16[2,512,512]{2,1,0:T(8,128)(2,1)} %pad_maximum_fusion.2), channel_id=1, source_target_pairs={{0,4},{4,0},{8,12},{12,8},{16,20},{20,16},{24,28},{28,24},{1,5},{5... | collective-permute-start | bytes 3145736 | tf_op jit(solution)/shard_map/ppermute | solution.py:131
  43.1 15.6 %collective-permute-start.12 = (bf16[128,1024]{1,0:T(8,128)(2,1)S(1)}, bf16[128,1024]{1,0:T(8,128)(2,1)S(1)}, u32[]{:S(2)}, u32[]{:S(2)}) collective-permute-start(bf16[128,1024]{1,0:T(8,128)(2,1)S(1)} %collective-permute-done.5), channel_id=1, source_target_pairs={{0,6},{1,7},{2,4},{3,5},{4,2},{5,3},{6,0},{7,1},{8,14},{9,15},{10,... | collective-permute-start | bytes 786440 | tf_op jit(solution)/shard_map/ppermute | solution.py:156
  51.6 26.8 %collective-permute-start.8 = (bf16[2,1024,128]{2,1,0:T(8,128)(2,1)S(1)}, bf16[2,1024,128]{2,1,0:T(8,128)(2,1)S(1)}, u32[]{:S(2)}, u32[]{:S(2)}) collective-permute-start(bf16[2,1024,128]{2,1,0:T(8,128)(2,1)S(1)} %get-tuple-element.109), channel_id=1, source_target_pairs={{24,16},{28,20},{25,17},{29,21},{26,18},{30,22},{27,19},{31,23}} | collective-permute-start | bytes 1572872 | tf_op jit(solution)/shard_map/ppermute | solution.py:171
  52.3 26.1 %collective-permute-start.7 = (bf16[2,1024,128]{2,1,0:T(8,128)(2,1)S(1)}, bf16[2,1024,128]{2,1,0:T(8,128)(2,1)S(1)}, u32[]{:S(2)}, u32[]{:S(2)}) collective-permute-start(bf16[2,1024,128]{2,1,0:T(8,128)(2,1)S(1)} %get-tuple-element.110), channel_id=1, source_target_pairs={{0,8},{4,12},{1,9},{5,13},{2,10},{6,14},{3,11},{7,15}} | collective-permute-start | bytes 1572872 | tf_op jit(solution)/shard_map/ppermute | solution.py:171
  58.0 20.3 %collective-permute-start.11 = (bf16[128,1024]{1,0:T(8,128)(2,1)S(1)}, bf16[128,1024]{1,0:T(8,128)(2,1)S(1)}, u32[]{:S(2)}, u32[]{:S(2)}) collective-permute-start(bf16[128,1024]{1,0:T(8,128)(2,1)S(1)} %collective-permute-done.5), channel_id=1, source_target_pairs={{0,4},{4,0},{8,12},{12,8},{16,20},{20,16},{24,28},{28,24},{1,5},{5... | collective-permute-start | bytes 786440 | tf_op jit(solution)/shard_map/ppermute | solution.py:131
  58.7 19.6 %collective-permute-start.10 = (bf16[128,1024]{1,0:T(8,128)(2,1)S(1)}, bf16[128,1024]{1,0:T(8,128)(2,1)S(1)}, u32[]{:S(2)}, u32[]{:S(2)}) collective-permute-start(bf16[128,1024]{1,0:T(8,128)(2,1)S(1)} %collective-permute-done.5), channel_id=1, source_target_pairs={{0,2},{1,3},{2,0},{3,1},{4,6},{5,7},{6,4},{7,5},{8,10},{9,11},{10,... | collective-permute-start | bytes 786440 | tf_op jit(solution)/shard_map/ppermute | solution.py:131
  91.1 17.5 %collective-permute-start.14 = (bf16[2,1024,128]{2,1,0:T(8,128)(2,1)}, bf16[2,1024,128]{2,1,0:T(8,128)(2,1)}, u32[]{:S(2)}, u32[]{:S(2)}) collective-permute-start(bf16[2,1024,128]{2,1,0:T(8,128)(2,1)} %get-tuple-element.108), channel_id=1, source_target_pairs={{0,8},{4,12},{1,9},{5,13},{2,10},{6,14},{3,11},{7,15}} | collective-permute-start | bytes 1572872 | tf_op jit(solution)/shard_map/ppermute | solution.py:171
  97.8 18.2 %collective-permute-start.22 = (bf16[2,1024,128]{2,1,0:T(8,128)(2,1)}, bf16[2,1024,128]{2,1,0:T(8,128)(2,1)}, u32[]{:S(2)}, u32[]{:S(2)}) collective-permute-start(bf16[2,1024,128]{2,1,0:T(8,128)(2,1)} %get-tuple-element.101), channel_id=1, source_target_pairs={{16,8},{20,12},{24,16},{28,20},{17,9},{21,13},{25,17},{29,21},{18,... | collective-permute-start | bytes 1572872 | tf_op jit(solution)/shard_map/ppermute | solution.py:171
  99.3 20.4 %collective-permute-start.20 = (bf16[2,1024,128]{2,1,0:T(8,128)(2,1)S(1)}, bf16[2,1024,128]{2,1,0:T(8,128)(2,1)}, u32[]{:S(2)}, u32[]{:S(2)}) collective-permute-start(bf16[2,1024,128]{2,1,0:T(8,128)(2,1)S(1)} %get-tuple-element.102), channel_id=1, source_target_pairs={{0,8},{4,12},{8,16},{12,20},{1,9},{5,13},{9,17},{13,21},{2,10},{6,... | collective-permute-start | bytes 1572872 | tf_op jit(solution)/shard_map/ppermute | solution.py:171
  110.2 17.5 %collective-permute-start.18 = (bf16[2,1024,128]{2,1,0:T(8,128)(2,1)S(1)}, bf16[2,1024,128]{2,1,0:T(8,128)(2,1)S(1)}, u32[]{:S(2)}, u32[]{:S(2)}) collective-permute-start(bf16[2,1024,128]{2,1,0:T(8,128)(2,1)S(1)} %get-tuple-element.105), channel_id=1, source_target_pairs={{16,8},{20,12},{24,16},{28,20},{17,9},{21,13},{25,17},{29,21},{18,... | collective-permute-start | bytes 1572872 | tf_op jit(solution)/shard_map/ppermute | solution.py:171
  111.0 19.9 %collective-permute-start.15 = (bf16[2,1024,128]{2,1,0:T(8,128)(2,1)S(1)}, bf16[2,1024,128]{2,1,0:T(8,128)(2,1)S(1)}, u32[]{:S(2)}, u32[]{:S(2)}) collective-permute-start(bf16[2,1024,128]{2,1,0:T(8,128)(2,1)S(1)} %get-tuple-element.106), channel_id=1, source_target_pairs={{0,8},{4,12},{8,16},{12,20},{1,9},{5,13},{9,17},{13,21},{2,10},{6,... | collective-permute-start | bytes 1572872 | tf_op jit(solution)/shard_map/ppermute | solution.py:171
  121.2 16.4 %collective-permute-start.23 = (bf16[2,1024,128]{2,1,0:T(8,128)(2,1)S(1)}, bf16[2,1024,128]{2,1,0:T(8,128)(2,1)S(1)}, u32[]{:S(2)}, u32[]{:S(2)}) collective-permute-start(bf16[2,1024,128]{2,1,0:T(8,128)(2,1)S(1)} %get-tuple-element.99), channel_id=1, source_target_pairs={{8,0},{12,4},{16,8},{20,12},{24,16},{28,20},{9,1},{13,5},{17,9},{2... | collective-permute-start | bytes 1572872 | tf_op jit(solution)/shard_map/ppermute | solution.py:171
  122.5 19.7 %collective-permute-start.21 = (bf16[2,1024,128]{2,1,0:T(8,128)(2,1)S(1)}, bf16[2,1024,128]{2,1,0:T(8,128)(2,1)S(1)}, u32[]{:S(2)}, u32[]{:S(2)}) collective-permute-start(bf16[2,1024,128]{2,1,0:T(8,128)(2,1)S(1)} %get-tuple-element.100), channel_id=1, source_target_pairs={{0,8},{4,12},{8,16},{12,20},{16,24},{20,28},{1,9},{5,13},{9,17},{1... | collective-permute-start | bytes 1572872 | tf_op jit(solution)/shard_map/ppermute | solution.py:171
  131.2 19.3 %collective-permute-start.19 = (bf16[2,1024,128]{2,1,0:T(8,128)(2,1)S(1)}, bf16[2,1024,128]{2,1,0:T(8,128)(2,1)S(1)}, u32[]{:S(2)}, u32[]{:S(2)}) collective-permute-start(bf16[2,1024,128]{2,1,0:T(8,128)(2,1)S(1)} %get-tuple-element.103), channel_id=1, source_target_pairs={{8,0},{12,4},{16,8},{20,12},{24,16},{28,20},{9,1},{13,5},{17,9},{2... | collective-permute-start | bytes 1572872 | tf_op jit(solution)/shard_map/ppermute | solution.py:171
  132.5 20.1 %collective-permute-start.16 = (bf16[2,1024,128]{2,1,0:T(8,128)(2,1)S(1)}, bf16[2,1024,128]{2,1,0:T(8,128)(2,1)S(1)}, u32[]{:S(2)}, u32[]{:S(2)}) collective-permute-start(bf16[2,1024,128]{2,1,0:T(8,128)(2,1)S(1)} %get-tuple-element.104), channel_id=1, source_target_pairs={{0,8},{4,12},{8,16},{12,20},{16,24},{20,28},{1,9},{5,13},{9,17},{1... | collective-permute-start | bytes 1572872 | tf_op jit(solution)/shard_map/ppermute | solution.py:171
  153.5 15.8 %collective-permute-start.25 = (bf16[2048,128]{1,0:T(8,128)(2,1)S(1)}, bf16[2048,128]{1,0:T(8,128)(2,1)S(1)}, u32[]{:S(2)}, u32[]{:S(2)}) collective-permute-start(bf16[2048,128]{1,0:T(8,128)(2,1)S(1)} %get-tuple-element.62.refs_0_), channel_id=1, source_target_pairs={{8,0},{12,4},{16,8},{20,12},{24,16},{28,20},{9,1},{13,5},{17,9},{2... | collective-permute-start | bytes 1572872 | tf_op jit(solution)/shard_map/ppermute | solution.py:171
  154.8 15.7 %collective-permute-start.24 = (bf16[2048,128]{1,0:T(8,128)(2,1)S(1)}, bf16[2048,128]{1,0:T(8,128)(2,1)S(1)}, u32[]{:S(2)}, u32[]{:S(2)}) collective-permute-start(bf16[2048,128]{1,0:T(8,128)(2,1)S(1)} %get-tuple-element.62.refs_0_), channel_id=1, source_target_pairs={{0,8},{4,12},{8,16},{12,20},{16,24},{20,28},{1,9},{5,13},{9,17},{1... | collective-permute-start | bytes 1572872 | tf_op jit(solution)/shard_map/ppermute | solution.py:171
  170.4 15.6 %collective-permute-start.27 = (bf16[2048,128]{1,0:T(8,128)(2,1)S(1)}, bf16[2048,128]{1,0:T(8,128)(2,1)S(1)}, u32[]{:S(2)}, u32[]{:S(2)}) collective-permute-start(bf16[2048,128]{1,0:T(8,128)(2,1)S(1)} %collective-permute-done.25.refs_4_), channel_id=1, source_target_pairs={{8,0},{12,4},{16,8},{20,12},{9,1},{13,5},{17,9},{21,13},{10,2},{14... | collective-permute-start | bytes 1572872 | tf_op jit(solution)/shard_map/ppermute | solution.py:171
  186.9 20.5 %collective-permute-start.29 = (bf16[2048,128]{1,0:T(8,128)(2,1)S(1)}, bf16[2048,128]{1,0:T(8,128)(2,1)S(1)}, u32[]{:S(2)}, u32[]{:S(2)}) collective-permute-start(bf16[2048,128]{1,0:T(8,128)(2,1)S(1)} %collective-permute-done.27.refs_5_), channel_id=1, source_target_pairs={{8,0},{12,4},{9,1},{13,5},{10,2},{14,6},{11,3},{15,7}} | collective-permute-start | bytes 1572872 | tf_op jit(solution)/shard_map/ppermute | solution.py:171
  188.2 28.2 %collective-permute-start.32 = (bf16[2176,128]{1,0:T(8,128)(2,1)S(1)}, bf16[2176,128]{1,0:T(8,128)(2,1)S(1)}, u32[]{:S(2)}, u32[]{:S(2)}) collective-permute-start(bf16[2176,128]{1,0:T(8,128)(2,1)S(1)} %backward_filter.1.refs_0_), channel_id=1, source_target_pairs={{8,0},{12,4},{16,8},{20,12},{24,16},{28,20},{9,1},{13,5},{17,9},{2... | collective-permute-start | bytes 1671176 | tf_op jit(solution)/shard_map/ppermute | solution.py:171
  189.5 28.2 %collective-permute-start.30 = (bf16[2176,128]{1,0:T(8,128)(2,1)S(1)}, bf16[2176,128]{1,0:T(8,128)(2,1)S(1)}, u32[]{:S(2)}, u32[]{:S(2)}) collective-permute-start(bf16[2176,128]{1,0:T(8,128)(2,1)S(1)} %backward_filter.1.refs_0_), channel_id=1, source_target_pairs={{0,8},{4,12},{8,16},{12,20},{16,24},{20,28},{1,9},{5,13},{9,17},{1... | collective-permute-start | bytes 1671176 | tf_op jit(solution)/shard_map/ppermute | solution.py:171
  215.7 19.7 %collective-permute-start.37 = (bf16[2,2,128,1024]{3,2,0,1:T(8,128)(2,1)S(1)}, bf16[2,2,128,1024]{3,2,0,1:T(8,128)(2,1)S(1)}, u32[]{:S(2)}, u32[]{:S(2)}) collective-permute-start(bf16[2,2,128,1024]{3,2,0,1:T(8,128)(2,1)S(1)} %copy.17), channel_id=1, source_target_pairs={{0,1},{1,0},{2,3},{3,2},{4,5},{5,4},{6,7},{7,6},{8,9},{9,8},{10,11... | collective-permute-start | bytes 3145736 | tf_op jit(solution)/shard_map/ppermute | solution.py:131
  216.4 16.2 %collective-permute-start.33 = (bf16[2176,128]{1,0:T(8,128)(2,1)S(1)}, bf16[2176,128]{1,0:T(8,128)(2,1)S(1)}, u32[]{:S(2)}, u32[]{:S(2)}) collective-permute-start(bf16[2176,128]{1,0:T(8,128)(2,1)S(1)} %collective-permute-done.32.refs_4_), channel_id=1, source_target_pairs={{8,0},{12,4},{16,8},{20,12},{9,1},{13,5},{17,9},{21,13},{10,2},{14... | collective-permute-start | bytes 1671176 | tf_op jit(solution)/shard_map/ppermute | solution.py:171
  232.7 15.3 %collective-permute-start.35 = (bf16[2176,128]{1,0:T(8,128)(2,1)S(1)}, bf16[2176,128]{1,0:T(8,128)(2,1)S(1)}, u32[]{:S(2)}, u32[]{:S(2)}) collective-permute-start(bf16[2176,128]{1,0:T(8,128)(2,1)S(1)} %collective-permute-done.33.refs_5_), channel_id=1, source_target_pairs={{8,0},{12,4},{9,1},{13,5},{10,2},{14,6},{11,3},{15,7}} | collective-permute-start | bytes 1671176 | tf_op jit(solution)/shard_map/ppermute | solution.py:171
  256.4 15.9 %collective-permute-start.39 = (bf16[512,1024]{1,0:T(8,128)(2,1)S(1)}, bf16[512,1024]{1,0:T(8,128)(2,1)}, u32[]{:S(2)}, u32[]{:S(2)}) collective-permute-start(bf16[512,1024]{1,0:T(8,128)(2,1)S(1)} %project_back.2), channel_id=1, source_target_pairs={{0,1},{1,0},{2,3},{3,2},{4,5},{5,4},{6,7},{7,6},{8,9},{9,8},{10,11... | collective-permute-start | bytes 3145736 | tf_op jit(solution)/shard_map/ppermute | solution.py:131
  258.8 33.5 %collective-permute-start.43 = (bf16[512,512]{1,0:T(8,128)(2,1)S(1)}, bf16[512,512]{1,0:T(8,128)(2,1)S(1)}, u32[]{:S(2)}, u32[]{:S(2)}) collective-permute-start(bf16[512,512]{1,0:T(8,128)(2,1)S(1)} %get-tuple-element.81), channel_id=1, source_target_pairs={{0,4},{4,0},{8,12},{12,8},{16,20},{20,16},{24,28},{28,24},{1,5},{5... | collective-permute-start | bytes 1572872 | tf_op jit(solution)/shard_map/ppermute | solution.py:131
  276.9 15.2 %collective-permute-start.41 = (bf16[128,1024]{1,0:T(8,128)(2,1)S(1)}, bf16[128,1024]{1,0:T(8,128)(2,1)S(1)}, u32[]{:S(2)}, u32[]{:S(2)}) collective-permute-start(bf16[128,1024]{1,0:T(8,128)(2,1)S(1)} %get-tuple-element.113), channel_id=1, source_target_pairs={{0,4},{4,0},{8,12},{12,8},{16,20},{20,16},{24,28},{28,24},{1,5},{5... | collective-permute-start | bytes 786440 | tf_op jit(solution)/shard_map/ppermute | solution.py:131
  280.8 26.5 %collective-permute-start.48 = (bf16[512,512]{1,0:T(8,128)(2,1)}, bf16[512,512]{1,0:T(8,128)(2,1)S(1)}, u32[]{:S(2)}, u32[]{:S(2)}) collective-permute-start(bf16[512,512]{1,0:T(8,128)(2,1)} %get-tuple-element.88), channel_id=1, source_target_pairs={{0,4},{4,0},{8,12},{12,8},{16,20},{20,16},{24,28},{28,24},{1,5},{5... | collective-permute-start | bytes 1572872 | tf_op jit(solution)/shard_map/ppermute | solution.py:131
  292.3 16.6 %collective-permute-start.47 = (bf16[128,1024]{1,0:T(8,128)(2,1)S(1)}, bf16[128,1024]{1,0:T(8,128)(2,1)S(1)}, u32[]{:S(2)}, u32[]{:S(2)}) collective-permute-start(bf16[128,1024]{1,0:T(8,128)(2,1)S(1)} %add_add_fusion), channel_id=1, source_target_pairs={{0,0},{8,1},{16,2},{24,3},{4,4},{12,5},{20,6},{28,7},{2,8},{10,9},... | collective-permute-start | bytes 786440 | tf_op jit(solution)/shard_map/ppermute | solution.py:146
  (45 other events, 549.2 us)

commit v6 on v5

--- a/solution.py
+++ b/solution.py
@@ -192,6 +192,15 @@
     return scatter_step(blocks, up, down, step)
 
 
+def around(value, by):
+    size = lax.axis_size("seq")
+    return lax.ppermute(value, "seq", [(i, (i + 2 * by) % size) for i in range(size)])
+
+
+def both_ways(before, behind):
+    return [[behind[k], before[-1 - k]] for k in range(len(before))]
+
+
 def next_block(block, by, step):
     length = lax.axis_size("seq") // 2
     if by > 0:
@@ -274,30 +283,32 @@
     return sums
 
 
-def own_sum(blocks, up, down, which, rows):
-    return (
-        blocks[0, which, rows, :].astype(f32)
-        + up[which, rows, :].astype(f32)
-        + down[which, rows, :].astype(f32)
-    ).astype(bf16)
-
-
-def forward_filter(order, blocks, up, down, spread_taps):
-    tokens = up.shape[1]
+def own_sum(blocks, received, which, rows):
+    total = blocks[0, which, rows, :].astype(f32)
+    for term in received:
+        total += term[which, rows, :].astype(f32)
+    return total
+
+
+def forward_filter(order, blocks, received, spread_taps):
+    tokens = blocks.shape[2]
+    count = len(received)
     taps = spread_taps.shape[0] // sublanes
     n_blocks = order.shape[0]
     size = tokens // n_blocks
     tiles = 8
 
-    def body(order_ref, blocks_ref, up_ref, down_ref, taps_ref, kv_ref, signal_ref, filtered_ref, moved):
+    def body(order_ref, blocks_ref, *refs):
+        terms = refs[:count]
+        taps_ref, kv_ref, signal_ref, filtered_ref, moved = refs[count:]
         for shift in range(sublanes):
             moved[shift, : taps + sublanes, :] = jnp.zeros((taps + sublanes, lanes), f32)
 
         def one_block(r, carry):
             rows = pl.ds(pl.multiple_of(r * size, size), size)
             place = block_rows(order_ref, r, size)
-            key_part = own_sum(blocks_ref, up_ref, down_ref, 0, rows)
-            value_part = own_sum(blocks_ref, up_ref, down_ref, 1, rows)
+            key_part = own_sum(blocks_ref, terms, 0, rows).astype(bf16)
+            value_part = own_sum(blocks_ref, terms, 1, rows).astype(bf16)
             kv_ref[0, place, :] = key_part
             kv_ref[1, place, :] = value_part
             product = (key_part.astype(f32) * value_part.astype(f32)).astype(bf16)
@@ -339,8 +350,7 @@
             grid=(1,),
             in_specs=[
                 whole((1, 2, tokens, lanes)),
-                whole((2, tokens, lanes)),
-                whole((2, tokens, lanes)),
+                *[whole((2, tokens, lanes))] * count,
                 whole(spread_taps.shape),
             ],
             out_specs=(
@@ -353,24 +363,24 @@
         compiler_params=params(),
         cost_estimate=cost(400 * tokens * lanes * taps, 12 * tokens * lanes),
         name="forward_filter",
-    )(order, blocks, up, down, spread_taps)
-
-
-def gate_rows(order, blocks, up, down, filtered):
-    tokens = up.shape[1]
+    )(order, blocks, *received, spread_taps)
+
+
+def gate_rows(order, blocks, received, filtered):
+    tokens = blocks.shape[2]
+    count = len(received)
     n_blocks = order.shape[0]
     size = tokens // n_blocks
 
-    def body(order_ref, blocks_ref, up_ref, down_ref, filtered_ref, out_ref, grad_ref):
+    def body(order_ref, blocks_ref, *refs):
+        terms = refs[:count]
+        filtered_ref, out_ref, grad_ref = refs[count:]
+
         def one_block(r, carry):
             rows = pl.ds(pl.multiple_of(r * size, size), size)
             place = block_rows(order_ref, r, size)
-            queries = own_sum(blocks_ref, up_ref, down_ref, 0, rows).astype(f32)
-            grad_gated = (
-                blocks_ref[0, 1, rows, :].astype(f32)
-                + up_ref[1, rows, :].astype(f32)
-                + down_ref[1, rows, :].astype(f32)
-            )
+            queries = own_sum(blocks_ref, terms, 0, rows).astype(bf16).astype(f32)
+            grad_gated = own_sum(blocks_ref, terms, 1, rows)
             kept = filtered_ref[place, :]
             out_ref[rows, :] = (queries * kept).astype(bf16)
             later = pl.ds(pl.multiple_of(tokens + r * size, size), size)
@@ -392,8 +402,7 @@
             grid=(1,),
             in_specs=[
                 whole((1, 2, tokens, lanes)),
-                whole((2, tokens, lanes)),
-                whole((2, tokens, lanes)),
+                *[whole((2, tokens, lanes))] * count,
                 whole((tokens, lanes)),
             ],
             out_specs=(whole((2 * tokens, lanes)), whole((tokens, lanes))),
@@ -401,7 +410,7 @@
         compiler_params=params(),
         cost_estimate=cost(20 * tokens * lanes, 20 * tokens * lanes),
         name="gate_rows",
-    )(order, blocks, up, down, filtered)
+    )(order, blocks, *received, filtered)
 
 
 def backward_filter(order, grad_filtered, key_values, signal, spread_taps):
@@ -498,21 +507,24 @@
     )(order, grad_filtered, key_values, signal, spread_taps)
 
 
-def merge_blocks(place, block, before, behind, tokens):
+def merge_blocks(place, block, others, tokens):
     matrices = block.shape[0] // tokens
-    length = len(before) + 1
+    length = len(others) + 1
+    sizes = [len(other) for other in others]
     rows = 256
     steps = tokens // rows
 
     def body(place_ref, *refs):
         out = refs[-1]
-        own, ups, downs = refs[0], refs[1:length], refs[length : 2 * length - 1]
+        own, rest = refs[0], list(refs[1:-1])
         line = place_ref[0]
         for offset in range(length):
             if offset == 0:
                 value = own[...]
             else:
-                value = downs[offset - 1][...] + ups[length - offset - 1][...]
+                value = rest.pop(0)[...]
+                for _ in range(sizes[offset - 1] - 1):
+                    value += rest.pop(0)[...]
             at = pl.multiple_of(lax.rem(line + offset, length) * lanes, lanes)
             out[0, :, pl.ds(at, lanes)] = value
 
@@ -523,28 +535,31 @@
         grid_spec=pltpu.PrefetchScalarGridSpec(
             num_scalar_prefetch=1,
             grid=(matrices, steps),
-            in_specs=[spec] * (2 * length - 1),
+            in_specs=[spec] * (1 + sum(sizes)),
             out_specs=pl.BlockSpec((1, rows, length * lanes), lambda which, g, place: (which, g, 0)),
         ),
         compiler_params=params(),
         cost_estimate=cost(tokens * lanes * 8, 2 * 2 * tokens * lanes * 11),
         name="merge_blocks",
-    )(place, block, *before, *behind)
-
-
-def merge_taps(place, block, before, behind, taps):
-    length = len(before) + 1
+    )(place, block, *[term for other in others for term in other])
+
+
+def merge_taps(place, block, others, taps):
+    length = len(others) + 1
+    sizes = [len(other) for other in others]
     last = block.shape[0] // taps - 1
 
     def body(place_ref, *refs):
         out = refs[-1]
-        own, ups, downs = refs[0], refs[1:length], refs[length : 2 * length - 1]
+        own, rest = refs[0], list(refs[1:-1])
         line = place_ref[0]
         for offset in range(length):
             if offset == 0:
                 value = own[...]
             else:
-                value = downs[offset - 1][...] + ups[length - offset - 1][...]
+                value = rest.pop(0)[...]
+                for _ in range(sizes[offset - 1] - 1):
+                    value += rest.pop(0)[...]
             at = pl.multiple_of(lax.rem(line + offset, length) * lanes, lanes)
             out[pl.ds(at, lanes), :] = jnp.transpose(value.astype(f32)).astype(bf16)
 
@@ -554,13 +569,13 @@
         grid_spec=pltpu.PrefetchScalarGridSpec(
             num_scalar_prefetch=1,
             grid=(1,),
-            in_specs=[pl.BlockSpec((taps, lanes), lambda g, place: (last, 0))] * (2 * length - 1),
+            in_specs=[pl.BlockSpec((taps, lanes), lambda g, place: (last, 0))] * (1 + sum(sizes)),
             out_specs=pl.BlockSpec((length * lanes, taps), lambda g, place: (0, 0)),
         ),
         compiler_params=params(),
         cost_estimate=cost(taps * lanes * 8, 2 * taps * lanes * 11),
         name="merge_taps",
-    )(place, block, *before, *behind)
+    )(place, block, *[term for other in others for term in other])
 
 
 def project_back(place, merged, in_weight, given, indices, part):
@@ -832,27 +847,18 @@
     qg_up, qg_down = scatter_start(qg_blocks)
     for step in (2, 3):
         qg_up, qg_down = scatter_next(qg_blocks, qg_up, qg_down, step)
-    key_values, signal, filtered = forward_filter(order, kv_blocks, kv_up, kv_down, spread_taps)
-    gated_rows, grad_filtered = gate_rows(order, qg_blocks, qg_up, qg_down, filtered)
-
-    gated_before = [next_block(gated_rows, 1, 1)]
-    gated_behind = [next_block(gated_rows, -1, 1)]
-    grad_filtered = after(grad_filtered, gated_before[0], gated_behind[0])
+    key_values, signal, filtered = forward_filter(order, kv_blocks, [kv_up, kv_down], spread_taps)
+    gated_rows, grad_filtered = gate_rows(order, qg_blocks, [qg_up, qg_down], filtered)
+
+    gated_others = [[around(gated_rows, -k)] for k in range(1, 4)]
     kv_grads = backward_filter(order, grad_filtered, key_values, signal, spread_taps)
-    gated_before.append(next_block(gated_before[0], 1, 2))
-    gated_behind.append(next_block(gated_behind[0], -1, 2))
-    kv_grads, gated_before[1], gated_behind[1] = lax.optimization_barrier(
-        (kv_grads, gated_before[1], gated_behind[1])
-    )
-    gated_before.append(next_block(gated_before[1], 1, 3))
-    gated_behind.append(next_block(gated_behind[1], -1, 3))
     kv_before = [next_block(kv_grads, 1, 1)]
     kv_behind = [next_block(kv_grads, -1, 1)]
     kv_before.append(next_block(kv_before[0], 1, 2))
     kv_behind.append(next_block(kv_behind[0], -1, 2))
 
     total_in = in_weight.shape[0]
-    first = merge_blocks(place, gated_rows, gated_before, gated_behind, count)
+    first = merge_blocks(place, gated_rows, gated_others, count)
     out_kept, out_sent = out_gradient(place, first, g_near, g_far)
     out_given = flip(out_sent, "seq", 1)
     in_kept, q_sent = in_gradient(place, x_near, x_far, first, 1, 0, total_in, None)
@@ -869,7 +875,7 @@
     kv_behind[2], kv_before[2], mixed_part, q_given = lax.optimization_barrier(
         (kv_behind[2], kv_before[2], mixed_part, q_given)
     )
-    second = merge_blocks(place, kv_grads, kv_before, kv_behind, count)
+    second = merge_blocks(place, kv_grads, both_ways(kv_before, kv_behind), count)
     in_kept, k_sent = in_gradient(place, x_near, x_far, second, 0, 1, total_in, in_kept)
     k_given = flip(k_sent, "seq", 1)
 
@@ -892,7 +898,7 @@
     total = parts[0].astype(f32) + flip(parts[1], "fsdp", 2).astype(f32)
     total += flip(parts[2], "seq", 1).astype(f32) + flip_both(parts[3]).astype(f32)
     in_kept, v_sent = in_gradient(place, x_near, x_far, after(second, parts), 1, 2, total_in, in_kept)
-    half_taps = merge_taps(place, kv_grads, kv_before, kv_behind, taps)
+    half_taps = merge_taps(place, kv_grads, both_ways(kv_before, kv_behind), taps)
     total, k_given, mixed_out = lax.optimization_barrier((total, k_given, mixed_out))
     v_given = flip(v_sent, "seq", 1)
     given_taps = flip(after(half_taps, v_sent), "seq", 1)

time: 312 us -> 309 us (level)
  starting transfers between devices: 101 us -> 88.8 us
  waiting for transfers between devices: 122 us -> 129 us
  Pallas kernels: 68 us -> 71.2 us
    ppermute x24 -> x18, starting transfers between devices: 60.6 us -> 42.6 us  [along_line(): return lax.ppermute(value, 'seq', pairs)]
    ppermute x0 -> x3, waiting for transfers between devices: none -> 13.7 us  [around(): lax.ppermute(value, 'seq', [(i, (i + 2 * by) % size) for i in range(size)])]
    ppermute x24 -> x18, waiting for transfers between devices: 41.6 us -> 34.7 us  [along_line(): return lax.ppermute(value, 'seq', pairs)]
    ppermute x0 -> x3, starting transfers between devices: none -> 5.89 us  [around(): lax.ppermute(value, 'seq', [(i, (i + 2 * by) % size) for i in range(size)])]
  transfers between devices with their start and end apart: 50 -> 47, of which waited for: 23 -> 22; matrix products, arithmetic and copies ran while one was open for 3% -> 3% of each run, Pallas kernels for 17% -> 18%
where the time goes in v6:
time: 309 us; the launch traced here: 308 us
  waiting for transfers between devices  129 us (42%)
  starting transfers between devices  88.8 us (29%)
  Pallas kernels  71.2 us (23%)
  local copies, waits for them, and re-layouts  9.26 us (3%)
  other arithmetic  8.1 us (3%)
    ppermute x19, waiting for transfers between devices, flip(): lax.ppermute(value, axis, [(i, i ^ bit) for i in range(lax.axis_size(axis...  70.2 us
    ppermute x18, starting transfers between devices, along_line(): return lax.ppermute(value, 'seq', pairs)  42.6 us
    ppermute x18, waiting for transfers between devices, along_line(): return lax.ppermute(value, 'seq', pairs)  34.7 us
    ppermute x3, starting transfers between devices, flip_both(): return lax.ppermute(value, ('seq', 'fsdp'), pairs)  21 us
    ppermute x19, starting transfers between devices, flip(): lax.ppermute(value, axis, [(i, i ^ bit) for i in range(lax.axis_size(axis...  16.6 us
    pallas_call x1, Pallas kernels, backward_filter(): pl.pallas_call(body, out_shape=jax.ShapeDtypeStruct((2 * tokens + taps, l...  15.2 us
    ppermute x3, waiting for transfers between devices, around(): lax.ppermute(value, 'seq', [(i, (i + 2 * by) % size) for i in range(size)])  13.7 us
    pallas_call x2, Pallas kernels, project_pair(): pl.pallas_call(body, out_shape=jax.ShapeDtypeStruct((count, 2, tokens, la...  11.8 us
  transfers between devices with their start and end apart: 47, of which 22 were waited for; matrix products, arithmetic and copies ran while one was open for 3% of the time, Pallas kernels for 18%

profile of v6, /device:TPU:0, one launch (start us, length us, event | category | flops | bytes accessed | tf_op | source)
XLA Modules:
  0.0 307.8 jit_solution(16111374370334908803)
XLA Ops:
  2.7 3.0 collective-permute-start.4
  7.1 18.2 %collective-permute-start.3 = (bf16[128,1024]{1,0:T(8,128)(2,1)S(1)}, bf16[128,1024]{1,0:T(8,128)(2,1)S(1)}, u32[]{:S(2)}, u32[]{:S(2)}) collective-permute-start(bf16[128,1024]{1,0:T(8,128)(2,1)S(1)} %collective-permute-done), channel_id=1, source_target_pairs={{0,6},{1,7},{2,4},{3,5},{4,2},{5,3},{6,0},{7,1},{8,14},{9,15},{10,... | collective-permute-start | bytes 786440 | tf_op jit(solution)/shard_map/ppermute | solution.py:156
  27.6 6.4 %collective-permute-done.3 = bf16[128,1024]{1,0:T(8,128)(2,1)S(1)} collective-permute-done((bf16[128,1024]{1,0:T(8,128)(2,1)S(1)}, bf16[128,1024]{1,0:T(8,128)(2,1)S(1)}, u32[]{:S(2)}, u32[]{:S(2)}) %collective-permute-start.3) | collective-permute-done | bytes 262176 | tf_op jit(solution)/shard_map/ppermute | solution.py:156
  34.0 6.1 %collective-permute-done.2 = bf16[128,1024]{1,0:T(8,128)(2,1)S(1)} collective-permute-done((bf16[128,1024]{1,0:T(8,128)(2,1)S(1)}, bf16[128,1024]{1,0:T(8,128)(2,1)S(1)}, u32[]{:S(2)}, u32[]{:S(2)}) %collective-permute-start.2) | collective-permute-done | bytes 262176 | tf_op jit(solution)/shard_map/ppermute | solution.py:131
  46.0 5.6 %project_pair.2.blocks_ref = bf16[4,2,1024,128]{3,2,1,0:T(8,128)(2,1)S(1)} custom-call(s32[2]{0:T(128)S(1)} %pad_add_fusion.place_ref, bf16[2,2,128,1024]{3,2,1,0:T(8,128)(2,1)S(1)} %bitcast.64, bf16[2,2,128,1024]{3,2,1,0:T(8,128)(2,1)S(1)} %collective-permute-done.6.refs_1_.refs_3_.refs_7_.refs_9_.own_far.other_far, bf16[2,2,128,1024]{3,2,1,0:T(8,128)(2,1)S(1)} %bitcast.65, ...), custom_call_target="tpu_custom_call" | custom-call | flops 2147483648 | bytes 8388608 | tf_op jit(solution)/shard_map/project_pair/pallas_call | solution.py:253
  52.4 5.6 %collective-permute-start.7 = (bf16[2,1024,128]{2,1,0:T(8,128)(2,1)S(1)}, bf16[2,1024,128]{2,1,0:T(8,128)(2,1)S(1)}, u32[]{:S(2)}, u32[]{:S(2)}) collective-permute-start(bf16[2,1024,128]{2,1,0:T(8,128)(2,1)S(1)} %get-tuple-element.102), channel_id=1, source_target_pairs={{0,8},{4,12},{1,9},{5,13},{2,10},{6,14},{3,11},{7,15}} | collective-permute-start | bytes 1572872 | tf_op jit(solution)/shard_map/ppermute | solution.py:171
  59.5 18.8 %collective-permute-done.11 = bf16[128,1024]{1,0:T(8,128)(2,1)S(1)} collective-permute-done((bf16[128,1024]{1,0:T(8,128)(2,1)S(1)}, bf16[128,1024]{1,0:T(8,128)(2,1)S(1)}, u32[]{:S(2)}, u32[]{:S(2)}) %collective-permute-start.11) | collective-permute-done | bytes 262176 | tf_op jit(solution)/shard_map/ppermute | solution.py:131
  81.2 6.2 %project_pair.3.blocks_ref = bf16[4,2,1024,128]{3,2,1,0:T(8,128)(2,1)} custom-call(s32[2]{0:T(128)S(1)} %pad_add_fusion.place_ref, bf16[2,2,128,1024]{3,2,1,0:T(8,128)(2,1)S(1)} %bitcast.68, bf16[2,2,128,1024]{3,2,1,0:T(8,128)(2,1)S(1)} %collective-permute-done.6.refs_1_.refs_3_.refs_7_.refs_9_.own_far.other_far, bf16[2,2,128,1024]{3,2,1,0:T(8,128)(2,1)S(1)} %bitcast.69, ...), custom_call_target="tpu_custom_call" | custom-call | flops 2147483648 | bytes 8388608 | tf_op jit(solution)/shard_map/project_pair/pallas_call | solution.py:253
  91.1 5.7 %collective-permute-start.14 = (bf16[2,1024,128]{2,1,0:T(8,128)(2,1)}, bf16[2,1024,128]{2,1,0:T(8,128)(2,1)}, u32[]{:S(2)}, u32[]{:S(2)}) collective-permute-start(bf16[2,1024,128]{2,1,0:T(8,128)(2,1)} %get-tuple-element.100), channel_id=1, source_target_pairs={{0,8},{4,12},{1,9},{5,13},{2,10},{6,14},{3,11},{7,15}} | collective-permute-start | bytes 1572872 | tf_op jit(solution)/shard_map/ppermute | solution.py:171
  101.6 7.0 %collective-permute-done.14 = bf16[2,1024,128]{2,1,0:T(8,128)(2,1)} collective-permute-done((bf16[2,1024,128]{2,1,0:T(8,128)(2,1)}, bf16[2,1024,128]{2,1,0:T(8,128)(2,1)}, u32[]{:S(2)}, u32[]{:S(2)}) %collective-permute-start.14) | collective-permute-done | bytes 524320 | tf_op jit(solution)/shard_map/ppermute | solution.py:171
  111.0 5.0 %collective-permute-start.15 = (bf16[2,1024,128]{2,1,0:T(8,128)(2,1)S(1)}, bf16[2,1024,128]{2,1,0:T(8,128)(2,1)S(1)}, u32[]{:S(2)}, u32[]{:S(2)}) collective-permute-start(bf16[2,1024,128]{2,1,0:T(8,128)(2,1)S(1)} %get-tuple-element.98), channel_id=1, source_target_pairs={{0,8},{4,12},{8,16},{12,20},{1,9},{5,13},{9,17},{13,21},{2,10},{6,... | collective-permute-start | bytes 1572872 | tf_op jit(solution)/shard_map/ppermute | solution.py:171
  116.1 3.7 %collective-permute-done.20 = bf16[2,1024,128]{2,1,0:T(8,128)(2,1)} collective-permute-done((bf16[2,1024,128]{2,1,0:T(8,128)(2,1)S(1)}, bf16[2,1024,128]{2,1,0:T(8,128)(2,1)}, u32[]{:S(2)}, u32[]{:S(2)}) %collective-permute-start.20) | collective-permute-done | bytes 524320 | tf_op jit(solution)/shard_map/ppermute | solution.py:171
  122.6 5.2 %collective-permute-start.21 = (bf16[2,1024,128]{2,1,0:T(8,128)(2,1)S(1)}, bf16[2,1024,128]{2,1,0:T(8,128)(2,1)S(1)}, u32[]{:S(2)}, u32[]{:S(2)}) collective-permute-start(bf16[2,1024,128]{2,1,0:T(8,128)(2,1)S(1)} %get-tuple-element.92), channel_id=1, source_target_pairs={{0,8},{4,12},{8,16},{12,20},{16,24},{20,28},{1,9},{5,13},{9,17},{1... | collective-permute-start | bytes 1572872 | tf_op jit(solution)/shard_map/ppermute | solution.py:171
  127.8 3.2 %collective-permute-done.15 = bf16[2,1024,128]{2,1,0:T(8,128)(2,1)S(1)} collective-permute-done((bf16[2,1024,128]{2,1,0:T(8,128)(2,1)S(1)}, bf16[2,1024,128]{2,1,0:T(8,128)(2,1)S(1)}, u32[]{:S(2)}, u32[]{:S(2)}) %collective-permute-start.15) | collective-permute-done | bytes 524320 | tf_op jit(solution)/shard_map/ppermute | solution.py:171
  132.5 5.0 %collective-permute-start.16 = (bf16[2,1024,128]{2,1,0:T(8,128)(2,1)S(1)}, bf16[2,1024,128]{2,1,0:T(8,128)(2,1)S(1)}, u32[]{:S(2)}, u32[]{:S(2)}) collective-permute-start(bf16[2,1024,128]{2,1,0:T(8,128)(2,1)S(1)} %get-tuple-element.96), channel_id=1, source_target_pairs={{0,8},{4,12},{8,16},{12,20},{16,24},{20,28},{1,9},{5,13},{9,17},{1... | collective-permute-start | bytes 1572872 | tf_op jit(solution)/shard_map/ppermute | solution.py:171
  137.7 4.5 %collective-permute-done.21.refs_0_ = bf16[2,1024,128]{2,1,0:T(8,128)(2,1)S(1)} collective-permute-done((bf16[2,1024,128]{2,1,0:T(8,128)(2,1)S(1)}, bf16[2,1024,128]{2,1,0:T(8,128)(2,1)S(1)}, u32[]{:S(2)}, u32[]{:S(2)}) %collective-permute-start.21) | collective-permute-done | bytes 524320 | tf_op jit(solution)/shard_map/ppermute | solution.py:171
  142.2 9.9 %forward_filter.1 = (bf16[2,1024,128]{2,1,0:T(8,128)(2,1)S(1)}, bf16[1024,128]{1,0:T(8,128)(2,1)S(1)}, f32[1024,128]{1,0:T(8,128)S(1)}) custom-call(s32[8]{0:T(128)S(1)} %fusion.14.order_ref, bf16[4,2,1024,128]{3,2,1,0:T(8,128)(2,1)S(1)} %copy-done.17, bf16[2,1024,128]{2,1,0:T(8,128)(2,1)S(1)} %collective-permute-done.21.refs_0_, ...), custom_call_target="tpu_custom_call" | custom-call | flops 6710886400 | bytes 1572864 | tf_op jit(solution)/shard_map/forward_filter/pallas_call | solution.py:341
  159.4 15.2 %backward_filter.1.refs_0_ = bf16[2176,128]{1,0:T(8,128)(2,1)S(1)} custom-call(s32[8]{0:T(128)S(1)} %fusion.14.order_ref, bf16[1024,128]{1,0:T(8,128)(2,1)S(1)} %get-tuple-element.59.grad_ref, bf16[2,1024,128]{2,1,0:T(8,128)(2,1)S(1)} %get-tuple-element.60.kv_ref, bf16[1024,128]{1,0:T(8,128)(2,1)S(1)} %get-tuple-element.61.signal_ref, ...), custom_call_target="tpu_custom_call" | custom-call | flops 13421772800 | bytes 1572864 | tf_op jit(solution)/shard_map/backward_filter/pallas_call | solution.py:484
  177.4 13.7 %collective-permute-done.25.refs_2_ = bf16[2048,128]{1,0:T(8,128)(2,1)S(1)} collective-permute-done((bf16[2048,128]{1,0:T(8,128)(2,1)S(1)}, bf16[2048,128]{1,0:T(8,128)(2,1)S(1)}, u32[]{:S(2)}, u32[]{:S(2)}) %collective-permute-start.25) | collective-permute-done | bytes 524320 | tf_op jit(solution)/shard_map/ppermute | solution.py:197
  195.1 3.8 %project_out.1 = bf16[1024,1024]{1,0:T(8,128)(2,1)S(1)} custom-call(s32[2]{0:T(128)S(1)} %pad_add_fusion.place_ref, bf16[2,1024,512]{2,1,0:T(8,128)(2,1)} %copy-done.4, bf16[1024,512]{1,0:T(8,128)(2,1)S(1)} %copy-done.19, bf16[2,512,512]{2,1,0:T(8,128)(2,1)S(1)} %copy-done.10), custom_call_target="tpu_custom_call" | custom-call | flops 1073741824 | bytes 4194304 | tf_op jit(solution)/shard_map/project_out/pallas_call | solution.py:636
  205.1 3.0 in_gradient.3
  208.0 10.3 %collective-permute-done.31.piece_ref = bf16[512,512]{1,0:T(8,128)(2,1)S(1)} collective-permute-done((bf16[512,512]{1,0:T(8,128)(2,1)S(1)}, bf16[512,512]{1,0:T(8,128)(2,1)S(1)}, u32[]{:S(2)}, u32[]{:S(2)}) %collective-permute-start.31) | collective-permute-done | bytes 524320 | tf_op jit(solution)/shard_map/ppermute | solution.py:131
  218.3 12.3 %collective-permute-done.30.refs_3_ = bf16[2176,128]{1,0:T(8,128)(2,1)S(1)} collective-permute-done((bf16[2176,128]{1,0:T(8,128)(2,1)S(1)}, bf16[2176,128]{1,0:T(8,128)(2,1)S(1)}, u32[]{:S(2)}, u32[]{:S(2)}) %collective-permute-start.30) | collective-permute-done | bytes 557088 | tf_op jit(solution)/shard_map/ppermute | solution.py:171
  233.9 10.1 %collective-permute-done.35.piece_ref = bf16[512,512]{1,0:T(8,128)(2,1)S(1)} collective-permute-done((bf16[512,512]{1,0:T(8,128)(2,1)S(1)}, bf16[512,512]{1,0:T(8,128)(2,1)S(1)}, u32[]{:S(2)}, u32[]{:S(2)}) %collective-permute-start.35) | collective-permute-done | bytes 524320 | tf_op jit(solution)/shard_map/ppermute | solution.py:131
  245.7 3.0 in_gradient.4
  248.7 4.2 %project_back.2 = bf16[512,1024]{1,0:T(8,128)(2,1)S(1)} custom-call(s32[2]{0:T(128)S(1)} %pad_add_fusion.place_ref, bf16[2,1024,512]{2,1,0:T(8,128)(2,1)S(1)} %copy-done.5, bf16[3,512,1024]{2,1,0:T(8,128)(2,1)} %refs_7_.3, bf16[2,512,512]{2,1,0:T(8,128)(2,1)S(1)} %copy-done.10, bf16[2,1024,512]{2,1,0:T(8,128)(2,1)} %copy-done.2, ...), custom_call_target="tpu_custom_call" | custom-call | flops 1610612736 | bytes 2097152 | tf_op jit(solution)/shard_map/project_back/pallas_call | solution.py:609
  256.5 4.2 %project_back.3 = bf16[512,1024]{1,0:T(8,128)(2,1)S(1)} custom-call(s32[2]{0:T(128)S(1)} %pad_add_fusion.place_ref, bf16[2,1024,512]{2,1,0:T(8,128)(2,1)S(1)} %copy-done.5, bf16[3,512,1024]{2,1,0:T(8,128)(2,1)} %refs_7_.3, bf16[2,512,512]{2,1,0:T(8,128)(2,1)S(1)} %copy-done.10, bf16[2,1024,512]{2,1,0:T(8,128)(2,1)} %copy-done.2, ...), custom_call_target="tpu_custom_call" | custom-call | flops 1610612736 | bytes 2097152 | tf_op jit(solution)/shard_map/project_back/pallas_call | solution.py:609
  260.7 7.9 %collective-permute-done.41 = bf16[2,128,1024]{2,1,0:T(8,128)(2,1)S(1)} collective-permute-done((bf16[2,128,1024]{2,1,0:T(8,128)(2,1)}, bf16[2,128,1024]{2,1,0:T(8,128)(2,1)S(1)}, u32[]{:S(2)}, u32[]{:S(2)}) %collective-permute-start.41) | collective-permute-done | bytes 524320 | tf_op jit(solution)/shard_map/ppermute | solution.py:131
  273.6 3.1 %in_gradient.5 = (f32[3,512,1024]{2,1,0:T(8,128)}, bf16[512,512]{1,0:T(8,128)(2,1)}) custom-call(s32[2]{0:T(128)S(1)} %pad_add_fusion.place_ref, bf16[2,2,128,1024]{3,2,1,0:T(8,128)(2,1)S(1)} %bitcast.74, bf16[2,2,128,1024]{3,2,1,0:T(8,128)(2,1)S(1)} %collective-permute-done.6.refs_1_.refs_3_.refs_7_.refs_9_.own_far.other_far, ...), custom_call_target="tpu_custom_call", output_to_operand_aliasing={{0}: (6, {})} | custom-call | flops 1073741824 | bytes 4194304 | tf_op jit(solution)/shard_map/in_gradient/pallas_call | solution.py:676
  280.5 4.0 %collective-permute-done.39 = bf16[128,1024]{1,0:T(8,128)(2,1)S(1)} collective-permute-done((bf16[128,1024]{1,0:T(8,128)(2,1)S(1)}, bf16[128,1024]{1,0:T(8,128)(2,1)S(1)}, u32[]{:S(2)}, u32[]{:S(2)}) %collective-permute-start.39) | collective-permute-done | bytes 262176 | tf_op jit(solution)/shard_map/ppermute | solution.py:156
  284.5 4.8 %collective-permute-done.38 = bf16[128,1024]{1,0:T(8,128)(2,1)S(1)} collective-permute-done((bf16[128,1024]{1,0:T(8,128)(2,1)S(1)}, bf16[128,1024]{1,0:T(8,128)(2,1)S(1)}, u32[]{:S(2)}, u32[]{:S(2)}) %collective-permute-start.38) | collective-permute-done | bytes 262176 | tf_op jit(solution)/shard_map/ppermute | solution.py:131
  294.8 7.5 %collective-permute-done.46 = bf16[512,128]{1,0:T(8,128)(2,1)S(1)} collective-permute-done((bf16[512,128]{1,0:T(8,128)(2,1)S(1)}, bf16[512,128]{1,0:T(8,128)(2,1)S(1)}, u32[]{:S(2)}, u32[]{:S(2)}) %collective-permute-start.46) | collective-permute-done | bytes 131104 | tf_op jit(solution)/shard_map/ppermute | solution.py:131
  (167 shorter events, 80.2 us)
Async XLA Ops:
  2.7 37.6 %collective-permute-start.4 = (bf16[2,512,512]{2,1,0:T(8,128)(2,1)S(1)}, bf16[2,512,512]{2,1,0:T(8,128)(2,1)S(1)}, u32[]{:S(2)}, u32[]{:S(2)}) collective-permute-start(bf16[2,512,512]{2,1,0:T(8,128)(2,1)S(1)} %pad_maximum_fusion.1), channel_id=1, source_target_pairs={{0,4},{4,0},{8,12},{12,8},{16,20},{20,16},{24,28},{28,24},{1,5},{5... | collective-permute-start | bytes 3145736 | tf_op jit(solution)/shard_map/ppermute | solution.py:131
  6.4 33.8 %collective-permute-start.5 = (bf16[128,1024]{1,0:T(8,128)(2,1)S(1)}, bf16[128,1024]{1,0:T(8,128)(2,1)S(1)}, u32[]{:S(2)}, u32[]{:S(2)}) collective-permute-start(bf16[128,1024]{1,0:T(8,128)(2,1)S(1)} %copy-done.25), channel_id=1, source_target_pairs={{0,0},{1,8},{2,16},{3,24},{4,4},{5,12},{6,20},{7,28},{8,2},{9,10},... | collective-permute-start | bytes 786440 | tf_op jit(solution)/shard_map/ppermute | solution.py:146
  7.1 26.9 %collective-permute-start.3 = (bf16[128,1024]{1,0:T(8,128)(2,1)S(1)}, bf16[128,1024]{1,0:T(8,128)(2,1)S(1)}, u32[]{:S(2)}, u32[]{:S(2)}) collective-permute-start(bf16[128,1024]{1,0:T(8,128)(2,1)S(1)} %collective-permute-done), channel_id=1, source_target_pairs={{0,6},{1,7},{2,4},{3,5},{4,2},{5,3},{6,0},{7,1},{8,14},{9,15},{10,... | collective-permute-start | bytes 786440 | tf_op jit(solution)/shard_map/ppermute | solution.py:156
  41.3 37.2 %collective-permute-start.9 = (bf16[2,512,512]{2,1,0:T(8,128)(2,1)}, bf16[2,512,512]{2,1,0:T(8,128)(2,1)S(1)}, u32[]{:S(2)}, u32[]{:S(2)}) collective-permute-start(bf16[2,512,512]{2,1,0:T(8,128)(2,1)} %pad_maximum_fusion.2), channel_id=1, source_target_pairs={{0,4},{4,0},{8,12},{12,8},{16,20},{20,16},{24,28},{28,24},{1,5},{5... | collective-permute-start | bytes 3145736 | tf_op jit(solution)/shard_map/ppermute | solution.py:131
  43.1 15.7 %collective-permute-start.12 = (bf16[128,1024]{1,0:T(8,128)(2,1)S(1)}, bf16[128,1024]{1,0:T(8,128)(2,1)S(1)}, u32[]{:S(2)}, u32[]{:S(2)}) collective-permute-start(bf16[128,1024]{1,0:T(8,128)(2,1)S(1)} %collective-permute-done.5), channel_id=1, source_target_pairs={{0,6},{1,7},{2,4},{3,5},{4,2},{5,3},{6,0},{7,1},{8,14},{9,15},{10,... | collective-permute-start | bytes 786440 | tf_op jit(solution)/shard_map/ppermute | solution.py:156
  51.7 26.7 %collective-permute-start.8 = (bf16[2,1024,128]{2,1,0:T(8,128)(2,1)S(1)}, bf16[2,1024,128]{2,1,0:T(8,128)(2,1)S(1)}, u32[]{:S(2)}, u32[]{:S(2)}) collective-permute-start(bf16[2,1024,128]{2,1,0:T(8,128)(2,1)S(1)} %get-tuple-element.101), channel_id=1, source_target_pairs={{24,16},{28,20},{25,17},{29,21},{26,18},{30,22},{27,19},{31,23}} | collective-permute-start | bytes 1572872 | tf_op jit(solution)/shard_map/ppermute | solution.py:171
  52.4 26.0 %collective-permute-start.7 = (bf16[2,1024,128]{2,1,0:T(8,128)(2,1)S(1)}, bf16[2,1024,128]{2,1,0:T(8,128)(2,1)S(1)}, u32[]{:S(2)}, u32[]{:S(2)}) collective-permute-start(bf16[2,1024,128]{2,1,0:T(8,128)(2,1)S(1)} %get-tuple-element.102), channel_id=1, source_target_pairs={{0,8},{4,12},{1,9},{5,13},{2,10},{6,14},{3,11},{7,15}} | collective-permute-start | bytes 1572872 | tf_op jit(solution)/shard_map/ppermute | solution.py:171
  58.1 20.2 %collective-permute-start.11 = (bf16[128,1024]{1,0:T(8,128)(2,1)S(1)}, bf16[128,1024]{1,0:T(8,128)(2,1)S(1)}, u32[]{:S(2)}, u32[]{:S(2)}) collective-permute-start(bf16[128,1024]{1,0:T(8,128)(2,1)S(1)} %collective-permute-done.5), channel_id=1, source_target_pairs={{0,4},{4,0},{8,12},{12,8},{16,20},{20,16},{24,28},{28,24},{1,5},{5... | collective-permute-start | bytes 786440 | tf_op jit(solution)/shard_map/ppermute | solution.py:131
  58.8 19.5 %collective-permute-start.10 = (bf16[128,1024]{1,0:T(8,128)(2,1)S(1)}, bf16[128,1024]{1,0:T(8,128)(2,1)S(1)}, u32[]{:S(2)}, u32[]{:S(2)}) collective-permute-start(bf16[128,1024]{1,0:T(8,128)(2,1)S(1)} %collective-permute-done.5), channel_id=1, source_target_pairs={{0,2},{1,3},{2,0},{3,1},{4,6},{5,7},{6,4},{7,5},{8,10},{9,11},{10,... | collective-permute-start | bytes 786440 | tf_op jit(solution)/shard_map/ppermute | solution.py:131
  91.1 17.5 %collective-permute-start.14 = (bf16[2,1024,128]{2,1,0:T(8,128)(2,1)}, bf16[2,1024,128]{2,1,0:T(8,128)(2,1)}, u32[]{:S(2)}, u32[]{:S(2)}) collective-permute-start(bf16[2,1024,128]{2,1,0:T(8,128)(2,1)} %get-tuple-element.100), channel_id=1, source_target_pairs={{0,8},{4,12},{1,9},{5,13},{2,10},{6,14},{3,11},{7,15}} | collective-permute-start | bytes 1572872 | tf_op jit(solution)/shard_map/ppermute | solution.py:171
  97.9 18.2 %collective-permute-start.22 = (bf16[2,1024,128]{2,1,0:T(8,128)(2,1)}, bf16[2,1024,128]{2,1,0:T(8,128)(2,1)}, u32[]{:S(2)}, u32[]{:S(2)}) collective-permute-start(bf16[2,1024,128]{2,1,0:T(8,128)(2,1)} %get-tuple-element.93), channel_id=1, source_target_pairs={{16,8},{20,12},{24,16},{28,20},{17,9},{21,13},{25,17},{29,21},{18,... | collective-permute-start | bytes 1572872 | tf_op jit(solution)/shard_map/ppermute | solution.py:171
  99.3 20.4 %collective-permute-start.20 = (bf16[2,1024,128]{2,1,0:T(8,128)(2,1)S(1)}, bf16[2,1024,128]{2,1,0:T(8,128)(2,1)}, u32[]{:S(2)}, u32[]{:S(2)}) collective-permute-start(bf16[2,1024,128]{2,1,0:T(8,128)(2,1)S(1)} %get-tuple-element.94), channel_id=1, source_target_pairs={{0,8},{4,12},{8,16},{12,20},{1,9},{5,13},{9,17},{13,21},{2,10},{6,... | collective-permute-start | bytes 1572872 | tf_op jit(solution)/shard_map/ppermute | solution.py:171
  110.2 17.6 %collective-permute-start.18 = (bf16[2,1024,128]{2,1,0:T(8,128)(2,1)S(1)}, bf16[2,1024,128]{2,1,0:T(8,128)(2,1)S(1)}, u32[]{:S(2)}, u32[]{:S(2)}) collective-permute-start(bf16[2,1024,128]{2,1,0:T(8,128)(2,1)S(1)} %get-tuple-element.97), channel_id=1, source_target_pairs={{16,8},{20,12},{24,16},{28,20},{17,9},{21,13},{25,17},{29,21},{18,... | collective-permute-start | bytes 1572872 | tf_op jit(solution)/shard_map/ppermute | solution.py:171
  111.0 19.9 %collective-permute-start.15 = (bf16[2,1024,128]{2,1,0:T(8,128)(2,1)S(1)}, bf16[2,1024,128]{2,1,0:T(8,128)(2,1)S(1)}, u32[]{:S(2)}, u32[]{:S(2)}) collective-permute-start(bf16[2,1024,128]{2,1,0:T(8,128)(2,1)S(1)} %get-tuple-element.98), channel_id=1, source_target_pairs={{0,8},{4,12},{8,16},{12,20},{1,9},{5,13},{9,17},{13,21},{2,10},{6,... | collective-permute-start | bytes 1572872 | tf_op jit(solution)/shard_map/ppermute | solution.py:171
  121.3 16.4 %collective-permute-start.23 = (bf16[2,1024,128]{2,1,0:T(8,128)(2,1)S(1)}, bf16[2,1024,128]{2,1,0:T(8,128)(2,1)S(1)}, u32[]{:S(2)}, u32[]{:S(2)}) collective-permute-start(bf16[2,1024,128]{2,1,0:T(8,128)(2,1)S(1)} %get-tuple-element.91), channel_id=1, source_target_pairs={{8,0},{12,4},{16,8},{20,12},{24,16},{28,20},{9,1},{13,5},{17,9},{2... | collective-permute-start | bytes 1572872 | tf_op jit(solution)/shard_map/ppermute | solution.py:171
  122.6 19.6 %collective-permute-start.21 = (bf16[2,1024,128]{2,1,0:T(8,128)(2,1)S(1)}, bf16[2,1024,128]{2,1,0:T(8,128)(2,1)S(1)}, u32[]{:S(2)}, u32[]{:S(2)}) collective-permute-start(bf16[2,1024,128]{2,1,0:T(8,128)(2,1)S(1)} %get-tuple-element.92), channel_id=1, source_target_pairs={{0,8},{4,12},{8,16},{12,20},{16,24},{20,28},{1,9},{5,13},{9,17},{1... | collective-permute-start | bytes 1572872 | tf_op jit(solution)/shard_map/ppermute | solution.py:171
  131.2 20.8 %collective-permute-start.19 = (bf16[2,1024,128]{2,1,0:T(8,128)(2,1)S(1)}, bf16[2,1024,128]{2,1,0:T(8,128)(2,1)S(1)}, u32[]{:S(2)}, u32[]{:S(2)}) collective-permute-start(bf16[2,1024,128]{2,1,0:T(8,128)(2,1)S(1)} %get-tuple-element.95), channel_id=1, source_target_pairs={{8,0},{12,4},{16,8},{20,12},{24,16},{28,20},{9,1},{13,5},{17,9},{2... | collective-permute-start | bytes 1572872 | tf_op jit(solution)/shard_map/ppermute | solution.py:171
  132.5 20.1 %collective-permute-start.16 = (bf16[2,1024,128]{2,1,0:T(8,128)(2,1)S(1)}, bf16[2,1024,128]{2,1,0:T(8,128)(2,1)S(1)}, u32[]{:S(2)}, u32[]{:S(2)}) collective-permute-start(bf16[2,1024,128]{2,1,0:T(8,128)(2,1)S(1)} %get-tuple-element.96), channel_id=1, source_target_pairs={{0,8},{4,12},{8,16},{12,20},{16,24},{20,28},{1,9},{5,13},{9,17},{1... | collective-permute-start | bytes 1572872 | tf_op jit(solution)/shard_map/ppermute | solution.py:171
  153.5 23.9 %collective-permute-start.26 = (bf16[2048,128]{1,0:T(8,128)(2,1)S(1)}, bf16[2048,128]{1,0:T(8,128)(2,1)S(1)}, u32[]{:S(2)}, u32[]{:S(2)}) collective-permute-start(bf16[2048,128]{1,0:T(8,128)(2,1)S(1)} %get-tuple-element.58.refs_0_), channel_id=1, source_target_pairs={{0,8},{4,12},{8,16},{12,20},{16,24},{20,28},{24,0},{28,4},{1,9},{5... | collective-permute-start | bytes 1572872 | tf_op jit(solution)/shard_map/ppermute | solution.py:197
  156.0 35.1 %collective-permute-start.25 = (bf16[2048,128]{1,0:T(8,128)(2,1)S(1)}, bf16[2048,128]{1,0:T(8,128)(2,1)S(1)}, u32[]{:S(2)}, u32[]{:S(2)}) collective-permute-start(bf16[2048,128]{1,0:T(8,128)(2,1)S(1)} %get-tuple-element.58.refs_0_), channel_id=1, source_target_pairs={{0,16},{4,20},{8,24},{12,28},{16,0},{20,4},{24,8},{28,12},{1,17},{... | collective-permute-start | bytes 1572872 | tf_op jit(solution)/shard_map/ppermute | solution.py:197
  156.5 34.6 %collective-permute-start.24 = (bf16[2048,128]{1,0:T(8,128)(2,1)S(1)}, bf16[2048,128]{1,0:T(8,128)(2,1)S(1)}, u32[]{:S(2)}, u32[]{:S(2)}) collective-permute-start(bf16[2048,128]{1,0:T(8,128)(2,1)S(1)} %get-tuple-element.58.refs_0_), channel_id=1, source_target_pairs={{0,24},{4,28},{8,0},{12,4},{16,8},{20,12},{24,16},{28,20},{1,25},{... | collective-permute-start | bytes 1572872 | tf_op jit(solution)/shard_map/ppermute | solution.py:197
  174.7 26.5 %collective-permute-start.28 = (bf16[2176,128]{1,0:T(8,128)(2,1)S(1)}, bf16[2176,128]{1,0:T(8,128)(2,1)S(1)}, u32[]{:S(2)}, u32[]{:S(2)}) collective-permute-start(bf16[2176,128]{1,0:T(8,128)(2,1)S(1)} %backward_filter.1.refs_0_), channel_id=1, source_target_pairs={{0,8},{4,12},{8,16},{12,20},{16,24},{20,28},{1,9},{5,13},{9,17},{1... | collective-permute-start | bytes 1671176 | tf_op jit(solution)/shard_map/ppermute | solution.py:171
  176.1 26.8 %collective-permute-start.27 = (bf16[2176,128]{1,0:T(8,128)(2,1)S(1)}, bf16[2176,128]{1,0:T(8,128)(2,1)S(1)}, u32[]{:S(2)}, u32[]{:S(2)}) collective-permute-start(bf16[2176,128]{1,0:T(8,128)(2,1)S(1)} %backward_filter.1.refs_0_), channel_id=1, source_target_pairs={{8,0},{12,4},{16,8},{20,12},{24,16},{28,20},{9,1},{13,5},{17,9},{2... | collective-permute-start | bytes 1671176 | tf_op jit(solution)/shard_map/ppermute | solution.py:171
  199.2 34.2 %collective-permute-start.34 = (bf16[2,2,128,1024]{3,2,0,1:T(8,128)(2,1)S(1)}, bf16[2,2,128,1024]{3,2,0,1:T(8,128)(2,1)S(1)}, u32[]{:S(2)}, u32[]{:S(2)}) collective-permute-start(bf16[2,2,128,1024]{3,2,0,1:T(8,128)(2,1)S(1)} %copy.17), channel_id=1, source_target_pairs={{0,1},{1,0},{2,3},{3,2},{4,5},{5,4},{6,7},{7,6},{8,9},{9,8},{10,11... | collective-permute-start | bytes 3145736 | tf_op jit(solution)/shard_map/ppermute | solution.py:131
  201.2 17.1 %collective-permute-start.29 = (bf16[2176,128]{1,0:T(8,128)(2,1)S(1)}, bf16[2176,128]{1,0:T(8,128)(2,1)S(1)}, u32[]{:S(2)}, u32[]{:S(2)}) collective-permute-start(bf16[2176,128]{1,0:T(8,128)(2,1)S(1)} %collective-permute-done.28.refs_6_), channel_id=1, source_target_pairs={{8,16},{12,20},{16,24},{20,28},{9,17},{13,21},{17,25},{21,29},{10,... | collective-permute-start | bytes 1671176 | tf_op jit(solution)/shard_map/ppermute | solution.py:171
  202.9 27.7 %collective-permute-start.30 = (bf16[2176,128]{1,0:T(8,128)(2,1)S(1)}, bf16[2176,128]{1,0:T(8,128)(2,1)S(1)}, u32[]{:S(2)}, u32[]{:S(2)}) collective-permute-start(bf16[2176,128]{1,0:T(8,128)(2,1)S(1)} %collective-permute-done.27.refs_1_), channel_id=1, source_target_pairs={{8,0},{12,4},{16,8},{20,12},{9,1},{13,5},{17,9},{21,13},{10,2},{14... | collective-permute-start | bytes 1671176 | tf_op jit(solution)/shard_map/ppermute | solution.py:171
  252.9 16.7 %collective-permute-start.36 = (bf16[512,1024]{1,0:T(8,128)(2,1)S(1)}, bf16[512,1024]{1,0:T(8,128)(2,1)S(1)}, u32[]{:S(2)}, u32[]{:S(2)}) collective-permute-start(bf16[512,1024]{1,0:T(8,128)(2,1)S(1)} %project_back.2), channel_id=1, source_target_pairs={{0,1},{1,0},{2,3},{3,2},{4,5},{5,4},{6,7},{7,6},{8,9},{9,8},{10,11... | collective-permute-start | bytes 3145736 | tf_op jit(solution)/shard_map/ppermute | solution.py:131
  253.8 14.8 %collective-permute-start.41 = (bf16[2,128,1024]{2,1,0:T(8,128)(2,1)}, bf16[2,128,1024]{2,1,0:T(8,128)(2,1)S(1)}, u32[]{:S(2)}, u32[]{:S(2)}) collective-permute-start(bf16[2,128,1024]{2,1,0:T(8,128)(2,1)} %slice_bitcast_fusion.6), channel_id=1, source_target_pairs={{0,2},{1,3},{2,0},{3,1},{4,6},{5,7},{6,4},{7,5},{8,10},{9,11},{10,... | collective-permute-start | bytes 1572872 | tf_op jit(solution)/shard_map/ppermute | solution.py:131
  255.9 33.7 %collective-permute-start.40 = (bf16[512,512]{1,0:T(8,128)(2,1)S(1)}, bf16[512,512]{1,0:T(8,128)(2,1)S(1)}, u32[]{:S(2)}, u32[]{:S(2)}) collective-permute-start(bf16[512,512]{1,0:T(8,128)(2,1)S(1)} %get-tuple-element.73), channel_id=1, source_target_pairs={{0,4},{4,0},{8,12},{12,8},{16,20},{20,16},{24,28},{28,24},{1,5},{5... | collective-permute-start | bytes 1572872 | tf_op jit(solution)/shard_map/ppermute | solution.py:131
  273.0 16.4 %collective-permute-start.38 = (bf16[128,1024]{1,0:T(8,128)(2,1)S(1)}, bf16[128,1024]{1,0:T(8,128)(2,1)S(1)}, u32[]{:S(2)}, u32[]{:S(2)}) collective-permute-start(bf16[128,1024]{1,0:T(8,128)(2,1)S(1)} %get-tuple-element.105), channel_id=1, source_target_pairs={{0,4},{4,0},{8,12},{12,8},{16,20},{20,16},{24,28},{28,24},{1,5},{5... | collective-permute-start | bytes 786440 | tf_op jit(solution)/shard_map/ppermute | solution.py:131
  278.8 26.0 %collective-permute-start.45 = (bf16[512,512]{1,0:T(8,128)(2,1)}, bf16[512,512]{1,0:T(8,128)(2,1)S(1)}, u32[]{:S(2)}, u32[]{:S(2)}) collective-permute-start(bf16[512,512]{1,0:T(8,128)(2,1)} %get-tuple-element.80), channel_id=1, source_target_pairs={{0,4},{4,0},{8,12},{12,8},{16,20},{20,16},{24,28},{28,24},{1,5},{5... | collective-permute-start | bytes 1572872 | tf_op jit(solution)/shard_map/ppermute | solution.py:131
  289.6 16.8 %collective-permute-start.44 = (bf16[128,1024]{1,0:T(8,128)(2,1)S(1)}, bf16[128,1024]{1,0:T(8,128)(2,1)S(1)}, u32[]{:S(2)}, u32[]{:S(2)}) collective-permute-start(bf16[128,1024]{1,0:T(8,128)(2,1)S(1)} %add_add_fusion), channel_id=1, source_target_pairs={{0,0},{8,1},{16,2},{24,3},{4,4},{12,5},{20,6},{28,7},{2,8},{10,9},... | collective-permute-start | bytes 786440 | tf_op jit(solution)/shard_map/ppermute | solution.py:146
  (42 other events, 497.0 us)

commit v7 on v6

--- a/solution.py
+++ b/solution.py
@@ -10,7 +10,7 @@
 f32 = jnp.float32
 lanes = 128
 sublanes = 8
-vmem_bytes = 48 * 1024 * 1024
+vmem_bytes = 24 * 1024 * 1024
 
 
 def causal_filter(extended, filters):

time: 309 us -> 304 us (0.984)
  Pallas kernels: 71.2 us -> 60.8 us
  waiting for transfers between devices: 129 us -> 133 us
  transfers between devices with their start and end apart: 47 -> 47, of which waited for: 22 -> 20; matrix products, arithmetic and copies ran while one was open for 3% -> 3% of each run, Pallas kernels for 18% -> 16%
where the time goes in v7:
time: 304 us; the launch traced here: 303 us
  waiting for transfers between devices  133 us (44%)
  starting transfers between devices  89.1 us (29%)
  Pallas kernels  60.8 us (20%)
  local copies, waits for them, and re-layouts  10.1 us (3%)
  other arithmetic  7.99 us (3%)
    ppermute x19, waiting for transfers between devices, flip(): lax.ppermute(value, axis, [(i, i ^ bit) for i in range(lax.axis_size(axis...  70.5 us
    ppermute x18, starting transfers between devices, along_line(): return lax.ppermute(value, 'seq', pairs)  42.9 us
    ppermute x18, waiting for transfers between devices, along_line(): return lax.ppermute(value, 'seq', pairs)  37.3 us
    ppermute x3, starting transfers between devices, flip_both(): return lax.ppermute(value, ('seq', 'fsdp'), pairs)  21 us
    ppermute x19, starting transfers between devices, flip(): lax.ppermute(value, axis, [(i, i ^ bit) for i in range(lax.axis_size(axis...  16.7 us
    ppermute x3, waiting for transfers between devices, around(): lax.ppermute(value, 'seq', [(i, (i + 2 * by) % size) for i in range(size)])  15.4 us
    pallas_call x1, Pallas kernels, backward_filter(): pl.pallas_call(body, out_shape=jax.ShapeDtypeStruct((2 * tokens + taps, l...  13.6 us
    ppermute x3, waiting for transfers between devices, flip_both(): return lax.ppermute(value, ('seq', 'fsdp'), pairs)  10.4 us
  transfers between devices with their start and end apart: 47, of which 20 were waited for; matrix products, arithmetic and copies ran while one was open for 3% of the time, Pallas kernels for 16%

profile of v7, /device:TPU:0, one launch (start us, length us, event | category | flops | bytes accessed | tf_op | source)
XLA Modules:
  0.0 302.9 jit_solution(6284760449088040274)
XLA Ops:
  2.7 3.0 %collective-permute-start.4 = (bf16[2,512,512]{2,1,0:T(8,128)(2,1)S(1)}, bf16[2,512,512]{2,1,0:T(8,128)(2,1)S(1)}, u32[]{:S(2)}, u32[]{:S(2)}) collective-permute-start(bf16[2,512,512]{2,1,0:T(8,128)(2,1)S(1)} %pad_maximum_fusion.1), channel_id=1, source_target_pairs={{0,4},{4,0},{8,12},{12,8},{16,20},{20,16},{24,28},{28,24},{1,5},{5... | collective-permute-start | bytes 3145736 | tf_op jit(solution)/shard_map/ppermute | solution.py:131
  7.1 18.2 %collective-permute-start.3 = (bf16[128,1024]{1,0:T(8,128)(2,1)S(1)}, bf16[128,1024]{1,0:T(8,128)(2,1)S(1)}, u32[]{:S(2)}, u32[]{:S(2)}) collective-permute-start(bf16[128,1024]{1,0:T(8,128)(2,1)S(1)} %collective-permute-done), channel_id=1, source_target_pairs={{0,6},{1,7},{2,4},{3,5},{4,2},{5,3},{6,0},{7,1},{8,14},{9,15},{10,... | collective-permute-start | bytes 786440 | tf_op jit(solution)/shard_map/ppermute | solution.py:156
  27.6 6.4 %collective-permute-done.3 = bf16[128,1024]{1,0:T(8,128)(2,1)S(1)} collective-permute-done((bf16[128,1024]{1,0:T(8,128)(2,1)S(1)}, bf16[128,1024]{1,0:T(8,128)(2,1)S(1)}, u32[]{:S(2)}, u32[]{:S(2)}) %collective-permute-start.3) | collective-permute-done | bytes 262176 | tf_op jit(solution)/shard_map/ppermute | solution.py:156
  34.0 6.1 %collective-permute-done.2 = bf16[128,1024]{1,0:T(8,128)(2,1)S(1)} collective-permute-done((bf16[128,1024]{1,0:T(8,128)(2,1)S(1)}, bf16[128,1024]{1,0:T(8,128)(2,1)S(1)}, u32[]{:S(2)}, u32[]{:S(2)}) %collective-permute-start.2) | collective-permute-done | bytes 262176 | tf_op jit(solution)/shard_map/ppermute | solution.py:131
  47.9 4.5 %project_pair.2.blocks_ref = bf16[4,2,1024,128]{3,2,1,0:T(8,128)(2,1)S(1)} custom-call(s32[2]{0:T(128)S(1)} %pad_add_fusion.place_ref, bf16[2,2,128,1024]{3,2,1,0:T(8,128)(2,1)S(1)} %bitcast.64, bf16[2,2,128,1024]{3,2,1,0:T(8,128)(2,1)S(1)} %collective-permute-done.6.refs_1_.refs_3_.refs_7_.refs_9_.own_far.other_far, bf16[2,2,128,1024]{3,2,1,0:T(8,128)(2,1)S(1)} %bitcast.65, ...), custom_call_target="tpu_custom_call" | custom-call | flops 2147483648 | bytes 8388608 | tf_op jit(solution)/shard_map/project_pair/pallas_call | solution.py:253
  53.4 5.8 %collective-permute-start.7 = (bf16[2,1024,128]{2,1,0:T(8,128)(2,1)S(1)}, bf16[2,1024,128]{2,1,0:T(8,128)(2,1)S(1)}, u32[]{:S(2)}, u32[]{:S(2)}) collective-permute-start(bf16[2,1024,128]{2,1,0:T(8,128)(2,1)S(1)} %get-tuple-element.102), channel_id=1, source_target_pairs={{0,8},{4,12},{1,9},{5,13},{2,10},{6,14},{3,11},{7,15}} | collective-permute-start | bytes 1572872 | tf_op jit(solution)/shard_map/ppermute | solution.py:171
  60.6 17.7 %collective-permute-done.11 = bf16[128,1024]{1,0:T(8,128)(2,1)S(1)} collective-permute-done((bf16[128,1024]{1,0:T(8,128)(2,1)S(1)}, bf16[128,1024]{1,0:T(8,128)(2,1)S(1)}, u32[]{:S(2)}, u32[]{:S(2)}) %collective-permute-start.11) | collective-permute-done | bytes 262176 | tf_op jit(solution)/shard_map/ppermute | solution.py:131
  81.2 4.4 %project_pair.3.blocks_ref = bf16[4,2,1024,128]{3,2,1,0:T(8,128)(2,1)S(1)} custom-call(s32[2]{0:T(128)S(1)} %pad_add_fusion.place_ref, bf16[2,2,128,1024]{3,2,1,0:T(8,128)(2,1)S(1)} %bitcast.68, bf16[2,2,128,1024]{3,2,1,0:T(8,128)(2,1)S(1)} %collective-permute-done.6.refs_1_.refs_3_.refs_7_.refs_9_.own_far.other_far, bf16[2,2,128,1024]{3,2,1,0:T(8,128)(2,1)S(1)} %bitcast.69, ...), custom_call_target="tpu_custom_call" | custom-call | flops 2147483648 | bytes 8388608 | tf_op jit(solution)/shard_map/project_pair/pallas_call | solution.py:253
  88.3 5.7 %collective-permute-start.14 = (bf16[2,1024,128]{2,1,0:T(8,128)(2,1)}, bf16[2,1024,128]{2,1,0:T(8,128)(2,1)}, u32[]{:S(2)}, u32[]{:S(2)}) collective-permute-start(bf16[2,1024,128]{2,1,0:T(8,128)(2,1)} %get-tuple-element.100), channel_id=1, source_target_pairs={{0,8},{4,12},{1,9},{5,13},{2,10},{6,14},{3,11},{7,15}} | collective-permute-start | bytes 1572872 | tf_op jit(solution)/shard_map/ppermute | solution.py:171
  98.8 7.0 %collective-permute-done.14 = bf16[2,1024,128]{2,1,0:T(8,128)(2,1)} collective-permute-done((bf16[2,1024,128]{2,1,0:T(8,128)(2,1)}, bf16[2,1024,128]{2,1,0:T(8,128)(2,1)}, u32[]{:S(2)}, u32[]{:S(2)}) %collective-permute-start.14) | collective-permute-done | bytes 524320 | tf_op jit(solution)/shard_map/ppermute | solution.py:171
  108.3 5.0 %collective-permute-start.15 = (bf16[2,1024,128]{2,1,0:T(8,128)(2,1)S(1)}, bf16[2,1024,128]{2,1,0:T(8,128)(2,1)S(1)}, u32[]{:S(2)}, u32[]{:S(2)}) collective-permute-start(bf16[2,1024,128]{2,1,0:T(8,128)(2,1)S(1)} %get-tuple-element.98), channel_id=1, source_target_pairs={{0,8},{4,12},{8,16},{12,20},{1,9},{5,13},{9,17},{13,21},{2,10},{6,... | collective-permute-start | bytes 1572872 | tf_op jit(solution)/shard_map/ppermute | solution.py:171
  113.3 3.7 %collective-permute-done.20 = bf16[2,1024,128]{2,1,0:T(8,128)(2,1)} collective-permute-done((bf16[2,1024,128]{2,1,0:T(8,128)(2,1)S(1)}, bf16[2,1024,128]{2,1,0:T(8,128)(2,1)}, u32[]{:S(2)}, u32[]{:S(2)}) %collective-permute-start.20) | collective-permute-done | bytes 524320 | tf_op jit(solution)/shard_map/ppermute | solution.py:171
  119.7 5.2 %collective-permute-start.21 = (bf16[2,1024,128]{2,1,0:T(8,128)(2,1)S(1)}, bf16[2,1024,128]{2,1,0:T(8,128)(2,1)S(1)}, u32[]{:S(2)}, u32[]{:S(2)}) collective-permute-start(bf16[2,1024,128]{2,1,0:T(8,128)(2,1)S(1)} %get-tuple-element.92), channel_id=1, source_target_pairs={{0,8},{4,12},{8,16},{12,20},{16,24},{20,28},{1,9},{5,13},{9,17},{1... | collective-permute-start | bytes 1572872 | tf_op jit(solution)/shard_map/ppermute | solution.py:171
  124.9 3.2 %collective-permute-done.15 = bf16[2,1024,128]{2,1,0:T(8,128)(2,1)S(1)} collective-permute-done((bf16[2,1024,128]{2,1,0:T(8,128)(2,1)S(1)}, bf16[2,1024,128]{2,1,0:T(8,128)(2,1)S(1)}, u32[]{:S(2)}, u32[]{:S(2)}) %collective-permute-start.15) | collective-permute-done | bytes 524320 | tf_op jit(solution)/shard_map/ppermute | solution.py:171
  129.8 5.0 %collective-permute-start.16 = (bf16[2,1024,128]{2,1,0:T(8,128)(2,1)S(1)}, bf16[2,1024,128]{2,1,0:T(8,128)(2,1)S(1)}, u32[]{:S(2)}, u32[]{:S(2)}) collective-permute-start(bf16[2,1024,128]{2,1,0:T(8,128)(2,1)S(1)} %get-tuple-element.96), channel_id=1, source_target_pairs={{0,8},{4,12},{8,16},{12,20},{16,24},{20,28},{1,9},{5,13},{9,17},{1... | collective-permute-start | bytes 1572872 | tf_op jit(solution)/shard_map/ppermute | solution.py:171
  134.8 4.6 %collective-permute-done.21.refs_0_ = bf16[2,1024,128]{2,1,0:T(8,128)(2,1)S(1)} collective-permute-done((bf16[2,1024,128]{2,1,0:T(8,128)(2,1)S(1)}, bf16[2,1024,128]{2,1,0:T(8,128)(2,1)S(1)}, u32[]{:S(2)}, u32[]{:S(2)}) %collective-permute-start.21) | collective-permute-done | bytes 524320 | tf_op jit(solution)/shard_map/ppermute | solution.py:171
  139.4 8.3 %forward_filter.1 = (bf16[2,1024,128]{2,1,0:T(8,128)(2,1)S(1)}, bf16[1024,128]{1,0:T(8,128)(2,1)S(1)}, f32[1024,128]{1,0:T(8,128)S(1)}) custom-call(s32[8]{0:T(128)S(1)} %fusion.14.order_ref, bf16[4,2,1024,128]{3,2,1,0:T(8,128)(2,1)S(1)} %copy-done.16, bf16[2,1024,128]{2,1,0:T(8,128)(2,1)S(1)} %collective-permute-done.21.refs_0_, ...), custom_call_target="tpu_custom_call" | custom-call | flops 6710886400 | bytes 1572864 | tf_op jit(solution)/shard_map/forward_filter/pallas_call | solution.py:341
  153.7 2.8 collective-permute-start.24
  156.6 13.6 %backward_filter.1.refs_0_ = bf16[2176,128]{1,0:T(8,128)(2,1)S(1)} custom-call(s32[8]{0:T(128)S(1)} %fusion.14.order_ref, bf16[1024,128]{1,0:T(8,128)(2,1)S(1)} %get-tuple-element.59.grad_ref, bf16[2,1024,128]{2,1,0:T(8,128)(2,1)S(1)} %get-tuple-element.60.kv_ref, bf16[1024,128]{1,0:T(8,128)(2,1)S(1)} %get-tuple-element.61.signal_ref, ...), custom_call_target="tpu_custom_call" | custom-call | flops 13421772800 | bytes 1572864 | tf_op jit(solution)/shard_map/backward_filter/pallas_call | solution.py:484
  173.0 15.3 %collective-permute-done.25.refs_2_ = bf16[2048,128]{1,0:T(8,128)(2,1)S(1)} collective-permute-done((bf16[2048,128]{1,0:T(8,128)(2,1)S(1)}, bf16[2048,128]{1,0:T(8,128)(2,1)S(1)}, u32[]{:S(2)}, u32[]{:S(2)}) %collective-permute-start.25) | collective-permute-done | bytes 524320 | tf_op jit(solution)/shard_map/ppermute | solution.py:197
  189.5 2.9 out_gradient.1
  195.0 3.4 %collective-permute-done.28.refs_6_ = bf16[2176,128]{1,0:T(8,128)(2,1)S(1)} collective-permute-done((bf16[2176,128]{1,0:T(8,128)(2,1)S(1)}, bf16[2176,128]{1,0:T(8,128)(2,1)S(1)}, u32[]{:S(2)}, u32[]{:S(2)}) %collective-permute-start.28) | collective-permute-done | bytes 557088 | tf_op jit(solution)/shard_map/ppermute | solution.py:171
  202.3 3.0 in_gradient.3
  205.2 10.3 %collective-permute-done.31.piece_ref = bf16[512,512]{1,0:T(8,128)(2,1)S(1)} collective-permute-done((bf16[512,512]{1,0:T(8,128)(2,1)S(1)}, bf16[512,512]{1,0:T(8,128)(2,1)S(1)}, u32[]{:S(2)}, u32[]{:S(2)}) %collective-permute-start.31) | collective-permute-done | bytes 524320 | tf_op jit(solution)/shard_map/ppermute | solution.py:131
  215.5 12.3 %collective-permute-done.30.refs_3_ = bf16[2176,128]{1,0:T(8,128)(2,1)S(1)} collective-permute-done((bf16[2176,128]{1,0:T(8,128)(2,1)S(1)}, bf16[2176,128]{1,0:T(8,128)(2,1)S(1)}, u32[]{:S(2)}, u32[]{:S(2)}) %collective-permute-start.30) | collective-permute-done | bytes 557088 | tf_op jit(solution)/shard_map/ppermute | solution.py:171
  231.1 10.1 %collective-permute-done.35.piece_ref = bf16[512,512]{1,0:T(8,128)(2,1)S(1)} collective-permute-done((bf16[512,512]{1,0:T(8,128)(2,1)S(1)}, bf16[512,512]{1,0:T(8,128)(2,1)S(1)}, u32[]{:S(2)}, u32[]{:S(2)}) %collective-permute-start.35) | collective-permute-done | bytes 524320 | tf_op jit(solution)/shard_map/ppermute | solution.py:131
  243.2 3.0 in_gradient.4
  254.6 9.2 %collective-permute-done.41 = bf16[2,128,1024]{2,1,0:T(8,128)(2,1)S(1)} collective-permute-done((bf16[2,128,1024]{2,1,0:T(8,128)(2,1)S(1)}, bf16[2,128,1024]{2,1,0:T(8,128)(2,1)S(1)}, u32[]{:S(2)}, u32[]{:S(2)}) %collective-permute-start.41) | collective-permute-done | bytes 524320 | tf_op jit(solution)/shard_map/ppermute | solution.py:131
  268.7 3.1 %in_gradient.5 = (f32[3,512,1024]{2,1,0:T(8,128)}, bf16[512,512]{1,0:T(8,128)(2,1)}) custom-call(s32[2]{0:T(128)S(1)} %pad_add_fusion.place_ref, bf16[2,2,128,1024]{3,2,1,0:T(8,128)(2,1)S(1)} %bitcast.74, bf16[2,2,128,1024]{3,2,1,0:T(8,128)(2,1)S(1)} %collective-permute-done.6.refs_1_.refs_3_.refs_7_.refs_9_.own_far.other_far, ...), custom_call_target="tpu_custom_call", output_to_operand_aliasing={{0}: (6, {})} | custom-call | flops 1073741824 | bytes 4194304 | tf_op jit(solution)/shard_map/in_gradient/pallas_call | solution.py:676
  275.6 4.0 %collective-permute-done.39 = bf16[128,1024]{1,0:T(8,128)(2,1)S(1)} collective-permute-done((bf16[128,1024]{1,0:T(8,128)(2,1)S(1)}, bf16[128,1024]{1,0:T(8,128)(2,1)S(1)}, u32[]{:S(2)}, u32[]{:S(2)}) %collective-permute-start.39) | collective-permute-done | bytes 262176 | tf_op jit(solution)/shard_map/ppermute | solution.py:156
  279.6 4.8 %collective-permute-done.38 = bf16[128,1024]{1,0:T(8,128)(2,1)S(1)} collective-permute-done((bf16[128,1024]{1,0:T(8,128)(2,1)S(1)}, bf16[128,1024]{1,0:T(8,128)(2,1)S(1)}, u32[]{:S(2)}, u32[]{:S(2)}) %collective-permute-start.38) | collective-permute-done | bytes 262176 | tf_op jit(solution)/shard_map/ppermute | solution.py:131
  289.9 7.5 %collective-permute-done.46 = bf16[512,128]{1,0:T(8,128)(2,1)S(1)} collective-permute-done((bf16[512,128]{1,0:T(8,128)(2,1)S(1)}, bf16[512,128]{1,0:T(8,128)(2,1)S(1)}, u32[]{:S(2)}, u32[]{:S(2)}) %collective-permute-start.46) | collective-permute-done | bytes 131104 | tf_op jit(solution)/shard_map/ppermute | solution.py:131
  (167 shorter events, 82.3 us)
Async XLA Ops:
  2.7 37.6 %collective-permute-start.4 = (bf16[2,512,512]{2,1,0:T(8,128)(2,1)S(1)}, bf16[2,512,512]{2,1,0:T(8,128)(2,1)S(1)}, u32[]{:S(2)}, u32[]{:S(2)}) collective-permute-start(bf16[2,512,512]{2,1,0:T(8,128)(2,1)S(1)} %pad_maximum_fusion.1), channel_id=1, source_target_pairs={{0,4},{4,0},{8,12},{12,8},{16,20},{20,16},{24,28},{28,24},{1,5},{5... | collective-permute-start | bytes 3145736 | tf_op jit(solution)/shard_map/ppermute | solution.py:131
  6.4 33.8 %collective-permute-start.5 = (bf16[128,1024]{1,0:T(8,128)(2,1)S(1)}, bf16[128,1024]{1,0:T(8,128)(2,1)S(1)}, u32[]{:S(2)}, u32[]{:S(2)}) collective-permute-start(bf16[128,1024]{1,0:T(8,128)(2,1)S(1)} %copy-done.25), channel_id=1, source_target_pairs={{0,0},{1,8},{2,16},{3,24},{4,4},{5,12},{6,20},{7,28},{8,2},{9,10},... | collective-permute-start | bytes 786440 | tf_op jit(solution)/shard_map/ppermute | solution.py:146
  7.1 26.9 %collective-permute-start.3 = (bf16[128,1024]{1,0:T(8,128)(2,1)S(1)}, bf16[128,1024]{1,0:T(8,128)(2,1)S(1)}, u32[]{:S(2)}, u32[]{:S(2)}) collective-permute-start(bf16[128,1024]{1,0:T(8,128)(2,1)S(1)} %collective-permute-done), channel_id=1, source_target_pairs={{0,6},{1,7},{2,4},{3,5},{4,2},{5,3},{6,0},{7,1},{8,14},{9,15},{10,... | collective-permute-start | bytes 786440 | tf_op jit(solution)/shard_map/ppermute | solution.py:156
  25.3 14.8 %collective-permute-start.2 = (bf16[128,1024]{1,0:T(8,128)(2,1)S(1)}, bf16[128,1024]{1,0:T(8,128)(2,1)S(1)}, u32[]{:S(2)}, u32[]{:S(2)}) collective-permute-start(bf16[128,1024]{1,0:T(8,128)(2,1)S(1)} %collective-permute-done), channel_id=1, source_target_pairs={{0,4},{4,0},{8,12},{12,8},{16,20},{20,16},{24,28},{28,24},{1,5},{5... | collective-permute-start | bytes 786440 | tf_op jit(solution)/shard_map/ppermute | solution.py:131
  41.3 37.2 %collective-permute-start.9 = (bf16[2,512,512]{2,1,0:T(8,128)(2,1)}, bf16[2,512,512]{2,1,0:T(8,128)(2,1)S(1)}, u32[]{:S(2)}, u32[]{:S(2)}) collective-permute-start(bf16[2,512,512]{2,1,0:T(8,128)(2,1)} %pad_maximum_fusion.2), channel_id=1, source_target_pairs={{0,4},{4,0},{8,12},{12,8},{16,20},{20,16},{24,28},{28,24},{1,5},{5... | collective-permute-start | bytes 3145736 | tf_op jit(solution)/shard_map/ppermute | solution.py:131
  43.1 16.8 %collective-permute-start.12 = (bf16[128,1024]{1,0:T(8,128)(2,1)S(1)}, bf16[128,1024]{1,0:T(8,128)(2,1)S(1)}, u32[]{:S(2)}, u32[]{:S(2)}) collective-permute-start(bf16[128,1024]{1,0:T(8,128)(2,1)S(1)} %collective-permute-done.5), channel_id=1, source_target_pairs={{0,6},{1,7},{2,4},{3,5},{4,2},{5,3},{6,0},{7,1},{8,14},{9,15},{10,... | collective-permute-start | bytes 786440 | tf_op jit(solution)/shard_map/ppermute | solution.py:156
  52.6 25.9 %collective-permute-start.8 = (bf16[2,1024,128]{2,1,0:T(8,128)(2,1)S(1)}, bf16[2,1024,128]{2,1,0:T(8,128)(2,1)S(1)}, u32[]{:S(2)}, u32[]{:S(2)}) collective-permute-start(bf16[2,1024,128]{2,1,0:T(8,128)(2,1)S(1)} %get-tuple-element.101), channel_id=1, source_target_pairs={{24,16},{28,20},{25,17},{29,21},{26,18},{30,22},{27,19},{31,23}} | collective-permute-start | bytes 1572872 | tf_op jit(solution)/shard_map/ppermute | solution.py:171
  53.4 25.1 %collective-permute-start.7 = (bf16[2,1024,128]{2,1,0:T(8,128)(2,1)S(1)}, bf16[2,1024,128]{2,1,0:T(8,128)(2,1)S(1)}, u32[]{:S(2)}, u32[]{:S(2)}) collective-permute-start(bf16[2,1024,128]{2,1,0:T(8,128)(2,1)S(1)} %get-tuple-element.102), channel_id=1, source_target_pairs={{0,8},{4,12},{1,9},{5,13},{2,10},{6,14},{3,11},{7,15}} | collective-permute-start | bytes 1572872 | tf_op jit(solution)/shard_map/ppermute | solution.py:171
  59.2 19.1 %collective-permute-start.11 = (bf16[128,1024]{1,0:T(8,128)(2,1)S(1)}, bf16[128,1024]{1,0:T(8,128)(2,1)S(1)}, u32[]{:S(2)}, u32[]{:S(2)}) collective-permute-start(bf16[128,1024]{1,0:T(8,128)(2,1)S(1)} %collective-permute-done.5), channel_id=1, source_target_pairs={{0,4},{4,0},{8,12},{12,8},{16,20},{20,16},{24,28},{28,24},{1,5},{5... | collective-permute-start | bytes 786440 | tf_op jit(solution)/shard_map/ppermute | solution.py:131
  59.9 18.4 %collective-permute-start.10 = (bf16[128,1024]{1,0:T(8,128)(2,1)S(1)}, bf16[128,1024]{1,0:T(8,128)(2,1)S(1)}, u32[]{:S(2)}, u32[]{:S(2)}) collective-permute-start(bf16[128,1024]{1,0:T(8,128)(2,1)S(1)} %collective-permute-done.5), channel_id=1, source_target_pairs={{0,2},{1,3},{2,0},{3,1},{4,6},{5,7},{6,4},{7,5},{8,10},{9,11},{10,... | collective-permute-start | bytes 786440 | tf_op jit(solution)/shard_map/ppermute | solution.py:131
  88.3 17.5 %collective-permute-start.14 = (bf16[2,1024,128]{2,1,0:T(8,128)(2,1)}, bf16[2,1024,128]{2,1,0:T(8,128)(2,1)}, u32[]{:S(2)}, u32[]{:S(2)}) collective-permute-start(bf16[2,1024,128]{2,1,0:T(8,128)(2,1)} %get-tuple-element.100), channel_id=1, source_target_pairs={{0,8},{4,12},{1,9},{5,13},{2,10},{6,14},{3,11},{7,15}} | collective-permute-start | bytes 1572872 | tf_op jit(solution)/shard_map/ppermute | solution.py:171
  95.1 18.2 %collective-permute-start.22 = (bf16[2,1024,128]{2,1,0:T(8,128)(2,1)}, bf16[2,1024,128]{2,1,0:T(8,128)(2,1)}, u32[]{:S(2)}, u32[]{:S(2)}) collective-permute-start(bf16[2,1024,128]{2,1,0:T(8,128)(2,1)} %get-tuple-element.93), channel_id=1, source_target_pairs={{16,8},{20,12},{24,16},{28,20},{17,9},{21,13},{25,17},{29,21},{18,... | collective-permute-start | bytes 1572872 | tf_op jit(solution)/shard_map/ppermute | solution.py:171
  96.5 20.4 %collective-permute-start.20 = (bf16[2,1024,128]{2,1,0:T(8,128)(2,1)S(1)}, bf16[2,1024,128]{2,1,0:T(8,128)(2,1)}, u32[]{:S(2)}, u32[]{:S(2)}) collective-permute-start(bf16[2,1024,128]{2,1,0:T(8,128)(2,1)S(1)} %get-tuple-element.94), channel_id=1, source_target_pairs={{0,8},{4,12},{8,16},{12,20},{1,9},{5,13},{9,17},{13,21},{2,10},{6,... | collective-permute-start | bytes 1572872 | tf_op jit(solution)/shard_map/ppermute | solution.py:171
  107.4 17.5 %collective-permute-start.18 = (bf16[2,1024,128]{2,1,0:T(8,128)(2,1)S(1)}, bf16[2,1024,128]{2,1,0:T(8,128)(2,1)S(1)}, u32[]{:S(2)}, u32[]{:S(2)}) collective-permute-start(bf16[2,1024,128]{2,1,0:T(8,128)(2,1)S(1)} %get-tuple-element.97), channel_id=1, source_target_pairs={{16,8},{20,12},{24,16},{28,20},{17,9},{21,13},{25,17},{29,21},{18,... | collective-permute-start | bytes 1572872 | tf_op jit(solution)/shard_map/ppermute | solution.py:171
  108.3 19.9 %collective-permute-start.15 = (bf16[2,1024,128]{2,1,0:T(8,128)(2,1)S(1)}, bf16[2,1024,128]{2,1,0:T(8,128)(2,1)S(1)}, u32[]{:S(2)}, u32[]{:S(2)}) collective-permute-start(bf16[2,1024,128]{2,1,0:T(8,128)(2,1)S(1)} %get-tuple-element.98), channel_id=1, source_target_pairs={{0,8},{4,12},{8,16},{12,20},{1,9},{5,13},{9,17},{13,21},{2,10},{6,... | collective-permute-start | bytes 1572872 | tf_op jit(solution)/shard_map/ppermute | solution.py:171
  118.4 16.4 %collective-permute-start.23 = (bf16[2,1024,128]{2,1,0:T(8,128)(2,1)S(1)}, bf16[2,1024,128]{2,1,0:T(8,128)(2,1)S(1)}, u32[]{:S(2)}, u32[]{:S(2)}) collective-permute-start(bf16[2,1024,128]{2,1,0:T(8,128)(2,1)S(1)} %get-tuple-element.91), channel_id=1, source_target_pairs={{8,0},{12,4},{16,8},{20,12},{24,16},{28,20},{9,1},{13,5},{17,9},{2... | collective-permute-start | bytes 1572872 | tf_op jit(solution)/shard_map/ppermute | solution.py:171
  119.7 19.7 %collective-permute-start.21 = (bf16[2,1024,128]{2,1,0:T(8,128)(2,1)S(1)}, bf16[2,1024,128]{2,1,0:T(8,128)(2,1)S(1)}, u32[]{:S(2)}, u32[]{:S(2)}) collective-permute-start(bf16[2,1024,128]{2,1,0:T(8,128)(2,1)S(1)} %get-tuple-element.92), channel_id=1, source_target_pairs={{0,8},{4,12},{8,16},{12,20},{16,24},{20,28},{1,9},{5,13},{9,17},{1... | collective-permute-start | bytes 1572872 | tf_op jit(solution)/shard_map/ppermute | solution.py:171
  128.5 19.3 %collective-permute-start.19 = (bf16[2,1024,128]{2,1,0:T(8,128)(2,1)S(1)}, bf16[2,1024,128]{2,1,0:T(8,128)(2,1)S(1)}, u32[]{:S(2)}, u32[]{:S(2)}) collective-permute-start(bf16[2,1024,128]{2,1,0:T(8,128)(2,1)S(1)} %get-tuple-element.95), channel_id=1, source_target_pairs={{8,0},{12,4},{16,8},{20,12},{24,16},{28,20},{9,1},{13,5},{17,9},{2... | collective-permute-start | bytes 1572872 | tf_op jit(solution)/shard_map/ppermute | solution.py:171
  129.8 20.1 %collective-permute-start.16 = (bf16[2,1024,128]{2,1,0:T(8,128)(2,1)S(1)}, bf16[2,1024,128]{2,1,0:T(8,128)(2,1)S(1)}, u32[]{:S(2)}, u32[]{:S(2)}) collective-permute-start(bf16[2,1024,128]{2,1,0:T(8,128)(2,1)S(1)} %get-tuple-element.96), channel_id=1, source_target_pairs={{0,8},{4,12},{8,16},{12,20},{16,24},{20,28},{1,9},{5,13},{9,17},{1... | collective-permute-start | bytes 1572872 | tf_op jit(solution)/shard_map/ppermute | solution.py:171
  150.7 22.3 %collective-permute-start.26 = (bf16[2048,128]{1,0:T(8,128)(2,1)S(1)}, bf16[2048,128]{1,0:T(8,128)(2,1)S(1)}, u32[]{:S(2)}, u32[]{:S(2)}) collective-permute-start(bf16[2048,128]{1,0:T(8,128)(2,1)S(1)} %get-tuple-element.58.refs_0_), channel_id=1, source_target_pairs={{0,8},{4,12},{8,16},{12,20},{16,24},{20,28},{24,0},{28,4},{1,9},{5... | collective-permute-start | bytes 1572872 | tf_op jit(solution)/shard_map/ppermute | solution.py:197
  153.2 35.1 %collective-permute-start.25 = (bf16[2048,128]{1,0:T(8,128)(2,1)S(1)}, bf16[2048,128]{1,0:T(8,128)(2,1)S(1)}, u32[]{:S(2)}, u32[]{:S(2)}) collective-permute-start(bf16[2048,128]{1,0:T(8,128)(2,1)S(1)} %get-tuple-element.58.refs_0_), channel_id=1, source_target_pairs={{0,16},{4,20},{8,24},{12,28},{16,0},{20,4},{24,8},{28,12},{1,17},{... | collective-permute-start | bytes 1572872 | tf_op jit(solution)/shard_map/ppermute | solution.py:197
  153.7 34.6 %collective-permute-start.24 = (bf16[2048,128]{1,0:T(8,128)(2,1)S(1)}, bf16[2048,128]{1,0:T(8,128)(2,1)S(1)}, u32[]{:S(2)}, u32[]{:S(2)}) collective-permute-start(bf16[2048,128]{1,0:T(8,128)(2,1)S(1)} %get-tuple-element.58.refs_0_), channel_id=1, source_target_pairs={{0,24},{4,28},{8,0},{12,4},{16,8},{20,12},{24,16},{28,20},{1,25},{... | collective-permute-start | bytes 1572872 | tf_op jit(solution)/shard_map/ppermute | solution.py:197
  170.2 28.2 %collective-permute-start.28 = (bf16[2176,128]{1,0:T(8,128)(2,1)S(1)}, bf16[2176,128]{1,0:T(8,128)(2,1)S(1)}, u32[]{:S(2)}, u32[]{:S(2)}) collective-permute-start(bf16[2176,128]{1,0:T(8,128)(2,1)S(1)} %backward_filter.1.refs_0_), channel_id=1, source_target_pairs={{0,8},{4,12},{8,16},{12,20},{16,24},{20,28},{1,9},{5,13},{9,17},{1... | collective-permute-start | bytes 1671176 | tf_op jit(solution)/shard_map/ppermute | solution.py:171
  171.7 28.4 %collective-permute-start.27 = (bf16[2176,128]{1,0:T(8,128)(2,1)S(1)}, bf16[2176,128]{1,0:T(8,128)(2,1)S(1)}, u32[]{:S(2)}, u32[]{:S(2)}) collective-permute-start(bf16[2176,128]{1,0:T(8,128)(2,1)S(1)} %backward_filter.1.refs_0_), channel_id=1, source_target_pairs={{8,0},{12,4},{16,8},{20,12},{24,16},{28,20},{9,1},{13,5},{17,9},{2... | collective-permute-start | bytes 1671176 | tf_op jit(solution)/shard_map/ppermute | solution.py:171
  194.9 35.7 %collective-permute-start.34 = (bf16[2,2,128,1024]{3,2,0,1:T(8,128)(2,1)S(1)}, bf16[2,2,128,1024]{3,2,0,1:T(8,128)(2,1)S(1)}, u32[]{:S(2)}, u32[]{:S(2)}) collective-permute-start(bf16[2,2,128,1024]{3,2,0,1:T(8,128)(2,1)S(1)} %copy.17), channel_id=1, source_target_pairs={{0,1},{1,0},{2,3},{3,2},{4,5},{5,4},{6,7},{7,6},{8,9},{9,8},{10,11... | collective-permute-start | bytes 3145736 | tf_op jit(solution)/shard_map/ppermute | solution.py:131
  198.4 17.1 %collective-permute-start.29 = (bf16[2176,128]{1,0:T(8,128)(2,1)S(1)}, bf16[2176,128]{1,0:T(8,128)(2,1)S(1)}, u32[]{:S(2)}, u32[]{:S(2)}) collective-permute-start(bf16[2176,128]{1,0:T(8,128)(2,1)S(1)} %collective-permute-done.28.refs_6_), channel_id=1, source_target_pairs={{8,16},{12,20},{16,24},{20,28},{9,17},{13,21},{17,25},{21,29},{10,... | collective-permute-start | bytes 1671176 | tf_op jit(solution)/shard_map/ppermute | solution.py:171
  200.1 27.7 %collective-permute-start.30 = (bf16[2176,128]{1,0:T(8,128)(2,1)S(1)}, bf16[2176,128]{1,0:T(8,128)(2,1)S(1)}, u32[]{:S(2)}, u32[]{:S(2)}) collective-permute-start(bf16[2176,128]{1,0:T(8,128)(2,1)S(1)} %collective-permute-done.27.refs_1_), channel_id=1, source_target_pairs={{8,0},{12,4},{16,8},{20,12},{9,1},{13,5},{17,9},{21,13},{10,2},{14... | collective-permute-start | bytes 1671176 | tf_op jit(solution)/shard_map/ppermute | solution.py:171
  248.9 15.8 %collective-permute-start.36 = (bf16[512,1024]{1,0:T(8,128)(2,1)S(1)}, bf16[512,1024]{1,0:T(8,128)(2,1)S(1)}, u32[]{:S(2)}, u32[]{:S(2)}) collective-permute-start(bf16[512,1024]{1,0:T(8,128)(2,1)S(1)} %project_back.2), channel_id=1, source_target_pairs={{0,1},{1,0},{2,3},{3,2},{4,5},{5,4},{6,7},{7,6},{8,9},{9,8},{10,11... | collective-permute-start | bytes 3145736 | tf_op jit(solution)/shard_map/ppermute | solution.py:131
  251.2 33.5 %collective-permute-start.40 = (bf16[512,512]{1,0:T(8,128)(2,1)S(1)}, bf16[512,512]{1,0:T(8,128)(2,1)S(1)}, u32[]{:S(2)}, u32[]{:S(2)}) collective-permute-start(bf16[512,512]{1,0:T(8,128)(2,1)S(1)} %get-tuple-element.73), channel_id=1, source_target_pairs={{0,4},{4,0},{8,12},{12,8},{16,20},{20,16},{24,28},{28,24},{1,5},{5... | collective-permute-start | bytes 1572872 | tf_op jit(solution)/shard_map/ppermute | solution.py:131
  268.1 16.4 %collective-permute-start.38 = (bf16[128,1024]{1,0:T(8,128)(2,1)S(1)}, bf16[128,1024]{1,0:T(8,128)(2,1)S(1)}, u32[]{:S(2)}, u32[]{:S(2)}) collective-permute-start(bf16[128,1024]{1,0:T(8,128)(2,1)S(1)} %get-tuple-element.105), channel_id=1, source_target_pairs={{0,4},{4,0},{8,12},{12,8},{16,20},{20,16},{24,28},{28,24},{1,5},{5... | collective-permute-start | bytes 786440 | tf_op jit(solution)/shard_map/ppermute | solution.py:131
  273.9 25.9 %collective-permute-start.45 = (bf16[512,512]{1,0:T(8,128)(2,1)}, bf16[512,512]{1,0:T(8,128)(2,1)S(1)}, u32[]{:S(2)}, u32[]{:S(2)}) collective-permute-start(bf16[512,512]{1,0:T(8,128)(2,1)} %get-tuple-element.80), channel_id=1, source_target_pairs={{0,4},{4,0},{8,12},{12,8},{16,20},{20,16},{24,28},{28,24},{1,5},{5... | collective-permute-start | bytes 1572872 | tf_op jit(solution)/shard_map/ppermute | solution.py:131
  284.7 16.8 %collective-permute-start.44 = (bf16[128,1024]{1,0:T(8,128)(2,1)S(1)}, bf16[128,1024]{1,0:T(8,128)(2,1)S(1)}, u32[]{:S(2)}, u32[]{:S(2)}) collective-permute-start(bf16[128,1024]{1,0:T(8,128)(2,1)S(1)} %add_add_fusion), channel_id=1, source_target_pairs={{0,0},{8,1},{16,2},{24,3},{4,4},{12,5},{20,6},{28,7},{2,8},{10,9},... | collective-permute-start | bytes 786440 | tf_op jit(solution)/shard_map/ppermute | solution.py:146
  (42 other events, 514.6 us)

commit v8 on v7

--- a/solution.py
+++ b/solution.py
@@ -902,6 +902,9 @@
     total, k_given, mixed_out = lax.optimization_barrier((total, k_given, mixed_out))
     v_given = flip(v_sent, "seq", 1)
     given_taps = flip(after(half_taps, v_sent), "seq", 1)
+    for index, given in enumerate((q_given, k_given)):
+        in_kept = take_in_half(place, in_kept, given, index)
+    in_kept, given_taps = lax.optimization_barrier((in_kept, given_taps))
     grad_tokens = trade_places(total.astype(bf16), True)
     grad_filters = jnp.where(
         pair == 0,
@@ -909,8 +912,7 @@
         jnp.concatenate([given_taps, half_taps], 0),
     ).astype(f32)
     grad_out_weight = take_out_half(place, out_kept, out_given)
-    for index, given in enumerate((q_given, k_given, v_given)):
-        in_kept = take_in_half(place, in_kept, given, index)
+    in_kept = take_in_half(place, in_kept, v_given, 2)
     return (mixed_out, grad_tokens, in_kept, grad_out_weight, grad_filters)
 
 

time: 304 us -> 303 us (level)
  no operation moved by 1% of the time
where the time goes in v8:
time: 303 us; the launch traced here: 301 us
  waiting for transfers between devices  132 us (44%)
  starting transfers between devices  89.2 us (29%)
  Pallas kernels  60.8 us (20%)
  local copies, waits for them, and re-layouts  10.1 us (3%)
  other arithmetic  7.99 us (3%)
    ppermute x19, waiting for transfers between devices, flip(): lax.ppermute(value, axis, [(i, i ^ bit) for i in range(lax.axis_size(axis...  68.8 us
    ppermute x18, starting transfers between devices, along_line(): return lax.ppermute(value, 'seq', pairs)  42.9 us
    ppermute x18, waiting for transfers between devices, along_line(): return lax.ppermute(value, 'seq', pairs)  37.3 us
    ppermute x3, starting transfers between devices, flip_both(): return lax.ppermute(value, ('seq', 'fsdp'), pairs)  21 us
    ppermute x19, starting transfers between devices, flip(): lax.ppermute(value, axis, [(i, i ^ bit) for i in range(lax.axis_size(axis...  16.7 us
    ppermute x3, waiting for transfers between devices, around(): lax.ppermute(value, 'seq', [(i, (i + 2 * by) % size) for i in range(size)])  15.4 us
    pallas_call x1, Pallas kernels, backward_filter(): pl.pallas_call(body, out_shape=jax.ShapeDtypeStruct((2 * tokens + taps, l...  13.6 us
    ppermute x3, waiting for transfers between devices, flip_both(): return lax.ppermute(value, ('seq', 'fsdp'), pairs)  10.4 us
  transfers between devices with their start and end apart: 47, of which 20 were waited for; matrix products, arithmetic and copies ran while one was open for 3% of the time, Pallas kernels for 16%

profile of v8, /device:TPU:0, one launch (start us, length us, event | category | flops | bytes accessed | tf_op | source)
XLA Modules:
  0.0 301.3 jit_solution(1212794209467164579)
XLA Ops:
  2.7 3.0 %collective-permute-start.4 = (bf16[2,512,512]{2,1,0:T(8,128)(2,1)S(1)}, bf16[2,512,512]{2,1,0:T(8,128)(2,1)S(1)}, u32[]{:S(2)}, u32[]{:S(2)}) collective-permute-start(bf16[2,512,512]{2,1,0:T(8,128)(2,1)S(1)} %pad_maximum_fusion.1), channel_id=1, source_target_pairs={{0,4},{4,0},{8,12},{12,8},{16,20},{20,16},{24,28},{28,24},{1,5},{5... | collective-permute-start | bytes 3145736 | tf_op jit(solution)/shard_map/ppermute | solution.py:131
  7.1 18.2 %collective-permute-start.3 = (bf16[128,1024]{1,0:T(8,128)(2,1)S(1)}, bf16[128,1024]{1,0:T(8,128)(2,1)S(1)}, u32[]{:S(2)}, u32[]{:S(2)}) collective-permute-start(bf16[128,1024]{1,0:T(8,128)(2,1)S(1)} %collective-permute-done), channel_id=1, source_target_pairs={{0,6},{1,7},{2,4},{3,5},{4,2},{5,3},{6,0},{7,1},{8,14},{9,15},{10,... | collective-permute-start | bytes 786440 | tf_op jit(solution)/shard_map/ppermute | solution.py:156
  27.6 6.4 %collective-permute-done.3 = bf16[128,1024]{1,0:T(8,128)(2,1)S(1)} collective-permute-done((bf16[128,1024]{1,0:T(8,128)(2,1)S(1)}, bf16[128,1024]{1,0:T(8,128)(2,1)S(1)}, u32[]{:S(2)}, u32[]{:S(2)}) %collective-permute-start.3) | collective-permute-done | bytes 262176 | tf_op jit(solution)/shard_map/ppermute | solution.py:156
  34.0 6.1 %collective-permute-done.2 = bf16[128,1024]{1,0:T(8,128)(2,1)S(1)} collective-permute-done((bf16[128,1024]{1,0:T(8,128)(2,1)S(1)}, bf16[128,1024]{1,0:T(8,128)(2,1)S(1)}, u32[]{:S(2)}, u32[]{:S(2)}) %collective-permute-start.2) | collective-permute-done | bytes 262176 | tf_op jit(solution)/shard_map/ppermute | solution.py:131
  47.9 4.5 %project_pair.2.blocks_ref = bf16[4,2,1024,128]{3,2,1,0:T(8,128)(2,1)S(1)} custom-call(s32[2]{0:T(128)S(1)} %pad_add_fusion.place_ref, bf16[2,2,128,1024]{3,2,1,0:T(8,128)(2,1)S(1)} %bitcast.64, bf16[2,2,128,1024]{3,2,1,0:T(8,128)(2,1)S(1)} %collective-permute-done.6.refs_1_.refs_3_.refs_7_.refs_9_.own_far.other_far, bf16[2,2,128,1024]{3,2,1,0:T(8,128)(2,1)S(1)} %bitcast.65, ...), custom_call_target="tpu_custom_call" | custom-call | flops 2147483648 | bytes 8388608 | tf_op jit(solution)/shard_map/project_pair/pallas_call | solution.py:253
  53.4 5.8 %collective-permute-start.7 = (bf16[2,1024,128]{2,1,0:T(8,128)(2,1)S(1)}, bf16[2,1024,128]{2,1,0:T(8,128)(2,1)S(1)}, u32[]{:S(2)}, u32[]{:S(2)}) collective-permute-start(bf16[2,1024,128]{2,1,0:T(8,128)(2,1)S(1)} %get-tuple-element.106), channel_id=1, source_target_pairs={{0,8},{4,12},{1,9},{5,13},{2,10},{6,14},{3,11},{7,15}} | collective-permute-start | bytes 1572872 | tf_op jit(solution)/shard_map/ppermute | solution.py:171
  60.6 17.7 %collective-permute-done.11 = bf16[128,1024]{1,0:T(8,128)(2,1)S(1)} collective-permute-done((bf16[128,1024]{1,0:T(8,128)(2,1)S(1)}, bf16[128,1024]{1,0:T(8,128)(2,1)S(1)}, u32[]{:S(2)}, u32[]{:S(2)}) %collective-permute-start.11) | collective-permute-done | bytes 262176 | tf_op jit(solution)/shard_map/ppermute | solution.py:131
  81.2 4.4 %project_pair.3.blocks_ref = bf16[4,2,1024,128]{3,2,1,0:T(8,128)(2,1)S(1)} custom-call(s32[2]{0:T(128)S(1)} %pad_add_fusion.place_ref, bf16[2,2,128,1024]{3,2,1,0:T(8,128)(2,1)S(1)} %bitcast.68, bf16[2,2,128,1024]{3,2,1,0:T(8,128)(2,1)S(1)} %collective-permute-done.6.refs_1_.refs_3_.refs_7_.refs_9_.own_far.other_far, bf16[2,2,128,1024]{3,2,1,0:T(8,128)(2,1)S(1)} %bitcast.69, ...), custom_call_target="tpu_custom_call" | custom-call | flops 2147483648 | bytes 8388608 | tf_op jit(solution)/shard_map/project_pair/pallas_call | solution.py:253
  88.3 5.7 %collective-permute-start.14 = (bf16[2,1024,128]{2,1,0:T(8,128)(2,1)}, bf16[2,1024,128]{2,1,0:T(8,128)(2,1)}, u32[]{:S(2)}, u32[]{:S(2)}) collective-permute-start(bf16[2,1024,128]{2,1,0:T(8,128)(2,1)} %get-tuple-element.104), channel_id=1, source_target_pairs={{0,8},{4,12},{1,9},{5,13},{2,10},{6,14},{3,11},{7,15}} | collective-permute-start | bytes 1572872 | tf_op jit(solution)/shard_map/ppermute | solution.py:171
  98.8 7.0 %collective-permute-done.14 = bf16[2,1024,128]{2,1,0:T(8,128)(2,1)} collective-permute-done((bf16[2,1024,128]{2,1,0:T(8,128)(2,1)}, bf16[2,1024,128]{2,1,0:T(8,128)(2,1)}, u32[]{:S(2)}, u32[]{:S(2)}) %collective-permute-start.14) | collective-permute-done | bytes 524320 | tf_op jit(solution)/shard_map/ppermute | solution.py:171
  108.3 5.0 %collective-permute-start.15 = (bf16[2,1024,128]{2,1,0:T(8,128)(2,1)S(1)}, bf16[2,1024,128]{2,1,0:T(8,128)(2,1)S(1)}, u32[]{:S(2)}, u32[]{:S(2)}) collective-permute-start(bf16[2,1024,128]{2,1,0:T(8,128)(2,1)S(1)} %get-tuple-element.102), channel_id=1, source_target_pairs={{0,8},{4,12},{8,16},{12,20},{1,9},{5,13},{9,17},{13,21},{2,10},{6,... | collective-permute-start | bytes 1572872 | tf_op jit(solution)/shard_map/ppermute | solution.py:171
  113.3 3.7 %collective-permute-done.20 = bf16[2,1024,128]{2,1,0:T(8,128)(2,1)} collective-permute-done((bf16[2,1024,128]{2,1,0:T(8,128)(2,1)S(1)}, bf16[2,1024,128]{2,1,0:T(8,128)(2,1)}, u32[]{:S(2)}, u32[]{:S(2)}) %collective-permute-start.20) | collective-permute-done | bytes 524320 | tf_op jit(solution)/shard_map/ppermute | solution.py:171
  119.7 5.2 %collective-permute-start.21 = (bf16[2,1024,128]{2,1,0:T(8,128)(2,1)S(1)}, bf16[2,1024,128]{2,1,0:T(8,128)(2,1)S(1)}, u32[]{:S(2)}, u32[]{:S(2)}) collective-permute-start(bf16[2,1024,128]{2,1,0:T(8,128)(2,1)S(1)} %get-tuple-element.96), channel_id=1, source_target_pairs={{0,8},{4,12},{8,16},{12,20},{16,24},{20,28},{1,9},{5,13},{9,17},{1... | collective-permute-start | bytes 1572872 | tf_op jit(solution)/shard_map/ppermute | solution.py:171
  124.9 3.2 %collective-permute-done.15 = bf16[2,1024,128]{2,1,0:T(8,128)(2,1)S(1)} collective-permute-done((bf16[2,1024,128]{2,1,0:T(8,128)(2,1)S(1)}, bf16[2,1024,128]{2,1,0:T(8,128)(2,1)S(1)}, u32[]{:S(2)}, u32[]{:S(2)}) %collective-permute-start.15) | collective-permute-done | bytes 524320 | tf_op jit(solution)/shard_map/ppermute | solution.py:171
  129.8 5.0 %collective-permute-start.16 = (bf16[2,1024,128]{2,1,0:T(8,128)(2,1)S(1)}, bf16[2,1024,128]{2,1,0:T(8,128)(2,1)S(1)}, u32[]{:S(2)}, u32[]{:S(2)}) collective-permute-start(bf16[2,1024,128]{2,1,0:T(8,128)(2,1)S(1)} %get-tuple-element.100), channel_id=1, source_target_pairs={{0,8},{4,12},{8,16},{12,20},{16,24},{20,28},{1,9},{5,13},{9,17},{1... | collective-permute-start | bytes 1572872 | tf_op jit(solution)/shard_map/ppermute | solution.py:171
  134.8 4.6 %collective-permute-done.21.refs_0_ = bf16[2,1024,128]{2,1,0:T(8,128)(2,1)S(1)} collective-permute-done((bf16[2,1024,128]{2,1,0:T(8,128)(2,1)S(1)}, bf16[2,1024,128]{2,1,0:T(8,128)(2,1)S(1)}, u32[]{:S(2)}, u32[]{:S(2)}) %collective-permute-start.21) | collective-permute-done | bytes 524320 | tf_op jit(solution)/shard_map/ppermute | solution.py:171
  139.4 8.3 %forward_filter.1 = (bf16[2,1024,128]{2,1,0:T(8,128)(2,1)S(1)}, bf16[1024,128]{1,0:T(8,128)(2,1)S(1)}, f32[1024,128]{1,0:T(8,128)S(1)}) custom-call(s32[8]{0:T(128)S(1)} %fusion.14.order_ref, bf16[4,2,1024,128]{3,2,1,0:T(8,128)(2,1)S(1)} %copy-done.16, bf16[2,1024,128]{2,1,0:T(8,128)(2,1)S(1)} %collective-permute-done.21.refs_0_, ...), custom_call_target="tpu_custom_call" | custom-call | flops 6710886400 | bytes 1572864 | tf_op jit(solution)/shard_map/forward_filter/pallas_call | solution.py:341
  153.7 2.8 collective-permute-start.24
  156.6 13.6 %backward_filter.1.refs_0_ = bf16[2176,128]{1,0:T(8,128)(2,1)S(1)} custom-call(s32[8]{0:T(128)S(1)} %fusion.14.order_ref, bf16[1024,128]{1,0:T(8,128)(2,1)S(1)} %get-tuple-element.61.grad_ref, bf16[2,1024,128]{2,1,0:T(8,128)(2,1)S(1)} %get-tuple-element.62.kv_ref, bf16[1024,128]{1,0:T(8,128)(2,1)S(1)} %get-tuple-element.63.signal_ref, ...), custom_call_target="tpu_custom_call" | custom-call | flops 13421772800 | bytes 1572864 | tf_op jit(solution)/shard_map/backward_filter/pallas_call | solution.py:484
  173.0 15.3 %collective-permute-done.25.refs_2_ = bf16[2048,128]{1,0:T(8,128)(2,1)S(1)} collective-permute-done((bf16[2048,128]{1,0:T(8,128)(2,1)S(1)}, bf16[2048,128]{1,0:T(8,128)(2,1)S(1)}, u32[]{:S(2)}, u32[]{:S(2)}) %collective-permute-start.25) | collective-permute-done | bytes 524320 | tf_op jit(solution)/shard_map/ppermute | solution.py:197
  189.5 2.9 out_gradient.1
  195.0 3.4 %collective-permute-done.28.refs_6_ = bf16[2176,128]{1,0:T(8,128)(2,1)S(1)} collective-permute-done((bf16[2176,128]{1,0:T(8,128)(2,1)S(1)}, bf16[2176,128]{1,0:T(8,128)(2,1)S(1)}, u32[]{:S(2)}, u32[]{:S(2)}) %collective-permute-start.28) | collective-permute-done | bytes 557088 | tf_op jit(solution)/shard_map/ppermute | solution.py:171
  202.3 3.0 in_gradient.3
  205.2 10.3 %collective-permute-done.31.piece_ref = bf16[512,512]{1,0:T(8,128)(2,1)S(1)} collective-permute-done((bf16[512,512]{1,0:T(8,128)(2,1)S(1)}, bf16[512,512]{1,0:T(8,128)(2,1)S(1)}, u32[]{:S(2)}, u32[]{:S(2)}) %collective-permute-start.31) | collective-permute-done | bytes 524320 | tf_op jit(solution)/shard_map/ppermute | solution.py:131
  215.5 12.3 %collective-permute-done.30.refs_3_ = bf16[2176,128]{1,0:T(8,128)(2,1)S(1)} collective-permute-done((bf16[2176,128]{1,0:T(8,128)(2,1)S(1)}, bf16[2176,128]{1,0:T(8,128)(2,1)S(1)}, u32[]{:S(2)}, u32[]{:S(2)}) %collective-permute-start.30) | collective-permute-done | bytes 557088 | tf_op jit(solution)/shard_map/ppermute | solution.py:171
  231.1 10.1 %collective-permute-done.35.piece_ref = bf16[512,512]{1,0:T(8,128)(2,1)S(1)} collective-permute-done((bf16[512,512]{1,0:T(8,128)(2,1)S(1)}, bf16[512,512]{1,0:T(8,128)(2,1)S(1)}, u32[]{:S(2)}, u32[]{:S(2)}) %collective-permute-start.35) | collective-permute-done | bytes 524320 | tf_op jit(solution)/shard_map/ppermute | solution.py:131
  243.2 3.0 in_gradient.4
  254.6 9.2 %collective-permute-done.41 = bf16[2,128,1024]{2,1,0:T(8,128)(2,1)S(1)} collective-permute-done((bf16[2,128,1024]{2,1,0:T(8,128)(2,1)S(1)}, bf16[2,128,1024]{2,1,0:T(8,128)(2,1)S(1)}, u32[]{:S(2)}, u32[]{:S(2)}) %collective-permute-start.41) | collective-permute-done | bytes 524320 | tf_op jit(solution)/shard_map/ppermute | solution.py:131
  268.7 3.1 %in_gradient.5 = (f32[3,512,1024]{2,1,0:T(8,128)}, bf16[512,512]{1,0:T(8,128)(2,1)}) custom-call(s32[2]{0:T(128)S(1)} %pad_add_fusion.place_ref, bf16[2,2,128,1024]{3,2,1,0:T(8,128)(2,1)S(1)} %bitcast.74, bf16[2,2,128,1024]{3,2,1,0:T(8,128)(2,1)S(1)} %collective-permute-done.6.refs_1_.refs_3_.refs_7_.refs_9_.own_far.other_far, ...), custom_call_target="tpu_custom_call", output_to_operand_aliasing={{0}: (6, {})} | custom-call | flops 1073741824 | bytes 4194304 | tf_op jit(solution)/shard_map/in_gradient/pallas_call | solution.py:676
  275.6 4.0 %collective-permute-done.39 = bf16[128,1024]{1,0:T(8,128)(2,1)S(1)} collective-permute-done((bf16[128,1024]{1,0:T(8,128)(2,1)S(1)}, bf16[128,1024]{1,0:T(8,128)(2,1)S(1)}, u32[]{:S(2)}, u32[]{:S(2)}) %collective-permute-start.39) | collective-permute-done | bytes 262176 | tf_op jit(solution)/shard_map/ppermute | solution.py:156
  279.6 4.8 %collective-permute-done.38 = bf16[128,1024]{1,0:T(8,128)(2,1)S(1)} collective-permute-done((bf16[128,1024]{1,0:T(8,128)(2,1)S(1)}, bf16[128,1024]{1,0:T(8,128)(2,1)S(1)}, u32[]{:S(2)}, u32[]{:S(2)}) %collective-permute-start.38) | collective-permute-done | bytes 262176 | tf_op jit(solution)/shard_map/ppermute | solution.py:131
  291.5 5.9 %collective-permute-done.46 = bf16[512,128]{1,0:T(8,128)(2,1)S(1)} collective-permute-done((bf16[512,128]{1,0:T(8,128)(2,1)S(1)}, bf16[512,128]{1,0:T(8,128)(2,1)S(1)}, u32[]{:S(2)}, u32[]{:S(2)}) %collective-permute-start.46) | collective-permute-done | bytes 131104 | tf_op jit(solution)/shard_map/ppermute | solution.py:131
  (167 shorter events, 82.3 us)
Async XLA Ops:
  2.7 37.6 %collective-permute-start.4 = (bf16[2,512,512]{2,1,0:T(8,128)(2,1)S(1)}, bf16[2,512,512]{2,1,0:T(8,128)(2,1)S(1)}, u32[]{:S(2)}, u32[]{:S(2)}) collective-permute-start(bf16[2,512,512]{2,1,0:T(8,128)(2,1)S(1)} %pad_maximum_fusion.1), channel_id=1, source_target_pairs={{0,4},{4,0},{8,12},{12,8},{16,20},{20,16},{24,28},{28,24},{1,5},{5... | collective-permute-start | bytes 3145736 | tf_op jit(solution)/shard_map/ppermute | solution.py:131
  6.4 33.8 %collective-permute-start.5 = (bf16[128,1024]{1,0:T(8,128)(2,1)S(1)}, bf16[128,1024]{1,0:T(8,128)(2,1)S(1)}, u32[]{:S(2)}, u32[]{:S(2)}) collective-permute-start(bf16[128,1024]{1,0:T(8,128)(2,1)S(1)} %copy-done.25), channel_id=1, source_target_pairs={{0,0},{1,8},{2,16},{3,24},{4,4},{5,12},{6,20},{7,28},{8,2},{9,10},... | collective-permute-start | bytes 786440 | tf_op jit(solution)/shard_map/ppermute | solution.py:146
  7.1 26.9 %collective-permute-start.3 = (bf16[128,1024]{1,0:T(8,128)(2,1)S(1)}, bf16[128,1024]{1,0:T(8,128)(2,1)S(1)}, u32[]{:S(2)}, u32[]{:S(2)}) collective-permute-start(bf16[128,1024]{1,0:T(8,128)(2,1)S(1)} %collective-permute-done), channel_id=1, source_target_pairs={{0,6},{1,7},{2,4},{3,5},{4,2},{5,3},{6,0},{7,1},{8,14},{9,15},{10,... | collective-permute-start | bytes 786440 | tf_op jit(solution)/shard_map/ppermute | solution.py:156
  25.3 14.8 %collective-permute-start.2 = (bf16[128,1024]{1,0:T(8,128)(2,1)S(1)}, bf16[128,1024]{1,0:T(8,128)(2,1)S(1)}, u32[]{:S(2)}, u32[]{:S(2)}) collective-permute-start(bf16[128,1024]{1,0:T(8,128)(2,1)S(1)} %collective-permute-done), channel_id=1, source_target_pairs={{0,4},{4,0},{8,12},{12,8},{16,20},{20,16},{24,28},{28,24},{1,5},{5... | collective-permute-start | bytes 786440 | tf_op jit(solution)/shard_map/ppermute | solution.py:131
  41.3 37.2 %collective-permute-start.9 = (bf16[2,512,512]{2,1,0:T(8,128)(2,1)}, bf16[2,512,512]{2,1,0:T(8,128)(2,1)S(1)}, u32[]{:S(2)}, u32[]{:S(2)}) collective-permute-start(bf16[2,512,512]{2,1,0:T(8,128)(2,1)} %pad_maximum_fusion.2), channel_id=1, source_target_pairs={{0,4},{4,0},{8,12},{12,8},{16,20},{20,16},{24,28},{28,24},{1,5},{5... | collective-permute-start | bytes 3145736 | tf_op jit(solution)/shard_map/ppermute | solution.py:131
  43.1 16.8 %collective-permute-start.12 = (bf16[128,1024]{1,0:T(8,128)(2,1)S(1)}, bf16[128,1024]{1,0:T(8,128)(2,1)S(1)}, u32[]{:S(2)}, u32[]{:S(2)}) collective-permute-start(bf16[128,1024]{1,0:T(8,128)(2,1)S(1)} %collective-permute-done.5), channel_id=1, source_target_pairs={{0,6},{1,7},{2,4},{3,5},{4,2},{5,3},{6,0},{7,1},{8,14},{9,15},{10,... | collective-permute-start | bytes 786440 | tf_op jit(solution)/shard_map/ppermute | solution.py:156
  52.6 25.9 %collective-permute-start.8 = (bf16[2,1024,128]{2,1,0:T(8,128)(2,1)S(1)}, bf16[2,1024,128]{2,1,0:T(8,128)(2,1)S(1)}, u32[]{:S(2)}, u32[]{:S(2)}) collective-permute-start(bf16[2,1024,128]{2,1,0:T(8,128)(2,1)S(1)} %get-tuple-element.105), channel_id=1, source_target_pairs={{24,16},{28,20},{25,17},{29,21},{26,18},{30,22},{27,19},{31,23}} | collective-permute-start | bytes 1572872 | tf_op jit(solution)/shard_map/ppermute | solution.py:171
  53.4 25.1 %collective-permute-start.7 = (bf16[2,1024,128]{2,1,0:T(8,128)(2,1)S(1)}, bf16[2,1024,128]{2,1,0:T(8,128)(2,1)S(1)}, u32[]{:S(2)}, u32[]{:S(2)}) collective-permute-start(bf16[2,1024,128]{2,1,0:T(8,128)(2,1)S(1)} %get-tuple-element.106), channel_id=1, source_target_pairs={{0,8},{4,12},{1,9},{5,13},{2,10},{6,14},{3,11},{7,15}} | collective-permute-start | bytes 1572872 | tf_op jit(solution)/shard_map/ppermute | solution.py:171
  59.2 19.1 %collective-permute-start.11 = (bf16[128,1024]{1,0:T(8,128)(2,1)S(1)}, bf16[128,1024]{1,0:T(8,128)(2,1)S(1)}, u32[]{:S(2)}, u32[]{:S(2)}) collective-permute-start(bf16[128,1024]{1,0:T(8,128)(2,1)S(1)} %collective-permute-done.5), channel_id=1, source_target_pairs={{0,4},{4,0},{8,12},{12,8},{16,20},{20,16},{24,28},{28,24},{1,5},{5... | collective-permute-start | bytes 786440 | tf_op jit(solution)/shard_map/ppermute | solution.py:131
  59.9 18.4 %collective-permute-start.10 = (bf16[128,1024]{1,0:T(8,128)(2,1)S(1)}, bf16[128,1024]{1,0:T(8,128)(2,1)S(1)}, u32[]{:S(2)}, u32[]{:S(2)}) collective-permute-start(bf16[128,1024]{1,0:T(8,128)(2,1)S(1)} %collective-permute-done.5), channel_id=1, source_target_pairs={{0,2},{1,3},{2,0},{3,1},{4,6},{5,7},{6,4},{7,5},{8,10},{9,11},{10,... | collective-permute-start | bytes 786440 | tf_op jit(solution)/shard_map/ppermute | solution.py:131
  88.3 17.5 %collective-permute-start.14 = (bf16[2,1024,128]{2,1,0:T(8,128)(2,1)}, bf16[2,1024,128]{2,1,0:T(8,128)(2,1)}, u32[]{:S(2)}, u32[]{:S(2)}) collective-permute-start(bf16[2,1024,128]{2,1,0:T(8,128)(2,1)} %get-tuple-element.104), channel_id=1, source_target_pairs={{0,8},{4,12},{1,9},{5,13},{2,10},{6,14},{3,11},{7,15}} | collective-permute-start | bytes 1572872 | tf_op jit(solution)/shard_map/ppermute | solution.py:171
  95.1 18.2 %collective-permute-start.22 = (bf16[2,1024,128]{2,1,0:T(8,128)(2,1)}, bf16[2,1024,128]{2,1,0:T(8,128)(2,1)}, u32[]{:S(2)}, u32[]{:S(2)}) collective-permute-start(bf16[2,1024,128]{2,1,0:T(8,128)(2,1)} %get-tuple-element.97), channel_id=1, source_target_pairs={{16,8},{20,12},{24,16},{28,20},{17,9},{21,13},{25,17},{29,21},{18,... | collective-permute-start | bytes 1572872 | tf_op jit(solution)/shard_map/ppermute | solution.py:171
  96.5 20.4 %collective-permute-start.20 = (bf16[2,1024,128]{2,1,0:T(8,128)(2,1)S(1)}, bf16[2,1024,128]{2,1,0:T(8,128)(2,1)}, u32[]{:S(2)}, u32[]{:S(2)}) collective-permute-start(bf16[2,1024,128]{2,1,0:T(8,128)(2,1)S(1)} %get-tuple-element.98), channel_id=1, source_target_pairs={{0,8},{4,12},{8,16},{12,20},{1,9},{5,13},{9,17},{13,21},{2,10},{6,... | collective-permute-start | bytes 1572872 | tf_op jit(solution)/shard_map/ppermute | solution.py:171
  107.4 17.5 %collective-permute-start.18 = (bf16[2,1024,128]{2,1,0:T(8,128)(2,1)S(1)}, bf16[2,1024,128]{2,1,0:T(8,128)(2,1)S(1)}, u32[]{:S(2)}, u32[]{:S(2)}) collective-permute-start(bf16[2,1024,128]{2,1,0:T(8,128)(2,1)S(1)} %get-tuple-element.101), channel_id=1, source_target_pairs={{16,8},{20,12},{24,16},{28,20},{17,9},{21,13},{25,17},{29,21},{18,... | collective-permute-start | bytes 1572872 | tf_op jit(solution)/shard_map/ppermute | solution.py:171
  108.3 19.9 %collective-permute-start.15 = (bf16[2,1024,128]{2,1,0:T(8,128)(2,1)S(1)}, bf16[2,1024,128]{2,1,0:T(8,128)(2,1)S(1)}, u32[]{:S(2)}, u32[]{:S(2)}) collective-permute-start(bf16[2,1024,128]{2,1,0:T(8,128)(2,1)S(1)} %get-tuple-element.102), channel_id=1, source_target_pairs={{0,8},{4,12},{8,16},{12,20},{1,9},{5,13},{9,17},{13,21},{2,10},{6,... | collective-permute-start | bytes 1572872 | tf_op jit(solution)/shard_map/ppermute | solution.py:171
  118.4 16.4 %collective-permute-start.23 = (bf16[2,1024,128]{2,1,0:T(8,128)(2,1)S(1)}, bf16[2,1024,128]{2,1,0:T(8,128)(2,1)S(1)}, u32[]{:S(2)}, u32[]{:S(2)}) collective-permute-start(bf16[2,1024,128]{2,1,0:T(8,128)(2,1)S(1)} %get-tuple-element.95), channel_id=1, source_target_pairs={{8,0},{12,4},{16,8},{20,12},{24,16},{28,20},{9,1},{13,5},{17,9},{2... | collective-permute-start | bytes 1572872 | tf_op jit(solution)/shard_map/ppermute | solution.py:171
  119.7 19.7 %collective-permute-start.21 = (bf16[2,1024,128]{2,1,0:T(8,128)(2,1)S(1)}, bf16[2,1024,128]{2,1,0:T(8,128)(2,1)S(1)}, u32[]{:S(2)}, u32[]{:S(2)}) collective-permute-start(bf16[2,1024,128]{2,1,0:T(8,128)(2,1)S(1)} %get-tuple-element.96), channel_id=1, source_target_pairs={{0,8},{4,12},{8,16},{12,20},{16,24},{20,28},{1,9},{5,13},{9,17},{1... | collective-permute-start | bytes 1572872 | tf_op jit(solution)/shard_map/ppermute | solution.py:171
  128.5 19.3 %collective-permute-start.19 = (bf16[2,1024,128]{2,1,0:T(8,128)(2,1)S(1)}, bf16[2,1024,128]{2,1,0:T(8,128)(2,1)S(1)}, u32[]{:S(2)}, u32[]{:S(2)}) collective-permute-start(bf16[2,1024,128]{2,1,0:T(8,128)(2,1)S(1)} %get-tuple-element.99), channel_id=1, source_target_pairs={{8,0},{12,4},{16,8},{20,12},{24,16},{28,20},{9,1},{13,5},{17,9},{2... | collective-permute-start | bytes 1572872 | tf_op jit(solution)/shard_map/ppermute | solution.py:171
  129.8 20.1 %collective-permute-start.16 = (bf16[2,1024,128]{2,1,0:T(8,128)(2,1)S(1)}, bf16[2,1024,128]{2,1,0:T(8,128)(2,1)S(1)}, u32[]{:S(2)}, u32[]{:S(2)}) collective-permute-start(bf16[2,1024,128]{2,1,0:T(8,128)(2,1)S(1)} %get-tuple-element.100), channel_id=1, source_target_pairs={{0,8},{4,12},{8,16},{12,20},{16,24},{20,28},{1,9},{5,13},{9,17},{1... | collective-permute-start | bytes 1572872 | tf_op jit(solution)/shard_map/ppermute | solution.py:171
  150.7 22.3 %collective-permute-start.26 = (bf16[2048,128]{1,0:T(8,128)(2,1)S(1)}, bf16[2048,128]{1,0:T(8,128)(2,1)S(1)}, u32[]{:S(2)}, u32[]{:S(2)}) collective-permute-start(bf16[2048,128]{1,0:T(8,128)(2,1)S(1)} %get-tuple-element.60.refs_0_), channel_id=1, source_target_pairs={{0,8},{4,12},{8,16},{12,20},{16,24},{20,28},{24,0},{28,4},{1,9},{5... | collective-permute-start | bytes 1572872 | tf_op jit(solution)/shard_map/ppermute | solution.py:197
  153.2 35.1 %collective-permute-start.25 = (bf16[2048,128]{1,0:T(8,128)(2,1)S(1)}, bf16[2048,128]{1,0:T(8,128)(2,1)S(1)}, u32[]{:S(2)}, u32[]{:S(2)}) collective-permute-start(bf16[2048,128]{1,0:T(8,128)(2,1)S(1)} %get-tuple-element.60.refs_0_), channel_id=1, source_target_pairs={{0,16},{4,20},{8,24},{12,28},{16,0},{20,4},{24,8},{28,12},{1,17},{... | collective-permute-start | bytes 1572872 | tf_op jit(solution)/shard_map/ppermute | solution.py:197
  153.7 34.6 %collective-permute-start.24 = (bf16[2048,128]{1,0:T(8,128)(2,1)S(1)}, bf16[2048,128]{1,0:T(8,128)(2,1)S(1)}, u32[]{:S(2)}, u32[]{:S(2)}) collective-permute-start(bf16[2048,128]{1,0:T(8,128)(2,1)S(1)} %get-tuple-element.60.refs_0_), channel_id=1, source_target_pairs={{0,24},{4,28},{8,0},{12,4},{16,8},{20,12},{24,16},{28,20},{1,25},{... | collective-permute-start | bytes 1572872 | tf_op jit(solution)/shard_map/ppermute | solution.py:197
  170.2 28.2 %collective-permute-start.28 = (bf16[2176,128]{1,0:T(8,128)(2,1)S(1)}, bf16[2176,128]{1,0:T(8,128)(2,1)S(1)}, u32[]{:S(2)}, u32[]{:S(2)}) collective-permute-start(bf16[2176,128]{1,0:T(8,128)(2,1)S(1)} %backward_filter.1.refs_0_), channel_id=1, source_target_pairs={{0,8},{4,12},{8,16},{12,20},{16,24},{20,28},{1,9},{5,13},{9,17},{1... | collective-permute-start | bytes 1671176 | tf_op jit(solution)/shard_map/ppermute | solution.py:171
  171.7 28.4 %collective-permute-start.27 = (bf16[2176,128]{1,0:T(8,128)(2,1)S(1)}, bf16[2176,128]{1,0:T(8,128)(2,1)S(1)}, u32[]{:S(2)}, u32[]{:S(2)}) collective-permute-start(bf16[2176,128]{1,0:T(8,128)(2,1)S(1)} %backward_filter.1.refs_0_), channel_id=1, source_target_pairs={{8,0},{12,4},{16,8},{20,12},{24,16},{28,20},{9,1},{13,5},{17,9},{2... | collective-permute-start | bytes 1671176 | tf_op jit(solution)/shard_map/ppermute | solution.py:171
  194.9 35.7 %collective-permute-start.34 = (bf16[2,2,128,1024]{3,2,0,1:T(8,128)(2,1)S(1)}, bf16[2,2,128,1024]{3,2,0,1:T(8,128)(2,1)S(1)}, u32[]{:S(2)}, u32[]{:S(2)}) collective-permute-start(bf16[2,2,128,1024]{3,2,0,1:T(8,128)(2,1)S(1)} %copy.17), channel_id=1, source_target_pairs={{0,1},{1,0},{2,3},{3,2},{4,5},{5,4},{6,7},{7,6},{8,9},{9,8},{10,11... | collective-permute-start | bytes 3145736 | tf_op jit(solution)/shard_map/ppermute | solution.py:131
  198.4 17.1 %collective-permute-start.29 = (bf16[2176,128]{1,0:T(8,128)(2,1)S(1)}, bf16[2176,128]{1,0:T(8,128)(2,1)S(1)}, u32[]{:S(2)}, u32[]{:S(2)}) collective-permute-start(bf16[2176,128]{1,0:T(8,128)(2,1)S(1)} %collective-permute-done.28.refs_6_), channel_id=1, source_target_pairs={{8,16},{12,20},{16,24},{20,28},{9,17},{13,21},{17,25},{21,29},{10,... | collective-permute-start | bytes 1671176 | tf_op jit(solution)/shard_map/ppermute | solution.py:171
  200.1 27.7 %collective-permute-start.30 = (bf16[2176,128]{1,0:T(8,128)(2,1)S(1)}, bf16[2176,128]{1,0:T(8,128)(2,1)S(1)}, u32[]{:S(2)}, u32[]{:S(2)}) collective-permute-start(bf16[2176,128]{1,0:T(8,128)(2,1)S(1)} %collective-permute-done.27.refs_1_), channel_id=1, source_target_pairs={{8,0},{12,4},{16,8},{20,12},{9,1},{13,5},{17,9},{21,13},{10,2},{14... | collective-permute-start | bytes 1671176 | tf_op jit(solution)/shard_map/ppermute | solution.py:171
  248.9 15.8 %collective-permute-start.36 = (bf16[512,1024]{1,0:T(8,128)(2,1)S(1)}, bf16[512,1024]{1,0:T(8,128)(2,1)S(1)}, u32[]{:S(2)}, u32[]{:S(2)}) collective-permute-start(bf16[512,1024]{1,0:T(8,128)(2,1)S(1)} %project_back.2), channel_id=1, source_target_pairs={{0,1},{1,0},{2,3},{3,2},{4,5},{5,4},{6,7},{7,6},{8,9},{9,8},{10,11... | collective-permute-start | bytes 3145736 | tf_op jit(solution)/shard_map/ppermute | solution.py:131
  251.2 33.5 %collective-permute-start.40 = (bf16[512,512]{1,0:T(8,128)(2,1)S(1)}, bf16[512,512]{1,0:T(8,128)(2,1)S(1)}, u32[]{:S(2)}, u32[]{:S(2)}) collective-permute-start(bf16[512,512]{1,0:T(8,128)(2,1)S(1)} %get-tuple-element.75), channel_id=1, source_target_pairs={{0,4},{4,0},{8,12},{12,8},{16,20},{20,16},{24,28},{28,24},{1,5},{5... | collective-permute-start | bytes 1572872 | tf_op jit(solution)/shard_map/ppermute | solution.py:131
  268.1 16.4 %collective-permute-start.38 = (bf16[128,1024]{1,0:T(8,128)(2,1)S(1)}, bf16[128,1024]{1,0:T(8,128)(2,1)S(1)}, u32[]{:S(2)}, u32[]{:S(2)}) collective-permute-start(bf16[128,1024]{1,0:T(8,128)(2,1)S(1)} %get-tuple-element.109), channel_id=1, source_target_pairs={{0,4},{4,0},{8,12},{12,8},{16,20},{20,16},{24,28},{28,24},{1,5},{5... | collective-permute-start | bytes 786440 | tf_op jit(solution)/shard_map/ppermute | solution.py:131
  273.9 23.5 %collective-permute-start.45 = (bf16[512,512]{1,0:T(8,128)(2,1)}, bf16[512,512]{1,0:T(8,128)(2,1)S(1)}, u32[]{:S(2)}, u32[]{:S(2)}) collective-permute-start(bf16[512,512]{1,0:T(8,128)(2,1)} %get-tuple-element.82), channel_id=1, source_target_pairs={{0,4},{4,0},{8,12},{12,8},{16,20},{20,16},{24,28},{28,24},{1,5},{5... | collective-permute-start | bytes 1572872 | tf_op jit(solution)/shard_map/ppermute | solution.py:131
  284.7 15.2 %collective-permute-start.44 = (bf16[128,1024]{1,0:T(8,128)(2,1)S(1)}, bf16[128,1024]{1,0:T(8,128)(2,1)S(1)}, u32[]{:S(2)}, u32[]{:S(2)}) collective-permute-start(bf16[128,1024]{1,0:T(8,128)(2,1)S(1)} %add_add_fusion), channel_id=1, source_target_pairs={{0,0},{8,1},{16,2},{24,3},{4,4},{12,5},{20,6},{28,7},{2,8},{10,9},... | collective-permute-start | bytes 786440 | tf_op jit(solution)/shard_map/ppermute | solution.py:146
  (42 other events, 507.1 us)
